TPU v7x, 32 devices: a whole 2x2x4 slice. The times are simulated.
32 devices in a mesh: dp: 8 (over y, x, core), tensor: 4 (over z).
Axes of the slice: x: 2, y: 2, z: 4, core: 2. Of those that a mesh axis runs over, the one named last changes fastest.
Arguments:
- tokens: bfloat16 [8, 1024, 1024], P('dp', 'tensor'), may hold values from -6 to 6
- segment_ids: int32 [8, 1024], P('dp'), may hold values from 0 to 128, as said below
- gain_attn: float32 [1024], replicated, may hold values from 0.5 to 1.5
- query_key_value_weight: bfloat16 [3, 1024, 1024], P(None, None, 'tensor'), may hold values from -0.25 to 0.25
- output_weight: bfloat16 [1024, 1024], P('tensor'), may hold values from -1.5 to 1.5
- gain_mlp: float32 [1024], replicated, may hold values from 0.5 to 1.5
- gate_up_weight: bfloat16 [2, 1024, 2624], P(None, None, 'tensor'), may hold values from -0.1875 to 0.1875
- down_weight: bfloat16 [2624, 1024], P('tensor'), may hold values from -0.25 to 0.25
- cotangent: bfloat16 [8, 1024, 1024], P('dp', 'tensor'), may hold values from -24 to 24
Outputs:
- layer_out: bfloat16 [8, 1024, 1024], P('dp', 'tensor')
- input_grad: bfloat16 [8, 1024, 1024], P('dp', 'tensor')
- grad_gain_attn: float32 [1024], replicated
- query_key_value_gradient: float32 [3, 1024, 1024], P(None, None, 'tensor')
- output_weight_gradient: float32 [1024, 1024], P('tensor')
- grad_gain_mlp: float32 [1024], replicated
- grad_gateup: float32 [2, 1024, 2624], P(None, None, 'tensor')
- down_weight_gradient: float32 [2624, 1024], P('tensor')
Inputs may be any that keep to these rules, and one draw needn't show every extreme that they name: `segment_ids`: segment ids never fall along a sequence and start at 0; each sequence holds one document of exactly 896 tokens, and every other token is a document of one token.
All inputs are finite; a program needn't handle non-finite values.
Results may differ from a plain program's by a relative error of at most 0.015.
Values may be sent and summed in bfloat16 or wider, within the bound.
No kernel may reach another device: no remote copies, remote signals or barrier semaphores. Data moves between devices by JAX's collectives and lax.ppermute only.
A program may use at most 128 MiB of HBM per device.

v0:
```python
import math

import jax
import jax.numpy as jnp
from jax import lax
from jax.sharding import PartitionSpec as P

HD = 64


epsilon = 1e-05
rope_base = 160000.0


def normalize(values):
    centered = values - jnp.mean(values, axis=-1, keepdims=True)
    variance = jnp.mean(centered * centered, axis=-1, keepdims=True)
    inverse = lax.rsqrt(variance + epsilon)
    return (centered * inverse, inverse)


def norm_back(grad, normal, inverse, gain):
    scaled = grad * gain
    return inverse * (
        scaled
        - jnp.mean(scaled, axis=-1, keepdims=True)
        - normal * jnp.mean(scaled * normal, axis=-1, keepdims=True)
    )


def rope_tables(segments):
    length = segments.shape[-1]
    before = jnp.sum((segments[..., None, :] < segments[..., :, None]).astype(jnp.int32), axis=-1)
    positions = jnp.arange(length, dtype=jnp.int32) - before
    half_size = HD // 2
    inverse = jnp.exp(jnp.arange(half_size, dtype=jnp.float32) * (-2.0 * math.log(rope_base) / HD))
    angles = positions.astype(jnp.float32)[..., None] * inverse
    angles = jnp.concatenate([angles, angles], axis=-1)
    return (jnp.cos(angles), jnp.sin(angles))


def rotate_half(values):
    half_size = values.shape[-1] // 2
    return jnp.concatenate([-values[..., half_size:], values[..., :half_size]], axis=-1)


def rotate_back(values):
    half_size = values.shape[-1] // 2
    return jnp.concatenate([values[..., half_size:], -values[..., :half_size]], axis=-1)


def apply_rope(values, cos_table, sin_table):
    return values * cos_table + rotate_half(values) * sin_table


def unrope(grad, cos_table, sin_table):
    return grad * cos_table + rotate_back(grad * sin_table)


def gated_unit(gate_proj, up_proj):
    return jax.nn.gelu(gate_proj, approximate=False) * up_proj


def on_device(
    tokens,
    segment_ids,
    gain_attn,
    query_key_value_weight,
    output_weight,
    gain_mlp,
    gate_up_weight,
    down_weight,
    cotangent,
):
    sequences, length = segment_ids.shape
    head_cols = query_key_value_weight.shape[2]
    head_count = head_cols // HD
    block_rows = min(512, length)
    per_row = length // block_rows
    blocks = sequences * per_row
    scale_factor = 1.0 / math.sqrt(HD)
    cos_table, sin_table = rope_tables(segment_ids)
    cos_heads = cos_table[:, :, None, :]
    sin_heads = sin_table[:, :, None, :]
    head_shape = (sequences, length, head_count, HD)
    token_f = tokens.astype(jnp.float32)
    normal_attn, inverse_attn = normalize(token_f)
    normed_attn = (normal_attn * gain_attn).astype(jnp.bfloat16)
    attention_row_block = lax.all_gather(normed_attn, "tensor", axis=1, tiled=True)
    projection_result = jnp.einsum(
        "uwk,ykb->yuwb",
        attention_row_block,
        query_key_value_weight,
        preferred_element_type=jnp.float32,
    )
    queries = apply_rope(projection_result[0].reshape(head_shape), cos_heads, sin_heads).astype(
        jnp.bfloat16
    )
    keys = apply_rope(projection_result[1].reshape(head_shape), cos_heads, sin_heads).astype(
        jnp.bfloat16
    )
    values = projection_result[2].reshape(head_shape).astype(jnp.bfloat16)
    query_blocks = queries.reshape(blocks, block_rows, head_count, HD)
    segment_blocks = segment_ids.reshape(blocks, block_rows)
    owners = jnp.arange(blocks, dtype=jnp.int32) // per_row

    def block_scores(query_block, segment_block, sequence):
        raw_scores = (
            jnp.einsum(
                "qhd,khd->hqk", query_block, keys[sequence], preferred_element_type=jnp.float32
            )
            * scale_factor
        )
        same_doc = segment_block[:, None] == segment_ids[sequence][None, :]
        return jnp.where(same_doc[None], raw_scores, -1000000000.0)

    def attend(inputs):
        query_block, segment_block, sequence = inputs
        scores = block_scores(query_block, segment_block, sequence)
        largest = jnp.max(scores, axis=-1, keepdims=True)
        weights = jnp.exp(scores - largest)
        row_total = jnp.sum(weights, axis=-1, keepdims=True)
        probabilities = (weights / row_total).astype(jnp.bfloat16)
        mixture = jnp.einsum(
            "hqk,khd->qhd", probabilities, values[sequence], preferred_element_type=jnp.float32
        )
        return (mixture, largest[..., 0] + jnp.log(row_total[..., 0]))

    mixture, log_totals = lax.map(attend, (query_blocks, segment_blocks, owners))
    attention_result = mixture.reshape(sequences, length, head_cols).astype(jnp.bfloat16)
    branch_share = jnp.einsum(
        "yog,gp->yop", attention_result, output_weight, preferred_element_type=jnp.float32
    )
    branch = lax.psum_scatter(branch_share, "tensor", scatter_dimension=1, tiled=True)
    hidden_state = token_f + branch
    normal_mlp, inverse_mlp = normalize(hidden_state)
    normed_mlp = (normal_mlp * gain_mlp).astype(jnp.bfloat16)
    feedforward_row_block = lax.all_gather(normed_mlp, "tensor", axis=1, tiled=True)
    gate_up_product = jnp.einsum(
        "vhw,twu->tvhu", feedforward_row_block, gate_up_weight, preferred_element_type=jnp.float32
    )
    activation_output, gated_back = jax.vjp(gated_unit, gate_up_product[0], gate_up_product[1])
    activation_output = activation_output.astype(jnp.bfloat16)
    feedforward_share = jnp.einsum(
        "xzu,ui->xzi", activation_output, down_weight, preferred_element_type=jnp.float32
    )
    mlp_output = lax.psum_scatter(
        feedforward_share.astype(jnp.bfloat16), "tensor", scatter_dimension=1, tiled=True
    ).astype(jnp.float32)
    layer_out = (hidden_state + mlp_output).astype(jnp.bfloat16)
    output_row_block = lax.all_gather(cotangent, "tensor", axis=1, tiled=True)
    down_weight_gradient = jnp.einsum(
        "byw,bya->wa", activation_output, output_row_block, preferred_element_type=jnp.float32
    )
    activation_gradient = jnp.einsum(
        "gth,eh->gte", output_row_block, down_weight, preferred_element_type=jnp.float32
    )
    gate_grad, up_grad = gated_back(activation_gradient)
    gate_up_gradient = jnp.stack([gate_grad, up_grad]).astype(jnp.bfloat16)
    grad_gateup = jnp.einsum(
        "oha,tohx->tax", feedforward_row_block, gate_up_gradient, preferred_element_type=jnp.float32
    )
    mlp_in_part = jnp.einsum(
        "gmjq,gpq->mjp", gate_up_gradient, gate_up_weight, preferred_element_type=jnp.float32
    )
    normed_mlp_grad = lax.psum_scatter(mlp_in_part, "tensor", scatter_dimension=1, tiled=True)
    gain_mlp_part = jnp.sum(normed_mlp_grad * normal_mlp, axis=(0, 1))
    hidden_grad = cotangent.astype(jnp.float32) + norm_back(
        normed_mlp_grad, normal_mlp, inverse_mlp, gain_mlp
    )
    branch_grad = hidden_grad.astype(jnp.bfloat16)
    branch_row_block = lax.all_gather(branch_grad, "tensor", axis=1, tiled=True)
    output_weight_gradient = jnp.einsum(
        "kgp,kgo->po", attention_result, branch_row_block, preferred_element_type=jnp.float32
    )
    attended_grad = jnp.einsum(
        "azr,mr->azm", branch_row_block, output_weight, preferred_element_type=jnp.float32
    ).astype(jnp.bfloat16)
    grad_blocks = attended_grad.reshape(blocks, block_rows, head_count, HD)

    def attend_back(inputs):
        query_block, segment_block, sequence, log_total, out_grad = inputs
        scores = block_scores(query_block, segment_block, sequence)
        probabilities = jnp.exp(scores - log_total[..., None])
        rounded = probabilities.astype(jnp.bfloat16)
        prob_grad = jnp.einsum(
            "qhd,khd->hqk", out_grad, values[sequence], preferred_element_type=jnp.float32
        )
        centre = jnp.sum(probabilities * prob_grad, axis=-1, keepdims=True)
        score_grad = (probabilities * (prob_grad - centre)).astype(jnp.bfloat16)
        query_grad = (
            jnp.einsum(
                "hqk,khd->qhd", score_grad, keys[sequence], preferred_element_type=jnp.float32
            )
            * scale_factor
        )
        key_grad = (
            jnp.einsum("hqk,qhd->khd", score_grad, query_block, preferred_element_type=jnp.float32)
            * scale_factor
        )
        value_grad = jnp.einsum(
            "hqk,qhd->khd", rounded, out_grad, preferred_element_type=jnp.float32
        )
        return (query_grad, key_grad, value_grad)

    query_grad, key_part, value_part = lax.map(
        attend_back, (query_blocks, segment_blocks, owners, log_totals, grad_blocks)
    )
    per_seq = (sequences, per_row, length, head_count, HD)
    key_grad = jnp.sum(key_part.reshape(per_seq), axis=1)
    value_grad = jnp.sum(value_part.reshape(per_seq), axis=1)
    query_grad = query_grad.reshape(head_shape)
    query_key_value_grad_rows = jnp.stack(
        [
            unrope(query_grad, cos_heads, sin_heads),
            unrope(key_grad, cos_heads, sin_heads),
            value_grad,
        ]
    )
    query_key_value_grad_rows = query_key_value_grad_rows.reshape(
        3, sequences, length, head_cols
    ).astype(jnp.bfloat16)
    query_key_value_gradient = jnp.einsum(
        "jof,gjoz->gfz",
        attention_row_block,
        query_key_value_grad_rows,
        preferred_element_type=jnp.float32,
    )
    attention_input_share = jnp.einsum(
        "jukz,jgz->ukg",
        query_key_value_grad_rows,
        query_key_value_weight,
        preferred_element_type=jnp.float32,
    )
    normed_attn_grad = lax.psum_scatter(
        attention_input_share, "tensor", scatter_dimension=1, tiled=True
    )
    gain_attn_part = jnp.sum(normed_attn_grad * normal_attn, axis=(0, 1))
    input_grad = (
        hidden_grad + norm_back(normed_attn_grad, normal_attn, inverse_attn, gain_attn)
    ).astype(jnp.bfloat16)
    grad_gain_attn, grad_gain_mlp = lax.psum((gain_attn_part, gain_mlp_part), ("dp", "tensor"))
    query_key_value_gradient, output_weight_gradient, grad_gateup, down_weight_gradient = lax.psum(
        (query_key_value_gradient, output_weight_gradient, grad_gateup, down_weight_gradient), "dp"
    )
    return (
        layer_out,
        input_grad,
        grad_gain_attn,
        query_key_value_gradient,
        output_weight_gradient,
        grad_gain_mlp,
        grad_gateup,
        down_weight_gradient,
    )


def solution(mesh):
    placed = (
        P("dp", "tensor", None),
        P("dp", None),
        P(),
        P(None, None, "tensor"),
        P("tensor", None),
        P(),
        P(None, None, "tensor"),
        P("tensor", None),
        P("dp", "tensor", None),
    )
    return jax.shard_map(
        on_device,
        mesh=mesh,
        in_specs=placed,
        out_specs=(
            P("dp", "tensor", None),
            P("dp", "tensor", None),
            P(),
            P(None, None, "tensor"),
            P("tensor", None),
            P(),
            P(None, None, "tensor"),
            P("tensor", None),
        ),
        check_vma=False,
    )
```

profile of v0, /device:TPU:0, one launch (start us, length us, event | category | flops | bytes accessed | tf_op | source)
XLA Modules:
  0.0 842.9 jit_solution(10957082175106231278)
XLA Ops:
  18.0 4.4 fusion.129
  22.5 38.4 %all-gather.5.cloned.1.call-done = bf16[1,1024,1024]{2,1,0:T(8,128)(2,1)} async-done(((bf16[1,256,1024]{2,1,0:T(8,128)(2,1)}), bf16[1,1024,1024]{2,1,0:T(8,128)(2,1)}) %all-gather.5.cloned.1.call-update) | async-done | bytes 2097168 | tf_op jit(solution)/shard_map/all_gather | solution.py:89
  60.8 3.9 fusion.92
  80.1 18.9 %while.30 = (s32[]{:T(128)}, bf16[2,512,4,64]{1,3,2,0:T(8,128)(2,1)}, f32[2,4,512]{2,1,0:T(4,128)S(1)}, s32[2,512]{1,0:T(2,128)S(1)}, s32[1,1024]{1,0:T(1,128)S(...) while((s32[]{:T(128)}, ...), condition=%wide.region_6.7_spmd.clone, body=%wide.region_3.6_spmd.sunk.clone | while | flops 562558976 | bytes 35465408 | solution.py:129
  101.5 3.8 convolution_bitcast_fusion.3
  106.1 74.8 %reduce-scatter.5.cloned.1.call-done = f32[1,256,1024]{2,1,0:T(8,128)} async-done(((f32[1,1024,1024]{2,1,0:T(8,128)}), f32[1,256,1024]{2,1,0:T(8,128)}) %reduce-scatter.5.cloned.1.call-update) | async-done | bytes 1048592 | tf_op jit(solution)/shard_map/reduce_scatter | solution.py:134
  184.5 44.5 %all-gather.9.cloned.1.call-done = bf16[1,1024,1024]{2,1,0:T(8,128)(2,1)} async-done(((bf16[1,256,1024]{2,1,0:T(8,128)(2,1)}), bf16[1,1024,1024]{2,1,0:T(8,128)(2,1)}) %all-gather.9.cloned.1.call-update) | async-done | bytes 2097168 | tf_op jit(solution)/shard_map/all_gather | solution.py:151
  229.1 5.1 fusion.83
  234.1 41.7 %all-gather.7.cloned.1.call-done = bf16[1,1024,1024]{2,1,0:T(8,128)(2,1)} async-done(((bf16[1,256,1024]{2,1,0:T(8,128)(2,1)}), bf16[1,1024,1024]{2,1,0:T(8,128)(2,1)}) %all-gather.7.cloned.1.call-update) | async-done | bytes 2097168 | tf_op jit(solution)/shard_map/all_gather | solution.py:138
  275.8 4.8 fusion.86
  280.6 6.5 fusion.102
  289.9 5.0 convolution_bitcast_fusion.2
  296.6 6.5 convert_bitcast_fusion
  303.2 67.3 %reduce-scatter.9.cloned.1.call-done = f32[1,256,1024]{2,1,0:T(8,128)} async-done(((f32[1,1024,1024]{2,1,0:T(8,128)}), f32[1,256,1024]{2,1,0:T(8,128)}) %reduce-scatter.9.cloned.1.call-update) | async-done | bytes 1048592 | tf_op jit(solution)/shard_map/reduce_scatter | solution.py:166
  372.9 44.8 %reduce-scatter.7.cloned.1.call-done = bf16[1,256,1024]{2,1,0:T(8,128)(2,1)} async-done(((bf16[1,1024,1024]{2,1,0:T(8,128)(2,1)}), bf16[1,256,1024]{2,1,0:T(8,128)(2,1)}) %reduce-scatter.7.cloned.1.call-update) | async-done | bytes 524304 | tf_op jit(solution)/shard_map/reduce_scatter | solution.py:147
  422.3 7.9 convolution_bitcast_fusion
  430.1 9.7 %fusion.81 = f32[656,1024]{1,0:T(8,128)} fusion(bf16[1,1024,1024]{2,1,0:T(8,128)(2,1)S(1)} %copy-done.51, f32[2,1,1024,656]{2,3,0,1:T(8,128)} %bitcast.359, f32[2,1,1024,656]{2,3,1,0:T(8,128)} %bitcast.360), kind=kOutput, calls=%fused_computation.116 | convolution fusion | flops 1420066816 | bytes 10158080 | tf_op jit(solution)/shard_map/byw,bya->wa/dot_general | solution.py:152
  439.9 26.3 %all-gather.11.cloned.1.call-done = bf16[1,1024,1024]{2,1,0:T(8,128)(2,1)} async-done(((bf16[1,256,1024]{2,1,0:T(8,128)(2,1)}), bf16[1,1024,1024]{2,1,0:T(8,128)(2,1)}) %all-gather.11.cloned.1.call-update) | async-done | bytes 2097168 | tf_op jit(solution)/shard_map/all_gather | solution.py:172
  471.5 28.1 %while.31 = (s32[]{:T(128)}, f32[2,512,4,64]{1,3,2,0:T(8,128)}, f32[2,1024,4,64]{1,3,2,0:T(8,128)}, f32[2,1024,4,64]{1,3,2,0:T(8,128)}, s32[2,512]{1,0:T(2,128)S...) while((s32[]{:T(128)}, f32[2,512,4,64]{1,3,2,0:T(8,128)}, ...), condition=%wide.region_16.17_spmd.clone, body=%wide.region_14.16_spmd.sunk.clone | while | flops 1374550016 | bytes 112267576 | solution.py:206
  535.3 4.3 convolution_bitcast_fusion.1
  539.7 163.2 %all-reduce.4.cloned.1.call-done = (f32[3,1024,256]{1,2,0:T(8,128)}, f32[256,1024]{1,0:T(8,128)}, f32[2,1024,656]{1,2,0:T(8,128)}, f32[656,1024]{1,0:T(8,128)}) async-done(((f32[3,1024,256]{1,2,0:T(8,128)}, f32[256,1024]{1,0:T(8,128)}, f32[2,1024,656]{1,2,0:T(8,128)}, f32[656,1024]{1,0:T(8,128)}), (f32[3,1024,256]{1,2,0:T(8,128)}, f32[256,1024]{1,0:T(8,128)}, f32[2,1024,656]{1,2,0:T(8,128)}, ...) | async-done | bytes 12255248 | tf_op jit(solution)/shard_map/psum | solution.py:243
  706.5 76.0 %reduce-scatter.11.cloned.1.call-done = f32[1,256,1024]{2,1,0:T(8,128)} async-done(((f32[1,1024,1024]{2,1,0:T(8,128)}), f32[1,256,1024]{2,1,0:T(8,128)}) %reduce-scatter.11.cloned.1.call-update) | async-done | bytes 1048592 | tf_op jit(solution)/shard_map/reduce_scatter | solution.py:235
  784.2 40.8 %all-reduce = (f32[1024]{0:T(1024)}, f32[1024]{0:T(1024)}) all-reduce(f32[1024]{0:T(1024)S(1)} %get-tuple-element.236, f32[1024]{0:T(1024)S(1)} %copy-done.47), channel_id=1, replica_groups=mesh['dp'=8,'tensor'=4] {'dp','tensor'}, use_global_device_ids=true, to_apply=%region_23.24 | all-reduce | flops 2048 | bytes 16384 | tf_op jit(solution)/shard_map/psum | solution.py:242
  828.5 6.0 copy.110
  (244 shorter events, 141.6 us)
Async XLA Ops:
  7.2 268.7 %copy-start = (bf16[2,1024,656]{1,2,0:T(8,128)(2,1)S(1)}, bf16[2,1024,656]{1,2,0:T(8,128)(2,1)}, u32[]{:S(2)}) copy-start(bf16[2,1024,656]{1,2,0:T(8,128)(2,1)} %param.19) | copy-start | bytes 8060932
  7.2 53.7 %all-gather.5.cloned.1.call-start = ((), (), s32[]{:S(2)}) async-start(), calls=%async_computation.4 | async-start | bytes 2621440 | tf_op jit(solution)/shard_map/all_gather | solution.py:89
  8.6 7.6 copy-start.45
  12.1 168.8 %reduce-scatter.5.cloned.1.call-start = ((), (), s32[]{:S(2)}) async-start(), calls=%async_computation.5 | async-start | bytes 5242880 | tf_op jit(solution)/shard_map/reduce_scatter | solution.py:134
  17.9 61.6 %copy-start.24 = (f32[1024,64]{0,1:T(8,128)}, f32[1024,64]{0,1:T(8,128)S(1)}, u32[]{:S(2)}) copy-start(f32[1024,64]{0,1:T(8,128)S(1)} %get-tuple-element.310) | copy-start | bytes 786436
  105.3 78.2 %copy-start.43 = (f32[1024]{0:T(1024)S(1)}, f32[1024]{0:T(1024)}, u32[]{:S(2)}) copy-start(f32[1024]{0:T(1024)} %param.18) | copy-start | bytes 12292
  105.3 123.8 %all-gather.9.cloned.1.call-start = ((), (), s32[]{:S(2)}) async-start(), calls=%async_computation.8 | async-start | bytes 2621440 | tf_op jit(solution)/shard_map/all_gather | solution.py:151
  106.0 169.8 %all-gather.7.cloned.1.call-start = ((), (), s32[]{:S(2)}) async-start(), calls=%async_computation.6 | async-start | bytes 2621440 | tf_op jit(solution)/shard_map/all_gather | solution.py:138
  184.5 186.1 %reduce-scatter.9.cloned.1.call-start = ((), (), s32[]{:S(2)}) async-start(), calls=%async_computation.9 | async-start | bytes 5242880 | tf_op jit(solution)/shard_map/reduce_scatter | solution.py:166
  294.9 122.8 %reduce-scatter.7.cloned.1.call-start = ((), (), s32[]{:S(2)}) async-start(), calls=%async_computation.7 | async-start | bytes 2621440 | tf_op jit(solution)/shard_map/reduce_scatter | solution.py:147
  303.2 67.4 %copy-start.5 = (f32[1,256,1024]{2,1,0:T(8,128)S(1)}, f32[1,256,1024]{2,1,0:T(8,128)}, u32[]{:S(2)}) copy-start(f32[1,256,1024]{2,1,0:T(8,128)} %copy-done.4) | copy-start | bytes 3145732
  303.2 163.0 %all-gather.11.cloned.1.call-start = ((), (), s32[]{:S(2)}) async-start(), calls=%async_computation.10 | async-start | bytes 2621440 | tf_op jit(solution)/shard_map/all_gather | solution.py:172
  370.5 47.1 %copy-start.16 = (f32[1,256,1024]{2,1,0:T(8,128)S(1)}, f32[1,256,1024]{2,1,0:T(8,128)}, u32[]{:S(2)}) copy-start(f32[1,256,1024]{2,1,0:T(8,128)} %reduce-scatter.9.cloned.1.call-done) | copy-start | bytes 3145732
  420.8 282.0 %all-reduce.4.cloned.1.call-start = ((), (), s32[]{:S(2)}) async-start(), calls=%async_computation.12 | async-start | bytes 24510464 | tf_op jit(solution)/shard_map/psum | solution.py:243
  422.3 7.9 copy-start.51
  430.1 36.0 %copy-start.42 = (bf16[256,1024]{1,0:T(8,128)(2,1)S(1)}, bf16[256,1024]{1,0:T(8,128)(2,1)}, u32[]{:S(2)}) copy-start(bf16[256,1024]{1,0:T(8,128)(2,1)} %param.17) | copy-start | bytes 1572868
  533.7 248.7 %reduce-scatter.11.cloned.1.call-start = ((), (), s32[]{:S(2)}) async-start(), calls=%async_computation.11 | async-start | bytes 5242880 | tf_op jit(solution)/shard_map/reduce_scatter | solution.py:235
  702.8 79.7 %copy-start.10 = (bf16[1,256,1024]{2,1,0:T(8,128)(2,1)S(1)}, bf16[1,256,1024]{2,1,0:T(8,128)(2,1)}, u32[]{:S(2)}) copy-start(bf16[1,256,1024]{2,1,0:T(8,128)(2,1)} %param.13) | copy-start | bytes 1572868
  702.8 79.7 %copy-start.44 = (f32[1024]{0:T(1024)S(1)}, f32[1024]{0:T(1024)}, u32[]{:S(2)}) copy-start(f32[1024]{0:T(1024)} %param.15) | copy-start | bytes 12292
  702.8 79.7 %copy-start.46 = (f32[256]{0:T(256)S(1)}, f32[256]{0:T(256)}, u32[]{:S(2)}) copy-start(f32[256]{0:T(256)} %copy-done.45) | copy-start | bytes 3076
  702.8 79.7 %copy-start.49 = (f32[256]{0:T(256)S(1)}, f32[256]{0:T(256)}, u32[]{:S(2)}) copy-start(f32[256]{0:T(256)} %copy-done.48) | copy-start | bytes 3076
  702.8 81.4 %copy-start.47 = (f32[1024]{0:T(1024)S(1)}, f32[1024]{0:T(1024)}, u32[]{:S(2)}) copy-start(f32[1024]{0:T(1024)} %get-tuple-element.234) | copy-start | bytes 12292
  702.8 122.3 %copy-start.15 = (f32[1,256,1024]{2,1,0:T(8,128)S(1)}, f32[1,256,1024]{2,1,0:T(8,128)}, u32[]{:S(2)}) copy-start(f32[1,256,1024]{2,1,0:T(8,128)} %get-tuple-element.285) | copy-start | bytes 3145732
  706.5 121.0 %copy-start.37 = (f32[256,1024]{1,0:T(8,128)S(1)}, f32[256,1024]{1,0:T(8,128)}, u32[]{:S(2)}) copy-start(f32[256,1024]{1,0:T(8,128)} %get-tuple-element.546) | copy-start | bytes 3145732
  (47 other events, 120.1 us)
Sparse Core Ops, SparseCore 0:
  12.2 48.5 all-gather.4
  105.4 75.4 reduce-scatter.4
  182.6 46.4 all-gather.8
  231.1 44.6 all-gather.6
  295.0 75.4 reduce-scatter.8
  373.3 44.3 reduce-scatter.6
  420.9 45.2 all-gather.10
  533.9 168.8 all-reduce.3
  705.7 76.7 reduce-scatter.10
where the time goes:
time: 853 us; the launch traced here: 843 us
  waiting for transfers between devices  578 us (68%)
  matrix products  88.2 us (10%)
  other arithmetic  61 us (7%)
  local copies, waits for them, and re-layouts  58.8 us (7%)
  blocking collectives  40.8 us (5%)
  between operations  14.8 us (2%)
    psum x1, waiting for transfers between devices, on_device(): lax.psum((query_key_value_gradient, output_weight_gradient, grad_gateup,...  163 us
    reduce_scatter x1, waiting for transfers between devices, on_device(): lax.psum_scatter(attention_input_share, 'tensor', scatter_dimension=1, ti...  76 us
    reduce_scatter x1, waiting for transfers between devices, on_device(): lax.psum_scatter(branch_share, 'tensor', scatter_dimension=1, tiled=True)  74.8 us
    reduce_scatter x1, waiting for transfers between devices, on_device(): lax.psum_scatter(mlp_in_part, 'tensor', scatter_dimension=1, tiled=True)  67.3 us
    reduce_scatter x1, waiting for transfers between devices, on_device(): lax.psum_scatter(feedforward_share.astype(jnp.bfloat16), 'tensor', scatte...  44.8 us
    all_gather x1, waiting for transfers between devices, on_device(): output_row_block = lax.all_gather(cotangent, 'tensor', axis=1, tiled=True)  44.5 us
    all_gather x1, waiting for transfers between devices, on_device(): lax.all_gather(normed_mlp, 'tensor', axis=1, tiled=True)  41.7 us
    psum x1, blocking collectives, on_device(): lax.psum((gain_attn_part, gain_mlp_part), ('dp', 'tensor'))  40.8 us
  transfers between devices with their start and end apart: 9, of which 9 were waited for; matrix products, arithmetic and copies ran while one was open for 6% of the time, Pallas kernels for 0%

commit v1 on v0

v1 whole, which is shorter than its diff:
```python
import math

import jax
import jax.numpy as jnp
from jax import lax
from jax.experimental import pallas as pl
from jax.experimental.pallas import tpu as pltpu
from jax.sharding import Mesh, PartitionSpec as P

HD = 64
EPSILON = 1e-05
ROPE_BASE = 160000.0
BF = jnp.bfloat16
F32 = jnp.float32


def normalize(values):
    centered = values - jnp.mean(values, axis=-1, keepdims=True)
    variance = jnp.mean(centered * centered, axis=-1, keepdims=True)
    inverse = lax.rsqrt(variance + EPSILON)
    return (centered * inverse, inverse)


def norm_back(grad, normal, inverse, gain):
    scaled = grad * gain
    return inverse * (
        scaled
        - jnp.mean(scaled, axis=-1, keepdims=True)
        - normal * jnp.mean(scaled * normal, axis=-1, keepdims=True)
    )


def nt(left, right):
    return lax.dot_general(left, right, (((1,), (1,)), ((), ())), preferred_element_type=F32)


def nn(left, right):
    return jnp.dot(left, right, preferred_element_type=F32)


def tn(left, right):
    return lax.dot_general(left, right, (((0,), (0,)), ((), ())), preferred_element_type=F32)


def swap_halves(values):
    lane = lax.broadcasted_iota(jnp.int32, values.shape, 1)
    width = values.shape[1]
    ahead = pltpu.roll(values, width - HD // 2, 1)
    behind = pltpu.roll(values, HD // 2, 1)
    return jnp.where(lane % HD < HD // 2, ahead, behind)


def project_kernel(n_ref, w_ref, cos_ref, sin_ref, q_ref, k_ref, v_ref):
    rows = n_ref[...]
    cos, sin = cos_ref[...], sin_ref[...]
    for c, out in ((0, q_ref), (1, k_ref), (2, v_ref)):
        wide = nn(rows, w_ref[c])
        if c == 2:
            out[...] = wide.astype(BF)
            continue
        for at in range(0, wide.shape[1], 128):
            part = wide[:, at : at + 128]
            turned = (part * cos + swap_halves(part) * sin).astype(BF)
            if c == 0:
                turned = turned * (1.0 / math.sqrt(HD))
            out[:, at : at + 128] = turned


def project(rows, weight, cos, sin):
    length, width = rows.shape
    cols = weight.shape[2]
    block = 256
    return pl.pallas_call(
        project_kernel,
        grid=(length // block,),
        in_specs=[
            pl.BlockSpec((block, width), lambda i: (i, 0)),
            pl.BlockSpec((3, width, cols), lambda i: (0, 0, 0)),
            pl.BlockSpec((block, 128), lambda i: (i, 0)),
            pl.BlockSpec((block, 128), lambda i: (i, 0)),
        ],
        out_specs=[pl.BlockSpec((block, cols), lambda i: (i, 0))] * 3,
        out_shape=[jax.ShapeDtypeStruct((length, cols), BF)] * 3,
        compiler_params=pltpu.CompilerParams(vmem_limit_bytes=40 * 2**20),
        cost_estimate=pl.CostEstimate(
            flops=6 * length * width * cols, bytes_accessed=5 * 2**20, transcendentals=0
        ),
    )(rows, weight, cos, sin)


def half_mask(values, half):
    lane = lax.broadcasted_iota(jnp.int32, values.shape, 1)
    return jnp.where((lane // HD) == half, values, jnp.zeros_like(values))


def row_blocks(count):
    at = 0
    while at < count:
        size = min(256, count - at)
        yield at, size
        at += size


def attend_kernel(doc, q_ref, k_ref, v_ref, o_ref, l_ref):
    keys = k_ref[:doc, :]
    values_t = v_ref[:doc, :].T
    for at, size in row_blocks(doc):
        queries = q_ref[at : at + size, :]
        mixed = []
        for half in range(2):
            scores = nt(keys, half_mask(queries, half))
            largest = jnp.max(scores, axis=0, keepdims=True)
            weights = jnp.exp(scores - largest)
            total = jnp.sum(weights, axis=0, keepdims=True)
            mix = nn(values_t[half * HD : half * HD + HD], weights.astype(BF))
            mixed.append(mix * (1.0 / total))
            l_ref[0, half : half + 1, at : at + size] = largest + jnp.log(total)
        o_ref[at : at + size, :] = jnp.concatenate(mixed, axis=0).T.astype(BF)
    o_ref[doc:, :] = v_ref[doc:, :]


def attend(queries, keys, values, doc):
    length, cols = queries.shape
    pairs = cols // 128
    spec = pl.BlockSpec((length, 128), lambda p: (0, p))
    return pl.pallas_call(
        lambda *refs: attend_kernel(doc, *refs),
        grid=(pairs,),
        in_specs=[spec] * 3,
        out_specs=[spec, pl.BlockSpec((1, 2, doc), lambda p: (p, 0, 0))],
        out_shape=[
            jax.ShapeDtypeStruct((length, cols), BF),
            jax.ShapeDtypeStruct((pairs, 2, doc), F32),
        ],
        compiler_params=pltpu.CompilerParams(vmem_limit_bytes=48 * 2**20),
        cost_estimate=pl.CostEstimate(
            flops=8 * doc * doc * cols, bytes_accessed=2 * 2**20, transcendentals=doc * doc * 4
        ),
    )(queries, keys, values)


def attend_back_kernel(
    doc, q_ref, k_ref, v_ref, d_ref, l_ref, cos_ref, sin_ref, dq_ref, dk_ref, dv_ref, ka_ref, va_ref
):
    keys = k_ref[:doc, :]
    keys_t = keys.T
    values = v_ref[:doc, :]
    first = True
    for at, size in row_blocks(doc):
        queries = q_ref[at : at + size, :]
        grads = d_ref[at : at + size, :]
        back = []
        for half in range(2):
            query = half_mask(queries, half)
            grad = half_mask(grads, half)
            probs = jnp.exp(nt(keys, query) - l_ref[0, half : half + 1, at : at + size])
            prob_grad = nt(values, grad)
            centre = jnp.sum(probs * prob_grad, axis=0, keepdims=True)
            score_grad = (probs * (prob_grad - centre)).astype(BF)
            value_part = nn(probs.astype(BF), grad)
            key_part = nn(score_grad, query)
            if first:
                va_ref[...] = value_part
                ka_ref[...] = key_part
                first = False
            else:
                va_ref[...] += value_part
                ka_ref[...] += key_part
            back.append(nn(keys_t[half * HD : half * HD + HD], score_grad))
        query_grad = jnp.concatenate(back, axis=0).T * (1.0 / math.sqrt(HD))
        cos = cos_ref[at : at + size, :]
        sin = sin_ref[at : at + size, :]
        dq_ref[at : at + size, :] = (query_grad * cos - swap_halves(query_grad) * sin).astype(BF)
    key_grad = ka_ref[...]
    cos = cos_ref[:doc, :]
    sin = sin_ref[:doc, :]
    dk_ref[:doc, :] = (key_grad * cos - swap_halves(key_grad) * sin).astype(BF)
    dv_ref[:doc, :] = va_ref[...].astype(BF)
    rest = dq_ref.shape[0] - doc
    dq_ref[doc:, :] = jnp.zeros((rest, 128), BF)
    dk_ref[doc:, :] = jnp.zeros((rest, 128), BF)
    dv_ref[doc:, :] = d_ref[doc:, :]


def attend_back(queries, keys, values, grads, logs, cos, sin, doc):
    length, cols = queries.shape
    pairs = cols // 128
    spec = pl.BlockSpec((length, 128), lambda p: (0, p))
    table = pl.BlockSpec((length, 128), lambda p: (0, 0))
    return pl.pallas_call(
        lambda *refs: attend_back_kernel(doc, *refs),
        grid=(pairs,),
        in_specs=[spec] * 4
        + [pl.BlockSpec((1, 2, doc), lambda p: (p, 0, 0))]
        + [table] * 2,
        out_specs=[spec] * 3,
        out_shape=[jax.ShapeDtypeStruct((length, cols), BF)] * 3,
        scratch_shapes=[pltpu.VMEM((doc, 128), F32), pltpu.VMEM((doc, 128), F32)],
        compiler_params=pltpu.CompilerParams(vmem_limit_bytes=48 * 2**20),
        cost_estimate=pl.CostEstimate(
            flops=20 * doc * doc * cols, bytes_accessed=5 * 2**20, transcendentals=doc * doc * 4
        ),
    )(queries, keys, values, grads, logs, cos, sin)


def shift(value, by, count):
    return lax.ppermute(value, "tensor", [(i, (i + by) % count) for i in range(count)])


def flip(value, axis, bit, count):
    return lax.ppermute(value, axis, [(i, i ^ bit) for i in range(count)])


def bits_of(count, turned):
    bits = [1 << b for b in range(count.bit_length() - 1)]
    return bits[::-1] if turned else bits


def gather_chips(value, count, turned):
    held = {0: value}
    for bit in bits_of(count, turned):
        held.update({i ^ bit: flip(v, "chip", bit, count) for i, v in list(held.items())})
    return [held[i] for i in range(count)]


def scatter_chips(blocks, count, turned):
    held = dict(enumerate(blocks))
    for bit in bits_of(count, turned):
        held = {
            i: (v.astype(F32) + flip(held[i ^ bit], "chip", bit, count).astype(F32)).astype(BF)
            for i, v in held.items()
            if not i & bit
        }
    return held[0]


def total_all(value, sizes):
    for axis, count in sizes:
        for bit in bits_of(count, False):
            value = value + flip(value, axis, bit, count)
    return value


def rotate(value, by):
    length = value.shape[0]
    return lax.dynamic_slice_in_dim(jnp.concatenate([value, value]), by, length)


def make(chips, cores, ranks):
    def on_device(
        tokens,
        segment_ids,
        gain_attn,
        query_key_value_weight,
        output_weight,
        gain_mlp,
        gate_up_weight,
        down_weight,
        cotangent,
    ):
        length = segment_ids.shape[1]
        own_rows, width = tokens.shape[1:]
        doc = length - length // 8
        rank = lax.axis_index("tensor")
        core = lax.axis_index("core")
        chip = lax.axis_index("chip")
        segments = segment_ids[0]
        middle = segments[length // 2]
        start = jnp.sum((segments < middle).astype(jnp.int32))
        mine_at = rank * own_rows
        into_doc = (start - mine_at) % length
        from_doc = (mine_at - start) % length

        places = jnp.arange(length, dtype=jnp.int32)
        places = jnp.where(places < doc, places, 0)
        half = HD // 2
        freq = jnp.exp(jnp.arange(half, dtype=F32) * (-2.0 * math.log(ROPE_BASE) / HD))
        angles = places.astype(F32)[:, None] * jnp.concatenate([freq] * 4)[None, :]
        cos_table = jnp.cos(angles)
        lane = jnp.arange(2 * HD, dtype=jnp.int32)
        sin_table = jnp.sin(angles) * jnp.where(lane % HD < half, -1.0, 1.0)

        hidden = down_weight.shape[0]
        share = hidden // cores
        per = -(-share // chips)
        piece = -(-per // 8) * 8
        hidden_t = jnp.concatenate([jnp.swapaxes(gate_up_weight, 1, 2), down_weight[None]])
        half_t = lax.dynamic_slice_in_dim(hidden_t, core * share, share, axis=1)
        half_t = jnp.pad(half_t, ((0, 0), (0, chips * per - share), (0, 0)))
        half_t = half_t.reshape(3, chips, per, width)
        half_t = jnp.pad(half_t, ((0, 0), (0, 0), (0, piece - per), (0, 0)))
        own = [
            lax.dynamic_index_in_dim(half_t, chip ^ i, axis=1, keepdims=False)
            for i in range(chips)
        ]
        gate_up_sent = own[0][:2]
        down_sent = own[0][2]
        gate_up_came = [shift(gate_up_sent, -k, ranks) for k in range(1, ranks)]
        down_came = jnp.concatenate([shift(down_sent, -k, ranks) for k in range(1, ranks)])
        gates = gather_chips(jnp.concatenate([g[0] for g in gate_up_came]), chips, False)
        ups = gather_chips(jnp.concatenate([g[1] for g in gate_up_came]), chips, True)
        cut = down_came.shape[0] // 16 * 8
        downs_a = gather_chips(down_came[:cut], chips, False)
        downs_b = gather_chips(down_came[cut:], chips, True)
        gate = jnp.concatenate([v for i in range(chips) for v in (own[i][0], gates[i])])
        up = jnp.concatenate([v for i in range(chips) for v in (own[i][1], ups[i])])
        down = jnp.concatenate(
            [v for i in range(chips) for v in (own[i][2], downs_a[i], downs_b[i])]
        )
        heads_rows = output_weight.shape[0]
        out_piece = heads_rows // (cores * chips)
        out_mine = lax.dynamic_slice_in_dim(
            output_weight, (core * chips + chip) * out_piece, out_piece
        )
        out_all = lax.all_gather(out_mine, ("tensor", "core", "chip"), axis=0, tiled=True)
        out_all = out_all.reshape(ranks, heads_rows, width)
        outs = [
            lax.dynamic_index_in_dim(out_all, (rank - k) % ranks, axis=0, keepdims=False)
            for k in range(ranks)
        ]
        out_weight = jnp.concatenate(outs)

        token_f = tokens[0].astype(F32)
        cot = cotangent[0]
        cot_pair = jnp.concatenate([cot, flip(cot, "core", 1, cores)])
        normal_attn, inverse_attn = normalize(token_f)
        normed_attn = (normal_attn * gain_attn).astype(BF)
        normed_rows = jnp.concatenate(
            [normed_attn] + [shift(normed_attn, -k, ranks) for k in range(1, ranks)]
        )
        normed_doc = rotate(normed_rows, into_doc)
        queries, keys, values = project(normed_doc, query_key_value_weight, cos_table, sin_table)
        mixture, logs = attend(queries, keys, values, doc)
        mixture = rotate(mixture, from_doc).reshape(ranks, own_rows, heads_rows)
        attention = jnp.concatenate(
            [mixture[0]] + [shift(mixture[k], k, ranks) for k in range(1, ranks)], axis=1
        )
        hidden_state = token_f + nn(attention, out_weight)
        normal_mlp, inverse_mlp = normalize(hidden_state)
        normed_mlp = (normal_mlp * gain_mlp).astype(BF)

        normed_pair = jnp.concatenate([normed_mlp, flip(normed_mlp, "core", 1, cores)])
        gate_proj = nt(normed_pair, gate)
        up_proj = nt(normed_pair, up)
        hid_grad = nt(cot_pair, down)
        cdf = 0.5 * (1.0 + lax.erf(gate_proj * (1.0 / math.sqrt(2.0))))
        pdf = jnp.exp(-0.5 * gate_proj * gate_proj) * (1.0 / math.sqrt(2.0 * math.pi))
        act = gate_proj * cdf
        hid = (act * up_proj).astype(BF)
        gate_grad = (hid_grad * up_proj * (cdf + gate_proj * pdf)).astype(BF)
        up_grad = (hid_grad * act).astype(BF)
        in_part = nn(gate_grad, gate) + nn(up_grad, up)
        normed_mlp_grad = in_part[:own_rows] + flip(
            in_part[own_rows:].astype(BF), "core", 1, cores
        ).astype(F32)
        down_grad = tn(hid, cot_pair).astype(BF)
        gate_w_grad = tn(gate_grad, normed_pair).astype(BF)
        up_w_grad = tn(up_grad, normed_pair).astype(BF)
        mlp_part = nn(hid, down)
        mlp_out = mlp_part[:own_rows] + flip(
            mlp_part[own_rows:].astype(BF), "core", 1, cores
        ).astype(F32)
        layer_out = (hidden_state + mlp_out).astype(BF)

        gain_mlp_part = jnp.sum(normed_mlp_grad * normal_mlp, axis=0)
        hidden_grad = cot.astype(F32) + norm_back(
            normed_mlp_grad, normal_mlp, inverse_mlp, gain_mlp
        )
        branch_grad = hidden_grad.astype(BF)
        attended_grad = nt(branch_grad, out_weight).astype(BF)
        attended_rows = jnp.concatenate(
            [attended_grad[:, :heads_rows]]
            + [
                shift(attended_grad[:, k * heads_rows : (k + 1) * heads_rows], -k, ranks)
                for k in range(1, ranks)
            ]
        )
        attended_doc = rotate(attended_rows, into_doc)
        out_w_grad = tn(attention, branch_grad).astype(BF)
        dq, dk, dv = attend_back(
            queries, keys, values, attended_doc, logs, cos_table, sin_table, doc
        )
        normed_attn_part = (
            nt(dq, query_key_value_weight[0])
            + nt(dk, query_key_value_weight[1])
            + nt(dv, query_key_value_weight[2])
        )
        gain_attn_part = jnp.sum(normed_attn_part * normed_doc.astype(F32), axis=0) / gain_attn
        part_rows = rotate(normed_attn_part.astype(BF), from_doc).reshape(ranks, own_rows, width)
        normed_attn_grad = part_rows[0].astype(F32)
        for k in range(1, ranks):
            normed_attn_grad = normed_attn_grad + shift(part_rows[k], k, ranks).astype(F32)
        input_grad = (
            hidden_grad + norm_back(normed_attn_grad, normal_attn, inverse_attn, gain_attn)
        ).astype(BF)
        gains = total_all(
            jnp.concatenate([gain_attn_part, gain_mlp_part]),
            (("core", cores), ("chip", chips), ("tensor", ranks)),
        )
        grad_gain_attn, grad_gain_mlp = gains[:width], gains[width:]

        def scatter_hidden(grad, turned):
            blocks = grad.reshape(chips, ranks * piece, width)
            here = scatter_chips([blocks[i] for i in range(chips)], chips, turned)
            here = here.reshape(ranks, piece, width)
            total = here[0].astype(F32)
            for k in range(1, ranks):
                total = total + shift(here[k], k, ranks).astype(F32)
            return total.astype(BF)

        pieces = jnp.stack(
            [
                scatter_hidden(gate_w_grad, False),
                scatter_hidden(up_w_grad, True),
                scatter_hidden(down_grad, False),
            ]
        )
        every = lax.all_gather(pieces, ("core", "chip"), axis=0, tiled=False)
        every = every[:, :, :per].reshape(cores, chips, 3, per, width)
        every = jnp.moveaxis(every, 2, 0).reshape(3, cores, chips * per, width)[:, :, :share]
        every = every.reshape(3, hidden, width).astype(F32)
        grad_gateup = jnp.swapaxes(every[:2], 1, 2)
        down_weight_gradient = every[2]

        back_order = [(ranks - k) % ranks for k in range(ranks)]
        out_blocks = out_w_grad.reshape(ranks, heads_rows, width)
        out_blocks = jnp.concatenate([out_blocks[k] for k in back_order])
        out_blocks = rotate(out_blocks, ((ranks - rank) % ranks) * heads_rows)
        out_here = lax.psum_scatter(
            out_blocks, ("tensor", "core", "chip"), scatter_dimension=0, tiled=True
        )
        output_weight_gradient = lax.all_gather(
            out_here, ("core", "chip"), axis=0, tiled=True
        ).astype(F32)

        qkv_grad = jnp.stack([tn(normed_doc, g) for g in (dq, dk, dv)]).astype(BF)
        qkv_here = lax.psum_scatter(qkv_grad, ("core", "chip"), scatter_dimension=1, tiled=True)
        query_key_value_gradient = lax.all_gather(
            qkv_here, ("core", "chip"), axis=1, tiled=True
        ).astype(F32)
        return (
            layer_out[None],
            input_grad[None],
            grad_gain_attn,
            query_key_value_gradient,
            output_weight_gradient,
            grad_gain_mlp,
            grad_gateup,
            down_weight_gradient,
        )

    return on_device


def solution(mesh):
    ranks = mesh.shape["tensor"]
    cores = 2
    chips = mesh.shape["dp"] // cores
    split = Mesh(mesh.devices.reshape(chips, cores, ranks), ("chip", "core", "tensor"))
    dp = ("chip", "core")
    rows = P(dp, "tensor", None)
    last = P(None, None, "tensor")
    first = P("tensor", None)
    return jax.shard_map(
        make(chips, cores, ranks),
        mesh=split,
        in_specs=(rows, P(dp, None), P(), last, first, P(), last, first, rows),
        out_specs=(rows, rows, P(), last, first, P(), last, first),
        check_vma=False,
    )
```

time: 853 us -> 567 us (0.66)
  waiting for transfers between devices: 578 us -> 256 us
  starting transfers between devices: 0.54 us -> 83.7 us
  matrix products: 88.2 us -> 37.3 us
  Pallas kernels: 0 us -> 25.1 us
  other arithmetic: 61 us -> 43.6 us
  blocking collectives: 40.8 us -> 27.2 us
  local copies, waits for them, and re-layouts: 58.8 us -> 71.3 us
    reduce_scatter x4 -> x2, waiting for transfers between devices: 263 us -> 4.24 us  [the longest x1 4.24 us: on_device(): lax.psum_scatter(qkv_grad, ('core', 'chip'), scatter_dimension=1, tiled=T...]
    ppermute x0 -> x57, waiting for transfers between devices: none -> 227 us  [the longest x30 124 us: flip(): return lax.ppermute(value, axis, [(i, i ^ bit) for i in range(count)])]
    psum x1 -> x0, waiting for transfers between devices: 163 us -> none  [on_device(): lax.psum((query_key_value_gradient, output_weight_gradient, grad_gateup,...]
    all_gather x4 -> x3, waiting for transfers between devices: 151 us -> 24.7 us  [the longest x1 24.7 us: on_device(): every = lax.all_gather(pieces, ('core', 'chip'), axis=0, tiled=False)]
    ppermute x0 -> x57, starting transfers between devices: none -> 83.3 us  [the longest x27 52.9 us: shift(): lax.ppermute(value, 'tensor', [(i, (i + by) % count) for i in range(count)])]
    dot_general x26 -> x18, matrix products: 88.2 us -> 37.3 us  [the longest x7 15.8 us: nt(): lax.dot_general(left, right, (((1,), (1,)), ((), ())), preferred_element_...]
    psum x1 -> x0, blocking collectives: 40.8 us -> none  [on_device(): lax.psum((gain_attn_part, gain_mlp_part), ('dp', 'tensor'))]
    all_gather x0 -> x1, blocking collectives: none -> 27.2 us  [on_device(): lax.all_gather(out_here, ('core', 'chip'), axis=0, tiled=True).astype(F32)]
  transfers between devices with their start and end apart: 9 -> 62, of which waited for: 9 -> 25; matrix products, arithmetic and copies ran while one was open for 6% -> 16% of each run, Pallas kernels for 0% -> 2%
where the time goes in v1:
time: 567 us; the launch traced here: 562 us
  waiting for transfers between devices  256 us (45%)
  starting transfers between devices  83.7 us (15%)
  local copies, waits for them, and re-layouts  71.3 us (13%)
  other arithmetic  43.6 us (8%)
  matrix products  37.3 us (7%)
  blocking collectives  27.2 us (5%)
  Pallas kernels  25.1 us (4%)
  between operations  17 us (3%)
    ppermute x30, waiting for transfers between devices, flip(): return lax.ppermute(value, axis, [(i, i ^ bit) for i in range(count)])  124 us
    ppermute x27, waiting for transfers between devices, shift(): lax.ppermute(value, 'tensor', [(i, (i + by) % count) for i in range(count)])  103 us
    ppermute x27, starting transfers between devices, shift(): lax.ppermute(value, 'tensor', [(i, (i + by) % count) for i in range(count)])  52.9 us
    unnamed x157, local copies, waits for them, and re-layouts  37.6 us
    ppermute x30, starting transfers between devices, flip(): return lax.ppermute(value, axis, [(i, i ^ bit) for i in range(count)])  30.4 us
    all_gather x1, blocking collectives, on_device(): lax.all_gather(out_here, ('core', 'chip'), axis=0, tiled=True).astype(F32)  27.2 us
    all_gather x1, waiting for transfers between devices, on_device(): every = lax.all_gather(pieces, ('core', 'chip'), axis=0, tiled=False)  24.7 us
    dot_general x7, matrix products, nt(): lax.dot_general(left, right, (((1,), (1,)), ((), ())), preferred_element_...  15.8 us
  transfers between devices with their start and end apart: 62, of which 25 were waited for; matrix products, arithmetic and copies ran while one was open for 16% of the time, Pallas kernels for 2%

profile of v1, /device:TPU:0, one launch (start us, length us, event | category | flops | bytes accessed | tf_op | source)
XLA Modules:
  0.0 561.6 jit_solution(4450600491112593283)
XLA Ops:
  12.2 5.0 collective-permute-start
  35.6 29.5 %collective-permute-done.17 = bf16[88,1024]{1,0:T(8,128)(2,1)S(1)} collective-permute-done((bf16[88,1024]{1,0:T(8,128)(2,1)}, bf16[88,1024]{1,0:T(8,128)(2,1)S(1)}, u32[]{:S(2)}, u32[]{:S(2)}) %collective-permute-start.17) | collective-permute-done | bytes 180256 | tf_op jit(solution)/shard_map/ppermute | solution.py:207
  73.9 18.6 %collective-permute-done.9 = bf16[2,88,1024]{2,1,0:T(8,128)(2,1)S(1)} collective-permute-done((bf16[2,88,1024]{2,1,0:T(8,128)(2,1)S(1)}, bf16[2,88,1024]{2,1,0:T(8,128)(2,1)S(1)}, u32[]{:S(2)}, u32[]{:S(2)}) %collective-permute-start.9) | collective-permute-done | bytes 360480 | tf_op jit(solution)/shard_map/ppermute | solution.py:207
  92.8 12.4 %collective-permute-done.8 = bf16[2,88,1024]{2,1,0:T(8,128)(2,1)S(1)} collective-permute-done((bf16[2,88,1024]{2,1,0:T(8,128)(2,1)S(1)}, bf16[2,88,1024]{2,1,0:T(8,128)(2,1)S(1)}, u32[]{:S(2)}, u32[]{:S(2)}) %collective-permute-start.8) | collective-permute-done | bytes 360480 | tf_op jit(solution)/shard_map/ppermute | solution.py:207
  106.7 11.3 %collective-permute-done.7 = bf16[2,88,1024]{2,1,0:T(8,128)(2,1)S(1)} collective-permute-done((bf16[2,88,1024]{2,1,0:T(8,128)(2,1)S(1)}, bf16[2,88,1024]{2,1,0:T(8,128)(2,1)S(1)}, u32[]{:S(2)}, u32[]{:S(2)}) %collective-permute-start.7) | collective-permute-done | bytes 360480 | tf_op jit(solution)/shard_map/ppermute | solution.py:207
  149.4 9.6 %shard_map.153 = (bf16[1024,256]{1,0:T(8,128)(2,1)S(1)}, f32[2,2,896]{2,1,0:T(2,128)S(1)}) custom-call(bf16[1024,256]{1,0:T(8,128)(2,1)S(1)} %get-tuple-element.16.refs_0_, bf16[1024,256]{1,0:T(8,128)(2,1)S(1)} %get-tuple-element.17.refs_1_, bf16[1024,256]{1,0:T(8,128)(2,1)S(1)} %get-tuple-element.18.refs_2_), custom_call_target="tpu_custom_call" | custom-call | flops 1644167168 | bytes 2097152 | tf_op jit(solution)/shard_map/pallas_call | solution.py:126
  164.5 10.8 %collective-permute-start.5 = (bf16[256,256]{1,0:T(8,128)(2,1)}, bf16[256,256]{1,0:T(8,128)(2,1)S(1)}, u32[]{:S(2)}, u32[]{:S(2)}) collective-permute-start(bf16[256,256]{1,0:T(8,128)(2,1)} %get-tuple-element.111), channel_id=1, source_target_pairs={{0,3},{1,0},{2,1},{3,2},{4,7},{5,4},{6,5},{7,6},{8,11},{9,8},{10,9... | collective-permute-start | bytes 393224 | tf_op jit(solution)/shard_map/ppermute | solution.py:207
  205.1 5.2 fusion.79
  227.5 7.8 %collective-permute-done.29 = bf16[256,256]{1,0:T(8,128)(2,1)S(1)} collective-permute-done((bf16[256,256]{1,0:T(8,128)(2,1)}, bf16[256,256]{1,0:T(8,128)(2,1)S(1)}, u32[]{:S(2)}, u32[]{:S(2)}) %collective-permute-start.29) | collective-permute-done | bytes 131104 | tf_op jit(solution)/shard_map/ppermute | solution.py:207
  244.7 12.6 %shard_map.154 = (bf16[1024,256]{1,0:T(8,128)(2,1)S(1)}, bf16[1024,256]{1,0:T(8,128)(2,1)S(1)}, bf16[1024,256]{1,0:T(8,128)(2,1)S(1)}) custom-call(bf16[1024,256]{1,0:T(8,128)(2,1)S(1)} %copy-done.10, bf16[1024,256]{1,0:T(8,128)(2,1)S(1)} %copy-done.12, bf16[1024,256]{1,0:T(8,128)(2,1)S(1)} %copy-done.14, ...), custom_call_target="tpu_custom_call" | custom-call | flops 4110417920 | bytes 5242880 | tf_op jit(solution)/shard_map/pallas_call | solution.py:190
  282.2 10.5 %collective-permute-done.52 = bf16[352,1024]{1,0:T(8,128)(2,1)S(1)} collective-permute-done((bf16[352,1024]{1,0:T(8,128)(2,1)S(1)}, bf16[352,1024]{1,0:T(8,128)(2,1)S(1)}, u32[]{:S(2)}, u32[]{:S(2)}) %collective-permute-start.52) | collective-permute-done | bytes 720928 | tf_op jit(solution)/shard_map/ppermute | solution.py:211
  304.4 6.0 %collective-permute-done.40 = bf16[352,1024]{1,0:T(8,128)(2,1)} collective-permute-done((bf16[352,1024]{1,0:T(8,128)(2,1)}, bf16[352,1024]{1,0:T(8,128)(2,1)}, u32[]{:S(2)}, u32[]{:S(2)}) %collective-permute-start.40) | collective-permute-done | bytes 720928 | tf_op jit(solution)/shard_map/ppermute | solution.py:211
  313.4 18.9 %collective-permute-done.51 = bf16[352,1024]{1,0:T(8,128)(2,1)} collective-permute-done((bf16[352,1024]{1,0:T(8,128)(2,1)}, bf16[352,1024]{1,0:T(8,128)(2,1)}, u32[]{:S(2)}, u32[]{:S(2)}) %collective-permute-start.51) | collective-permute-done | bytes 720928 | tf_op jit(solution)/shard_map/ppermute | solution.py:211
  336.2 40.7 %collective-permute-done.47 = bf16[352,1024]{1,0:T(8,128)(2,1)S(1)} collective-permute-done((bf16[352,1024]{1,0:T(8,128)(2,1)}, bf16[352,1024]{1,0:T(8,128)(2,1)S(1)}, u32[]{:S(2)}, u32[]{:S(2)}) %collective-permute-start.47) | collective-permute-done | bytes 720928 | tf_op jit(solution)/shard_map/ppermute | solution.py:211
  389.4 7.8 %collective-permute-start.43 = (bf16[88,1024]{1,0:T(8,128)(2,1)S(1)}, bf16[88,1024]{1,0:T(8,128)(2,1)S(1)}, u32[]{:S(2)}, u32[]{:S(2)}) collective-permute-start(bf16[88,1024]{1,0:T(8,128)(2,1)S(1)} %get-tuple-element.97), channel_id=1, source_target_pairs={{0,2},{1,3},{2,0},{3,1},{4,6},{5,7},{6,4},{7,5},{8,10},{9,11},{10,... | collective-permute-start | bytes 540680 | tf_op jit(solution)/shard_map/ppermute | solution.py:207
  398.4 12.6 %collective-permute-done.49 = bf16[88,1024]{1,0:T(8,128)(2,1)S(1)} collective-permute-done((bf16[88,1024]{1,0:T(8,128)(2,1)S(1)}, bf16[88,1024]{1,0:T(8,128)(2,1)S(1)}, u32[]{:S(2)}, u32[]{:S(2)}) %collective-permute-start.49) | collective-permute-done | bytes 180256 | tf_op jit(solution)/shard_map/ppermute | solution.py:207
  411.1 6.7 %collective-permute-done.43 = bf16[88,1024]{1,0:T(8,128)(2,1)S(1)} collective-permute-done((bf16[88,1024]{1,0:T(8,128)(2,1)S(1)}, bf16[88,1024]{1,0:T(8,128)(2,1)S(1)}, u32[]{:S(2)}, u32[]{:S(2)}) %collective-permute-start.43) | collective-permute-done | bytes 180256 | tf_op jit(solution)/shard_map/ppermute | solution.py:207
  438.2 22.2 %collective-permute-done.37 = f32[2048]{0:T(1024)S(1)} collective-permute-done((f32[2048]{0:T(1024)S(1)}, f32[2048]{0:T(1024)S(1)}, u32[]{:S(2)}, u32[]{:S(2)}) %collective-permute-start.37) | collective-permute-done | bytes 8224 | tf_op jit(solution)/shard_map/ppermute | solution.py:211
  462.7 10.0 %collective-permute-done.38 = f32[2048]{0:T(1024)S(1)} collective-permute-done((f32[2048]{0:T(1024)S(1)}, f32[2048]{0:T(1024)S(1)}, u32[]{:S(2)}, u32[]{:S(2)}) %collective-permute-start.38) | collective-permute-done | bytes 8224 | tf_op jit(solution)/shard_map/ppermute | solution.py:211
  475.1 27.2 %all_gather.17 = bf16[256,1024]{1,0:T(8,128)(2,1)S(1)} all-gather(bf16[32,1024]{1,0:T(8,128)(2,1)} %reduce-scatter.5.cloned.1.call-done), channel_id=1, replica_groups=mesh['chip'=4,'core'=2,'tensor'=4] {'core','chip'}, dimensions={0}, use_global_device_ids=true | all-gather | bytes 589824 | tf_op jit(solution)/shard_map/all_gather | solution.py:432
  506.8 24.7 %all-gather.9.cloned.1.call-done = bf16[24,88,1024]{2,1,0:T(8,128)(2,1)} async-done(((bf16[3,88,1024]{2,1,0:T(8,128)(2,1)}), bf16[24,88,1024]{2,1,0:T(8,128)(2,1)}) %all-gather.9.cloned.1.call-update) | async-done | bytes 4325392 | tf_op jit(solution)/shard_map/all_gather | solution.py:418
  531.5 4.6 copy_convert_fusion
  536.1 4.7 copy.31
  543.0 4.4 copy.29
  (368 shorter events, 220.5 us)
Async XLA Ops:
  7.2 177.4 %all-gather.5.cloned.1.call-start = ((), (), s32[]{:S(2)}) async-start(), calls=%async_computation.2 | async-start | bytes 2162688 | tf_op jit(solution)/shard_map/all_gather | solution.py:315
  12.2 124.6 %collective-permute-start = (bf16[256,1024]{1,0:T(8,128)(2,1)}, bf16[256,1024]{1,0:T(8,128)(2,1)}, u32[]{:S(2)}, u32[]{:S(2)}) collective-permute-start(bf16[256,1024]{1,0:T(8,128)(2,1)} %get-tuple-element.69), channel_id=1, source_target_pairs={{0,3},{1,0},{2,1},{3,2},{4,7},{5,4},{6,5},{7,6},{8,11},{9,8},{10,9... | collective-permute-start | bytes 1572872 | tf_op jit(solution)/shard_map/ppermute | solution.py:207
  17.2 122.2 %collective-permute-start.1 = (bf16[256,1024]{1,0:T(8,128)(2,1)}, bf16[256,1024]{1,0:T(8,128)(2,1)}, u32[]{:S(2)}, u32[]{:S(2)}) collective-permute-start(bf16[256,1024]{1,0:T(8,128)(2,1)} %get-tuple-element.69), channel_id=1, source_target_pairs={{0,2},{1,3},{2,0},{3,1},{4,6},{5,7},{6,4},{7,5},{8,10},{9,11},{10,... | collective-permute-start | bytes 1572872 | tf_op jit(solution)/shard_map/ppermute | solution.py:207
  23.5 41.6 %collective-permute-start.17 = (bf16[88,1024]{1,0:T(8,128)(2,1)}, bf16[88,1024]{1,0:T(8,128)(2,1)S(1)}, u32[]{:S(2)}, u32[]{:S(2)}) collective-permute-start(bf16[88,1024]{1,0:T(8,128)(2,1)} %get-tuple-element.67), channel_id=1, source_target_pairs={{0,2},{1,3},{2,0},{3,1},{4,6},{5,7},{6,4},{7,5},{8,10},{9,11},{10,... | collective-permute-start | bytes 540680 | tf_op jit(solution)/shard_map/ppermute | solution.py:207
  26.5 39.4 %collective-permute-start.16 = (bf16[88,1024]{1,0:T(8,128)(2,1)}, bf16[88,1024]{1,0:T(8,128)(2,1)}, u32[]{:S(2)}, u32[]{:S(2)}) collective-permute-start(bf16[88,1024]{1,0:T(8,128)(2,1)} %get-tuple-element.67), channel_id=1, source_target_pairs={{0,3},{1,0},{2,1},{3,2},{4,7},{5,4},{6,5},{7,6},{8,11},{9,8},{10,9... | collective-permute-start | bytes 540680 | tf_op jit(solution)/shard_map/ppermute | solution.py:207
  26.9 43.3 %collective-permute-start.18 = (bf16[88,1024]{1,0:T(8,128)(2,1)}, bf16[88,1024]{1,0:T(8,128)(2,1)S(1)}, u32[]{:S(2)}, u32[]{:S(2)}) collective-permute-start(bf16[88,1024]{1,0:T(8,128)(2,1)} %get-tuple-element.67), channel_id=1, source_target_pairs={{0,1},{1,2},{2,3},{3,0},{4,5},{5,6},{6,7},{7,4},{8,9},{9,10},{10,1... | collective-permute-start | bytes 540680 | tf_op jit(solution)/shard_map/ppermute | solution.py:207
  29.1 275.2 %reduce-scatter.3.cloned.1.call-start = ((), (), s32[]{:S(2)}) async-start(), calls=%async_computation.3 | async-start | bytes 1769472 | tf_op jit(solution)/shard_map/reduce_scatter | solution.py:437
  65.1 76.0 %collective-permute-start.2 = (bf16[256,1024]{1,0:T(8,128)(2,1)}, bf16[256,1024]{1,0:T(8,128)(2,1)S(1)}, u32[]{:S(2)}, u32[]{:S(2)}) collective-permute-start(bf16[256,1024]{1,0:T(8,128)(2,1)} %get-tuple-element.69), channel_id=1, source_target_pairs={{0,1},{1,2},{2,3},{3,0},{4,5},{5,6},{6,7},{7,4},{8,9},{9,10},{10,1... | collective-permute-start | bytes 1572872 | tf_op jit(solution)/shard_map/ppermute | solution.py:207
  131.7 47.1 %collective-permute-start.10 = (bf16[264,1024]{1,0:T(8,128)(2,1)S(1)}, bf16[264,1024]{1,0:T(8,128)(2,1)}, u32[]{:S(2)}, u32[]{:S(2)}) collective-permute-start(bf16[264,1024]{1,0:T(8,128)(2,1)S(1)} %pad_maximum_fusion.6), channel_id=1, source_target_pairs={{0,8},{8,0},{16,24},{24,16},{1,9},{9,1},{17,25},{25,17},{2,10},{10... | collective-permute-start | bytes 1622024 | tf_op jit(solution)/shard_map/ppermute | solution.py:211
  136.8 43.2 %collective-permute-start.11 = (bf16[264,1024]{1,0:T(8,128)(2,1)S(1)}, bf16[264,1024]{1,0:T(8,128)(2,1)S(1)}, u32[]{:S(2)}, u32[]{:S(2)}) collective-permute-start(bf16[264,1024]{1,0:T(8,128)(2,1)S(1)} %pad_maximum_fusion.6), channel_id=1, source_target_pairs={{0,16},{8,24},{16,0},{24,8},{1,17},{9,25},{17,1},{25,9},{2,18},{10... | collective-permute-start | bytes 1622024 | tf_op jit(solution)/shard_map/ppermute | solution.py:211
  261.0 214.1 %reduce-scatter.5.cloned.1.call-start = ((), (), s32[]{:S(2)}) async-start(), calls=%async_computation.5 | async-start | bytes 2162688 | tf_op jit(solution)/shard_map/reduce_scatter | solution.py:429
  265.0 238.4 %all-gather.7.cloned.1.call-start = ((), (), s32[]{:S(2)}) async-start(), calls=%async_computation.4 | async-start | bytes 1769472 | tf_op jit(solution)/shard_map/all_gather | solution.py:438
  281.6 50.7 %collective-permute-start.51 = (bf16[352,1024]{1,0:T(8,128)(2,1)}, bf16[352,1024]{1,0:T(8,128)(2,1)}, u32[]{:S(2)}, u32[]{:S(2)}) collective-permute-start(bf16[352,1024]{1,0:T(8,128)(2,1)} %get-tuple-element.79), channel_id=1, source_target_pairs={{0,8},{8,0},{16,24},{24,16},{1,9},{9,1},{17,25},{25,17},{2,10},{10... | collective-permute-start | bytes 2162696 | tf_op jit(solution)/shard_map/ppermute | solution.py:211
  293.9 39.7 %collective-permute-start.53 = (bf16[352,1024]{1,0:T(8,128)(2,1)}, bf16[352,1024]{1,0:T(8,128)(2,1)}, u32[]{:S(2)}, u32[]{:S(2)}) collective-permute-start(bf16[352,1024]{1,0:T(8,128)(2,1)} %add_convert_fusion.1), channel_id=1, source_target_pairs={{0,16},{8,24},{16,0},{24,8},{1,17},{9,25},{17,1},{25,9},{2,18},{10... | collective-permute-start | bytes 2162696 | tf_op jit(solution)/shard_map/ppermute | solution.py:211
  295.3 40.3 %collective-permute-start.45 = (bf16[352,1024]{1,0:T(8,128)(2,1)}, bf16[352,1024]{1,0:T(8,128)(2,1)}, u32[]{:S(2)}, u32[]{:S(2)}) collective-permute-start(bf16[352,1024]{1,0:T(8,128)(2,1)} %get-tuple-element.77), channel_id=1, source_target_pairs={{0,16},{8,24},{16,0},{24,8},{1,17},{9,25},{17,1},{25,9},{2,18},{10... | collective-permute-start | bytes 2162696 | tf_op jit(solution)/shard_map/ppermute | solution.py:211
  297.5 82.0 %collective-permute-start.39 = (bf16[352,1024]{1,0:T(8,128)(2,1)}, bf16[352,1024]{1,0:T(8,128)(2,1)}, u32[]{:S(2)}, u32[]{:S(2)}) collective-permute-start(bf16[352,1024]{1,0:T(8,128)(2,1)} %get-tuple-element.75), channel_id=1, source_target_pairs={{0,8},{8,0},{16,24},{24,16},{1,9},{9,1},{17,25},{25,17},{2,10},{10... | collective-permute-start | bytes 2162696 | tf_op jit(solution)/shard_map/ppermute | solution.py:211
  304.3 227.2 %all-gather.9.cloned.1.call-start = ((), (), s32[]{:S(2)}) async-start(), calls=%async_computation.6 | async-start | bytes 4866048 | tf_op jit(solution)/shard_map/all_gather | solution.py:418
  310.4 66.6 %collective-permute-start.47 = (bf16[352,1024]{1,0:T(8,128)(2,1)}, bf16[352,1024]{1,0:T(8,128)(2,1)S(1)}, u32[]{:S(2)}, u32[]{:S(2)}) collective-permute-start(bf16[352,1024]{1,0:T(8,128)(2,1)} %add_convert_fusion.4), channel_id=1, source_target_pairs={{0,8},{8,0},{16,24},{24,16},{1,9},{9,1},{17,25},{25,17},{2,10},{10... | collective-permute-start | bytes 2162696 | tf_op jit(solution)/shard_map/ppermute | solution.py:211
  332.3 50.3 %collective-permute-start.41 = (bf16[352,1024]{1,0:T(8,128)(2,1)S(1)}, bf16[352,1024]{1,0:T(8,128)(2,1)S(1)}, u32[]{:S(2)}, u32[]{:S(2)}) collective-permute-start(bf16[352,1024]{1,0:T(8,128)(2,1)S(1)} %add_convert_fusion.7), channel_id=1, source_target_pairs={{0,16},{8,24},{16,0},{24,8},{1,17},{9,25},{17,1},{25,9},{2,18},{10... | collective-permute-start | bytes 2162696 | tf_op jit(solution)/shard_map/ppermute | solution.py:211
  335.6 49.9 %collective-permute-start.56 = (bf16[88,1024]{1,0:T(8,128)(2,1)S(1)}, bf16[88,1024]{1,0:T(8,128)(2,1)S(1)}, u32[]{:S(2)}, u32[]{:S(2)}) collective-permute-start(bf16[88,1024]{1,0:T(8,128)(2,1)S(1)} %get-tuple-element.102), channel_id=1, source_target_pairs={{0,3},{1,0},{2,1},{3,2},{4,7},{5,4},{6,5},{7,6},{8,11},{9,8},{10,9... | collective-permute-start | bytes 540680 | tf_op jit(solution)/shard_map/ppermute | solution.py:207
  335.6 49.9 %collective-permute-start.55 = (bf16[88,1024]{1,0:T(8,128)(2,1)S(1)}, bf16[88,1024]{1,0:T(8,128)(2,1)S(1)}, u32[]{:S(2)}, u32[]{:S(2)}) collective-permute-start(bf16[88,1024]{1,0:T(8,128)(2,1)S(1)} %get-tuple-element.103), channel_id=1, source_target_pairs={{0,2},{1,3},{2,0},{3,1},{4,6},{5,7},{6,4},{7,5},{8,10},{9,11},{10,... | collective-permute-start | bytes 540680 | tf_op jit(solution)/shard_map/ppermute | solution.py:207
  426.0 47.2 %collective-permute-start.33 = (bf16[256,1024]{1,0:T(8,128)(2,1)S(1)}, bf16[256,1024]{1,0:T(8,128)(2,1)S(1)}, u32[]{:S(2)}, u32[]{:S(2)}) collective-permute-start(bf16[256,1024]{1,0:T(8,128)(2,1)S(1)} %get-tuple-element.88), channel_id=1, source_target_pairs={{0,3},{1,0},{2,1},{3,2},{4,7},{5,4},{6,5},{7,6},{8,11},{9,8},{10,9... | collective-permute-start | bytes 1572872 | tf_op jit(solution)/shard_map/ppermute | solution.py:207
  426.1 47.2 %collective-permute-start.32 = (bf16[256,1024]{1,0:T(8,128)(2,1)S(1)}, bf16[256,1024]{1,0:T(8,128)(2,1)S(1)}, u32[]{:S(2)}, u32[]{:S(2)}) collective-permute-start(bf16[256,1024]{1,0:T(8,128)(2,1)S(1)} %get-tuple-element.87), channel_id=1, source_target_pairs={{0,2},{1,3},{2,0},{3,1},{4,6},{5,7},{6,4},{7,5},{8,10},{9,11},{10,... | collective-permute-start | bytes 1572872 | tf_op jit(solution)/shard_map/ppermute | solution.py:207
  427.5 45.7 %collective-permute-start.31 = (bf16[256,1024]{1,0:T(8,128)(2,1)S(1)}, bf16[256,1024]{1,0:T(8,128)(2,1)S(1)}, u32[]{:S(2)}, u32[]{:S(2)}) collective-permute-start(bf16[256,1024]{1,0:T(8,128)(2,1)S(1)} %get-tuple-element.86), channel_id=1, source_target_pairs={{0,1},{1,2},{2,3},{3,0},{4,5},{5,6},{6,7},{7,4},{8,9},{9,10},{10,1... | collective-permute-start | bytes 1572872 | tf_op jit(solution)/shard_map/ppermute | solution.py:207
  (96 other events, 1296.8 us)
Sparse Core Ops, SparseCore 0:
  29.3 93.7 all-gather.4
  261.1 43.1 reduce-scatter.2
  307.1 141.7 reduce-scatter.4
  450.8 40.9 all-gather.6
  494.3 37.2 all-gather.8

commit v2 on v1

--- a/solution.py
+++ b/solution.py
@@ -203,6 +203,43 @@
     )(queries, keys, values, grads, logs, cos, sin)
 
 
+def assemble_kernel(cores, chips, share, per, piece, out_piece, in_ref, gu_ref, d_ref, held):
+    hidden = cores * share
+    for m, first in ((0, 0), (1, piece), (2, 2 * piece + out_piece)):
+        for c in range(cores):
+            for j in range(chips):
+                at = c * share + j * per
+                rows = in_ref[c * chips + j].astype(F32)
+                held[at : at + piece, :] = rows[first : first + piece, :]
+        if m == 2:
+            d_ref[...] = held[:hidden, :]
+        else:
+            gu_ref[m] = held[...].T[:, :hidden]
+
+
+def assemble(every, cores, chips, share, per, piece, out_piece):
+    devices, rows, width = every.shape
+    hidden = cores * share
+    block = 256
+    tall = -(-((cores - 1) * share + (chips - 1) * per + piece) // 128) * 128
+    return pl.pallas_call(
+        lambda *refs: assemble_kernel(cores, chips, share, per, piece, out_piece, *refs),
+        grid=(width // block,),
+        in_specs=[pl.BlockSpec((devices, rows, block), lambda i: (0, 0, i))],
+        out_specs=[
+            pl.BlockSpec((2, block, hidden), lambda i: (0, i, 0)),
+            pl.BlockSpec((hidden, block), lambda i: (0, i)),
+        ],
+        out_shape=[
+            jax.ShapeDtypeStruct((2, width, hidden), F32),
+            jax.ShapeDtypeStruct((hidden, width), F32),
+        ],
+        scratch_shapes=[pltpu.VMEM((tall, block), F32)],
+        compiler_params=pltpu.CompilerParams(vmem_limit_bytes=40 * 2**20),
+        cost_estimate=pl.CostEstimate(flops=0, bytes_accessed=12 * 2**20, transcendentals=0),
+    )(every)
+
+
 def shift(value, by, count):
     return lax.ppermute(value, "tensor", [(i, (i + by) % count) for i in range(count)])
 
@@ -216,22 +253,32 @@
     return bits[::-1] if turned else bits
 
 
-def gather_chips(value, count, turned):
-    held = {0: value}
-    for bit in bits_of(count, turned):
-        held.update({i ^ bit: flip(v, "chip", bit, count) for i, v in list(held.items())})
-    return [held[i] for i in range(count)]
-
-
-def scatter_chips(blocks, count, turned):
-    held = dict(enumerate(blocks))
-    for bit in bits_of(count, turned):
-        held = {
-            i: (v.astype(F32) + flip(held[i ^ bit], "chip", bit, count).astype(F32)).astype(BF)
-            for i, v in held.items()
-            if not i & bit
-        }
-    return held[0]
+def halving(value, chip, count, turned):
+    bits = count.bit_length() - 1
+    held = value.reshape((2,) * bits + (-1,) + value.shape[-1:])
+    order = list(range(bits))
+    if not turned:
+        order = order[::-1]
+    left = list(range(bits))
+    for axis in order:
+        bit = bits - 1 - axis
+        mine = (chip >> bit) & 1
+        at = left.index(axis)
+        left.remove(axis)
+        kept = lax.dynamic_index_in_dim(held, mine, at, keepdims=False)
+        sent = lax.dynamic_index_in_dim(held, 1 - mine, at, keepdims=False)
+        came = flip(sent, "chip", 1 << bit, count)
+        tied = yield came
+        came = came if tied is None else tied
+        held = (kept.astype(F32) + came.astype(F32)).astype(BF)
+    yield held
+
+
+def finish(steps, tied):
+    last = next(steps) if tied is None else steps.send(tied)
+    for value in steps:
+        last = value
+    return last
 
 
 def total_all(value, sizes):
@@ -284,50 +331,58 @@
         share = hidden // cores
         per = -(-share // chips)
         piece = -(-per // 8) * 8
+        heads_rows = output_weight.shape[0]
+        out_piece = heads_rows // (cores * chips)
         hidden_t = jnp.concatenate([jnp.swapaxes(gate_up_weight, 1, 2), down_weight[None]])
         half_t = lax.dynamic_slice_in_dim(hidden_t, core * share, share, axis=1)
         half_t = jnp.pad(half_t, ((0, 0), (0, chips * per - share), (0, 0)))
         half_t = half_t.reshape(3, chips, per, width)
         half_t = jnp.pad(half_t, ((0, 0), (0, 0), (0, piece - per), (0, 0)))
-        own = [
-            lax.dynamic_index_in_dim(half_t, chip ^ i, axis=1, keepdims=False)
-            for i in range(chips)
-        ]
-        gate_up_sent = own[0][:2]
-        down_sent = own[0][2]
-        gate_up_came = [shift(gate_up_sent, -k, ranks) for k in range(1, ranks)]
-        down_came = jnp.concatenate([shift(down_sent, -k, ranks) for k in range(1, ranks)])
-        gates = gather_chips(jnp.concatenate([g[0] for g in gate_up_came]), chips, False)
-        ups = gather_chips(jnp.concatenate([g[1] for g in gate_up_came]), chips, True)
-        cut = down_came.shape[0] // 16 * 8
-        downs_a = gather_chips(down_came[:cut], chips, False)
-        downs_b = gather_chips(down_came[cut:], chips, True)
-        gate = jnp.concatenate([v for i in range(chips) for v in (own[i][0], gates[i])])
-        up = jnp.concatenate([v for i in range(chips) for v in (own[i][1], ups[i])])
-        down = jnp.concatenate(
-            [v for i in range(chips) for v in (own[i][2], downs_a[i], downs_b[i])]
-        )
-        heads_rows = output_weight.shape[0]
-        out_piece = heads_rows // (cores * chips)
+        mine = lax.dynamic_index_in_dim(half_t, chip, axis=1, keepdims=False)
         out_mine = lax.dynamic_slice_in_dim(
             output_weight, (core * chips + chip) * out_piece, out_piece
         )
-        out_all = lax.all_gather(out_mine, ("tensor", "core", "chip"), axis=0, tiled=True)
-        out_all = out_all.reshape(ranks, heads_rows, width)
-        outs = [
-            lax.dynamic_index_in_dim(out_all, (rank - k) % ranks, axis=0, keepdims=False)
-            for k in range(ranks)
-        ]
-        out_weight = jnp.concatenate(outs)
+        gate_up_mine = mine[:2].reshape(2 * piece, width)
+        down_out_mine = jnp.concatenate([mine[2], out_mine])
+        gate_up_came = [shift(gate_up_mine, -k, ranks) for k in range(1, ranks)]
 
         token_f = tokens[0].astype(F32)
+        normal_attn, inverse_attn = normalize(token_f)
+        normed_attn = (normal_attn * gain_attn).astype(BF)
+        normed_sent, *gate_up_came = lax.optimization_barrier((normed_attn, *gate_up_came))
+        normed_came = [shift(normed_sent, -k, ranks) for k in range(1, ranks)]
+        down_out_sent, *normed_came = lax.optimization_barrier((down_out_mine, *normed_came))
+        down_out_came = [shift(down_out_sent, -k, ranks) for k in range(1, ranks)]
+        others = ranks - 1
+        gate_up_all = lax.all_gather(jnp.concatenate(gate_up_came), "chip")
+        gate_up_all = gate_up_all.reshape(chips, others, 2, piece, width)
+        down_out_all = lax.all_gather(jnp.concatenate(down_out_came), "chip")
+        down_out_all = down_out_all.reshape(chips, others, piece + out_piece, width)
+
+        def whole(own, rest):
+            joined = jnp.concatenate([own[:, None], rest], axis=1)
+            return joined.reshape(chips * ranks * piece, width)
+
+        gate = whole(half_t[0], gate_up_all[:, :, 0])
+        up = whole(half_t[1], gate_up_all[:, :, 1])
+        down = whole(half_t[2], down_out_all[:, :, :piece])
+        out_half = jnp.swapaxes(down_out_all[:, :, piece:], 0, 1)
+        out_half = out_half.reshape(others, heads_rows // cores, width)
+        out_other = flip(out_half, "core", 1, cores)
+        out_rest = jnp.concatenate(
+            [
+                jnp.where(core == 0, out_half, out_other),
+                jnp.where(core == 0, out_other, out_half),
+            ],
+            axis=1,
+        )
+        out_weight = jnp.concatenate(
+            [output_weight] + [out_rest[ranks - 1 - k] for k in range(1, ranks)]
+        )
+
         cot = cotangent[0]
         cot_pair = jnp.concatenate([cot, flip(cot, "core", 1, cores)])
-        normal_attn, inverse_attn = normalize(token_f)
-        normed_attn = (normal_attn * gain_attn).astype(BF)
-        normed_rows = jnp.concatenate(
-            [normed_attn] + [shift(normed_attn, -k, ranks) for k in range(1, ranks)]
-        )
+        normed_rows = jnp.concatenate([normed_attn] + normed_came)
         normed_doc = rotate(normed_rows, into_doc)
         queries, keys, values = project(normed_doc, query_key_value_weight, cos_table, sin_table)
         mixture, logs = attend(queries, keys, values, doc)
@@ -350,12 +405,20 @@
         gate_grad = (hid_grad * up_proj * (cdf + gate_proj * pdf)).astype(BF)
         up_grad = (hid_grad * act).astype(BF)
         in_part = nn(gate_grad, gate) + nn(up_grad, up)
+        down_grad = tn(hid, cot_pair).astype(BF)
+        gate_w_grad = tn(gate_grad, normed_pair).astype(BF)
+        up_w_grad = tn(up_grad, normed_pair).astype(BF)
+        down_sum = halving(down_grad, chip, chips, False)
+        next(down_sum)
+        in_part, gate_w_grad, up_w_grad = lax.optimization_barrier(
+            (in_part, gate_w_grad, up_w_grad)
+        )
+        gate_sum = halving(gate_w_grad, chip, chips, False)
+        up_sum = halving(up_w_grad, chip, chips, True)
+        came = [next(gate_sum), next(up_sum)]
         normed_mlp_grad = in_part[:own_rows] + flip(
             in_part[own_rows:].astype(BF), "core", 1, cores
         ).astype(F32)
-        down_grad = tn(hid, cot_pair).astype(BF)
-        gate_w_grad = tn(gate_grad, normed_pair).astype(BF)
-        up_w_grad = tn(up_grad, normed_pair).astype(BF)
         mlp_part = nn(hid, down)
         mlp_out = mlp_part[:own_rows] + flip(
             mlp_part[own_rows:].astype(BF), "core", 1, cores
@@ -377,6 +440,10 @@
         )
         attended_doc = rotate(attended_rows, into_doc)
         out_w_grad = tn(attention, branch_grad).astype(BF)
+        attended_doc, *came = lax.optimization_barrier((attended_doc, *came))
+        gate_here = finish(gate_sum, came[0])
+        up_here = finish(up_sum, came[1])
+        down_here = finish(down_sum, None)
         dq, dk, dv = attend_back(
             queries, keys, values, attended_doc, logs, cos_table, sin_table, doc
         )
@@ -399,45 +466,53 @@
         )
         grad_gain_attn, grad_gain_mlp = gains[:width], gains[width:]
 
-        def scatter_hidden(grad, turned):
-            blocks = grad.reshape(chips, ranks * piece, width)
-            here = scatter_chips([blocks[i] for i in range(chips)], chips, turned)
-            here = here.reshape(ranks, piece, width)
+        def sum_ranks(here):
             total = here[0].astype(F32)
             for k in range(1, ranks):
                 total = total + shift(here[k], k, ranks).astype(F32)
             return total.astype(BF)
 
-        pieces = jnp.stack(
-            [
-                scatter_hidden(gate_w_grad, False),
-                scatter_hidden(up_w_grad, True),
-                scatter_hidden(down_grad, False),
-            ]
-        )
-        every = lax.all_gather(pieces, ("core", "chip"), axis=0, tiled=False)
-        every = every[:, :, :per].reshape(cores, chips, 3, per, width)
-        every = jnp.moveaxis(every, 2, 0).reshape(3, cores, chips * per, width)[:, :, :share]
-        every = every.reshape(3, hidden, width).astype(F32)
-        grad_gateup = jnp.swapaxes(every[:2], 1, 2)
-        down_weight_gradient = every[2]
-
-        back_order = [(ranks - k) % ranks for k in range(ranks)]
-        out_blocks = out_w_grad.reshape(ranks, heads_rows, width)
-        out_blocks = jnp.concatenate([out_blocks[k] for k in back_order])
-        out_blocks = rotate(out_blocks, ((ranks - rank) % ranks) * heads_rows)
-        out_here = lax.psum_scatter(
-            out_blocks, ("tensor", "core", "chip"), scatter_dimension=0, tiled=True
-        )
-        output_weight_gradient = lax.all_gather(
-            out_here, ("core", "chip"), axis=0, tiled=True
-        ).astype(F32)
-
+        def sum_cores(value, axis):
+            kept = lax.dynamic_index_in_dim(value, core, axis, keepdims=False)
+            sent = lax.dynamic_index_in_dim(value, 1 - core, axis, keepdims=False)
+            return (kept.astype(F32) + flip(sent, "core", 1, cores).astype(F32)).astype(BF)
+
+        out_blocks = out_w_grad.reshape(ranks, cores, chips, out_piece, width)
+        out_blocks = jnp.stack([out_blocks[(ranks - k) % ranks] for k in range(ranks)])
+        out_blocks = jnp.swapaxes(sum_cores(out_blocks, 1), 0, 1)
+        out_here = finish(halving(out_blocks, chip, chips, True), None)
+        down_total = sum_ranks(down_here.reshape(ranks, piece, width))
+        rest_total = sum_ranks(
+            jnp.concatenate(
+                [
+                    gate_here.reshape(ranks, piece, width),
+                    up_here.reshape(ranks, piece, width),
+                    out_here.reshape(ranks, out_piece, width),
+                ],
+                axis=1,
+            )
+        )
         qkv_grad = jnp.stack([tn(normed_doc, g) for g in (dq, dk, dv)]).astype(BF)
-        qkv_here = lax.psum_scatter(qkv_grad, ("core", "chip"), scatter_dimension=1, tiled=True)
-        query_key_value_gradient = lax.all_gather(
-            qkv_here, ("core", "chip"), axis=1, tiled=True
-        ).astype(F32)
+        qkv_rows = width // (cores * chips)
+        qkv_blocks = qkv_grad.reshape(3, cores, chips, qkv_rows, heads_rows)
+        qkv_blocks = jnp.swapaxes(sum_cores(qkv_blocks, 1), 0, 1)
+        qkv_here = finish(halving(qkv_blocks, chip, chips, False), None)
+        pieces = jnp.concatenate([rest_total, down_total, qkv_here.reshape(-1, width)])
+        every = lax.all_gather(pieces, ("core", "chip"))
+        hidden_rows = 3 * piece + out_piece
+        grad_gateup, down_weight_gradient = assemble(
+            every[:, :hidden_rows], cores, chips, share, per, piece, out_piece
+        )
+        output_weight_gradient = every[:, 2 * piece : 2 * piece + out_piece].astype(F32)
+        output_weight_gradient = output_weight_gradient.reshape(heads_rows, width)
+        query_key_value_gradient = every[:, hidden_rows:].reshape(
+            cores * chips, 3, qkv_rows, heads_rows
+        )
+        query_key_value_gradient = (
+            jnp.swapaxes(query_key_value_gradient, 0, 1)
+            .astype(F32)
+            .reshape(3, width, heads_rows)
+        )
         return (
             layer_out[None],
             input_grad[None],

time: 567 us -> 520 us (0.917)
  blocking collectives: 27.2 us -> 0 us
  starting transfers between devices: 83.7 us -> 61.4 us
  waiting for transfers between devices: 256 us -> 272 us
  local copies, waits for them, and re-layouts: 71.3 us -> 57.5 us
    ppermute x30 -> x22, waiting for transfers between devices: 124 us -> 89.1 us  [flip(): return lax.ppermute(value, axis, [(i, i ^ bit) for i in range(count)])]
    all_gather x3, waiting for transfers between devices: 24.7 us -> 53.7 us  [the longest x1 31.1 us: on_device(): down_out_all = lax.all_gather(jnp.concatenate(down_out_came), 'chip')]
    all_gather x1 -> x0, blocking collectives: 27.2 us -> none  [on_device(): lax.all_gather(out_here, ('core', 'chip'), axis=0, tiled=True).astype(F32)]
    ppermute x27 -> x24, waiting for transfers between devices: 103 us -> 130 us  [shift(): lax.ppermute(value, 'tensor', [(i, (i + by) % count) for i in range(count)])]
    unnamed x157 -> x145, local copies, waits for them, and re-layouts: 37.6 us -> 14.3 us
    ppermute x27 -> x24, starting transfers between devices: 52.9 us -> 39.7 us  [shift(): lax.ppermute(value, 'tensor', [(i, (i + by) % count) for i in range(count)])]
    slice x1, local copies, waits for them, and re-layouts: 0.07 us -> 12.3 us  [on_device(): mlp_part[own_rows:].astype(BF)]
    convert_element_type x9 -> x14, other arithmetic: 18.2 us -> 8.28 us  [the longest x10 4.44 us: halving(): held = (kept.astype(F32) + came.astype(F32)).astype(BF)]
  transfers between devices with their start and end apart: 62 -> 49, of which waited for: 25 -> 27; matrix products, arithmetic and copies ran while one was open for 16% -> 15% of each run, Pallas kernels for 2% -> 5%
where the time goes in v2:
time: 520 us; the launch traced here: 511 us
  waiting for transfers between devices  272 us (52%)
  starting transfers between devices  61.4 us (12%)
  local copies, waits for them, and re-layouts  57.5 us (11%)
  other arithmetic  40.3 us (8%)
  matrix products  33.6 us (6%)
  Pallas kernels  28.7 us (6%)
  between operations  16.9 us (3%)
    ppermute x24, waiting for transfers between devices, shift(): lax.ppermute(value, 'tensor', [(i, (i + by) % count) for i in range(count)])  130 us
    ppermute x22, waiting for transfers between devices, flip(): return lax.ppermute(value, axis, [(i, i ^ bit) for i in range(count)])  89.1 us
    ppermute x24, starting transfers between devices, shift(): lax.ppermute(value, 'tensor', [(i, (i + by) % count) for i in range(count)])  39.7 us
    all_gather x1, waiting for transfers between devices, on_device(): down_out_all = lax.all_gather(jnp.concatenate(down_out_came), 'chip')  31.1 us
    all_gather x1, waiting for transfers between devices, on_device(): gate_up_all = lax.all_gather(jnp.concatenate(gate_up_came), 'chip')  22.6 us
    ppermute x22, starting transfers between devices, flip(): return lax.ppermute(value, axis, [(i, i ^ bit) for i in range(count)])  21.5 us
    dot_general x7, matrix products, nt(): lax.dot_general(left, right, (((1,), (1,)), ((), ())), preferred_element_...  14.9 us
    unnamed x145, local copies, waits for them, and re-layouts  14.3 us
  transfers between devices with their start and end apart: 49, of which 27 were waited for; matrix products, arithmetic and copies ran while one was open for 15% of the time, Pallas kernels for 5%

profile of v2, /device:TPU:0, one launch (start us, length us, event | category | flops | bytes accessed | tf_op | source)
XLA Modules:
  0.0 510.8 jit_solution(8679535095382064542)
XLA Ops:
  12.8 5.1 collective-permute-start
  20.4 6.3 %collective-permute-done = bf16[176,1024]{1,0:T(8,128)(2,1)S(1)} collective-permute-done((bf16[176,1024]{1,0:T(8,128)(2,1)S(1)}, bf16[176,1024]{1,0:T(8,128)(2,1)S(1)}, u32[]{:S(2)}, u32[]{:S(2)}) %collective-permute-start) | collective-permute-done | bytes 360480 | tf_op jit(solution)/shard_map/ppermute | solution.py:244
  26.8 21.9 %collective-permute-done.1 = bf16[176,1024]{1,0:T(8,128)(2,1)S(1)} collective-permute-done((bf16[176,1024]{1,0:T(8,128)(2,1)S(1)}, bf16[176,1024]{1,0:T(8,128)(2,1)S(1)}, u32[]{:S(2)}, u32[]{:S(2)}) %collective-permute-start.1) | collective-permute-done | bytes 360480 | tf_op jit(solution)/shard_map/ppermute | solution.py:244
  54.4 7.3 %collective-permute-done.3 = bf16[256,1024]{1,0:T(8,128)(2,1)S(1)} collective-permute-done((bf16[256,1024]{1,0:T(8,128)(2,1)S(1)}, bf16[256,1024]{1,0:T(8,128)(2,1)S(1)}, u32[]{:S(2)}, u32[]{:S(2)}) %collective-permute-start.3) | collective-permute-done | bytes 524320 | tf_op jit(solution)/shard_map/ppermute | solution.py:244
  61.7 34.8 %collective-permute-done.4 = bf16[256,1024]{1,0:T(8,128)(2,1)} collective-permute-done((bf16[256,1024]{1,0:T(8,128)(2,1)S(1)}, bf16[256,1024]{1,0:T(8,128)(2,1)}, u32[]{:S(2)}, u32[]{:S(2)}) %collective-permute-start.4) | collective-permute-done | bytes 524320 | tf_op jit(solution)/shard_map/ppermute | solution.py:244
  100.4 7.0 %collective-permute-done.11 = bf16[120,1024]{1,0:T(8,128)(2,1)S(1)} collective-permute-done((bf16[120,1024]{1,0:T(8,128)(2,1)S(1)}, bf16[120,1024]{1,0:T(8,128)(2,1)S(1)}, u32[]{:S(2)}, u32[]{:S(2)}) %collective-permute-start.11) | collective-permute-done | bytes 245792 | tf_op jit(solution)/shard_map/ppermute | solution.py:244
  107.4 8.2 %collective-permute-done.10 = bf16[120,1024]{1,0:T(8,128)(2,1)S(1)} collective-permute-done((bf16[120,1024]{1,0:T(8,128)(2,1)S(1)}, bf16[120,1024]{1,0:T(8,128)(2,1)S(1)}, u32[]{:S(2)}, u32[]{:S(2)}) %collective-permute-start.10) | collective-permute-done | bytes 245792 | tf_op jit(solution)/shard_map/ppermute | solution.py:244
  131.1 31.1 %all-gather.7.cloned.1.call-done = bf16[1440,1024]{1,0:T(8,128)(2,1)} async-done(((bf16[360,1024]{1,0:T(8,128)(2,1)}), bf16[1440,1024]{1,0:T(8,128)(2,1)}) %all-gather.7.cloned.1.call-update) | async-done | bytes 2949136 | tf_op jit(solution)/shard_map/all_gather | solution.py:359
  166.8 9.6 %shard_map.153 = (bf16[1024,256]{1,0:T(8,128)(2,1)S(1)}, f32[2,2,896]{2,1,0:T(2,128)S(1)}) custom-call(bf16[1024,256]{1,0:T(8,128)(2,1)S(1)} %get-tuple-element.36.refs_0_, bf16[1024,256]{1,0:T(8,128)(2,1)S(1)} %get-tuple-element.37.refs_1_, bf16[1024,256]{1,0:T(8,128)(2,1)S(1)} %get-tuple-element.38.refs_2_), custom_call_target="tpu_custom_call" | custom-call | flops 1644167168 | bytes 2097152 | tf_op jit(solution)/shard_map/pallas_call | solution.py:126
  185.6 8.0 %collective-permute-done.7 = bf16[256,256]{1,0:T(8,128)(2,1)S(1)} collective-permute-done((bf16[256,256]{1,0:T(8,128)(2,1)S(1)}, bf16[256,256]{1,0:T(8,128)(2,1)S(1)}, u32[]{:S(2)}, u32[]{:S(2)}) %collective-permute-start.7) | collective-permute-done | bytes 131104 | tf_op jit(solution)/shard_map/ppermute | solution.py:244
  195.9 22.6 %all-gather.9.cloned.1.call-done = bf16[2112,1024]{1,0:T(8,128)(2,1)} async-done(((bf16[528,1024]{1,0:T(8,128)(2,1)}), bf16[2112,1024]{1,0:T(8,128)(2,1)}) %all-gather.9.cloned.1.call-update) | async-done | bytes 4325392 | tf_op jit(solution)/shard_map/all_gather | solution.py:357
  244.5 12.3 %slice.339 = bf16[256,1024]{1,0:T(8,128)(2,1)S(1)} slice(f32[512,1024]{1,0:T(8,128)S(1)} %fusion.81), slice={[256:512], [0:1024]} | slice | bytes 1048576 | tf_op jit(solution)/shard_map/slice | solution.py:424
  284.7 7.3 %collective-permute-done.20 = bf16[2,352,1024]{2,1,0:T(8,128)(2,1)S(1)} collective-permute-done((bf16[2,352,1024]{2,1,0:T(8,128)(2,1)S(1)}, bf16[2,352,1024]{2,1,0:T(8,128)(2,1)S(1)}, u32[]{:S(2)}, u32[]{:S(2)}) %collective-permute-start.20) | collective-permute-done | bytes 1441824 | tf_op jit(solution)/shard_map/ppermute | solution.py:248
  293.7 12.6 %shard_map.154 = (bf16[1024,256]{1,0:T(8,128)(2,1)S(1)}, bf16[1024,256]{1,0:T(8,128)(2,1)S(1)}, bf16[1024,256]{1,0:T(8,128)(2,1)S(1)}) custom-call(bf16[1024,256]{1,0:T(8,128)(2,1)S(1)} %copy-done.9, bf16[1024,256]{1,0:T(8,128)(2,1)S(1)} %copy-done.11, bf16[1024,256]{1,0:T(8,128)(2,1)S(1)} %copy-done.13, ...), custom_call_target="tpu_custom_call" | custom-call | flops 4110417920 | bytes 5242880 | tf_op jit(solution)/shard_map/pallas_call | solution.py:190
  308.9 13.2 %collective-permute-done.38 = bf16[2,352,1024]{2,1,0:T(8,128)(2,1)} collective-permute-done((bf16[2,352,1024]{2,1,0:T(8,128)(2,1)}, bf16[2,352,1024]{2,1,0:T(8,128)(2,1)}, u32[]{:S(2)}, u32[]{:S(2)}) %collective-permute-start.38) | collective-permute-done | bytes 1441824 | tf_op jit(solution)/shard_map/ppermute | solution.py:248
  331.8 22.8 %collective-permute-done.33 = bf16[2,128,1024]{2,1,0:T(8,128)(2,1)S(1)} collective-permute-done((bf16[2,128,1024]{2,1,0:T(8,128)(2,1)S(1)}, bf16[2,128,1024]{2,1,0:T(8,128)(2,1)S(1)}, u32[]{:S(2)}, u32[]{:S(2)}) %collective-permute-start.33) | collective-permute-done | bytes 524320 | tf_op jit(solution)/shard_map/ppermute | solution.py:248
  360.5 7.6 %collective-permute-done.30 = bf16[352,1024]{1,0:T(8,128)(2,1)S(1)} collective-permute-done((bf16[352,1024]{1,0:T(8,128)(2,1)S(1)}, bf16[352,1024]{1,0:T(8,128)(2,1)S(1)}, u32[]{:S(2)}, u32[]{:S(2)}) %collective-permute-start.30) | collective-permute-done | bytes 720928 | tf_op jit(solution)/shard_map/ppermute | solution.py:248
  384.8 27.1 %collective-permute-done.36 = bf16[208,1024]{1,0:T(8,128)(2,1)S(1)} collective-permute-done((bf16[208,1024]{1,0:T(8,128)(2,1)S(1)}, bf16[208,1024]{1,0:T(8,128)(2,1)S(1)}, u32[]{:S(2)}, u32[]{:S(2)}) %collective-permute-start.36) | collective-permute-done | bytes 426016 | tf_op jit(solution)/shard_map/ppermute | solution.py:244
  434.9 20.5 %collective-permute-done.28 = f32[2048]{0:T(1024)S(1)} collective-permute-done((f32[2048]{0:T(1024)S(1)}, f32[2048]{0:T(1024)S(1)}, u32[]{:S(2)}, u32[]{:S(2)}) %collective-permute-start.28) | collective-permute-done | bytes 8224 | tf_op jit(solution)/shard_map/ppermute | solution.py:248
  455.4 4.3 collective-permute-start.29
  459.7 9.6 %collective-permute-done.29 = f32[2048]{0:T(1024)S(1)} collective-permute-done((f32[2048]{0:T(1024)S(1)}, f32[2048]{0:T(1024)S(1)}, u32[]{:S(2)}, u32[]{:S(2)}) %collective-permute-start.29) | collective-permute-done | bytes 8224 | tf_op jit(solution)/shard_map/ppermute | solution.py:248
  476.3 5.1 %slice.268.refs_0_ = bf16[8,296,1024]{2,1,0:T(8,128)(2,1)} slice(bf16[8,392,1024]{2,1,0:T(8,128)(2,1)} %bitcast.226), slice={[0:8], [0:296], [0:1024]} | slice | bytes 9699328 | tf_op jit(solution)/shard_map/slice | solution.py:504
  481.4 4.9 reshape.261
  497.6 6.2 %copy.48 = f32[2,1024,656]{1,2,0:T(8,128)} copy(f32[2,1024,656]{2,1,0:T(8,128)} %copy-done) | data formatting | bytes 10747904
  (344 shorter events, 178.3 us)
Async XLA Ops:
  7.2 155.1 %all-gather.7.cloned.1.call-start = ((), (), s32[]{:S(2)}) async-start(), calls=%async_computation | async-start | bytes 3686400 | tf_op jit(solution)/shard_map/all_gather | solution.py:359
  17.9 30.7 %collective-permute-start.1 = (bf16[176,1024]{1,0:T(8,128)(2,1)S(1)}, bf16[176,1024]{1,0:T(8,128)(2,1)S(1)}, u32[]{:S(2)}, u32[]{:S(2)}) collective-permute-start(bf16[176,1024]{1,0:T(8,128)(2,1)S(1)} %bitcast.261), channel_id=1, source_target_pairs={{0,2},{1,3},{2,0},{3,1},{4,6},{5,7},{6,4},{7,5},{8,10},{9,11},{10,... | collective-permute-start | bytes 1081352 | tf_op jit(solution)/shard_map/ppermute | solution.py:244
  17.9 30.7 %collective-permute-start.2 = (bf16[176,1024]{1,0:T(8,128)(2,1)S(1)}, bf16[176,1024]{1,0:T(8,128)(2,1)S(1)}, u32[]{:S(2)}, u32[]{:S(2)}) collective-permute-start(bf16[176,1024]{1,0:T(8,128)(2,1)S(1)} %bitcast.262), channel_id=1, source_target_pairs={{0,1},{1,2},{2,3},{3,0},{4,5},{5,6},{6,7},{7,4},{8,9},{9,10},{10,1... | collective-permute-start | bytes 1081352 | tf_op jit(solution)/shard_map/ppermute | solution.py:244
  48.7 47.9 %collective-permute-start.4 = (bf16[256,1024]{1,0:T(8,128)(2,1)S(1)}, bf16[256,1024]{1,0:T(8,128)(2,1)}, u32[]{:S(2)}, u32[]{:S(2)}) collective-permute-start(bf16[256,1024]{1,0:T(8,128)(2,1)S(1)} %get-tuple-element.32), channel_id=1, source_target_pairs={{0,2},{1,3},{2,0},{3,1},{4,6},{5,7},{6,4},{7,5},{8,10},{9,11},{10,... | collective-permute-start | bytes 1572872 | tf_op jit(solution)/shard_map/ppermute | solution.py:244
  51.5 45.0 %collective-permute-start.5 = (bf16[256,1024]{1,0:T(8,128)(2,1)S(1)}, bf16[256,1024]{1,0:T(8,128)(2,1)}, u32[]{:S(2)}, u32[]{:S(2)}) collective-permute-start(bf16[256,1024]{1,0:T(8,128)(2,1)S(1)} %get-tuple-element.32), channel_id=1, source_target_pairs={{0,1},{1,2},{2,3},{3,0},{4,5},{5,6},{6,7},{7,4},{8,9},{9,10},{10,1... | collective-permute-start | bytes 1572872 | tf_op jit(solution)/shard_map/ppermute | solution.py:244
  116.5 101.9 %all-gather.9.cloned.1.call-start = ((), (), s32[]{:S(2)}) async-start(), calls=%async_computation.1 | async-start | bytes 5406720 | tf_op jit(solution)/shard_map/all_gather | solution.py:357
  118.9 352.9 %all-gather.11.cloned.1.call-start = ((), (), s32[]{:S(2)}) async-start(), calls=%async_computation.2 | async-start | bytes 7225344 | tf_op jit(solution)/shard_map/all_gather | solution.py:501
  118.9 109.3 %collective-permute-start.15 = (bf16[256,1024]{1,0:T(8,128)(2,1)}, bf16[256,1024]{1,0:T(8,128)(2,1)}, u32[]{:S(2)}, u32[]{:S(2)}) collective-permute-start(bf16[256,1024]{1,0:T(8,128)(2,1)} %bitcast.25), channel_id=1, source_target_pairs={{0,4},{4,0},{1,5},{5,1},{2,6},{6,2},{3,7},{7,3},{8,12},{12,8},{9,1... | collective-permute-start | bytes 1572872 | tf_op jit(solution)/shard_map/ppermute | solution.py:248
  195.9 26.0 %collective-permute-start.13 = (bf16[256,1024]{1,0:T(8,128)(2,1)}, bf16[256,1024]{1,0:T(8,128)(2,1)}, u32[]{:S(2)}, u32[]{:S(2)}) collective-permute-start(bf16[256,1024]{1,0:T(8,128)(2,1)} %multiply_convert_fusion.2), channel_id=1, source_target_pairs={{0,4},{4,0},{1,5},{5,1},{2,6},{6,2},{3,7},{7,3},{8,12},{12,8},{9,1... | collective-permute-start | bytes 1572872 | tf_op jit(solution)/shard_map/ppermute | solution.py:248
  257.6 34.5 %collective-permute-start.20 = (bf16[2,352,1024]{2,1,0:T(8,128)(2,1)S(1)}, bf16[2,352,1024]{2,1,0:T(8,128)(2,1)S(1)}, u32[]{:S(2)}, u32[]{:S(2)}) collective-permute-start(bf16[2,352,1024]{2,1,0:T(8,128)(2,1)S(1)} %dynamic-slice_bitcast_fusion.2), channel_id=1, source_target_pairs={{0,8},{8,0},{16,24},{24,16},{1,9},{9,1},{17,25},{25,17},{2,10},{10... | collective-permute-start | bytes 4325384 | tf_op jit(solution)/shard_map/ppermute | solution.py:248
  259.2 33.3 %collective-permute-start.21 = (bf16[2,352,1024]{2,1,0:T(8,128)(2,1)S(1)}, bf16[2,352,1024]{2,1,0:T(8,128)(2,1)S(1)}, u32[]{:S(2)}, u32[]{:S(2)}) collective-permute-start(bf16[2,352,1024]{2,1,0:T(8,128)(2,1)S(1)} %dynamic-slice_bitcast_fusion.1), channel_id=1, source_target_pairs={{0,16},{8,24},{16,0},{24,8},{1,17},{9,25},{17,1},{25,9},{2,18},{10... | collective-permute-start | bytes 4325384 | tf_op jit(solution)/shard_map/ppermute | solution.py:248
  264.0 58.2 %collective-permute-start.38 = (bf16[2,352,1024]{2,1,0:T(8,128)(2,1)}, bf16[2,352,1024]{2,1,0:T(8,128)(2,1)}, u32[]{:S(2)}, u32[]{:S(2)}) collective-permute-start(bf16[2,352,1024]{2,1,0:T(8,128)(2,1)} %dynamic-slice_bitcast_fusion), channel_id=1, source_target_pairs={{0,8},{8,0},{16,24},{24,16},{1,9},{9,1},{17,25},{25,17},{2,10},{10... | collective-permute-start | bytes 4325384 | tf_op jit(solution)/shard_map/ppermute | solution.py:248
  282.9 43.5 %collective-permute-start.32 = (bf16[4,4,32,1024]{3,2,0,1:T(8,128)(2,1)}, bf16[4,4,32,1024]{3,2,0,1:T(8,128)(2,1)}, u32[]{:S(2)}, u32[]{:S(2)}) collective-permute-start(bf16[4,4,32,1024]{3,2,0,1:T(8,128)(2,1)} %dynamic-slice_bitcast_fusion.3), channel_id=1, source_target_pairs={{0,4},{4,0},{1,5},{5,1},{2,6},{6,2},{3,7},{7,3},{8,12},{12,8},{9,1... | collective-permute-start | bytes 3145736 | tf_op jit(solution)/shard_map/ppermute | solution.py:248
  308.9 61.1 %collective-permute-start.43 = (bf16[3,4,128,256]{3,2,0,1:T(8,128)(2,1)S(1)}, bf16[3,4,128,256]{3,2,0,1:T(8,128)(2,1)S(1)}, u32[]{:S(2)}, u32[]{:S(2)}) collective-permute-start(bf16[3,4,128,256]{3,2,0,1:T(8,128)(2,1)S(1)} %dynamic-slice_bitcast_fusion.4), channel_id=1, source_target_pairs={{0,4},{4,0},{1,5},{5,1},{2,6},{6,2},{3,7},{7,3},{8,12},{12,8},{9,1... | collective-permute-start | bytes 2359304 | tf_op jit(solution)/shard_map/ppermute | solution.py:248
  324.2 32.2 %collective-permute-start.39 = (bf16[352,1024]{1,0:T(8,128)(2,1)S(1)}, bf16[352,1024]{1,0:T(8,128)(2,1)S(1)}, u32[]{:S(2)}, u32[]{:S(2)}) collective-permute-start(bf16[352,1024]{1,0:T(8,128)(2,1)S(1)} %dynamic-slice_bitcast_fusion.5), channel_id=1, source_target_pairs={{0,16},{8,24},{16,0},{24,8},{1,17},{9,25},{17,1},{25,9},{2,18},{10... | collective-permute-start | bytes 2162696 | tf_op jit(solution)/shard_map/ppermute | solution.py:248
  328.2 26.3 %collective-permute-start.33 = (bf16[2,128,1024]{2,1,0:T(8,128)(2,1)S(1)}, bf16[2,128,1024]{2,1,0:T(8,128)(2,1)S(1)}, u32[]{:S(2)}, u32[]{:S(2)}) collective-permute-start(bf16[2,128,1024]{2,1,0:T(8,128)(2,1)S(1)} %dynamic-slice_bitcast_fusion.8), channel_id=1, source_target_pairs={{0,16},{8,24},{16,0},{24,8},{1,17},{9,25},{17,1},{25,9},{2,18},{10... | collective-permute-start | bytes 1572872 | tf_op jit(solution)/shard_map/ppermute | solution.py:248
  328.9 31.3 %collective-permute-start.31 = (bf16[352,1024]{1,0:T(8,128)(2,1)S(1)}, bf16[352,1024]{1,0:T(8,128)(2,1)S(1)}, u32[]{:S(2)}, u32[]{:S(2)}) collective-permute-start(bf16[352,1024]{1,0:T(8,128)(2,1)S(1)} %dynamic-slice_bitcast_fusion.6), channel_id=1, source_target_pairs={{0,8},{8,0},{16,24},{24,16},{1,9},{9,1},{17,25},{25,17},{2,10},{10... | collective-permute-start | bytes 2162696 | tf_op jit(solution)/shard_map/ppermute | solution.py:248
  331.2 37.0 %collective-permute-start.30 = (bf16[352,1024]{1,0:T(8,128)(2,1)S(1)}, bf16[352,1024]{1,0:T(8,128)(2,1)S(1)}, u32[]{:S(2)}, u32[]{:S(2)}) collective-permute-start(bf16[352,1024]{1,0:T(8,128)(2,1)S(1)} %dynamic-slice_bitcast_fusion.7), channel_id=1, source_target_pairs={{0,16},{8,24},{16,0},{24,8},{1,17},{9,25},{17,1},{25,9},{2,18},{10... | collective-permute-start | bytes 2162696 | tf_op jit(solution)/shard_map/ppermute | solution.py:248
  374.5 37.3 %collective-permute-start.36 = (bf16[208,1024]{1,0:T(8,128)(2,1)S(1)}, bf16[208,1024]{1,0:T(8,128)(2,1)S(1)}, u32[]{:S(2)}, u32[]{:S(2)}) collective-permute-start(bf16[208,1024]{1,0:T(8,128)(2,1)S(1)} %get-tuple-element.107), channel_id=1, source_target_pairs={{0,2},{1,3},{2,0},{3,1},{4,6},{5,7},{6,4},{7,5},{8,10},{9,11},{10,... | collective-permute-start | bytes 1277960 | tf_op jit(solution)/shard_map/ppermute | solution.py:244
  375.1 36.7 %collective-permute-start.35 = (bf16[208,1024]{1,0:T(8,128)(2,1)S(1)}, bf16[208,1024]{1,0:T(8,128)(2,1)S(1)}, u32[]{:S(2)}, u32[]{:S(2)}) collective-permute-start(bf16[208,1024]{1,0:T(8,128)(2,1)S(1)} %get-tuple-element.105), channel_id=1, source_target_pairs={{0,1},{1,2},{2,3},{3,0},{4,5},{5,6},{6,7},{7,4},{8,9},{9,10},{10,1... | collective-permute-start | bytes 1277960 | tf_op jit(solution)/shard_map/ppermute | solution.py:244
  379.4 33.4 %collective-permute-start.45 = (bf16[384,256]{1,0:T(8,128)(2,1)S(1)}, bf16[384,256]{1,0:T(8,128)(2,1)S(1)}, u32[]{:S(2)}, u32[]{:S(2)}) collective-permute-start(bf16[384,256]{1,0:T(8,128)(2,1)S(1)} %dynamic-slice_bitcast_fusion.11), channel_id=1, source_target_pairs={{0,16},{8,24},{16,0},{24,8},{1,17},{9,25},{17,1},{25,9},{2,18},{10... | collective-permute-start | bytes 589832 | tf_op jit(solution)/shard_map/ppermute | solution.py:248
  422.3 47.6 %collective-permute-start.24 = (bf16[256,1024]{1,0:T(8,128)(2,1)S(1)}, bf16[256,1024]{1,0:T(8,128)(2,1)S(1)}, u32[]{:S(2)}, u32[]{:S(2)}) collective-permute-start(bf16[256,1024]{1,0:T(8,128)(2,1)S(1)} %get-tuple-element.104), channel_id=1, source_target_pairs={{0,3},{1,0},{2,1},{3,2},{4,7},{5,4},{6,5},{7,6},{8,11},{9,8},{10,9... | collective-permute-start | bytes 1572872 | tf_op jit(solution)/shard_map/ppermute | solution.py:244
  422.4 47.5 %collective-permute-start.23 = (bf16[256,1024]{1,0:T(8,128)(2,1)S(1)}, bf16[256,1024]{1,0:T(8,128)(2,1)S(1)}, u32[]{:S(2)}, u32[]{:S(2)}) collective-permute-start(bf16[256,1024]{1,0:T(8,128)(2,1)S(1)} %get-tuple-element.103), channel_id=1, source_target_pairs={{0,2},{1,3},{2,0},{3,1},{4,6},{5,7},{6,4},{7,5},{8,10},{9,11},{10,... | collective-permute-start | bytes 1572872 | tf_op jit(solution)/shard_map/ppermute | solution.py:244
  423.2 46.7 %collective-permute-start.22 = (bf16[256,1024]{1,0:T(8,128)(2,1)S(1)}, bf16[256,1024]{1,0:T(8,128)(2,1)S(1)}, u32[]{:S(2)}, u32[]{:S(2)}) collective-permute-start(bf16[256,1024]{1,0:T(8,128)(2,1)S(1)} %get-tuple-element.102), channel_id=1, source_target_pairs={{0,1},{1,2},{2,3},{3,0},{4,5},{5,6},{6,7},{7,4},{8,9},{9,10},{10,1... | collective-permute-start | bytes 1572872 | tf_op jit(solution)/shard_map/ppermute | solution.py:244
  (91 other events, 1198.5 us)
Sparse Core Ops, SparseCore 0:
  116.7 45.5 all-gather.6
  164.6 53.7 all-gather.8
  415.3 43.5 all-gather.10

commit v3 on v1

v3 whole, which is shorter than its diff:
```python
import math

import jax
import jax.numpy as jnp
from jax import lax
from jax.experimental import pallas as pl
from jax.experimental.pallas import tpu as pltpu
from jax.sharding import Mesh, PartitionSpec as P

HD = 64
EPSILON = 1e-05
ROPE_BASE = 160000.0
BF = jnp.bfloat16
F32 = jnp.float32


def normalize(values):
    centered = values - jnp.mean(values, axis=-1, keepdims=True)
    variance = jnp.mean(centered * centered, axis=-1, keepdims=True)
    inverse = lax.rsqrt(variance + EPSILON)
    return (centered * inverse, inverse)


def norm_back(grad, normal, inverse, gain):
    scaled = grad * gain
    return inverse * (
        scaled
        - jnp.mean(scaled, axis=-1, keepdims=True)
        - normal * jnp.mean(scaled * normal, axis=-1, keepdims=True)
    )


def nt(left, right):
    return lax.dot_general(left, right, (((1,), (1,)), ((), ())), preferred_element_type=F32)


def nn(left, right):
    return jnp.dot(left, right, preferred_element_type=F32)


def tn(left, right):
    return lax.dot_general(left, right, (((0,), (0,)), ((), ())), preferred_element_type=F32)


def swap_halves(values):
    lane = lax.broadcasted_iota(jnp.int32, values.shape, 1)
    width = values.shape[1]
    ahead = pltpu.roll(values, width - HD // 2, 1)
    behind = pltpu.roll(values, HD // 2, 1)
    return jnp.where(lane % HD < HD // 2, ahead, behind)


def project_kernel(n_ref, w_ref, cos_ref, sin_ref, q_ref, k_ref, v_ref):
    rows = n_ref[...]
    cos, sin = cos_ref[...], sin_ref[...]
    for c, out in ((0, q_ref), (1, k_ref), (2, v_ref)):
        wide = nn(rows, w_ref[c])
        if c == 2:
            out[...] = wide.astype(BF)
            continue
        for at in range(0, wide.shape[1], 128):
            part = wide[:, at : at + 128]
            turned = (part * cos + swap_halves(part) * sin).astype(BF)
            if c == 0:
                turned = turned * (1.0 / math.sqrt(HD))
            out[:, at : at + 128] = turned


def project(rows, weight, cos, sin):
    length, width = rows.shape
    cols = weight.shape[2]
    block = 256
    return pl.pallas_call(
        project_kernel,
        grid=(length // block,),
        in_specs=[
            pl.BlockSpec((block, width), lambda i: (i, 0)),
            pl.BlockSpec((3, width, cols), lambda i: (0, 0, 0)),
            pl.BlockSpec((block, 128), lambda i: (i, 0)),
            pl.BlockSpec((block, 128), lambda i: (i, 0)),
        ],
        out_specs=[pl.BlockSpec((block, cols), lambda i: (i, 0))] * 3,
        out_shape=[jax.ShapeDtypeStruct((length, cols), BF)] * 3,
        compiler_params=pltpu.CompilerParams(vmem_limit_bytes=40 * 2**20),
        cost_estimate=pl.CostEstimate(
            flops=6 * length * width * cols, bytes_accessed=5 * 2**20, transcendentals=0
        ),
    )(rows, weight, cos, sin)


def half_mask(values, half):
    lane = lax.broadcasted_iota(jnp.int32, values.shape, 1)
    return jnp.where((lane // HD) == half, values, jnp.zeros_like(values))


def row_blocks(count):
    at = 0
    while at < count:
        size = min(256, count - at)
        yield at, size
        at += size


def turn(value, by):
    return pltpu.roll(value.astype(F32), by, 0)


def attend_kernel(doc, by_ref, q_ref, k_ref, v_ref, o_ref, l_ref, qd_ref, kd_ref, vd_ref, od_ref):
    length = q_ref.shape[0]
    into = lax.rem(length - by_ref[0], length)
    qd_ref[...] = turn(q_ref[...], into).astype(BF)
    kd_ref[...] = turn(k_ref[...], into).astype(BF)
    values = turn(v_ref[...], into)
    vd_ref[...] = values.astype(BF)
    od_ref[doc:, :] = values[doc:, :]
    keys = kd_ref[:doc, :]
    values_t = values[:doc, :].T.astype(BF)
    for at, size in row_blocks(doc):
        queries = qd_ref[at : at + size, :]
        mixed = []
        for half in range(2):
            scores = nt(keys, half_mask(queries, half))
            largest = jnp.max(scores, axis=0, keepdims=True)
            weights = jnp.exp(scores - largest)
            total = jnp.sum(weights, axis=0, keepdims=True)
            mix = nn(values_t[half * HD : half * HD + HD], weights.astype(BF))
            mixed.append(mix * (1.0 / total))
            l_ref[0, half : half + 1, at : at + size] = largest + jnp.log(total)
        od_ref[at : at + size, :] = jnp.concatenate(mixed, axis=0).T
    o_ref[...] = turn(od_ref[...], by_ref[0]).astype(BF)


def attend(by, queries, keys, values, doc):
    length, cols = queries.shape
    pairs = cols // 128
    spec = pl.BlockSpec((length, 128), lambda p: (0, p))
    return pl.pallas_call(
        lambda *refs: attend_kernel(doc, *refs),
        grid=(pairs,),
        in_specs=[pl.BlockSpec(memory_space=pltpu.SMEM)] + [spec] * 3,
        out_specs=[spec, pl.BlockSpec((1, 2, doc), lambda p: (p, 0, 0))] + [spec] * 3,
        out_shape=[
            jax.ShapeDtypeStruct((length, cols), BF),
            jax.ShapeDtypeStruct((pairs, 2, doc), F32),
        ]
        + [jax.ShapeDtypeStruct((length, cols), BF)] * 3,
        scratch_shapes=[pltpu.VMEM((length, 128), F32)],
        compiler_params=pltpu.CompilerParams(vmem_limit_bytes=48 * 2**20),
        cost_estimate=pl.CostEstimate(
            flops=8 * doc * doc * cols, bytes_accessed=2 * 2**20, transcendentals=doc * doc * 4
        ),
    )(by, queries, keys, values)


def attend_back_kernel(
    doc, by_ref, q_ref, k_ref, v_ref, d_ref, l_ref, cos_ref, sin_ref,
    dq_ref, dk_ref, dv_ref, qa_ref, ka_ref, va_ref, dd_ref,
):
    length = q_ref.shape[0]
    into = lax.rem(length - by_ref[0], length)
    turned = turn(d_ref[...], into)
    dd_ref[...] = turned.astype(BF)
    zero = jnp.zeros((length - doc, 128), F32)
    qa_ref[doc:, :] = zero
    ka_ref[doc:, :] = zero
    va_ref[doc:, :] = turned[doc:, :]
    keys = k_ref[:doc, :]
    keys_t = keys.T
    values = v_ref[:doc, :]
    first = True
    for at, size in row_blocks(doc):
        queries = q_ref[at : at + size, :]
        grads = dd_ref[at : at + size, :]
        back = []
        for half in range(2):
            query = half_mask(queries, half)
            grad = half_mask(grads, half)
            probs = jnp.exp(nt(keys, query) - l_ref[0, half : half + 1, at : at + size])
            prob_grad = nt(values, grad)
            centre = jnp.sum(probs * prob_grad, axis=0, keepdims=True)
            score_grad = (probs * (prob_grad - centre)).astype(BF)
            value_part = nn(probs.astype(BF), grad)
            key_part = nn(score_grad, query)
            if first:
                va_ref[:doc, :] = value_part
                ka_ref[:doc, :] = key_part
                first = False
            else:
                va_ref[:doc, :] += value_part
                ka_ref[:doc, :] += key_part
            back.append(nn(keys_t[half * HD : half * HD + HD], score_grad))
        qa_ref[at : at + size, :] = jnp.concatenate(back, axis=0).T * (1.0 / math.sqrt(HD))
    cos, sin = cos_ref[...], sin_ref[...]
    for held, out in ((qa_ref, dq_ref), (ka_ref, dk_ref)):
        grad = turn(held[...], by_ref[0])
        out[...] = (grad * cos - swap_halves(grad) * sin).astype(BF)
    dv_ref[...] = turn(va_ref[...], by_ref[0]).astype(BF)


def attend_back(by, queries, keys, values, grads, logs, cos, sin, doc):
    length, cols = queries.shape
    pairs = cols // 128
    spec = pl.BlockSpec((length, 128), lambda p: (0, p))
    table = pl.BlockSpec((length, 128), lambda p: (0, 0))
    return pl.pallas_call(
        lambda *refs: attend_back_kernel(doc, *refs),
        grid=(pairs,),
        in_specs=[pl.BlockSpec(memory_space=pltpu.SMEM)]
        + [spec] * 4
        + [pl.BlockSpec((1, 2, doc), lambda p: (p, 0, 0))]
        + [table] * 2,
        out_specs=[spec] * 3,
        out_shape=[jax.ShapeDtypeStruct((length, cols), BF)] * 3,
        scratch_shapes=[pltpu.VMEM((length, 128), F32)] * 3 + [pltpu.VMEM((length, 128), BF)],
        compiler_params=pltpu.CompilerParams(vmem_limit_bytes=48 * 2**20),
        cost_estimate=pl.CostEstimate(
            flops=20 * doc * doc * cols, bytes_accessed=5 * 2**20, transcendentals=doc * doc * 4
        ),
    )(by, queries, keys, values, grads, logs, cos, sin)


def assemble_kernel(sizes, in_ref, gu_ref, d_ref, o_ref, qkv_ref, held):
    cores, chips, share, per, piece, out_piece, qkv_part = sizes
    hidden = cores * share
    firsts = (0, piece, 2 * piece + out_piece)
    for m, first in enumerate(firsts):
        for device in range(cores * chips):
            at = device // chips * share + device % chips * per
            rows = in_ref[device].astype(F32)
            held[at : at + piece, :] = rows[first : first + piece, :]
            if m == 0:
                o_ref[device] = rows[2 * piece : 2 * piece + out_piece, :]
                last = 3 * piece + out_piece
                for c in range(3):
                    start = last + c * qkv_part
                    qkv_ref[c, device, 0] = rows[start : start + qkv_part, :]
        if m == 2:
            d_ref[...] = held[:hidden, :]
        else:
            gu_ref[m] = held[:hidden, :]


def assemble(every, sizes):
    cores, chips, share, per, piece, out_piece, qkv_part = sizes
    devices, rows, width = every.shape
    hidden = cores * share
    block = 256
    groups = width // block
    tall = -(-((cores - 1) * share + (chips - 1) * per + piece) // 8) * 8
    return pl.pallas_call(
        lambda *refs: assemble_kernel(sizes, *refs),
        grid=(groups,),
        in_specs=[pl.BlockSpec((devices, rows, block), lambda i: (0, 0, i))],
        out_specs=[
            pl.BlockSpec((2, hidden, block), lambda i: (0, 0, i)),
            pl.BlockSpec((hidden, block), lambda i: (0, i)),
            pl.BlockSpec((devices, out_piece, block), lambda i: (0, 0, i)),
            pl.BlockSpec((3, devices, 1, qkv_part, block), lambda i: (0, 0, i, 0, 0)),
        ],
        out_shape=[
            jax.ShapeDtypeStruct((2, hidden, width), F32),
            jax.ShapeDtypeStruct((hidden, width), F32),
            jax.ShapeDtypeStruct((devices, out_piece, width), F32),
            jax.ShapeDtypeStruct((3, devices, groups, qkv_part, block), F32),
        ],
        scratch_shapes=[pltpu.VMEM((tall, block), F32)],
        compiler_params=pltpu.CompilerParams(vmem_limit_bytes=40 * 2**20),
        cost_estimate=pl.CostEstimate(flops=0, bytes_accessed=18 * 2**20, transcendentals=0),
    )(every)


def shift(value, by, count):
    return lax.ppermute(value, "tensor", [(i, (i + by) % count) for i in range(count)])


def flip(value, axis, bit, count):
    return lax.ppermute(value, axis, [(i, i ^ bit) for i in range(count)])


def bits_of(count):
    return [1 << b for b in range(count.bit_length() - 1)]


def gather_ranks(value, count):
    ups, downs = [value], [value]
    for step in range(1, count):
        ups.append(lax.ppermute(ups[-1], "tensor", [(z, z + 1) for z in range(step - 1, count - 1)]))
        downs.append(lax.ppermute(downs[-1], "tensor", [(z, z - 1) for z in range(1, count - step + 1)]))
    return [downs[k] + ups[count - k] for k in range(1, count)]


def scatter_ranks(blocks, count):
    up, down = blocks[count - 1], blocks[1]
    for step in range(1, count):
        up = lax.ppermute(up, "tensor", [(z, z + 1) for z in range(step)])
        down = lax.ppermute(down, "tensor", [(z, z - 1) for z in range(count - step, count)])
        if step < count - 1:
            up = (up.astype(F32) + blocks[count - 1 - step].astype(F32)).astype(BF)
            down = (down.astype(F32) + blocks[step + 1].astype(F32)).astype(BF)
    return blocks[0].astype(F32) + up.astype(F32) + down.astype(F32)


class Halving:
    def __init__(self, value, chip, count, turned):
        self.chip, self.count = chip, count
        self.bits = count.bit_length() - 1
        self.held = value.reshape((2,) * self.bits + (-1,) + value.shape[-1:])
        order = list(range(self.bits))
        self.order = order if turned else order[::-1]
        self.left = list(range(self.bits))

    def send(self):
        axis = self.order.pop(0)
        bit = self.bits - 1 - axis
        mine = (self.chip >> bit) & 1
        at = self.left.index(axis)
        self.left.remove(axis)
        self.kept = lax.dynamic_index_in_dim(self.held, mine, at, keepdims=False)
        sent = lax.dynamic_index_in_dim(self.held, 1 - mine, at, keepdims=False)
        self.came = flip(sent, "chip", 1 << bit, self.count)

    def take(self):
        self.held = (self.kept.astype(F32) + self.came.astype(F32)).astype(BF)

    def finish(self):
        while self.order:
            self.send()
            self.take()
        return self.held


def tie(value, sums):
    tied = lax.optimization_barrier((value, *(s.came for s in sums)))
    for s, came in zip(sums, tied[1:]):
        s.came = came
        s.take()
    return tied[0]


def total_all(value, sizes):
    for axis, count in sizes:
        for bit in bits_of(count):
            value = value + flip(value, axis, bit, count)
    return value


def make(chips, cores, ranks):
    def on_device(
        tokens,
        segment_ids,
        gain_attn,
        query_key_value_weight,
        output_weight,
        gain_mlp,
        gate_up_weight,
        down_weight,
        cotangent,
    ):
        length = segment_ids.shape[1]
        own_rows, width = tokens.shape[1:]
        doc = length - length // 8
        others = ranks - 1
        rank = lax.axis_index("tensor")
        core = lax.axis_index("core")
        chip = lax.axis_index("chip")
        hold = lax.optimization_barrier

        hidden = down_weight.shape[0]
        share = hidden // cores
        per = -(-share // chips)
        piece = -(-per // 8) * 8
        heads_rows = output_weight.shape[0]
        out_piece = heads_rows // (cores * chips)
        gate_t, up_t = jnp.swapaxes(gate_up_weight, 1, 2)

        def part(weight, j):
            padded = jnp.pad(weight, ((0, chips * per + piece - share), (0, 0)))
            rows = lax.dynamic_slice_in_dim(padded, core * share + j * per, piece)
            at = lax.broadcasted_iota(jnp.int32, rows.shape, 0)
            return jnp.where((at < per) & (j * per + at < share), rows, jnp.zeros_like(rows))

        gate_mine = part(gate_t, chip)
        out_mine = lax.dynamic_slice_in_dim(
            output_weight, (core * chips + chip) * out_piece, out_piece
        )
        rest_mine = jnp.concatenate([part(up_t, chip), out_mine, part(down_weight, chip)])

        gate_came = jnp.concatenate([shift(gate_mine, -k, ranks) for k in range(1, ranks)])
        token_f = tokens[0].astype(F32)
        normal_attn, inverse_attn = normalize(token_f)
        normed_attn = (normal_attn * gain_attn).astype(BF)
        rest_sent, gate_came = hold((rest_mine, gate_came))
        gate_all = lax.all_gather(gate_came, "chip").reshape(chips, others * piece, width)
        rest_came = jnp.concatenate(gather_ranks(rest_sent, ranks))
        normed_sent, rest_came = hold((normed_attn, rest_came))
        rest_all = lax.all_gather(rest_came, "chip").reshape(chips, others, -1, width)
        normed_came = gather_ranks(normed_sent, ranks)
        normed_rows = jnp.concatenate([normed_attn] + normed_came)

        segments = segment_ids[0]
        middle = segments[length // 2]
        start = jnp.sum((segments < middle).astype(jnp.int32))
        by = (start - rank * own_rows) % length
        places = (jnp.arange(length, dtype=jnp.int32) - by) % length
        places = jnp.where(places < doc, places, 0)
        half = HD // 2
        freq = jnp.exp(jnp.arange(half, dtype=F32) * (-2.0 * math.log(ROPE_BASE) / HD))
        angles = places.astype(F32)[:, None] * jnp.concatenate([freq] * 4)[None, :]
        cos_table = jnp.cos(angles)
        lane = jnp.arange(2 * HD, dtype=jnp.int32)
        sin_table = jnp.sin(angles) * jnp.where(lane % HD < half, -1.0, 1.0)
        by = by[None]

        cot = cotangent[0]
        cot_pair = jnp.concatenate([cot, flip(cot, "core", 1, cores)])
        normed_rows, cos_table, sin_table, cot_pair = hold(
            (normed_rows, cos_table, sin_table, cot_pair)
        )

        queries, keys, values = project(normed_rows, query_key_value_weight, cos_table, sin_table)
        mixture, logs, queries, keys, values = attend(by, queries, keys, values, doc)
        mixture = mixture.reshape(ranks, own_rows, heads_rows)
        attention = jnp.concatenate(
            [mixture[0]] + [shift(mixture[k], k, ranks) for k in range(1, ranks)], axis=1
        )
        attention, gate_all, rest_all = hold((attention, gate_all, rest_all))

        def whole(weight, rest):
            blocks = []
            for j in range(chips):
                blocks += [part(weight, j), rest[j].reshape(-1, width)]
            return jnp.concatenate(blocks)

        out_half = jnp.swapaxes(rest_all[:, :, piece : piece + out_piece], 0, 1)
        out_half = out_half.reshape(others, heads_rows // cores, width)
        out_other = flip(out_half, "core", 1, cores)
        out_rest = jnp.concatenate(
            [
                jnp.where(core == 0, out_half, out_other),
                jnp.where(core == 0, out_other, out_half),
            ],
            axis=1,
        )
        out_weight = jnp.concatenate(
            [output_weight] + [out_rest[others - k] for k in range(1, ranks)]
        )
        hidden_state = token_f + nn(attention, out_weight)
        normal_mlp, inverse_mlp = normalize(hidden_state)
        normed_mlp = (normal_mlp * gain_mlp).astype(BF)
        gate = whole(gate_t, gate_all)
        up = whole(up_t, rest_all[:, :, :piece])
        down = whole(down_weight, rest_all[:, :, piece + out_piece :])

        normed_pair = jnp.concatenate([normed_mlp, flip(normed_mlp, "core", 1, cores)])
        gate_proj = nt(normed_pair, gate)
        up_proj = nt(normed_pair, up)
        cdf = 0.5 * (1.0 + lax.erf(gate_proj * (1.0 / math.sqrt(2.0))))
        pdf = jnp.exp(-0.5 * gate_proj * gate_proj) * (1.0 / math.sqrt(2.0 * math.pi))
        act = gate_proj * cdf
        hid = (act * up_proj).astype(BF)
        down_grad = tn(hid, cot_pair).astype(BF).reshape(chips, ranks * piece, width)
        cut = ranks * piece // 2
        down_sums = [
            Halving(down_grad[:, :cut], chip, chips, False),
            Halving(down_grad[:, cut:], chip, chips, True),
        ]
        for s in down_sums:
            s.send()
        hid_grad = nt(cot_pair, down)
        gate_grad = (hid_grad * up_proj * (cdf + gate_proj * pdf)).astype(BF)
        up_grad = (hid_grad * act).astype(BF)
        gate_sum = Halving(tn(gate_grad, normed_pair).astype(BF), chip, chips, False)
        up_sum = Halving(tn(up_grad, normed_pair).astype(BF), chip, chips, True)
        gate_grad, gate_sum.held, up_sum.held = hold((gate_grad, gate_sum.held, up_sum.held))
        gate_grad = tie(gate_grad, down_sums)
        gate_sum.send()
        up_sum.send()
        in_other = nn(gate_grad[own_rows:], gate) + nn(up_grad[own_rows:], up)
        in_came = flip(in_other.astype(BF), "core", 1, cores)
        in_part = nn(gate_grad[:own_rows], gate) + nn(up_grad[:own_rows], up)
        normed_mlp_grad = in_part + in_came.astype(F32)
        gain_mlp_part = jnp.sum(normed_mlp_grad * normal_mlp, axis=0)
        hidden_grad = cot.astype(F32) + norm_back(
            normed_mlp_grad, normal_mlp, inverse_mlp, gain_mlp
        )
        branch_grad = hidden_grad.astype(BF)

        attended_grad = nt(branch_grad, out_weight).astype(BF)
        attended_came = [
            shift(attended_grad[:, k * heads_rows : (k + 1) * heads_rows], -k, ranks)
            for k in range(1, ranks)
        ]
        mlp_part = nn(hid, down)
        mlp_out = mlp_part[:own_rows] + flip(
            mlp_part[own_rows:].astype(BF), "core", 1, cores
        ).astype(F32)
        layer_out = (hidden_state + mlp_out).astype(BF)

        def sum_cores(value, axis):
            kept = lax.dynamic_index_in_dim(value, core, axis, keepdims=False)
            sent = lax.dynamic_index_in_dim(value, 1 - core, axis, keepdims=False)
            return (kept.astype(F32) + flip(sent, "core", 1, cores).astype(F32)).astype(BF)

        out_w_grad = tn(attention, branch_grad).astype(BF)
        out_blocks = out_w_grad.reshape(ranks, cores, chips, out_piece, width)
        out_blocks = jnp.stack([out_blocks[(ranks - k) % ranks] for k in range(ranks)])
        out_blocks = jnp.swapaxes(sum_cores(out_blocks, 1), 0, 1)
        down_here = jnp.concatenate(
            [s.finish().reshape(-1, width) for s in down_sums]
        )
        attended_rows = jnp.concatenate([attended_grad[:, :heads_rows]] + attended_came)
        attended_rows, layer_out, out_blocks, down_here = hold(
            (attended_rows, layer_out, out_blocks, down_here)
        )

        def sum_ranks(here):
            rows = here.shape[1]
            flat = here.reshape(ranks * rows, width)
            twice = jnp.concatenate([flat, flat])
            flat = lax.dynamic_slice_in_dim(twice, (ranks - rank) % ranks * rows, ranks * rows)
            return lax.psum_scatter(flat, "tensor", scatter_dimension=0, tiled=True)

        down_total = sum_ranks(down_here.reshape(ranks, piece, width))
        attended_rows = tie(attended_rows, [gate_sum, up_sum])
        out_sum = Halving(out_blocks, chip, chips, True)
        gate_sum.send()
        up_sum.send()
        out_sum.send()
        dq, dk, dv = attend_back(
            by, queries, keys, values, attended_rows, logs, cos_table, sin_table, doc
        )
        normed_attn_part = (
            nt(dq, query_key_value_weight[0])
            + nt(dk, query_key_value_weight[1])
            + nt(dv, query_key_value_weight[2])
        )
        gain_attn_part = jnp.sum(normed_attn_part * normed_rows.astype(F32), axis=0) / gain_attn
        part_rows = normed_attn_part.astype(BF).reshape(ranks, own_rows, width)
        qkv_grad = jnp.stack([tn(normed_rows, g) for g in (dq, dk, dv)]).astype(BF)
        part_rows, qkv_grad, gain_attn_part = hold((part_rows, qkv_grad, gain_attn_part))
        part_rows = tie(part_rows, [gate_sum, up_sum, out_sum])
        rest_total = sum_ranks(
            jnp.concatenate(
                [
                    gate_sum.finish().reshape(ranks, piece, width),
                    up_sum.finish().reshape(ranks, piece, width),
                    out_sum.finish().reshape(ranks, out_piece, width),
                ],
                axis=1,
            )
        )
        normed_attn_grad = scatter_ranks(part_rows, ranks)
        input_grad = (
            hidden_grad + norm_back(normed_attn_grad, normal_attn, inverse_attn, gain_attn)
        ).astype(BF)

        qkv_rows = width // (cores * chips)
        qkv_blocks = qkv_grad.reshape(3, cores, chips, qkv_rows, heads_rows)
        qkv_blocks = jnp.swapaxes(sum_cores(qkv_blocks, 1), 0, 1)
        qkv_here = Halving(qkv_blocks, chip, chips, False).finish()
        gains = total_all(
            jnp.concatenate([gain_attn_part, gain_mlp_part]),
            (("core", cores), ("chip", chips), ("tensor", ranks)),
        )
        qkv_here, gains = hold((qkv_here, gains))
        grad_gain_attn, grad_gain_mlp = gains[:width], gains[width:]
        groups = width // heads_rows
        qkv_part = qkv_rows // groups
        qkv_here = qkv_here.reshape(3, groups, qkv_part, heads_rows)
        qkv_here = jnp.concatenate(
            [qkv_here[:, g].reshape(3 * qkv_part, heads_rows) for g in range(groups)], axis=1
        )
        pieces = jnp.concatenate([rest_total, down_total, qkv_here])
        every = lax.all_gather(pieces, ("core", "chip"))
        grads = assemble(every, (cores, chips, share, per, piece, out_piece, qkv_part))
        grad_gateup = jnp.swapaxes(grads[0], 1, 2)
        down_weight_gradient = grads[1]
        output_weight_gradient = grads[2].reshape(heads_rows, width)
        query_key_value_gradient = grads[3].reshape(3, width, heads_rows)
        return (
            layer_out[None],
            input_grad[None],
            grad_gain_attn,
            query_key_value_gradient,
            output_weight_gradient,
            grad_gain_mlp,
            grad_gateup,
            down_weight_gradient,
        )

    return on_device


def solution(mesh):
    ranks = mesh.shape["tensor"]
    cores = 2
    chips = mesh.shape["dp"] // cores
    split = Mesh(mesh.devices.reshape(chips, cores, ranks), ("chip", "core", "tensor"))
    dp = ("chip", "core")
    rows = P(dp, "tensor", None)
    last = P(None, None, "tensor")
    first = P("tensor", None)
    return jax.shard_map(
        make(chips, cores, ranks),
        mesh=split,
        in_specs=(rows, P(dp, None), P(), last, first, P(), last, first, rows),
        out_specs=(rows, rows, P(), last, first, P(), last, first),
        check_vma=False,
    )
```

time: 567 us -> 417 us (0.74)
  waiting for transfers between devices: 256 us -> 194 us
  local copies, waits for them, and re-layouts: 71.3 us -> 27.2 us
  blocking collectives: 27.2 us -> 0 us
  starting transfers between devices: 83.7 us -> 72.9 us
  Pallas kernels: 25.1 us -> 34 us
  other arithmetic: 43.6 us -> 37.1 us
  matrix products: 37.3 us -> 31.5 us
    ppermute x0 -> x18, waiting for transfers between devices: none -> 82 us  [the longest x6 36.9 us: gather_ranks(): lax.ppermute(downs[-1], 'tensor', [(z, z - 1) for z in range(1, count - s...]
    ppermute x27 -> x9, waiting for transfers between devices: 103 us -> 26 us  [shift(): lax.ppermute(value, 'tensor', [(i, (i + by) % count) for i in range(count)])]
    ppermute x30 -> x24, waiting for transfers between devices: 124 us -> 80.5 us  [flip(): return lax.ppermute(value, axis, [(i, i ^ bit) for i in range(count)])]
    ppermute x27 -> x9, starting transfers between devices: 52.9 us -> 11.9 us  [shift(): lax.ppermute(value, 'tensor', [(i, (i + by) % count) for i in range(count)])]
    ppermute x0 -> x18, starting transfers between devices: none -> 40.1 us  [the longest x3 17.3 us: scatter_ranks(): up = lax.ppermute(up, 'tensor', [(z, z + 1) for z in range(step)])]
    all_gather x1 -> x0, blocking collectives: 27.2 us -> none  [on_device(): lax.all_gather(out_here, ('core', 'chip'), axis=0, tiled=True).astype(F32)]
    all_gather x3, waiting for transfers between devices: 24.7 us -> 0.01 us  [the longest x1 0.01 us: on_device(): lax.all_gather(gate_came, 'chip').reshape(chips, others * piece, width)]
    unnamed x157 -> x102, local copies, waits for them, and re-layouts: 37.6 us -> 14 us
  transfers between devices with their start and end apart: 62 -> 56, of which waited for: 25 -> 34; matrix products, arithmetic and copies ran while one was open for 16% -> 12% of each run, Pallas kernels for 2% -> 3%
where the time goes in v3:
time: 417 us; the launch traced here: 413 us
  waiting for transfers between devices  194 us (47%)
  starting transfers between devices  72.9 us (17%)
  other arithmetic  37.1 us (9%)
  Pallas kernels  34 us (8%)
  matrix products  31.5 us (8%)
  local copies, waits for them, and re-layouts  27.2 us (7%)
  between operations  16.1 us (4%)
    ppermute x24, waiting for transfers between devices, flip(): return lax.ppermute(value, axis, [(i, i ^ bit) for i in range(count)])  80.5 us
    ppermute x6, waiting for transfers between devices, gather_ranks(): lax.ppermute(downs[-1], 'tensor', [(z, z - 1) for z in range(1, count - s...  36.9 us
    ppermute x9, waiting for transfers between devices, shift(): lax.ppermute(value, 'tensor', [(i, (i + by) % count) for i in range(count)])  26 us
    ppermute x3, waiting for transfers between devices, scatter_ranks(): up = lax.ppermute(up, 'tensor', [(z, z + 1) for z in range(step)])  25.6 us
    ppermute x24, starting transfers between devices, flip(): return lax.ppermute(value, axis, [(i, i ^ bit) for i in range(count)])  20.6 us
    ppermute x3, starting transfers between devices, scatter_ranks(): up = lax.ppermute(up, 'tensor', [(z, z + 1) for z in range(step)])  17.3 us
    dot_general x7, matrix products, nt(): lax.dot_general(left, right, (((1,), (1,)), ((), ())), preferred_element_...  15.5 us
    ppermute x6, waiting for transfers between devices, gather_ranks(): lax.ppermute(ups[-1], 'tensor', [(z, z + 1) for z in range(step - 1, coun...  15.3 us
  transfers between devices with their start and end apart: 56, of which 34 were waited for; matrix products, arithmetic and copies ran while one was open for 12% of the time, Pallas kernels for 3%

profile of v3, /device:TPU:0, one launch (start us, length us, event | category | flops | bytes accessed | tf_op | source)
XLA Modules:
  0.0 412.5 jit_solution(403489020044631532)
XLA Ops:
  22.7 6.9 %collective-permute-done.1 = bf16[88,1024]{1,0:T(8,128)(2,1)S(1)} collective-permute-done((bf16[88,1024]{1,0:T(8,128)(2,1)}, bf16[88,1024]{1,0:T(8,128)(2,1)S(1)}, u32[]{:S(2)}, u32[]{:S(2)}) %collective-permute-start.1) | collective-permute-done | bytes 180256 | tf_op jit(solution)/shard_map/ppermute | solution.py:273
  30.6 6.3 %collective-permute-start.4 = (bf16[208,1024]{1,0:T(8,128)(2,1)S(1)}, bf16[208,1024]{1,0:T(8,128)(2,1)S(1)}, u32[]{:S(2)}, u32[]{:S(2)}) collective-permute-start(bf16[208,1024]{1,0:T(8,128)(2,1)S(1)} %pad_maximum_fusion.13), channel_id=1, source_target_pairs={{0,1},{1,2},{2,3},{4,5},{5,6},{6,7},{8,9},{9,10},{10,11},{12,13},{... | collective-permute-start | bytes 1277960 | tf_op jit(solution)/shard_map/ppermute | solution.py:287
  38.1 7.9 %collective-permute-done.4 = bf16[208,1024]{1,0:T(8,128)(2,1)S(1)} collective-permute-done((bf16[208,1024]{1,0:T(8,128)(2,1)S(1)}, bf16[208,1024]{1,0:T(8,128)(2,1)S(1)}, u32[]{:S(2)}, u32[]{:S(2)}) %collective-permute-start.4) | collective-permute-done | bytes 426016 | tf_op jit(solution)/shard_map/ppermute | solution.py:287
  52.7 10.1 %collective-permute-done.7 = bf16[208,1024]{1,0:T(8,128)(2,1)S(1)} collective-permute-done((bf16[208,1024]{1,0:T(8,128)(2,1)S(1)}, bf16[208,1024]{1,0:T(8,128)(2,1)S(1)}, u32[]{:S(2)}, u32[]{:S(2)}) %collective-permute-start.7) | collective-permute-done | bytes 426016 | tf_op jit(solution)/shard_map/ppermute | solution.py:288
  64.8 9.8 %collective-permute-done.8 = bf16[208,1024]{1,0:T(8,128)(2,1)S(1)} collective-permute-done((bf16[208,1024]{1,0:T(8,128)(2,1)S(1)}, bf16[208,1024]{1,0:T(8,128)(2,1)S(1)}, u32[]{:S(2)}, u32[]{:S(2)}) %collective-permute-start.8) | collective-permute-done | bytes 426016 | tf_op jit(solution)/shard_map/ppermute | solution.py:288
  78.8 7.4 %collective-permute-done.10 = bf16[256,1024]{1,0:T(8,128)(2,1)S(1)} collective-permute-done((bf16[256,1024]{1,0:T(8,128)(2,1)S(1)}, bf16[256,1024]{1,0:T(8,128)(2,1)S(1)}, u32[]{:S(2)}, u32[]{:S(2)}) %collective-permute-start.10) | collective-permute-done | bytes 524320 | tf_op jit(solution)/shard_map/ppermute | solution.py:287
  95.0 7.3 %collective-permute-done.13 = bf16[256,1024]{1,0:T(8,128)(2,1)S(1)} collective-permute-done((bf16[256,1024]{1,0:T(8,128)(2,1)S(1)}, bf16[256,1024]{1,0:T(8,128)(2,1)S(1)}, u32[]{:S(2)}, u32[]{:S(2)}) %collective-permute-start.13) | collective-permute-done | bytes 524320 | tf_op jit(solution)/shard_map/ppermute | solution.py:288
  119.2 11.5 %shard_map.153 = (bf16[1024,256]{1,0:T(8,128)(2,1)S(1)}, f32[2,2,896]{2,1,0:T(2,128)S(1)}, bf16[1024,256]{1,0:T(8,128)(2,1)S(1)}, bf16[1024,256]{1,0:T(8,128)(2,1)S(1)}, bf16[1024,256]{1,0:T(8,128)(2,1)S(1)}) custom-call(s32[1]{0:T(128)} %bitcast.3.refs_0_, bf16[1024,256]{1,0:T(8,128)(2,1)S(1)} %get-tuple-element.61.refs_1_, ...), custom_call_target="tpu_custom_call" | custom-call | flops 1644167168 | bytes 2097152 | tf_op jit(solution)/shard_map/pallas_call | solution.py:137
  178.5 9.1 %collective-permute-done.22 = bf16[2,176,1024]{2,1,0:T(8,128)(2,1)S(1)} collective-permute-done((bf16[2,176,1024]{2,1,0:T(8,128)(2,1)S(1)}, bf16[2,176,1024]{2,1,0:T(8,128)(2,1)S(1)}, u32[]{:S(2)}, u32[]{:S(2)}) %collective-permute-start.22) | collective-permute-done | bytes 720928 | tf_op jit(solution)/shard_map/ppermute | solution.py:277
  198.0 29.0 %collective-permute-done.30 = bf16[176,1024]{1,0:T(8,128)(2,1)S(1)} collective-permute-done((bf16[176,1024]{1,0:T(8,128)(2,1)S(1)}, bf16[176,1024]{1,0:T(8,128)(2,1)S(1)}, u32[]{:S(2)}, u32[]{:S(2)}) %collective-permute-start.30) | collective-permute-done | bytes 360480 | tf_op jit(solution)/shard_map/ppermute | solution.py:277
  229.7 5.5 %collective-permute-done.26 = bf16[256,256]{1,0:T(8,128)(2,1)S(1)} collective-permute-done((bf16[256,256]{1,0:T(8,128)(2,1)S(1)}, bf16[256,256]{1,0:T(8,128)(2,1)S(1)}, u32[]{:S(2)}, u32[]{:S(2)}) %collective-permute-start.26) | collective-permute-done | bytes 131104 | tf_op jit(solution)/shard_map/ppermute | solution.py:273
  242.8 14.4 %shard_map.154 = (bf16[1024,256]{1,0:T(8,128)(2,1)S(1)}, bf16[1024,256]{1,0:T(8,128)(2,1)S(1)}, bf16[1024,256]{1,0:T(8,128)(2,1)S(1)}) custom-call(s32[1]{0:T(128)} %bitcast.3.refs_0_, bf16[1024,256]{1,0:T(8,128)(2,1)S(1)} %copy-done.8, bf16[1024,256]{1,0:T(8,128)(2,1)S(1)} %copy-done.10, bf16[1024,256]{1,0:T(8,128)(2,1)S(1)} %copy-done.12, ...), custom_call_target="tpu_custom_call" | custom-call | flops 4110417920 | bytes 5242880 | tf_op jit(solution)/shard_map/pallas_call | solution.py:205
  282.2 4.9 %collective-permute-done.34 = bf16[352,1024]{1,0:T(8,128)(2,1)S(1)} collective-permute-done((bf16[352,1024]{1,0:T(8,128)(2,1)S(1)}, bf16[352,1024]{1,0:T(8,128)(2,1)S(1)}, u32[]{:S(2)}, u32[]{:S(2)}) %collective-permute-start.34) | collective-permute-done | bytes 720928 | tf_op jit(solution)/shard_map/ppermute | solution.py:277
  287.1 6.6 %collective-permute-done.33 = bf16[352,1024]{1,0:T(8,128)(2,1)S(1)} collective-permute-done((bf16[352,1024]{1,0:T(8,128)(2,1)S(1)}, bf16[352,1024]{1,0:T(8,128)(2,1)S(1)}, u32[]{:S(2)}, u32[]{:S(2)}) %collective-permute-start.33) | collective-permute-done | bytes 720928 | tf_op jit(solution)/shard_map/ppermute | solution.py:277
  297.1 4.4 %collective-permute-done.50 = bf16[128,1024]{1,0:T(8,128)(2,1)S(1)} collective-permute-done((bf16[128,1024]{1,0:T(8,128)(2,1)S(1)}, bf16[128,1024]{1,0:T(8,128)(2,1)S(1)}, u32[]{:S(2)}, u32[]{:S(2)}) %collective-permute-start.50) | collective-permute-done | bytes 262176 | tf_op jit(solution)/shard_map/ppermute | solution.py:277
  309.5 9.7 %collective-permute-done.43 = bf16[2,384,256]{2,1,0:T(8,128)(2,1)S(1)} collective-permute-done((bf16[2,384,256]{2,1,0:T(8,128)(2,1)S(1)}, bf16[2,384,256]{2,1,0:T(8,128)(2,1)S(1)}, u32[]{:S(2)}, u32[]{:S(2)}) %collective-permute-start.43) | collective-permute-done | bytes 393248 | tf_op jit(solution)/shard_map/ppermute | solution.py:277
  337.3 5.1 %reduce-scatter.3.cloned.1.call-done = bf16[208,1024]{1,0:T(8,128)(2,1)} async-done(((bf16[832,1024]{1,0:T(8,128)(2,1)}), bf16[208,1024]{1,0:T(8,128)(2,1)}) %reduce-scatter.3.cloned.1.call-update) | async-done | bytes 426000 | tf_op jit(solution)/shard_map/reduce_scatter | solution.py:521
  347.7 9.6 %collective-permute-done.36 = bf16[256,1024]{1,0:T(8,128)(2,1)S(1)} collective-permute-done((bf16[256,1024]{1,0:T(8,128)(2,1)S(1)}, bf16[256,1024]{1,0:T(8,128)(2,1)S(1)}, u32[]{:S(2)}, u32[]{:S(2)}) %collective-permute-start.36) | collective-permute-done | bytes 524320 | tf_op jit(solution)/shard_map/ppermute | solution.py:295
  357.6 4.5 %collective-permute-start.37 = (bf16[256,1024]{1,0:T(8,128)(2,1)S(1)}, bf16[256,1024]{1,0:T(8,128)(2,1)S(1)}, u32[]{:S(2)}, u32[]{:S(2)}) collective-permute-start(bf16[256,1024]{1,0:T(8,128)(2,1)S(1)} %get-tuple-element.128), channel_id=1, source_target_pairs={{0,1},{1,2},{4,5},{5,6},{8,9},{9,10},{12,13},{13,14},{16,17},{17,1... | collective-permute-start | bytes 1572872 | tf_op jit(solution)/shard_map/ppermute | solution.py:295
  363.0 8.6 %collective-permute-done.37 = bf16[256,1024]{1,0:T(8,128)(2,1)S(1)} collective-permute-done((bf16[256,1024]{1,0:T(8,128)(2,1)S(1)}, bf16[256,1024]{1,0:T(8,128)(2,1)S(1)}, u32[]{:S(2)}, u32[]{:S(2)}) %collective-permute-start.37) | collective-permute-done | bytes 524320 | tf_op jit(solution)/shard_map/ppermute | solution.py:295
  372.0 10.3 %collective-permute-start.38 = (bf16[256,1024]{1,0:T(8,128)(2,1)S(1)}, bf16[256,1024]{1,0:T(8,128)(2,1)S(1)}, u32[]{:S(2)}, u32[]{:S(2)}) collective-permute-start(bf16[256,1024]{1,0:T(8,128)(2,1)S(1)} %get-tuple-element.126), channel_id=1, source_target_pairs={{0,1},{1,2},{2,3},{4,5},{5,6},{6,7},{8,9},{9,10},{10,11},{12,13},{... | collective-permute-start | bytes 1572872 | tf_op jit(solution)/shard_map/ppermute | solution.py:295
  384.3 7.4 %collective-permute-done.38 = bf16[256,1024]{1,0:T(8,128)(2,1)S(1)} collective-permute-done((bf16[256,1024]{1,0:T(8,128)(2,1)S(1)}, bf16[256,1024]{1,0:T(8,128)(2,1)S(1)}, u32[]{:S(2)}, u32[]{:S(2)}) %collective-permute-start.38) | collective-permute-done | bytes 524320 | tf_op jit(solution)/shard_map/ppermute | solution.py:295
  391.7 4.1 %collective-permute-done.41 = bf16[256,1024]{1,0:T(8,128)(2,1)S(1)} collective-permute-done((bf16[256,1024]{1,0:T(8,128)(2,1)S(1)}, bf16[256,1024]{1,0:T(8,128)(2,1)S(1)}, u32[]{:S(2)}, u32[]{:S(2)}) %collective-permute-start.41) | collective-permute-done | bytes 524320 | tf_op jit(solution)/shard_map/ppermute | solution.py:296
  400.6 5.2 %shard_map.155 = (f32[2,656,1024]{2,1,0:T(8,128)}, f32[656,1024]{1,0:T(8,128)}, f32[8,32,1024]{2,1,0:T(8,128)}, f32[3,8,4,32,256]{4,3,2,1,0:T(8,128)}) custom-call(bf16[8,392,1024]{2,1,0:T(8,128)(2,1)S(1)} %bitcast.247), custom_call_target="tpu_custom_call" | custom-call | bytes 18874368 | tf_op jit(solution)/shard_map/pallas_call | solution.py:250
  (327 shorter events, 190.7 us)
Async XLA Ops:
  7.2 136.0 %all-gather.7.cloned.1.call-start = ((), (), s32[]{:S(2)}) async-start(), calls=%async_computation.4 | async-start | bytes 2703360 | tf_op jit(solution)/shard_map/all_gather | solution.py:393
  15.0 14.6 %collective-permute-start.1 = (bf16[88,1024]{1,0:T(8,128)(2,1)}, bf16[88,1024]{1,0:T(8,128)(2,1)S(1)}, u32[]{:S(2)}, u32[]{:S(2)}) collective-permute-start(bf16[88,1024]{1,0:T(8,128)(2,1)} %get-tuple-element.167), channel_id=1, source_target_pairs={{0,2},{1,3},{2,0},{3,1},{4,6},{5,7},{6,4},{7,5},{8,10},{9,11},{10,... | collective-permute-start | bytes 540680 | tf_op jit(solution)/shard_map/ppermute | solution.py:273
  30.5 112.6 %all-gather.9.cloned.1.call-start = ((), (), s32[]{:S(2)}) async-start(), calls=%async_computation.5 | async-start | bytes 6389760 | tf_op jit(solution)/shard_map/all_gather | solution.py:396
  30.6 15.5 %collective-permute-start.4 = (bf16[208,1024]{1,0:T(8,128)(2,1)S(1)}, bf16[208,1024]{1,0:T(8,128)(2,1)S(1)}, u32[]{:S(2)}, u32[]{:S(2)}) collective-permute-start(bf16[208,1024]{1,0:T(8,128)(2,1)S(1)} %pad_maximum_fusion.13), channel_id=1, source_target_pairs={{0,1},{1,2},{2,3},{4,5},{5,6},{6,7},{8,9},{9,10},{10,11},{12,13},{... | collective-permute-start | bytes 1277960 | tf_op jit(solution)/shard_map/ppermute | solution.py:287
  75.9 261.3 %reduce-scatter.5.cloned.1.call-start = ((), (), s32[]{:S(2)}) async-start(), calls=%async_computation.3 | async-start | bytes 901120 | tf_op jit(solution)/shard_map/reduce_scatter | solution.py:521
  91.6 14.8 %collective-permute-start.15 = (bf16[256,1024]{1,0:T(8,128)(2,1)S(1)}, bf16[256,1024]{1,0:T(8,128)(2,1)S(1)}, u32[]{:S(2)}, u32[]{:S(2)}) collective-permute-start(bf16[256,1024]{1,0:T(8,128)(2,1)S(1)} %bitcast.286), channel_id=1, source_target_pairs={{0,4},{4,0},{1,5},{5,1},{2,6},{6,2},{3,7},{7,3},{8,12},{12,8},{9,1... | collective-permute-start | bytes 1572872 | tf_op jit(solution)/shard_map/ppermute | solution.py:277
  93.5 15.4 %collective-permute-start.12 = (bf16[256,1024]{1,0:T(8,128)(2,1)}, bf16[256,1024]{1,0:T(8,128)(2,1)}, u32[]{:S(2)}, u32[]{:S(2)}) collective-permute-start(bf16[256,1024]{1,0:T(8,128)(2,1)} %collective-permute-done.11), channel_id=1, source_target_pairs={{2,3},{6,7},{10,11},{14,15},{18,19},{22,23},{26,27},{30,31}} | collective-permute-start | bytes 1572872 | tf_op jit(solution)/shard_map/ppermute | solution.py:287
  168.4 26.1 %collective-permute-start.27 = (bf16[256,1024]{1,0:T(8,128)(2,1)S(1)}, bf16[256,1024]{1,0:T(8,128)(2,1)S(1)}, u32[]{:S(2)}, u32[]{:S(2)}) collective-permute-start(bf16[256,1024]{1,0:T(8,128)(2,1)S(1)} %slice.319), channel_id=1, source_target_pairs={{0,4},{4,0},{1,5},{5,1},{2,6},{6,2},{3,7},{7,3},{8,12},{12,8},{9,1... | collective-permute-start | bytes 1572872 | tf_op jit(solution)/shard_map/ppermute | solution.py:277
  168.6 19.0 %collective-permute-start.22 = (bf16[2,176,1024]{2,1,0:T(8,128)(2,1)S(1)}, bf16[2,176,1024]{2,1,0:T(8,128)(2,1)S(1)}, u32[]{:S(2)}, u32[]{:S(2)}) collective-permute-start(bf16[2,176,1024]{2,1,0:T(8,128)(2,1)S(1)} %dynamic-slice_bitcast_fusion.5), channel_id=1, source_target_pairs={{0,16},{8,24},{16,0},{24,8},{1,17},{9,25},{17,1},{25,9},{2,18},{10... | collective-permute-start | bytes 2162696 | tf_op jit(solution)/shard_map/ppermute | solution.py:277
  170.1 19.1 %collective-permute-start.21 = (bf16[2,176,1024]{2,1,0:T(8,128)(2,1)S(1)}, bf16[2,176,1024]{2,1,0:T(8,128)(2,1)S(1)}, u32[]{:S(2)}, u32[]{:S(2)}) collective-permute-start(bf16[2,176,1024]{2,1,0:T(8,128)(2,1)S(1)} %dynamic-slice_bitcast_fusion.6), channel_id=1, source_target_pairs={{0,8},{8,0},{16,24},{24,16},{1,9},{9,1},{17,25},{25,17},{2,10},{10... | collective-permute-start | bytes 2162696 | tf_op jit(solution)/shard_map/ppermute | solution.py:277
  175.3 65.6 %collective-permute-start.32 = (bf16[2,352,1024]{2,1,0:T(8,128)(2,1)S(1)}, bf16[2,352,1024]{2,1,0:T(8,128)(2,1)S(1)}, u32[]{:S(2)}, u32[]{:S(2)}) collective-permute-start(bf16[2,352,1024]{2,1,0:T(8,128)(2,1)S(1)} %dynamic-slice_bitcast_fusion), channel_id=1, source_target_pairs={{0,16},{8,24},{16,0},{24,8},{1,17},{9,25},{17,1},{25,9},{2,18},{10... | collective-permute-start | bytes 4325384 | tf_op jit(solution)/shard_map/ppermute | solution.py:277
  175.9 65.0 %collective-permute-start.31 = (bf16[2,352,1024]{2,1,0:T(8,128)(2,1)S(1)}, bf16[2,352,1024]{2,1,0:T(8,128)(2,1)S(1)}, u32[]{:S(2)}, u32[]{:S(2)}) collective-permute-start(bf16[2,352,1024]{2,1,0:T(8,128)(2,1)S(1)} %dynamic-slice_bitcast_fusion.1), channel_id=1, source_target_pairs={{0,8},{8,0},{16,24},{24,16},{1,9},{9,1},{17,25},{25,17},{2,10},{10... | collective-permute-start | bytes 4325384 | tf_op jit(solution)/shard_map/ppermute | solution.py:277
  190.6 36.4 %collective-permute-start.30 = (bf16[176,1024]{1,0:T(8,128)(2,1)S(1)}, bf16[176,1024]{1,0:T(8,128)(2,1)S(1)}, u32[]{:S(2)}, u32[]{:S(2)}) collective-permute-start(bf16[176,1024]{1,0:T(8,128)(2,1)S(1)} %dynamic-slice_bitcast_fusion.9), channel_id=1, source_target_pairs={{0,8},{8,0},{16,24},{24,16},{1,9},{9,1},{17,25},{25,17},{2,10},{10... | collective-permute-start | bytes 1081352 | tf_op jit(solution)/shard_map/ppermute | solution.py:277
  192.4 34.6 %collective-permute-start.29 = (bf16[176,1024]{1,0:T(8,128)(2,1)S(1)}, bf16[176,1024]{1,0:T(8,128)(2,1)S(1)}, u32[]{:S(2)}, u32[]{:S(2)}) collective-permute-start(bf16[176,1024]{1,0:T(8,128)(2,1)S(1)} %dynamic-slice_bitcast_fusion.10), channel_id=1, source_target_pairs={{0,16},{8,24},{16,0},{24,8},{1,17},{9,25},{17,1},{25,9},{2,18},{10... | collective-permute-start | bytes 1081352 | tf_op jit(solution)/shard_map/ppermute | solution.py:277
  197.1 43.4 %collective-permute-start.28 = (bf16[4,4,32,1024]{3,2,0,1:T(8,128)(2,1)S(1)}, bf16[4,4,32,1024]{3,2,0,1:T(8,128)(2,1)S(1)}, u32[]{:S(2)}, u32[]{:S(2)}) collective-permute-start(bf16[4,4,32,1024]{3,2,0,1:T(8,128)(2,1)S(1)} %dynamic-slice_bitcast_fusion.2), channel_id=1, source_target_pairs={{0,4},{4,0},{1,5},{5,1},{2,6},{6,2},{3,7},{7,3},{8,12},{12,8},{9,1... | collective-permute-start | bytes 3145736 | tf_op jit(solution)/shard_map/ppermute | solution.py:277
  267.0 15.2 %collective-permute-start.35 = (bf16[2,128,1024]{2,1,0:T(8,128)(2,1)}, bf16[2,128,1024]{2,1,0:T(8,128)(2,1)}, u32[]{:S(2)}, u32[]{:S(2)}) collective-permute-start(bf16[2,128,1024]{2,1,0:T(8,128)(2,1)} %dynamic-slice_bitcast_fusion.7), channel_id=1, source_target_pairs={{0,16},{8,24},{16,0},{24,8},{1,17},{9,25},{17,1},{25,9},{2,18},{10... | collective-permute-start | bytes 1572872 | tf_op jit(solution)/shard_map/ppermute | solution.py:277
  269.3 73.0 %reduce-scatter.3.cloned.1.call-start = ((), (), s32[]{:S(2)}) async-start(), calls=%async_computation.2 | async-start | bytes 2129920 | tf_op jit(solution)/shard_map/reduce_scatter | solution.py:521
  272.1 15.1 %collective-permute-start.34 = (bf16[352,1024]{1,0:T(8,128)(2,1)S(1)}, bf16[352,1024]{1,0:T(8,128)(2,1)S(1)}, u32[]{:S(2)}, u32[]{:S(2)}) collective-permute-start(bf16[352,1024]{1,0:T(8,128)(2,1)S(1)} %dynamic-slice_bitcast_fusion.3), channel_id=1, source_target_pairs={{0,8},{8,0},{16,24},{24,16},{1,9},{9,1},{17,25},{25,17},{2,10},{10... | collective-permute-start | bytes 2162696 | tf_op jit(solution)/shard_map/ppermute | solution.py:277
  273.5 20.2 %collective-permute-start.33 = (bf16[352,1024]{1,0:T(8,128)(2,1)S(1)}, bf16[352,1024]{1,0:T(8,128)(2,1)S(1)}, u32[]{:S(2)}, u32[]{:S(2)}) collective-permute-start(bf16[352,1024]{1,0:T(8,128)(2,1)S(1)} %dynamic-slice_bitcast_fusion.4), channel_id=1, source_target_pairs={{0,16},{8,24},{16,0},{24,8},{1,17},{9,25},{17,1},{25,9},{2,18},{10... | collective-permute-start | bytes 2162696 | tf_op jit(solution)/shard_map/ppermute | solution.py:277
  305.1 92.6 %all-gather.11.cloned.1.call-start = ((), (), s32[]{:S(2)}) async-start(), calls=%async_computation.6 | async-start | bytes 7225344 | tf_op jit(solution)/shard_map/all_gather | solution.py:574
  319.4 17.8 %collective-permute-start.44 = (bf16[384,256]{1,0:T(8,128)(2,1)S(1)}, bf16[384,256]{1,0:T(8,128)(2,1)S(1)}, u32[]{:S(2)}, u32[]{:S(2)}) collective-permute-start(bf16[384,256]{1,0:T(8,128)(2,1)S(1)} %dynamic-slice_bitcast_fusion.12), channel_id=1, source_target_pairs={{0,16},{8,24},{16,0},{24,8},{1,17},{9,25},{17,1},{25,9},{2,18},{10... | collective-permute-start | bytes 589832 | tf_op jit(solution)/shard_map/ppermute | solution.py:277
  357.6 14.0 %collective-permute-start.37 = (bf16[256,1024]{1,0:T(8,128)(2,1)S(1)}, bf16[256,1024]{1,0:T(8,128)(2,1)S(1)}, u32[]{:S(2)}, u32[]{:S(2)}) collective-permute-start(bf16[256,1024]{1,0:T(8,128)(2,1)S(1)} %get-tuple-element.128), channel_id=1, source_target_pairs={{0,1},{1,2},{4,5},{5,6},{8,9},{9,10},{12,13},{13,14},{16,17},{17,1... | collective-permute-start | bytes 1572872 | tf_op jit(solution)/shard_map/ppermute | solution.py:295
  372.0 19.7 %collective-permute-start.38 = (bf16[256,1024]{1,0:T(8,128)(2,1)S(1)}, bf16[256,1024]{1,0:T(8,128)(2,1)S(1)}, u32[]{:S(2)}, u32[]{:S(2)}) collective-permute-start(bf16[256,1024]{1,0:T(8,128)(2,1)S(1)} %get-tuple-element.126), channel_id=1, source_target_pairs={{0,1},{1,2},{2,3},{4,5},{5,6},{6,7},{8,9},{9,10},{10,11},{12,13},{... | collective-permute-start | bytes 1572872 | tf_op jit(solution)/shard_map/ppermute | solution.py:295
  382.4 13.5 %collective-permute-start.41 = (bf16[256,1024]{1,0:T(8,128)(2,1)S(1)}, bf16[256,1024]{1,0:T(8,128)(2,1)S(1)}, u32[]{:S(2)}, u32[]{:S(2)}) collective-permute-start(bf16[256,1024]{1,0:T(8,128)(2,1)S(1)} %get-tuple-element.127), channel_id=1, source_target_pairs={{1,0},{2,1},{3,2},{5,4},{6,5},{7,6},{9,8},{10,9},{11,10},{13,12},{... | collective-permute-start | bytes 1572872 | tf_op jit(solution)/shard_map/ppermute | solution.py:296
  (79 other events, 666.5 us)
Sparse Core Ops, SparseCore 0:
  30.6 38.8 all-gather.6
  76.0 58.4 all-gather.8
  269.4 23.3 reduce-scatter.4
  305.3 37.0 reduce-scatter.2
  344.6 45.1 all-gather.10

commit v4 on v3

--- a/solution.py
+++ b/solution.py
@@ -50,7 +50,27 @@
     return jnp.where(lane % HD < HD // 2, ahead, behind)
 
 
-def project_kernel(n_ref, w_ref, cos_ref, sin_ref, q_ref, k_ref, v_ref):
+def project_kernel(ranks, rank_ref, *refs):
+    own_ref, *came = refs[: 2 * ranks - 1]
+    w_ref, cos_ref, sin_ref, n_ref, q_ref, k_ref, v_ref = refs[2 * ranks - 1 :]
+    ups, downs = came[: ranks - 1], came[ranks - 1 :]
+    step = pl.program_id(0)
+
+    @pl.when(step == 0)
+    def _():
+        n_ref[...] = own_ref[...]
+
+    for k in range(1, ranks):
+        below = rank_ref[0] + k < ranks
+
+        @pl.when((step == k) & below)
+        def _():
+            n_ref[...] = downs[k - 1][...]
+
+        @pl.when((step == k) & jnp.logical_not(below))
+        def _():
+            n_ref[...] = ups[ranks - k - 1][...]
+
     rows = n_ref[...]
     cos, sin = cos_ref[...], sin_ref[...]
     for c, out in ((0, q_ref), (1, k_ref), (2, v_ref)):
@@ -66,26 +86,30 @@
             out[:, at : at + 128] = turned
 
 
-def project(rows, weight, cos, sin):
-    length, width = rows.shape
+def project(rank, own, ups, downs, weight, cos, sin):
+    block, width = own.shape
+    ranks = len(ups) + 1
+    length = ranks * block
     cols = weight.shape[2]
-    block = 256
     return pl.pallas_call(
-        project_kernel,
-        grid=(length // block,),
-        in_specs=[
-            pl.BlockSpec((block, width), lambda i: (i, 0)),
+        lambda *refs: project_kernel(ranks, *refs),
+        grid=(ranks,),
+        in_specs=[pl.BlockSpec(memory_space=pltpu.SMEM)]
+        + [pl.BlockSpec((block, width), lambda i: (0, 0))] * (2 * ranks - 1)
+        + [
             pl.BlockSpec((3, width, cols), lambda i: (0, 0, 0)),
             pl.BlockSpec((block, 128), lambda i: (i, 0)),
             pl.BlockSpec((block, 128), lambda i: (i, 0)),
         ],
-        out_specs=[pl.BlockSpec((block, cols), lambda i: (i, 0))] * 3,
-        out_shape=[jax.ShapeDtypeStruct((length, cols), BF)] * 3,
+        out_specs=[pl.BlockSpec((block, width), lambda i: (i, 0))]
+        + [pl.BlockSpec((block, cols), lambda i: (i, 0))] * 3,
+        out_shape=[jax.ShapeDtypeStruct((length, width), BF)]
+        + [jax.ShapeDtypeStruct((length, cols), BF)] * 3,
         compiler_params=pltpu.CompilerParams(vmem_limit_bytes=40 * 2**20),
         cost_estimate=pl.CostEstimate(
-            flops=6 * length * width * cols, bytes_accessed=5 * 2**20, transcendentals=0
+            flops=6 * length * width * cols, bytes_accessed=9 * 2**20, transcendentals=0
         ),
-    )(rows, weight, cos, sin)
+    )(rank, own, *ups, *downs, weight, cos, sin)
 
 
 def half_mask(values, half):
@@ -281,12 +305,12 @@
     return [1 << b for b in range(count.bit_length() - 1)]
 
 
-def gather_ranks(value, count):
+def relay_ranks(value, count):
     ups, downs = [value], [value]
     for step in range(1, count):
         ups.append(lax.ppermute(ups[-1], "tensor", [(z, z + 1) for z in range(step - 1, count - 1)]))
         downs.append(lax.ppermute(downs[-1], "tensor", [(z, z - 1) for z in range(1, count - step + 1)]))
-    return [downs[k] + ups[count - k] for k in range(1, count)]
+    return ups[1:], downs[1:]
 
 
 def scatter_ranks(blocks, count):
@@ -379,23 +403,22 @@
             at = lax.broadcasted_iota(jnp.int32, rows.shape, 0)
             return jnp.where((at < per) & (j * per + at < share), rows, jnp.zeros_like(rows))
 
-        gate_mine = part(gate_t, chip)
         out_mine = lax.dynamic_slice_in_dim(
             output_weight, (core * chips + chip) * out_piece, out_piece
         )
-        rest_mine = jnp.concatenate([part(up_t, chip), out_mine, part(down_weight, chip)])
-
-        gate_came = jnp.concatenate([shift(gate_mine, -k, ranks) for k in range(1, ranks)])
+        gate_out_mine = jnp.concatenate([part(gate_t, chip), out_mine])
+        up_down_mine = jnp.concatenate([part(up_t, chip), part(down_weight, chip)])
+
+        gate_out_came = jnp.concatenate([shift(gate_out_mine, -k, ranks) for k in range(1, ranks)])
         token_f = tokens[0].astype(F32)
         normal_attn, inverse_attn = normalize(token_f)
         normed_attn = (normal_attn * gain_attn).astype(BF)
-        rest_sent, gate_came = hold((rest_mine, gate_came))
-        gate_all = lax.all_gather(gate_came, "chip").reshape(chips, others * piece, width)
-        rest_came = jnp.concatenate(gather_ranks(rest_sent, ranks))
-        normed_sent, rest_came = hold((normed_attn, rest_came))
-        rest_all = lax.all_gather(rest_came, "chip").reshape(chips, others, -1, width)
-        normed_came = gather_ranks(normed_sent, ranks)
-        normed_rows = jnp.concatenate([normed_attn] + normed_came)
+        up_down_sent, normed_sent, gate_out_came = hold((up_down_mine, normed_attn, gate_out_came))
+        gate_out_all = lax.all_gather(gate_out_came, "chip").reshape(chips, others, -1, width)
+        ups, downs = relay_ranks(up_down_sent, ranks)
+        up_down_came = jnp.concatenate([downs[k] + ups[others - 1 - k] for k in range(others)])
+        up_down_all = lax.all_gather(up_down_came, "chip").reshape(chips, others, -1, width)
+        normed_ups, normed_downs = relay_ranks(normed_sent, ranks)
 
         segments = segment_ids[0]
         middle = segments[length // 2]
@@ -413,17 +436,26 @@
 
         cot = cotangent[0]
         cot_pair = jnp.concatenate([cot, flip(cot, "core", 1, cores)])
-        normed_rows, cos_table, sin_table, cot_pair = hold(
-            (normed_rows, cos_table, sin_table, cot_pair)
-        )
-
-        queries, keys, values = project(normed_rows, query_key_value_weight, cos_table, sin_table)
+        normed_attn, cos_table, sin_table, cot_pair = hold(
+            (normed_attn, cos_table, sin_table, cot_pair)
+        )
+
+        normed_rows, queries, keys, values = project(
+            rank[None],
+            normed_attn,
+            normed_ups,
+            normed_downs,
+            query_key_value_weight,
+            cos_table,
+            sin_table,
+        )
         mixture, logs, queries, keys, values = attend(by, queries, keys, values, doc)
         mixture = mixture.reshape(ranks, own_rows, heads_rows)
+        mixture_own, gate_out_all = hold((mixture[0], gate_out_all))
         attention = jnp.concatenate(
-            [mixture[0]] + [shift(mixture[k], k, ranks) for k in range(1, ranks)], axis=1
-        )
-        attention, gate_all, rest_all = hold((attention, gate_all, rest_all))
+            [mixture_own] + [shift(mixture[k], k, ranks) for k in range(1, ranks)], axis=1
+        )
+        attention, up_down_all = hold((attention, up_down_all))
 
         def whole(weight, rest):
             blocks = []
@@ -431,7 +463,7 @@
                 blocks += [part(weight, j), rest[j].reshape(-1, width)]
             return jnp.concatenate(blocks)
 
-        out_half = jnp.swapaxes(rest_all[:, :, piece : piece + out_piece], 0, 1)
+        out_half = jnp.swapaxes(gate_out_all[:, :, piece:], 0, 1)
         out_half = out_half.reshape(others, heads_rows // cores, width)
         out_other = flip(out_half, "core", 1, cores)
         out_rest = jnp.concatenate(
@@ -447,9 +479,9 @@
         hidden_state = token_f + nn(attention, out_weight)
         normal_mlp, inverse_mlp = normalize(hidden_state)
         normed_mlp = (normal_mlp * gain_mlp).astype(BF)
-        gate = whole(gate_t, gate_all)
-        up = whole(up_t, rest_all[:, :, :piece])
-        down = whole(down_weight, rest_all[:, :, piece + out_piece :])
+        gate = whole(gate_t, gate_out_all[:, :, :piece])
+        up = whole(up_t, up_down_all[:, :, :piece])
+        down = whole(down_weight, up_down_all[:, :, piece:])
 
         normed_pair = jnp.concatenate([normed_mlp, flip(normed_mlp, "core", 1, cores)])
         gate_proj = nt(normed_pair, gate)
@@ -459,6 +491,7 @@
         act = gate_proj * cdf
         hid = (act * up_proj).astype(BF)
         down_grad = tn(hid, cot_pair).astype(BF).reshape(chips, ranks * piece, width)
+        cot_pair, down_grad = hold((cot_pair, down_grad))
         cut = ranks * piece // 2
         down_sums = [
             Halving(down_grad[:, :cut], chip, chips, False),
@@ -472,7 +505,6 @@
         gate_sum = Halving(tn(gate_grad, normed_pair).astype(BF), chip, chips, False)
         up_sum = Halving(tn(up_grad, normed_pair).astype(BF), chip, chips, True)
         gate_grad, gate_sum.held, up_sum.held = hold((gate_grad, gate_sum.held, up_sum.held))
-        gate_grad = tie(gate_grad, down_sums)
         gate_sum.send()
         up_sum.send()
         in_other = nn(gate_grad[own_rows:], gate) + nn(up_grad[own_rows:], up)
@@ -483,7 +515,7 @@
         hidden_grad = cot.astype(F32) + norm_back(
             normed_mlp_grad, normal_mlp, inverse_mlp, gain_mlp
         )
-        branch_grad = hidden_grad.astype(BF)
+        branch_grad = tie(hidden_grad.astype(BF), down_sums)
 
         attended_grad = nt(branch_grad, out_weight).astype(BF)
         attended_came = [
@@ -521,14 +553,14 @@
             return lax.psum_scatter(flat, "tensor", scatter_dimension=0, tiled=True)
 
         down_total = sum_ranks(down_here.reshape(ranks, piece, width))
-        attended_rows = tie(attended_rows, [gate_sum, up_sum])
         out_sum = Halving(out_blocks, chip, chips, True)
-        gate_sum.send()
-        up_sum.send()
         out_sum.send()
         dq, dk, dv = attend_back(
             by, queries, keys, values, attended_rows, logs, cos_table, sin_table, doc
         )
+        dq = tie(dq, [gate_sum, up_sum])
+        gate_sum.send()
+        up_sum.send()
         normed_attn_part = (
             nt(dq, query_key_value_weight[0])
             + nt(dk, query_key_value_weight[1])
@@ -562,7 +594,7 @@
             jnp.concatenate([gain_attn_part, gain_mlp_part]),
             (("core", cores), ("chip", chips), ("tensor", ranks)),
         )
-        qkv_here, gains = hold((qkv_here, gains))
+        qkv_here, gains, input_grad = hold((qkv_here, gains, input_grad))
         grad_gain_attn, grad_gain_mlp = gains[:width], gains[width:]
         groups = width // heads_rows
         qkv_part = qkv_rows // groups

time: 417 us -> 465 us (1.12)
  waiting for transfers between devices: 194 us -> 215 us
  starting transfers between devices: 72.9 us -> 83.7 us
  local copies, waits for them, and re-layouts: 27.2 us -> 37.2 us
  other arithmetic: 37.1 us -> 46 us
  matrix products: 31.5 us -> 25.7 us
    all_gather x1, waiting for transfers between devices: 0.01 us -> 44.3 us  [on_device(): every = lax.all_gather(pieces, ('core', 'chip'))]
    ppermute x24, waiting for transfers between devices: 80.5 us -> 65.8 us  [flip(): return lax.ppermute(value, axis, [(i, i ^ bit) for i in range(count)])]
    ppermute x9, waiting for transfers between devices: 26 us -> 38.2 us  [shift(): lax.ppermute(value, 'tensor', [(i, (i + by) % count) for i in range(count)])]
    ppermute x3, starting transfers between devices: 17.3 us -> 27.9 us  [scatter_ranks(): up = lax.ppermute(up, 'tensor', [(z, z + 1) for z in range(step)])]
    ppermute x12, waiting for transfers between devices: 52.2 us -> 46.7 us  [the longest x6 34.2 us: relay_ranks(): lax.ppermute(downs[-1], 'tensor', [(z, z - 1) for z in range(1, count - s...]
    dot_general x7, matrix products: 15.5 us -> 10.1 us  [nt(): lax.dot_general(left, right, (((1,), (1,)), ((), ())), preferred_element_...]
    ppermute x3, waiting for transfers between devices: 25.6 us -> 20.3 us  [scatter_ranks(): up = lax.ppermute(up, 'tensor', [(z, z + 1) for z in range(step)])]
    reduce_scatter x2, waiting for transfers between devices: 5.08 us -> 0.04 us  [sum_ranks(): return lax.psum_scatter(flat, 'tensor', scatter_dimension=0, tiled=True)]
  transfers between devices with their start and end apart: 56 -> 56, of which waited for: 34 -> 25; matrix products, arithmetic and copies ran while one was open for 12% -> 16% of each run, Pallas kernels for 3% -> 7%
where the time goes in v4:
time: 465 us; the launch traced here: 461 us
  waiting for transfers between devices  215 us (46%)
  starting transfers between devices  83.7 us (18%)
  other arithmetic  46 us (10%)
  local copies, waits for them, and re-layouts  37.2 us (8%)
  Pallas kernels  36.2 us (8%)
  matrix products  25.7 us (6%)
  between operations  16.3 us (4%)
    ppermute x24, waiting for transfers between devices, flip(): return lax.ppermute(value, axis, [(i, i ^ bit) for i in range(count)])  65.8 us
    all_gather x1, waiting for transfers between devices, on_device(): every = lax.all_gather(pieces, ('core', 'chip'))  44.3 us
    ppermute x9, waiting for transfers between devices, shift(): lax.ppermute(value, 'tensor', [(i, (i + by) % count) for i in range(count)])  38.2 us
    ppermute x6, waiting for transfers between devices, relay_ranks(): lax.ppermute(downs[-1], 'tensor', [(z, z - 1) for z in range(1, count - s...  34.2 us
    ppermute x3, starting transfers between devices, scatter_ranks(): up = lax.ppermute(up, 'tensor', [(z, z + 1) for z in range(step)])  27.9 us
    ppermute x24, starting transfers between devices, flip(): return lax.ppermute(value, axis, [(i, i ^ bit) for i in range(count)])  20.4 us
    ppermute x3, waiting for transfers between devices, scatter_ranks(): up = lax.ppermute(up, 'tensor', [(z, z + 1) for z in range(step)])  20.3 us
    unnamed x115, local copies, waits for them, and re-layouts  15.5 us
  transfers between devices with their start and end apart: 56, of which 25 were waited for; matrix products, arithmetic and copies ran while one was open for 16% of the time, Pallas kernels for 7%

profile of v4, /device:TPU:0, one launch (start us, length us, event | category | flops | bytes accessed | tf_op | source)
XLA Modules:
  0.0 460.7 jit_solution(18053444704907574466)
XLA Ops:
  12.4 5.1 %collective-permute-start.1 = (bf16[120,1024]{1,0:T(8,128)(2,1)S(1)}, bf16[120,1024]{1,0:T(8,128)(2,1)S(1)}, u32[]{:S(2)}, u32[]{:S(2)}) collective-permute-start(bf16[120,1024]{1,0:T(8,128)(2,1)S(1)} %pad_maximum_fusion.15), channel_id=1, source_target_pairs={{0,3},{1,0},{2,1},{3,2},{4,7},{5,4},{6,5},{7,6},{8,11},{9,8},{10,9... | collective-permute-start | bytes 737288 | tf_op jit(solution)/shard_map/ppermute | solution.py:297
  19.4 4.6 collective-permute-done.1
  24.0 14.5 %collective-permute-done.2 = bf16[120,1024]{1,0:T(8,128)(2,1)S(1)} collective-permute-done((bf16[120,1024]{1,0:T(8,128)(2,1)S(1)}, bf16[120,1024]{1,0:T(8,128)(2,1)S(1)}, u32[]{:S(2)}, u32[]{:S(2)}) %collective-permute-start.2) | collective-permute-done | bytes 245792 | tf_op jit(solution)/shard_map/ppermute | solution.py:297
  43.6 5.7 %collective-permute-done.14 = bf16[176,1024]{1,0:T(8,128)(2,1)S(1)} collective-permute-done((bf16[176,1024]{1,0:T(8,128)(2,1)S(1)}, bf16[176,1024]{1,0:T(8,128)(2,1)S(1)}, u32[]{:S(2)}, u32[]{:S(2)}) %collective-permute-start.14) | collective-permute-done | bytes 360480 | tf_op jit(solution)/shard_map/ppermute | solution.py:311
  50.0 4.2 collective-permute-done.13
  56.2 8.6 %collective-permute-done.17 = bf16[176,1024]{1,0:T(8,128)(2,1)S(1)} collective-permute-done((bf16[176,1024]{1,0:T(8,128)(2,1)S(1)}, bf16[176,1024]{1,0:T(8,128)(2,1)S(1)}, u32[]{:S(2)}, u32[]{:S(2)}) %collective-permute-start.17) | collective-permute-done | bytes 360480 | tf_op jit(solution)/shard_map/ppermute | solution.py:312
  66.4 8.1 %collective-permute-done.18 = bf16[176,1024]{1,0:T(8,128)(2,1)S(1)} collective-permute-done((bf16[176,1024]{1,0:T(8,128)(2,1)S(1)}, bf16[176,1024]{1,0:T(8,128)(2,1)S(1)}, u32[]{:S(2)}, u32[]{:S(2)}) %collective-permute-start.18) | collective-permute-done | bytes 360480 | tf_op jit(solution)/shard_map/ppermute | solution.py:312
  78.7 6.8 %collective-permute-done.4.refs_2_ = bf16[256,1024]{1,0:T(8,128)(2,1)S(1)} collective-permute-done((bf16[256,1024]{1,0:T(8,128)(2,1)S(1)}, bf16[256,1024]{1,0:T(8,128)(2,1)S(1)}, u32[]{:S(2)}, u32[]{:S(2)}) %collective-permute-start.4) | collective-permute-done | bytes 524320 | tf_op jit(solution)/shard_map/ppermute | solution.py:311
  94.9 6.5 %collective-permute-done.8.refs_6_ = bf16[256,1024]{1,0:T(8,128)(2,1)} collective-permute-done((bf16[256,1024]{1,0:T(8,128)(2,1)S(1)}, bf16[256,1024]{1,0:T(8,128)(2,1)}, u32[]{:S(2)}, u32[]{:S(2)}) %collective-permute-start.8) | collective-permute-done | bytes 524320 | tf_op jit(solution)/shard_map/ppermute | solution.py:312
  107.9 4.9 %collective-permute-done.9.refs_7_ = bf16[256,1024]{1,0:T(8,128)(2,1)} collective-permute-done((bf16[256,1024]{1,0:T(8,128)(2,1)}, bf16[256,1024]{1,0:T(8,128)(2,1)}, u32[]{:S(2)}, u32[]{:S(2)}) %collective-permute-start.9) | collective-permute-done | bytes 524320 | tf_op jit(solution)/shard_map/ppermute | solution.py:312
  112.8 4.9 %shard_map.152 = (bf16[1024,1024]{1,0:T(8,128)(2,1)S(1)}, bf16[1024,256]{1,0:T(8,128)(2,1)S(1)}, bf16[1024,256]{1,0:T(8,128)(2,1)S(1)}, bf16[1024,256]{1,0:T(8,128)(2,1)S(1)}) custom-call(s32[1]{0:T(128)} %bitcast.4.refs_0_, bf16[256,1024]{1,0:T(8,128)(2,1)S(1)} %fusion.25.refs_1_, bf16[256,1024]{1,0:T(8,128)(2,1)S(1)} %copy-done.5, ...), custom_call_target="tpu_custom_call" | custom-call | flops 1610612736 | bytes 9437184 | tf_op jit(solution)/shard_map/pallas_call | solution.py:94
  119.1 11.5 %shard_map.153 = (bf16[1024,256]{1,0:T(8,128)(2,1)S(1)}, f32[2,2,896]{2,1,0:T(2,128)S(1)}, bf16[1024,256]{1,0:T(8,128)(2,1)S(1)}, bf16[1024,256]{1,0:T(8,128)(2,1)S(1)}, bf16[1024,256]{1,0:T(8,128)(2,1)S(1)}) custom-call(s32[1]{0:T(128)} %bitcast.3.refs_0_, bf16[1024,256]{1,0:T(8,128)(2,1)S(1)} %get-tuple-element.64.refs_1_, ...), custom_call_target="tpu_custom_call" | custom-call | flops 1644167168 | bytes 2097152 | tf_op jit(solution)/shard_map/pallas_call | solution.py:161
  144.2 4.4 collective-permute-done.11
  195.8 8.3 %collective-permute-done.22 = bf16[2,176,1024]{2,1,0:T(8,128)(2,1)S(1)} collective-permute-done((bf16[2,176,1024]{2,1,0:T(8,128)(2,1)S(1)}, bf16[2,176,1024]{2,1,0:T(8,128)(2,1)S(1)}, u32[]{:S(2)}, u32[]{:S(2)}) %collective-permute-start.22) | collective-permute-done | bytes 720928 | tf_op jit(solution)/shard_map/ppermute | solution.py:301
  217.4 9.0 %collective-permute-done.25 = bf16[256,256]{1,0:T(8,128)(2,1)S(1)} collective-permute-done((bf16[256,256]{1,0:T(8,128)(2,1)S(1)}, bf16[256,256]{1,0:T(8,128)(2,1)S(1)}, u32[]{:S(2)}, u32[]{:S(2)}) %collective-permute-start.25) | collective-permute-done | bytes 131104 | tf_op jit(solution)/shard_map/ppermute | solution.py:297
  227.7 30.5 %collective-permute-done.30 = bf16[176,1024]{1,0:T(8,128)(2,1)S(1)} collective-permute-done((bf16[176,1024]{1,0:T(8,128)(2,1)S(1)}, bf16[176,1024]{1,0:T(8,128)(2,1)S(1)}, u32[]{:S(2)}, u32[]{:S(2)}) %collective-permute-start.30) | collective-permute-done | bytes 360480 | tf_op jit(solution)/shard_map/ppermute | solution.py:301
  259.8 14.7 %shard_map.154 = (bf16[1024,256]{1,0:T(8,128)(2,1)S(1)}, bf16[1024,256]{1,0:T(8,128)(2,1)S(1)}, bf16[1024,256]{1,0:T(8,128)(2,1)S(1)}) custom-call(s32[1]{0:T(128)} %bitcast.3.refs_0_, bf16[1024,256]{1,0:T(8,128)(2,1)S(1)} %get-tuple-element.82.refs_1_, bf16[1024,256]{1,0:T(8,128)(2,1)S(1)} %copy-done.9, bf16[1024,256]{1,0:T(8,128)(2,1)S(1)} %copy-done.11, ...), custom_call_target="tpu_custom_call" | custom-call | flops 4110417920 | bytes 5242880 | tf_op jit(solution)/shard_map/pallas_call | solution.py:229
  294.7 14.5 %collective-permute-done.43 = bf16[2,128,1024]{2,1,0:T(8,128)(2,1)S(1)} collective-permute-done((bf16[2,128,1024]{2,1,0:T(8,128)(2,1)}, bf16[2,128,1024]{2,1,0:T(8,128)(2,1)S(1)}, u32[]{:S(2)}, u32[]{:S(2)}) %collective-permute-start.43) | collective-permute-done | bytes 524320 | tf_op jit(solution)/shard_map/ppermute | solution.py:301
  315.7 8.3 %collective-permute-start.44 = (bf16[256,1024]{1,0:T(8,128)(2,1)}, bf16[256,1024]{1,0:T(8,128)(2,1)S(1)}, u32[]{:S(2)}, u32[]{:S(2)}) collective-permute-start(bf16[256,1024]{1,0:T(8,128)(2,1)} %get-tuple-element.145), channel_id=1, source_target_pairs={{0,1},{4,5},{8,9},{12,13},{16,17},{20,21},{24,25},{28,29}} | collective-permute-start | bytes 1572872 | tf_op jit(solution)/shard_map/ppermute | solution.py:319
  334.4 4.0 collective-permute-start.45
  340.0 20.3 %collective-permute-done.45 = bf16[256,1024]{1,0:T(8,128)(2,1)S(1)} collective-permute-done((bf16[256,1024]{1,0:T(8,128)(2,1)S(1)}, bf16[256,1024]{1,0:T(8,128)(2,1)S(1)}, u32[]{:S(2)}, u32[]{:S(2)}) %collective-permute-start.45) | collective-permute-done | bytes 524320 | tf_op jit(solution)/shard_map/ppermute | solution.py:319
  360.7 15.6 %collective-permute-start.46 = (bf16[256,1024]{1,0:T(8,128)(2,1)S(1)}, bf16[256,1024]{1,0:T(8,128)(2,1)S(1)}, u32[]{:S(2)}, u32[]{:S(2)}) collective-permute-start(bf16[256,1024]{1,0:T(8,128)(2,1)S(1)} %get-tuple-element.141), channel_id=1, source_target_pairs={{0,1},{1,2},{2,3},{4,5},{5,6},{6,7},{8,9},{9,10},{10,11},{12,13},{... | collective-permute-start | bytes 1572872 | tf_op jit(solution)/shard_map/ppermute | solution.py:319
  401.4 44.3 %all-gather.11.cloned.1.call-done = bf16[3136,1024]{1,0:T(8,128)(2,1)} async-done(((bf16[392,1024]{1,0:T(8,128)(2,1)}), bf16[3136,1024]{1,0:T(8,128)(2,1)}) %all-gather.11.cloned.1.call-update) | async-done | bytes 6422544 | tf_op jit(solution)/shard_map/all_gather | solution.py:606
  448.6 5.2 %shard_map.155 = (f32[2,656,1024]{2,1,0:T(8,128)}, f32[656,1024]{1,0:T(8,128)}, f32[8,32,1024]{2,1,0:T(8,128)}, f32[3,8,4,32,256]{4,3,2,1,0:T(8,128)}) custom-call(bf16[8,392,1024]{2,1,0:T(8,128)(2,1)S(1)} %bitcast.244), custom_call_target="tpu_custom_call" | custom-call | bytes 18874368 | tf_op jit(solution)/shard_map/pallas_call | solution.py:274
  (337 shorter events, 179.7 us)
Async XLA Ops:
  7.2 125.7 %all-gather.7.cloned.1.call-start = ((), (), s32[]{:S(2)}) async-start(), calls=%async_computation.4 | async-start | bytes 3686400 | tf_op jit(solution)/shard_map/all_gather | solution.py:417
  17.6 20.9 %collective-permute-start.2 = (bf16[120,1024]{1,0:T(8,128)(2,1)S(1)}, bf16[120,1024]{1,0:T(8,128)(2,1)S(1)}, u32[]{:S(2)}, u32[]{:S(2)}) collective-permute-start(bf16[120,1024]{1,0:T(8,128)(2,1)S(1)} %pad_maximum_fusion.15), channel_id=1, source_target_pairs={{0,2},{1,3},{2,0},{3,1},{4,6},{5,7},{6,4},{7,5},{8,10},{9,11},{10,... | collective-permute-start | bytes 737288 | tf_op jit(solution)/shard_map/ppermute | solution.py:297
  17.6 20.9 %collective-permute-start.3 = (bf16[120,1024]{1,0:T(8,128)(2,1)S(1)}, bf16[120,1024]{1,0:T(8,128)(2,1)S(1)}, u32[]{:S(2)}, u32[]{:S(2)}) collective-permute-start(bf16[120,1024]{1,0:T(8,128)(2,1)S(1)} %pad_maximum_fusion.15), channel_id=1, source_target_pairs={{0,1},{1,2},{2,3},{3,0},{4,5},{5,6},{6,7},{7,4},{8,9},{9,10},{10,1... | collective-permute-start | bytes 737288 | tf_op jit(solution)/shard_map/ppermute | solution.py:297
  39.4 117.3 %all-gather.9.cloned.1.call-start = ((), (), s32[]{:S(2)}) async-start(), calls=%async_computation.5 | async-start | bytes 5406720 | tf_op jit(solution)/shard_map/all_gather | solution.py:420
  75.7 323.0 %reduce-scatter.5.cloned.1.call-start = ((), (), s32[]{:S(2)}) async-start(), calls=%async_computation.3 | async-start | bytes 901120 | tf_op jit(solution)/shard_map/reduce_scatter | solution.py:553
  135.1 19.0 %collective-permute-start.19 = (bf16[3,128,1024]{2,1,0:T(8,128)(2,1)}, bf16[3,128,1024]{2,1,0:T(8,128)(2,1)}, u32[]{:S(2)}, u32[]{:S(2)}) collective-permute-start(bf16[3,128,1024]{2,1,0:T(8,128)(2,1)} %bitcast.11), channel_id=1, source_target_pairs={{0,4},{4,0},{1,5},{5,1},{2,6},{6,2},{3,7},{7,3},{8,12},{12,8},{9,1... | collective-permute-start | bytes 2359304 | tf_op jit(solution)/shard_map/ppermute | solution.py:301
  174.2 18.9 %collective-permute-start.27 = (bf16[256,1024]{1,0:T(8,128)(2,1)S(1)}, bf16[256,1024]{1,0:T(8,128)(2,1)S(1)}, u32[]{:S(2)}, u32[]{:S(2)}) collective-permute-start(bf16[256,1024]{1,0:T(8,128)(2,1)S(1)} %slice.320), channel_id=1, source_target_pairs={{0,4},{4,0},{1,5},{5,1},{2,6},{6,2},{3,7},{7,3},{8,12},{12,8},{9,1... | collective-permute-start | bytes 1572872 | tf_op jit(solution)/shard_map/ppermute | solution.py:301
  207.5 20.1 %collective-permute-start.29 = (bf16[176,1024]{1,0:T(8,128)(2,1)S(1)}, bf16[176,1024]{1,0:T(8,128)(2,1)S(1)}, u32[]{:S(2)}, u32[]{:S(2)}) collective-permute-start(bf16[176,1024]{1,0:T(8,128)(2,1)S(1)} %dynamic-slice_bitcast_fusion.10), channel_id=1, source_target_pairs={{0,16},{8,24},{16,0},{24,8},{1,17},{9,25},{17,1},{25,9},{2,18},{10... | collective-permute-start | bytes 1081352 | tf_op jit(solution)/shard_map/ppermute | solution.py:301
  209.6 49.7 %collective-permute-start.28 = (bf16[4,4,32,1024]{3,2,0,1:T(8,128)(2,1)S(1)}, bf16[4,4,32,1024]{3,2,0,1:T(8,128)(2,1)S(1)}, u32[]{:S(2)}, u32[]{:S(2)}) collective-permute-start(bf16[4,4,32,1024]{3,2,0,1:T(8,128)(2,1)S(1)} %dynamic-slice_bitcast_fusion.2), channel_id=1, source_target_pairs={{0,4},{4,0},{1,5},{5,1},{2,6},{6,2},{3,7},{7,3},{8,12},{12,8},{9,1... | collective-permute-start | bytes 3145736 | tf_op jit(solution)/shard_map/ppermute | solution.py:301
  216.9 57.6 %collective-permute-start.31 = (bf16[2,352,1024]{2,1,0:T(8,128)(2,1)}, bf16[2,352,1024]{2,1,0:T(8,128)(2,1)}, u32[]{:S(2)}, u32[]{:S(2)}) collective-permute-start(bf16[2,352,1024]{2,1,0:T(8,128)(2,1)} %dynamic-slice_bitcast_fusion.1), channel_id=1, source_target_pairs={{0,8},{8,0},{16,24},{24,16},{1,9},{9,1},{17,25},{25,17},{2,10},{10... | collective-permute-start | bytes 4325384 | tf_op jit(solution)/shard_map/ppermute | solution.py:301
  226.5 48.0 %collective-permute-start.32 = (bf16[2,352,1024]{2,1,0:T(8,128)(2,1)S(1)}, bf16[2,352,1024]{2,1,0:T(8,128)(2,1)}, u32[]{:S(2)}, u32[]{:S(2)}) collective-permute-start(bf16[2,352,1024]{2,1,0:T(8,128)(2,1)S(1)} %dynamic-slice_bitcast_fusion), channel_id=1, source_target_pairs={{0,16},{8,24},{16,0},{24,8},{1,17},{9,25},{17,1},{25,9},{2,18},{10... | collective-permute-start | bytes 4325384 | tf_op jit(solution)/shard_map/ppermute | solution.py:301
  227.1 31.2 %collective-permute-start.30 = (bf16[176,1024]{1,0:T(8,128)(2,1)S(1)}, bf16[176,1024]{1,0:T(8,128)(2,1)S(1)}, u32[]{:S(2)}, u32[]{:S(2)}) collective-permute-start(bf16[176,1024]{1,0:T(8,128)(2,1)S(1)} %dynamic-slice_bitcast_fusion.9), channel_id=1, source_target_pairs={{0,8},{8,0},{16,24},{24,16},{1,9},{9,1},{17,25},{25,17},{2,10},{10... | collective-permute-start | bytes 1081352 | tf_op jit(solution)/shard_map/ppermute | solution.py:301
  277.4 31.9 %collective-permute-start.42 = (bf16[352,1024]{1,0:T(8,128)(2,1)}, bf16[352,1024]{1,0:T(8,128)(2,1)}, u32[]{:S(2)}, u32[]{:S(2)}) collective-permute-start(bf16[352,1024]{1,0:T(8,128)(2,1)} %dynamic-slice_bitcast_fusion.3), channel_id=1, source_target_pairs={{0,8},{8,0},{16,24},{24,16},{1,9},{9,1},{17,25},{25,17},{2,10},{10... | collective-permute-start | bytes 2162696 | tf_op jit(solution)/shard_map/ppermute | solution.py:301
  280.9 28.4 %collective-permute-start.41 = (bf16[352,1024]{1,0:T(8,128)(2,1)}, bf16[352,1024]{1,0:T(8,128)(2,1)}, u32[]{:S(2)}, u32[]{:S(2)}) collective-permute-start(bf16[352,1024]{1,0:T(8,128)(2,1)} %dynamic-slice_bitcast_fusion.4), channel_id=1, source_target_pairs={{0,16},{8,24},{16,0},{24,8},{1,17},{9,25},{17,1},{25,9},{2,18},{10... | collective-permute-start | bytes 2162696 | tf_op jit(solution)/shard_map/ppermute | solution.py:301
  286.0 23.3 %collective-permute-start.43 = (bf16[2,128,1024]{2,1,0:T(8,128)(2,1)}, bf16[2,128,1024]{2,1,0:T(8,128)(2,1)S(1)}, u32[]{:S(2)}, u32[]{:S(2)}) collective-permute-start(bf16[2,128,1024]{2,1,0:T(8,128)(2,1)} %dynamic-slice_bitcast_fusion.7), channel_id=1, source_target_pairs={{0,16},{8,24},{16,0},{24,8},{1,17},{9,25},{17,1},{25,9},{2,18},{10... | collective-permute-start | bytes 1572872 | tf_op jit(solution)/shard_map/ppermute | solution.py:301
  292.9 37.7 %collective-permute-start.33 = (bf16[3,4,128,256]{3,2,0,1:T(8,128)(2,1)}, bf16[3,4,128,256]{3,2,0,1:T(8,128)(2,1)}, u32[]{:S(2)}, u32[]{:S(2)}) collective-permute-start(bf16[3,4,128,256]{3,2,0,1:T(8,128)(2,1)} %bitcast.243), channel_id=1, source_target_pairs={{0,4},{4,0},{1,5},{5,1},{2,6},{6,2},{3,7},{7,3},{8,12},{12,8},{9,1... | collective-permute-start | bytes 2359304 | tf_op jit(solution)/shard_map/ppermute | solution.py:301
  294.7 104.1 %reduce-scatter.3.cloned.1.call-start = ((), (), s32[]{:S(2)}) async-start(), calls=%async_computation.2 | async-start | bytes 2129920 | tf_op jit(solution)/shard_map/reduce_scatter | solution.py:553
  330.6 115.2 %all-gather.11.cloned.1.call-start = ((), (), s32[]{:S(2)}) async-start(), calls=%async_computation.6 | async-start | bytes 7225344 | tf_op jit(solution)/shard_map/all_gather | solution.py:606
  334.4 25.9 %collective-permute-start.45 = (bf16[256,1024]{1,0:T(8,128)(2,1)S(1)}, bf16[256,1024]{1,0:T(8,128)(2,1)S(1)}, u32[]{:S(2)}, u32[]{:S(2)}) collective-permute-start(bf16[256,1024]{1,0:T(8,128)(2,1)S(1)} %get-tuple-element.143), channel_id=1, source_target_pairs={{0,1},{1,2},{4,5},{5,6},{8,9},{9,10},{12,13},{13,14},{16,17},{17,1... | collective-permute-start | bytes 1572872 | tf_op jit(solution)/shard_map/ppermute | solution.py:319
  338.5 21.8 %collective-permute-start.48 = (bf16[256,1024]{1,0:T(8,128)(2,1)S(1)}, bf16[256,1024]{1,0:T(8,128)(2,1)S(1)}, u32[]{:S(2)}, u32[]{:S(2)}) collective-permute-start(bf16[256,1024]{1,0:T(8,128)(2,1)S(1)} %get-tuple-element.144), channel_id=1, source_target_pairs={{2,1},{3,2},{6,5},{7,6},{10,9},{11,10},{14,13},{15,14},{18,17},{19... | collective-permute-start | bytes 1572872 | tf_op jit(solution)/shard_map/ppermute | solution.py:320
  339.4 41.1 %collective-permute-start.36 = (f32[2048]{0:T(1024)S(1)}, f32[2048]{0:T(1024)S(1)}, u32[]{:S(2)}, u32[]{:S(2)}) collective-permute-start(f32[2048]{0:T(1024)S(1)} %pad_maximum_fusion.16), channel_id=1, source_target_pairs={{0,4},{4,0},{1,5},{5,1},{2,6},{6,2},{3,7},{7,3},{8,12},{12,8},{9,1... | collective-permute-start | bytes 24584 | tf_op jit(solution)/shard_map/ppermute | solution.py:301
  360.7 36.0 %collective-permute-start.46 = (bf16[256,1024]{1,0:T(8,128)(2,1)S(1)}, bf16[256,1024]{1,0:T(8,128)(2,1)S(1)}, u32[]{:S(2)}, u32[]{:S(2)}) collective-permute-start(bf16[256,1024]{1,0:T(8,128)(2,1)S(1)} %get-tuple-element.141), channel_id=1, source_target_pairs={{0,1},{1,2},{2,3},{4,5},{5,6},{6,7},{8,9},{9,10},{10,11},{12,13},{... | collective-permute-start | bytes 1572872 | tf_op jit(solution)/shard_map/ppermute | solution.py:319
  376.3 20.4 %collective-permute-start.49 = (bf16[256,1024]{1,0:T(8,128)(2,1)S(1)}, bf16[256,1024]{1,0:T(8,128)(2,1)S(1)}, u32[]{:S(2)}, u32[]{:S(2)}) collective-permute-start(bf16[256,1024]{1,0:T(8,128)(2,1)S(1)} %get-tuple-element.142), channel_id=1, source_target_pairs={{1,0},{2,1},{3,2},{5,4},{6,5},{7,6},{9,8},{10,9},{11,10},{13,12},{... | collective-permute-start | bytes 1572872 | tf_op jit(solution)/shard_map/ppermute | solution.py:320
  377.7 19.0 %collective-permute-start.35 = (bf16[384,256]{1,0:T(8,128)(2,1)S(1)}, bf16[384,256]{1,0:T(8,128)(2,1)S(1)}, u32[]{:S(2)}, u32[]{:S(2)}) collective-permute-start(bf16[384,256]{1,0:T(8,128)(2,1)S(1)} %dynamic-slice_bitcast_fusion.12), channel_id=1, source_target_pairs={{0,16},{8,24},{16,0},{24,8},{1,17},{9,25},{17,1},{25,9},{2,18},{10... | collective-permute-start | bytes 589832 | tf_op jit(solution)/shard_map/ppermute | solution.py:301
  (85 other events, 868.0 us)
Sparse Core Ops, SparseCore 0:
  39.5 42.7 all-gather.6
  84.2 53.7 all-gather.8
  294.8 26.6 reduce-scatter.4
  330.7 44.9 reduce-scatter.2
  401.0 44.7 all-gather.10

commit v5 on v4

--- a/solution.py
+++ b/solution.py
@@ -238,9 +238,99 @@
         scratch_shapes=[pltpu.VMEM((length, 128), F32)] * 3 + [pltpu.VMEM((length, 128), BF)],
         compiler_params=pltpu.CompilerParams(vmem_limit_bytes=48 * 2**20),
         cost_estimate=pl.CostEstimate(
-            flops=20 * doc * doc * cols, bytes_accessed=5 * 2**20, transcendentals=doc * doc * 4
+            flops=0, bytes_accessed=2**20, transcendentals=0
         ),
     )(by, queries, keys, values, grads, logs, cos, sin)
+
+
+def feed_kernel(
+    sizes, n_ref, c_ref, own_ref, gate_ref, rest_ref,
+    dg_ref, du_ref, dd_ref, in_ref, in_other_ref, out_ref, out_other_ref, in_held, out_held,
+):
+    piece, out_piece, ranks, group, steps = sizes
+    step = pl.program_id(0)
+
+    def join(m, ref, first):
+        rows = []
+        for j in range(group):
+            rows.append(own_ref[j, m].astype(F32))
+            for k in range(ranks - 1):
+                rows.append(ref[j, k].astype(F32)[first : first + piece])
+        return jnp.concatenate(rows).astype(BF)
+
+    gate = join(0, gate_ref, 0)
+    up = join(1, rest_ref, 0)
+    down = join(2, rest_ref, piece + out_piece)
+    normed, cot = n_ref[...], c_ref[...]
+    gate_proj = nt(normed, gate)
+    up_proj = nt(normed, up)
+    hid_grad = nt(cot, down)
+    cdf = 0.5 * (1.0 + lax.erf(gate_proj * (1.0 / math.sqrt(2.0))))
+    pdf = jnp.exp(-0.5 * gate_proj * gate_proj) * (1.0 / math.sqrt(2.0 * math.pi))
+    act = gate_proj * cdf
+    hid = (act * up_proj).astype(BF)
+    gate_grad = (hid_grad * up_proj * (cdf + gate_proj * pdf)).astype(BF)
+    up_grad = (hid_grad * act).astype(BF)
+    for ref, left, right in ((dg_ref, gate_grad, normed), (du_ref, up_grad, normed), (dd_ref, hid, cot)):
+        ref[...] = tn(left, right).astype(BF).reshape(ref.shape)
+    in_part = nn(gate_grad, gate) + nn(up_grad, up)
+    out_part = nn(hid, down)
+
+    @pl.when(step == 0)
+    def _():
+        in_held[...] = in_part
+        out_held[...] = out_part
+
+    @pl.when(step > 0)
+    def _():
+        in_held[...] += in_part
+        out_held[...] += out_part
+
+    @pl.when(step == steps - 1)
+    def _():
+        rows = in_ref.shape[0]
+        in_ref[...] = in_held[:rows, :]
+        in_other_ref[...] = in_held[rows:, :].astype(BF)
+        out_ref[...] = out_held[:rows, :]
+        out_other_ref[...] = out_held[rows:, :].astype(BF)
+
+
+def feed(normed, cot, own, gate_all, rest_all, piece, out_piece):
+    rows, width = normed.shape
+    chips, others, rest_rows = rest_all.shape[:3]
+    hidden = (others + 1) * piece
+    half = rows // 2
+    group = 1
+    same = pl.BlockSpec((rows, width), lambda i: (0, 0))
+    grad = pl.BlockSpec((group, hidden, width), lambda i: (i, 0, 0))
+    kept = pl.BlockSpec((half, width), lambda i: (0, 0))
+    sizes = (piece, out_piece, others + 1, group, chips // group)
+    return pl.pallas_call(
+        lambda *refs: feed_kernel(sizes, *refs),
+        grid=(chips // group,),
+        in_specs=[
+            same,
+            same,
+            pl.BlockSpec((group, 3, piece, width), lambda i: (i, 0, 0, 0)),
+            pl.BlockSpec((group, others, piece, width), lambda i: (i, 0, 0, 0)),
+            pl.BlockSpec((group, others, rest_rows, width), lambda i: (i, 0, 0, 0)),
+        ],
+        out_specs=[grad] * 3 + [kept] * 4,
+        out_shape=[jax.ShapeDtypeStruct((chips, hidden, width), BF)] * 3
+        + [
+            jax.ShapeDtypeStruct((half, width), F32),
+            jax.ShapeDtypeStruct((half, width), BF),
+            jax.ShapeDtypeStruct((half, width), F32),
+            jax.ShapeDtypeStruct((half, width), BF),
+        ],
+        scratch_shapes=[pltpu.VMEM((rows, width), F32)] * 2,
+        compiler_params=pltpu.CompilerParams(vmem_limit_bytes=62 * 2**20),
+        cost_estimate=pl.CostEstimate(
+            flops=18 * rows * width * hidden * chips,
+            bytes_accessed=25 * 2**20,
+            transcendentals=2 * rows * hidden * chips,
+        ),
+    )(normed, cot, own, gate_all, rest_all)
 
 
 def assemble_kernel(sizes, in_ref, gu_ref, d_ref, o_ref, qkv_ref, held):
@@ -254,7 +344,7 @@
             held[at : at + piece, :] = rows[first : first + piece, :]
             if m == 0:
                 o_ref[device] = rows[2 * piece : 2 * piece + out_piece, :]
-                last = 3 * piece + out_piece
+                last = 3 * piece + out_piece + 8
                 for c in range(3):
                     start = last + c * qkv_part
                     qkv_ref[c, device, 0] = rows[start : start + qkv_part, :]
@@ -288,7 +378,7 @@
             jax.ShapeDtypeStruct((3, devices, groups, qkv_part, block), F32),
         ],
         scratch_shapes=[pltpu.VMEM((tall, block), F32)],
-        compiler_params=pltpu.CompilerParams(vmem_limit_bytes=40 * 2**20),
+        compiler_params=pltpu.CompilerParams(vmem_limit_bytes=60 * 2**20),
         cost_estimate=pl.CostEstimate(flops=0, bytes_accessed=18 * 2**20, transcendentals=0),
     )(every)
 
@@ -299,10 +389,6 @@
 
 def flip(value, axis, bit, count):
     return lax.ppermute(value, axis, [(i, i ^ bit) for i in range(count)])
-
-
-def bits_of(count):
-    return [1 << b for b in range(count.bit_length() - 1)]
 
 
 def relay_ranks(value, count):
@@ -326,7 +412,7 @@
 
 class Halving:
     def __init__(self, value, chip, count, turned):
-        self.chip, self.count = chip, count
+        self.chip, self.count, self.came = chip, count, None
         self.bits = count.bit_length() - 1
         self.held = value.reshape((2,) * self.bits + (-1,) + value.shape[-1:])
         order = list(range(self.bits))
@@ -345,8 +431,11 @@
 
     def take(self):
         self.held = (self.kept.astype(F32) + self.came.astype(F32)).astype(BF)
+        self.came = None
 
     def finish(self):
+        if self.came is not None:
+            self.take()
         while self.order:
             self.send()
             self.take()
@@ -359,13 +448,6 @@
         s.came = came
         s.take()
     return tied[0]
-
-
-def total_all(value, sizes):
-    for axis, count in sizes:
-        for bit in bits_of(count):
-            value = value + flip(value, axis, bit, count)
-    return value
 
 
 def make(chips, cores, ranks):
@@ -403,22 +485,26 @@
             at = lax.broadcasted_iota(jnp.int32, rows.shape, 0)
             return jnp.where((at < per) & (j * per + at < share), rows, jnp.zeros_like(rows))
 
+        gate_mine = part(gate_t, chip)
         out_mine = lax.dynamic_slice_in_dim(
             output_weight, (core * chips + chip) * out_piece, out_piece
         )
-        gate_out_mine = jnp.concatenate([part(gate_t, chip), out_mine])
-        up_down_mine = jnp.concatenate([part(up_t, chip), part(down_weight, chip)])
-
-        gate_out_came = jnp.concatenate([shift(gate_out_mine, -k, ranks) for k in range(1, ranks)])
+        rest_mine = jnp.concatenate([part(up_t, chip), out_mine, part(down_weight, chip)])
+
+        gate_came = jnp.concatenate([shift(gate_mine, -k, ranks) for k in range(1, ranks)])
         token_f = tokens[0].astype(F32)
         normal_attn, inverse_attn = normalize(token_f)
         normed_attn = (normal_attn * gain_attn).astype(BF)
-        up_down_sent, normed_sent, gate_out_came = hold((up_down_mine, normed_attn, gate_out_came))
-        gate_out_all = lax.all_gather(gate_out_came, "chip").reshape(chips, others, -1, width)
-        ups, downs = relay_ranks(up_down_sent, ranks)
-        up_down_came = jnp.concatenate([downs[k] + ups[others - 1 - k] for k in range(others)])
-        up_down_all = lax.all_gather(up_down_came, "chip").reshape(chips, others, -1, width)
+        rest_sent, gate_came = hold((rest_mine, gate_came))
+        gate_all = lax.all_gather(gate_came, "chip").reshape(chips, others, piece, width)
+        ups, downs = relay_ranks(rest_sent, ranks)
+        rest_came = jnp.concatenate([downs[k] + ups[others - 1 - k] for k in range(others)])
+        normed_sent, rest_came = hold((normed_attn, rest_came))
+        rest_all = lax.all_gather(rest_came, "chip").reshape(chips, others, -1, width)
         normed_ups, normed_downs = relay_ranks(normed_sent, ranks)
+        own = jnp.stack(
+            [jnp.stack([part(w, j) for w in (gate_t, up_t, down_weight)]) for j in range(chips)]
+        )
 
         segments = segment_ids[0]
         middle = segments[length // 2]
@@ -436,8 +522,8 @@
 
         cot = cotangent[0]
         cot_pair = jnp.concatenate([cot, flip(cot, "core", 1, cores)])
-        normed_attn, cos_table, sin_table, cot_pair = hold(
-            (normed_attn, cos_table, sin_table, cot_pair)
+        normed_attn, cos_table, sin_table, cot_pair, own = hold(
+            (normed_attn, cos_table, sin_table, cot_pair, own)
         )
 
         normed_rows, queries, keys, values = project(
@@ -451,19 +537,12 @@
         )
         mixture, logs, queries, keys, values = attend(by, queries, keys, values, doc)
         mixture = mixture.reshape(ranks, own_rows, heads_rows)
-        mixture_own, gate_out_all = hold((mixture[0], gate_out_all))
         attention = jnp.concatenate(
-            [mixture_own] + [shift(mixture[k], k, ranks) for k in range(1, ranks)], axis=1
-        )
-        attention, up_down_all = hold((attention, up_down_all))
-
-        def whole(weight, rest):
-            blocks = []
-            for j in range(chips):
-                blocks += [part(weight, j), rest[j].reshape(-1, width)]
-            return jnp.concatenate(blocks)
-
-        out_half = jnp.swapaxes(gate_out_all[:, :, piece:], 0, 1)
+            [mixture[0]] + [shift(mixture[k], k, ranks) for k in range(1, ranks)], axis=1
+        )
+        attention, gate_all, rest_all = hold((attention, gate_all, rest_all))
+
+        out_half = jnp.swapaxes(rest_all[:, :, piece : piece + out_piece], 0, 1)
         out_half = out_half.reshape(others, heads_rows // cores, width)
         out_other = flip(out_half, "core", 1, cores)
         out_rest = jnp.concatenate(
@@ -479,82 +558,55 @@
         hidden_state = token_f + nn(attention, out_weight)
         normal_mlp, inverse_mlp = normalize(hidden_state)
         normed_mlp = (normal_mlp * gain_mlp).astype(BF)
-        gate = whole(gate_t, gate_out_all[:, :, :piece])
-        up = whole(up_t, up_down_all[:, :, :piece])
-        down = whole(down_weight, up_down_all[:, :, piece:])
-
         normed_pair = jnp.concatenate([normed_mlp, flip(normed_mlp, "core", 1, cores)])
-        gate_proj = nt(normed_pair, gate)
-        up_proj = nt(normed_pair, up)
-        cdf = 0.5 * (1.0 + lax.erf(gate_proj * (1.0 / math.sqrt(2.0))))
-        pdf = jnp.exp(-0.5 * gate_proj * gate_proj) * (1.0 / math.sqrt(2.0 * math.pi))
-        act = gate_proj * cdf
-        hid = (act * up_proj).astype(BF)
-        down_grad = tn(hid, cot_pair).astype(BF).reshape(chips, ranks * piece, width)
-        cot_pair, down_grad = hold((cot_pair, down_grad))
+        gate_w_grad, up_w_grad, down_grad, in_part, in_other, mlp_part, mlp_other = feed(
+            normed_pair, cot_pair, own, gate_all, rest_all, piece, out_piece
+        )
+        gate_sum = Halving(gate_w_grad, chip, chips, False)
+        up_sum = Halving(up_w_grad, chip, chips, True)
+        gate_sum.send()
+        up_sum.send()
+        normed_mlp_grad = in_part + flip(in_other, "core", 1, cores).astype(F32)
+        gain_mlp_part = jnp.sum(normed_mlp_grad * normal_mlp, axis=0)
+        hidden_grad = cot.astype(F32) + norm_back(
+            normed_mlp_grad, normal_mlp, inverse_mlp, gain_mlp
+        )
+        branch_grad = hidden_grad.astype(BF)
+
+        attended_grad = nt(branch_grad, out_weight).astype(BF)
+        attended_came = [
+            shift(attended_grad[:, k * heads_rows : (k + 1) * heads_rows], -k, ranks)
+            for k in range(1, ranks)
+        ]
+        mlp_out = mlp_part + flip(mlp_other, "core", 1, cores).astype(F32)
+        layer_out = (hidden_state + mlp_out).astype(BF)
+
+        def sum_cores(value, axis):
+            kept = lax.dynamic_index_in_dim(value, core, axis, keepdims=False)
+            sent = lax.dynamic_index_in_dim(value, 1 - core, axis, keepdims=False)
+            return (kept.astype(F32) + flip(sent, "core", 1, cores).astype(F32)).astype(BF)
+
+        out_w_grad = tn(attention, branch_grad).astype(BF)
+        out_blocks = out_w_grad.reshape(ranks, cores, chips, out_piece, width)
+        out_blocks = jnp.stack([out_blocks[(ranks - k) % ranks] for k in range(ranks)])
+        out_blocks = jnp.swapaxes(sum_cores(out_blocks, 1), 0, 1)
         cut = ranks * piece // 2
         down_sums = [
             Halving(down_grad[:, :cut], chip, chips, False),
             Halving(down_grad[:, cut:], chip, chips, True),
         ]
-        for s in down_sums:
-            s.send()
-        hid_grad = nt(cot_pair, down)
-        gate_grad = (hid_grad * up_proj * (cdf + gate_proj * pdf)).astype(BF)
-        up_grad = (hid_grad * act).astype(BF)
-        gate_sum = Halving(tn(gate_grad, normed_pair).astype(BF), chip, chips, False)
-        up_sum = Halving(tn(up_grad, normed_pair).astype(BF), chip, chips, True)
-        gate_grad, gate_sum.held, up_sum.held = hold((gate_grad, gate_sum.held, up_sum.held))
-        gate_sum.send()
-        up_sum.send()
-        in_other = nn(gate_grad[own_rows:], gate) + nn(up_grad[own_rows:], up)
-        in_came = flip(in_other.astype(BF), "core", 1, cores)
-        in_part = nn(gate_grad[:own_rows], gate) + nn(up_grad[:own_rows], up)
-        normed_mlp_grad = in_part + in_came.astype(F32)
-        gain_mlp_part = jnp.sum(normed_mlp_grad * normal_mlp, axis=0)
-        hidden_grad = cot.astype(F32) + norm_back(
-            normed_mlp_grad, normal_mlp, inverse_mlp, gain_mlp
-        )
-        branch_grad = tie(hidden_grad.astype(BF), down_sums)
-
-        attended_grad = nt(branch_grad, out_weight).astype(BF)
-        attended_came = [
-            shift(attended_grad[:, k * heads_rows : (k + 1) * heads_rows], -k, ranks)
-            for k in range(1, ranks)
-        ]
-        mlp_part = nn(hid, down)
-        mlp_out = mlp_part[:own_rows] + flip(
-            mlp_part[own_rows:].astype(BF), "core", 1, cores
-        ).astype(F32)
-        layer_out = (hidden_state + mlp_out).astype(BF)
-
-        def sum_cores(value, axis):
-            kept = lax.dynamic_index_in_dim(value, core, axis, keepdims=False)
-            sent = lax.dynamic_index_in_dim(value, 1 - core, axis, keepdims=False)
-            return (kept.astype(F32) + flip(sent, "core", 1, cores).astype(F32)).astype(BF)
-
-        out_w_grad = tn(attention, branch_grad).astype(BF)
-        out_blocks = out_w_grad.reshape(ranks, cores, chips, out_piece, width)
-        out_blocks = jnp.stack([out_blocks[(ranks - k) % ranks] for k in range(ranks)])
-        out_blocks = jnp.swapaxes(sum_cores(out_blocks, 1), 0, 1)
-        down_here = jnp.concatenate(
-            [s.finish().reshape(-1, width) for s in down_sums]
-        )
         attended_rows = jnp.concatenate([attended_grad[:, :heads_rows]] + attended_came)
-        attended_rows, layer_out, out_blocks, down_here = hold(
-            (attended_rows, layer_out, out_blocks, down_here)
-        )
-
-        def sum_ranks(here):
+        attended_rows, layer_out, out_blocks = hold((attended_rows, layer_out, out_blocks))
+
+        def in_rank_order(here):
             rows = here.shape[1]
             flat = here.reshape(ranks * rows, width)
             twice = jnp.concatenate([flat, flat])
-            flat = lax.dynamic_slice_in_dim(twice, (ranks - rank) % ranks * rows, ranks * rows)
-            return lax.psum_scatter(flat, "tensor", scatter_dimension=0, tiled=True)
-
-        down_total = sum_ranks(down_here.reshape(ranks, piece, width))
-        out_sum = Halving(out_blocks, chip, chips, True)
-        out_sum.send()
+            return lax.dynamic_slice_in_dim(twice, (ranks - rank) % ranks * rows, ranks * rows)
+
+        sums = [Halving(out_blocks, chip, chips, True)] + down_sums
+        for s in sums:
+            s.send()
         dq, dk, dv = attend_back(
             by, queries, keys, values, attended_rows, logs, cos_table, sin_table, doc
         )
@@ -570,17 +622,23 @@
         part_rows = normed_attn_part.astype(BF).reshape(ranks, own_rows, width)
         qkv_grad = jnp.stack([tn(normed_rows, g) for g in (dq, dk, dv)]).astype(BF)
         part_rows, qkv_grad, gain_attn_part = hold((part_rows, qkv_grad, gain_attn_part))
-        part_rows = tie(part_rows, [gate_sum, up_sum, out_sum])
-        rest_total = sum_ranks(
+        gate_up_here = in_rank_order(
             jnp.concatenate(
                 [
                     gate_sum.finish().reshape(ranks, piece, width),
                     up_sum.finish().reshape(ranks, piece, width),
-                    out_sum.finish().reshape(ranks, out_piece, width),
                 ],
                 axis=1,
             )
         )
+        gate_up_total = lax.psum_scatter(gate_up_here, "tensor", scatter_dimension=0, tiled=True)
+        tie(gate_up_here, sums)
+        gain_rows = jnp.pad(jnp.stack([gain_attn_part, gain_mlp_part]), ((0, 6), (0, 0))).astype(BF)
+        out_here = sums[0].finish().reshape(ranks, out_piece, width)
+        down_here = jnp.concatenate([s.finish() for s in sums[1:]]).reshape(ranks, piece, width)
+        rest_total = scatter_ranks(
+            [jnp.concatenate([out_here[k], down_here[k], gain_rows]) for k in range(ranks)], ranks
+        ).astype(BF)
         normed_attn_grad = scatter_ranks(part_rows, ranks)
         input_grad = (
             hidden_grad + norm_back(normed_attn_grad, normal_attn, inverse_attn, gain_attn)
@@ -590,21 +648,17 @@
         qkv_blocks = qkv_grad.reshape(3, cores, chips, qkv_rows, heads_rows)
         qkv_blocks = jnp.swapaxes(sum_cores(qkv_blocks, 1), 0, 1)
         qkv_here = Halving(qkv_blocks, chip, chips, False).finish()
-        gains = total_all(
-            jnp.concatenate([gain_attn_part, gain_mlp_part]),
-            (("core", cores), ("chip", chips), ("tensor", ranks)),
-        )
-        qkv_here, gains, input_grad = hold((qkv_here, gains, input_grad))
-        grad_gain_attn, grad_gain_mlp = gains[:width], gains[width:]
         groups = width // heads_rows
         qkv_part = qkv_rows // groups
         qkv_here = qkv_here.reshape(3, groups, qkv_part, heads_rows)
         qkv_here = jnp.concatenate(
             [qkv_here[:, g].reshape(3 * qkv_part, heads_rows) for g in range(groups)], axis=1
         )
-        pieces = jnp.concatenate([rest_total, down_total, qkv_here])
+        pieces = jnp.concatenate([gate_up_total, rest_total, qkv_here])
         every = lax.all_gather(pieces, ("core", "chip"))
         grads = assemble(every, (cores, chips, share, per, piece, out_piece, qkv_part))
+        at = 3 * piece + out_piece
+        grad_gain_attn, grad_gain_mlp = jnp.sum(every[:, at : at + 2].astype(F32), axis=0)
         grad_gateup = jnp.swapaxes(grads[0], 1, 2)
         down_weight_gradient = grads[1]
         output_weight_gradient = grads[2].reshape(heads_rows, width)

time: 465 us -> 398 us (0.86)
  waiting for transfers between devices: 215 us -> 154 us
  Pallas kernels: 36.2 us -> 64.1 us
  matrix products: 25.7 us -> 8.65 us
  local copies, waits for them, and re-layouts: 37.2 us -> 25.3 us
    all_gather x1, waiting for transfers between devices: 44.3 us -> 3.42 us  [on_device(): every = lax.all_gather(pieces, ('core', 'chip'))]
    ppermute x24 -> x19, waiting for transfers between devices: 65.8 us -> 39 us  [flip(): return lax.ppermute(value, axis, [(i, i ^ bit) for i in range(count)])]
    pallas_call x0 -> x1, Pallas kernels: none -> 25.5 us  [feed(): pl.pallas_call(lambda *refs: feed_kernel(sizes, *refs), grid=(chips // gr...]
    ppermute x9, waiting for transfers between devices: 38.2 us -> 24 us  [shift(): lax.ppermute(value, 'tensor', [(i, (i + by) % count) for i in range(count)])]
    ppermute x3 -> x6, waiting for transfers between devices: 20.3 us -> 29.3 us  [scatter_ranks(): up = lax.ppermute(up, 'tensor', [(z, z + 1) for z in range(step)])]
    ppermute x3 -> x6, waiting for transfers between devices: 0.01 us -> 8.84 us  [scatter_ranks(): lax.ppermute(down, 'tensor', [(z, z - 1) for z in range(count - step, cou...]
    slice x5 -> x4, local copies, waits for them, and re-layouts: 6.93 us -> 0.11 us  [the longest x2 0.05 us: on_device(): down_here[k]]
    dot_general x6 -> x1, matrix products: 7.42 us -> 1.06 us  [nn(): return jnp.dot(left, right, preferred_element_type=F32)]
  transfers between devices with their start and end apart: 56 -> 56, of which waited for: 25 -> 30; matrix products, arithmetic and copies ran while one was open for 16% -> 13% of each run, Pallas kernels for 7% -> 8%
where the time goes in v5:
time: 398 us; the launch traced here: 393 us
  waiting for transfers between devices  154 us (39%)
  starting transfers between devices  81.9 us (21%)
  Pallas kernels  64.1 us (16%)
  other arithmetic  42.4 us (11%)
  local copies, waits for them, and re-layouts  25.3 us (6%)
  between operations  16 us (4%)
  matrix products  8.65 us (2%)
    ppermute x19, waiting for transfers between devices, flip(): return lax.ppermute(value, axis, [(i, i ^ bit) for i in range(count)])  39 us
    ppermute x6, waiting for transfers between devices, relay_ranks(): lax.ppermute(downs[-1], 'tensor', [(z, z - 1) for z in range(1, count - s...  36.1 us
    ppermute x6, starting transfers between devices, scatter_ranks(): up = lax.ppermute(up, 'tensor', [(z, z + 1) for z in range(step)])  30.5 us
    ppermute x6, waiting for transfers between devices, scatter_ranks(): up = lax.ppermute(up, 'tensor', [(z, z + 1) for z in range(step)])  29.3 us
    pallas_call x1, Pallas kernels, feed(): pl.pallas_call(lambda *refs: feed_kernel(sizes, *refs), grid=(chips // gr...  25.5 us
    ppermute x9, waiting for transfers between devices, shift(): lax.ppermute(value, 'tensor', [(i, (i + by) % count) for i in range(count)])  24 us
    ppermute x19, starting transfers between devices, flip(): return lax.ppermute(value, axis, [(i, i ^ bit) for i in range(count)])  14.7 us
    pallas_call x1, Pallas kernels, attend_back(): pl.pallas_call(lambda *refs: attend_back_kernel(doc, *refs), grid=(pairs,...  14.6 us
  transfers between devices with their start and end apart: 56, of which 30 were waited for; matrix products, arithmetic and copies ran while one was open for 13% of the time, Pallas kernels for 8%

profile of v5, /device:TPU:0, one launch (start us, length us, event | category | flops | bytes accessed | tf_op | source)
XLA Modules:
  0.0 392.8 jit_solution(13190878753359277824)
XLA Ops:
  10.3 5.0 %collective-permute-start.1 = (bf16[88,1024]{1,0:T(8,128)(2,1)}, bf16[88,1024]{1,0:T(8,128)(2,1)}, u32[]{:S(2)}, u32[]{:S(2)}) collective-permute-start(bf16[88,1024]{1,0:T(8,128)(2,1)} %get-tuple-element.130), channel_id=1, source_target_pairs={{0,3},{1,0},{2,1},{3,2},{4,7},{5,4},{6,5},{7,6},{8,11},{9,8},{10,9... | collective-permute-start | bytes 540680 | tf_op jit(solution)/shard_map/ppermute | solution.py:387
  20.6 10.3 %collective-permute-done.2 = bf16[88,1024]{1,0:T(8,128)(2,1)} collective-permute-done((bf16[88,1024]{1,0:T(8,128)(2,1)}, bf16[88,1024]{1,0:T(8,128)(2,1)}, u32[]{:S(2)}, u32[]{:S(2)}) %collective-permute-start.2) | collective-permute-done | bytes 180256 | tf_op jit(solution)/shard_map/ppermute | solution.py:387
  37.0 7.5 %collective-permute-done.5 = bf16[208,1024]{1,0:T(8,128)(2,1)S(1)} collective-permute-done((bf16[208,1024]{1,0:T(8,128)(2,1)}, bf16[208,1024]{1,0:T(8,128)(2,1)S(1)}, u32[]{:S(2)}, u32[]{:S(2)}) %collective-permute-start.5) | collective-permute-done | bytes 426016 | tf_op jit(solution)/shard_map/ppermute | solution.py:397
  51.7 9.6 %collective-permute-done.8 = bf16[208,1024]{1,0:T(8,128)(2,1)S(1)} collective-permute-done((bf16[208,1024]{1,0:T(8,128)(2,1)S(1)}, bf16[208,1024]{1,0:T(8,128)(2,1)S(1)}, u32[]{:S(2)}, u32[]{:S(2)}) %collective-permute-start.8) | collective-permute-done | bytes 426016 | tf_op jit(solution)/shard_map/ppermute | solution.py:398
  63.2 9.3 %collective-permute-done.9 = bf16[208,1024]{1,0:T(8,128)(2,1)S(1)} collective-permute-done((bf16[208,1024]{1,0:T(8,128)(2,1)S(1)}, bf16[208,1024]{1,0:T(8,128)(2,1)S(1)}, u32[]{:S(2)}, u32[]{:S(2)}) %collective-permute-start.9) | collective-permute-done | bytes 426016 | tf_op jit(solution)/shard_map/ppermute | solution.py:398
  77.4 6.2 %collective-permute-done.10.refs_2_ = bf16[256,1024]{1,0:T(8,128)(2,1)S(1)} collective-permute-done((bf16[256,1024]{1,0:T(8,128)(2,1)S(1)}, bf16[256,1024]{1,0:T(8,128)(2,1)S(1)}, u32[]{:S(2)}, u32[]{:S(2)}) %collective-permute-start.10) | collective-permute-done | bytes 524320 | tf_op jit(solution)/shard_map/ppermute | solution.py:397
  93.7 5.9 %collective-permute-done.14.refs_6_ = bf16[256,1024]{1,0:T(8,128)(2,1)} collective-permute-done((bf16[256,1024]{1,0:T(8,128)(2,1)S(1)}, bf16[256,1024]{1,0:T(8,128)(2,1)}, u32[]{:S(2)}, u32[]{:S(2)}) %collective-permute-start.14) | collective-permute-done | bytes 524320 | tf_op jit(solution)/shard_map/ppermute | solution.py:398
  106.4 4.6 %collective-permute-done.15.refs_7_ = bf16[256,1024]{1,0:T(8,128)(2,1)} collective-permute-done((bf16[256,1024]{1,0:T(8,128)(2,1)}, bf16[256,1024]{1,0:T(8,128)(2,1)}, u32[]{:S(2)}, u32[]{:S(2)}) %collective-permute-start.15) | collective-permute-done | bytes 524320 | tf_op jit(solution)/shard_map/ppermute | solution.py:398
  111.0 4.7 %shard_map.152 = (bf16[1024,1024]{1,0:T(8,128)(2,1)S(1)}, bf16[1024,256]{1,0:T(8,128)(2,1)S(1)}, bf16[1024,256]{1,0:T(8,128)(2,1)S(1)}, bf16[1024,256]{1,0:T(8,128)(2,1)S(1)}) custom-call(s32[1]{0:T(128)} %bitcast.4.refs_0_, bf16[256,1024]{1,0:T(8,128)(2,1)S(1)} %fusion.18.refs_1_, bf16[256,1024]{1,0:T(8,128)(2,1)S(1)} %collective-permute-done.10.refs_2_, ...), custom_call_target="tpu_custom_call" | custom-call | flops 1610612736 | bytes 9437184 | tf_op jit(solution)/shard_map/pallas_call | solution.py:94
  117.2 11.5 %shard_map.153 = (bf16[1024,256]{1,0:T(8,128)(2,1)S(1)}, f32[2,2,896]{2,1,0:T(2,128)S(1)}, bf16[1024,256]{1,0:T(8,128)(2,1)S(1)}, bf16[1024,256]{1,0:T(8,128)(2,1)S(1)}, bf16[1024,256]{1,0:T(8,128)(2,1)S(1)}) custom-call(s32[1]{0:T(128)} %bitcast.3.refs_0_, bf16[1024,256]{1,0:T(8,128)(2,1)S(1)} %get-tuple-element.60.refs_1_, ...), custom_call_target="tpu_custom_call" | custom-call | flops 1644167168 | bytes 2097152 | tf_op jit(solution)/shard_map/pallas_call | solution.py:161
  151.3 25.5 %shard_map.154 = (bf16[4,352,1024]{2,1,0:T(8,128)(2,1)}, bf16[4,352,1024]{2,1,0:T(8,128)(2,1)}, bf16[4,352,1024]{2,1,0:T(8,128)(2,1)}, f32[256,1024]{1,0:T(8,128...) custom-call(bf16[512,1024]{1,0:T(8,128)(2,1)} %pad_maximum_fusion.7.refs_0_, ...), custom_call_target="tpu_custom_call" | custom-call | flops 13287555072 | bytes 26214400 | tf_op jit(solution)/shard_map/pallas_call | solution.py:308
  199.6 7.3 %collective-permute-done.23 = bf16[256,256]{1,0:T(8,128)(2,1)S(1)} collective-permute-done((bf16[256,256]{1,0:T(8,128)(2,1)S(1)}, bf16[256,256]{1,0:T(8,128)(2,1)S(1)}, u32[]{:S(2)}, u32[]{:S(2)}) %collective-permute-start.23) | collective-permute-done | bytes 131104 | tf_op jit(solution)/shard_map/ppermute | solution.py:387
  211.0 14.6 %shard_map.155 = (bf16[1024,256]{1,0:T(8,128)(2,1)S(1)}, bf16[1024,256]{1,0:T(8,128)(2,1)S(1)}, bf16[1024,256]{1,0:T(8,128)(2,1)S(1)}) custom-call(s32[1]{0:T(128)} %bitcast.3.refs_0_, bf16[1024,256]{1,0:T(8,128)(2,1)S(1)} %copy-done.10, bf16[1024,256]{1,0:T(8,128)(2,1)S(1)} %copy-done.12, bf16[1024,256]{1,0:T(8,128)(2,1)S(1)} %copy-done.14, ...), custom_call_target="tpu_custom_call" | custom-call | bytes 1048576 | tf_op jit(solution)/shard_map/pallas_call | solution.py:229
  247.1 16.8 %collective-permute-done.35 = bf16[352,1024]{1,0:T(8,128)(2,1)S(1)} collective-permute-done((bf16[352,1024]{1,0:T(8,128)(2,1)S(1)}, bf16[352,1024]{1,0:T(8,128)(2,1)S(1)}, u32[]{:S(2)}, u32[]{:S(2)}) %collective-permute-start.35) | collective-permute-done | bytes 720928 | tf_op jit(solution)/shard_map/ppermute | solution.py:391
  267.7 5.3 %collective-permute-done.37 = bf16[2,128,1024]{2,1,0:T(8,128)(2,1)} collective-permute-done((bf16[2,128,1024]{2,1,0:T(8,128)(2,1)}, bf16[2,128,1024]{2,1,0:T(8,128)(2,1)}, u32[]{:S(2)}, u32[]{:S(2)}) %collective-permute-start.37) | collective-permute-done | bytes 524320 | tf_op jit(solution)/shard_map/ppermute | solution.py:391
  290.9 5.0 %collective-permute-start.43 = (bf16[128,1024]{1,0:T(8,128)(2,1)S(1)}, bf16[128,1024]{1,0:T(8,128)(2,1)S(1)}, u32[]{:S(2)}, u32[]{:S(2)}) collective-permute-start(bf16[128,1024]{1,0:T(8,128)(2,1)S(1)} %get-tuple-element.171), channel_id=1, source_target_pairs={{0,1},{4,5},{8,9},{12,13},{16,17},{20,21},{24,25},{28,29}} | collective-permute-start | bytes 786440 | tf_op jit(solution)/shard_map/ppermute | solution.py:405
  297.4 7.3 %collective-permute-done.43 = bf16[128,1024]{1,0:T(8,128)(2,1)S(1)} collective-permute-done((bf16[128,1024]{1,0:T(8,128)(2,1)S(1)}, bf16[128,1024]{1,0:T(8,128)(2,1)S(1)}, u32[]{:S(2)}, u32[]{:S(2)}) %collective-permute-start.43) | collective-permute-done | bytes 262176 | tf_op jit(solution)/shard_map/ppermute | solution.py:405
  314.2 8.1 %collective-permute-start.45 = (bf16[128,1024]{1,0:T(8,128)(2,1)S(1)}, bf16[128,1024]{1,0:T(8,128)(2,1)S(1)}, u32[]{:S(2)}, u32[]{:S(2)}) collective-permute-start(bf16[128,1024]{1,0:T(8,128)(2,1)S(1)} %get-tuple-element.169), channel_id=1, source_target_pairs={{0,1},{1,2},{2,3},{4,5},{5,6},{6,7},{8,9},{9,10},{10,11},{12,13},{... | collective-permute-start | bytes 786440 | tf_op jit(solution)/shard_map/ppermute | solution.py:405
  335.4 6.5 %collective-permute-done.29 = bf16[256,1024]{1,0:T(8,128)(2,1)S(1)} collective-permute-done((bf16[256,1024]{1,0:T(8,128)(2,1)S(1)}, bf16[256,1024]{1,0:T(8,128)(2,1)S(1)}, u32[]{:S(2)}, u32[]{:S(2)}) %collective-permute-start.29) | collective-permute-done | bytes 524320 | tf_op jit(solution)/shard_map/ppermute | solution.py:405
  342.3 4.5 %collective-permute-start.30 = (bf16[256,1024]{1,0:T(8,128)(2,1)S(1)}, bf16[256,1024]{1,0:T(8,128)(2,1)S(1)}, u32[]{:S(2)}, u32[]{:S(2)}) collective-permute-start(bf16[256,1024]{1,0:T(8,128)(2,1)S(1)} %get-tuple-element.115), channel_id=1, source_target_pairs={{0,1},{1,2},{4,5},{5,6},{8,9},{9,10},{12,13},{13,14},{16,17},{17,1... | collective-permute-start | bytes 1572872 | tf_op jit(solution)/shard_map/ppermute | solution.py:405
  347.7 5.8 %collective-permute-done.30 = bf16[256,1024]{1,0:T(8,128)(2,1)S(1)} collective-permute-done((bf16[256,1024]{1,0:T(8,128)(2,1)S(1)}, bf16[256,1024]{1,0:T(8,128)(2,1)S(1)}, u32[]{:S(2)}, u32[]{:S(2)}) %collective-permute-start.30) | collective-permute-done | bytes 524320 | tf_op jit(solution)/shard_map/ppermute | solution.py:405
  353.8 6.5 %collective-permute-start.31 = (bf16[256,1024]{1,0:T(8,128)(2,1)S(1)}, bf16[256,1024]{1,0:T(8,128)(2,1)S(1)}, u32[]{:S(2)}, u32[]{:S(2)}) collective-permute-start(bf16[256,1024]{1,0:T(8,128)(2,1)S(1)} %get-tuple-element.113), channel_id=1, source_target_pairs={{0,1},{1,2},{2,3},{4,5},{5,6},{6,7},{8,9},{9,10},{10,11},{12,13},{... | collective-permute-start | bytes 1572872 | tf_op jit(solution)/shard_map/ppermute | solution.py:405
  361.6 5.3 %collective-permute-done.31 = bf16[256,1024]{1,0:T(8,128)(2,1)S(1)} collective-permute-done((bf16[256,1024]{1,0:T(8,128)(2,1)S(1)}, bf16[256,1024]{1,0:T(8,128)(2,1)S(1)}, u32[]{:S(2)}, u32[]{:S(2)}) %collective-permute-start.31) | collective-permute-done | bytes 524320 | tf_op jit(solution)/shard_map/ppermute | solution.py:405
  376.7 7.8 %shard_map.156 = (f32[2,656,1024]{2,1,0:T(8,128)}, f32[656,1024]{1,0:T(8,128)}, f32[8,32,1024]{2,1,0:T(8,128)}, f32[3,8,4,32,256]{4,3,2,1,0:T(8,128)}) custom-call(bf16[8,400,1024]{2,1,0:T(8,128)(2,1)} %bitcast.249), custom_call_target="tpu_custom_call" | custom-call | bytes 18874368 | tf_op jit(solution)/shard_map/pallas_call | solution.py:364
  (316 shorter events, 175.8 us)
Async XLA Ops:
  7.2 132.1 %all-gather.7.cloned.1.call-start = ((), (), s32[]{:S(2)}) async-start(), calls=%async_computation.2 | async-start | bytes 2703360 | tf_op jit(solution)/shard_map/all_gather | solution.py:499
  15.3 15.6 %collective-permute-start.2 = (bf16[88,1024]{1,0:T(8,128)(2,1)}, bf16[88,1024]{1,0:T(8,128)(2,1)}, u32[]{:S(2)}, u32[]{:S(2)}) collective-permute-start(bf16[88,1024]{1,0:T(8,128)(2,1)} %get-tuple-element.130), channel_id=1, source_target_pairs={{0,2},{1,3},{2,0},{3,1},{4,6},{5,7},{6,4},{7,5},{8,10},{9,11},{10,... | collective-permute-start | bytes 540680 | tf_op jit(solution)/shard_map/ppermute | solution.py:387
  15.3 15.6 %collective-permute-start.3 = (bf16[88,1024]{1,0:T(8,128)(2,1)}, bf16[88,1024]{1,0:T(8,128)(2,1)}, u32[]{:S(2)}, u32[]{:S(2)}) collective-permute-start(bf16[88,1024]{1,0:T(8,128)(2,1)} %get-tuple-element.130), channel_id=1, source_target_pairs={{0,1},{1,2},{2,3},{3,0},{4,5},{5,6},{6,7},{7,4},{8,9},{9,10},{10,1... | collective-permute-start | bytes 540680 | tf_op jit(solution)/shard_map/ppermute | solution.py:387
  32.9 106.4 %all-gather.9.cloned.1.call-start = ((), (), s32[]{:S(2)}) async-start(), calls=%async_computation.3 | async-start | bytes 6389760 | tf_op jit(solution)/shard_map/all_gather | solution.py:503
  35.7 13.5 %collective-permute-start.4 = (bf16[208,1024]{1,0:T(8,128)(2,1)}, bf16[208,1024]{1,0:T(8,128)(2,1)S(1)}, u32[]{:S(2)}, u32[]{:S(2)}) collective-permute-start(bf16[208,1024]{1,0:T(8,128)(2,1)} %pad_maximum_fusion.16), channel_id=1, source_target_pairs={{1,0},{2,1},{3,2},{5,4},{6,5},{7,6},{9,8},{10,9},{11,10},{13,12},{... | collective-permute-start | bytes 1277960 | tf_op jit(solution)/shard_map/ppermute | solution.py:398
  73.8 256.9 %reduce-scatter.2.cloned.1.call-start = ((), (), s32[]{:S(2)}) async-start(), calls=%async_computation.1 | async-start | bytes 1802240 | tf_op jit(solution)/shard_map/reduce_scatter | solution.py:634
  75.4 12.3 %collective-permute-start.13 = (bf16[256,1024]{1,0:T(8,128)(2,1)S(1)}, bf16[256,1024]{1,0:T(8,128)(2,1)S(1)}, u32[]{:S(2)}, u32[]{:S(2)}) collective-permute-start(bf16[256,1024]{1,0:T(8,128)(2,1)S(1)} %fusion.18.refs_1_), channel_id=1, source_target_pairs={{1,0},{2,1},{3,2},{5,4},{6,5},{7,6},{9,8},{10,9},{11,10},{13,12},{... | collective-permute-start | bytes 1572872 | tf_op jit(solution)/shard_map/ppermute | solution.py:398
  76.7 27.1 %collective-permute-start = (bf16[256,1024]{1,0:T(8,128)(2,1)}, bf16[256,1024]{1,0:T(8,128)(2,1)}, u32[]{:S(2)}, u32[]{:S(2)}) collective-permute-start(bf16[256,1024]{1,0:T(8,128)(2,1)} %bitcast), channel_id=1, source_target_pairs={{0,4},{4,0},{1,5},{5,1},{2,6},{6,2},{3,7},{7,3},{8,12},{12,8},{9,1... | collective-permute-start | bytes 1572872 | tf_op jit(solution)/shard_map/ppermute | solution.py:391
  92.0 14.4 %collective-permute-start.12 = (bf16[256,1024]{1,0:T(8,128)(2,1)}, bf16[256,1024]{1,0:T(8,128)(2,1)}, u32[]{:S(2)}, u32[]{:S(2)}) collective-permute-start(bf16[256,1024]{1,0:T(8,128)(2,1)} %collective-permute-done.11.refs_3_), channel_id=1, source_target_pairs={{2,3},{6,7},{10,11},{14,15},{18,19},{22,23},{26,27},{30,31}} | collective-permute-start | bytes 1572872 | tf_op jit(solution)/shard_map/ppermute | solution.py:397
  180.2 48.5 %collective-permute-start.27 = (bf16[2,352,1024]{2,1,0:T(8,128)(2,1)}, bf16[2,352,1024]{2,1,0:T(8,128)(2,1)}, u32[]{:S(2)}, u32[]{:S(2)}) collective-permute-start(bf16[2,352,1024]{2,1,0:T(8,128)(2,1)} %dynamic-slice_bitcast_fusion.1), channel_id=1, source_target_pairs={{0,8},{8,0},{16,24},{24,16},{1,9},{9,1},{17,25},{25,17},{2,10},{10... | collective-permute-start | bytes 4325384 | tf_op jit(solution)/shard_map/ppermute | solution.py:391
  188.4 20.7 %collective-permute-start.26 = (bf16[4,4,32,1024]{3,2,1,0:T(8,128)(2,1)S(1)}, bf16[4,4,32,1024]{3,2,1,0:T(8,128)(2,1)S(1)}, u32[]{:S(2)}, u32[]{:S(2)}) collective-permute-start(bf16[4,4,32,1024]{3,2,1,0:T(8,128)(2,1)S(1)} %dynamic-slice_bitcast_fusion.2), channel_id=1, source_target_pairs={{0,4},{4,0},{1,5},{5,1},{2,6},{6,2},{3,7},{7,3},{8,12},{12,8},{9,1... | collective-permute-start | bytes 3145736 | tf_op jit(solution)/shard_map/ppermute | solution.py:391
  194.3 12.6 %collective-permute-start.23 = (bf16[256,256]{1,0:T(8,128)(2,1)S(1)}, bf16[256,256]{1,0:T(8,128)(2,1)S(1)}, u32[]{:S(2)}, u32[]{:S(2)}) collective-permute-start(bf16[256,256]{1,0:T(8,128)(2,1)S(1)} %get-tuple-element.149), channel_id=1, source_target_pairs={{0,2},{1,3},{2,0},{3,1},{4,6},{5,7},{6,4},{7,5},{8,10},{9,11},{10,... | collective-permute-start | bytes 393224 | tf_op jit(solution)/shard_map/ppermute | solution.py:387
  198.2 34.8 %collective-permute-start.28 = (bf16[2,352,1024]{2,1,0:T(8,128)(2,1)}, bf16[2,352,1024]{2,1,0:T(8,128)(2,1)}, u32[]{:S(2)}, u32[]{:S(2)}) collective-permute-start(bf16[2,352,1024]{2,1,0:T(8,128)(2,1)} %dynamic-slice_bitcast_fusion), channel_id=1, source_target_pairs={{0,16},{8,24},{16,0},{24,8},{1,17},{9,25},{17,1},{25,9},{2,18},{10... | collective-permute-start | bytes 4325384 | tf_op jit(solution)/shard_map/ppermute | solution.py:391
  206.9 60.7 %collective-permute-start.38 = (bf16[2,176,1024]{2,1,0:T(8,128)(2,1)}, bf16[2,176,1024]{2,1,0:T(8,128)(2,1)}, u32[]{:S(2)}, u32[]{:S(2)}) collective-permute-start(bf16[2,176,1024]{2,1,0:T(8,128)(2,1)} %dynamic-slice_bitcast_fusion.4), channel_id=1, source_target_pairs={{0,8},{8,0},{16,24},{24,16},{1,9},{9,1},{17,25},{25,17},{2,10},{10... | collective-permute-start | bytes 2162696 | tf_op jit(solution)/shard_map/ppermute | solution.py:391
  207.5 60.2 %collective-permute-start.39 = (bf16[2,176,1024]{2,1,0:T(8,128)(2,1)}, bf16[2,176,1024]{2,1,0:T(8,128)(2,1)}, u32[]{:S(2)}, u32[]{:S(2)}) collective-permute-start(bf16[2,176,1024]{2,1,0:T(8,128)(2,1)} %dynamic-slice_bitcast_fusion.3), channel_id=1, source_target_pairs={{0,16},{8,24},{16,0},{24,8},{1,17},{9,25},{17,1},{25,9},{2,18},{10... | collective-permute-start | bytes 2162696 | tf_op jit(solution)/shard_map/ppermute | solution.py:391
  235.2 28.6 %collective-permute-start.35 = (bf16[352,1024]{1,0:T(8,128)(2,1)S(1)}, bf16[352,1024]{1,0:T(8,128)(2,1)S(1)}, u32[]{:S(2)}, u32[]{:S(2)}) collective-permute-start(bf16[352,1024]{1,0:T(8,128)(2,1)S(1)} %dynamic-slice_bitcast_fusion.6), channel_id=1, source_target_pairs={{0,16},{8,24},{16,0},{24,8},{1,17},{9,25},{17,1},{25,9},{2,18},{10... | collective-permute-start | bytes 2162696 | tf_op jit(solution)/shard_map/ppermute | solution.py:391
  238.8 25.3 %collective-permute-start.36 = (bf16[352,1024]{1,0:T(8,128)(2,1)S(1)}, bf16[352,1024]{1,0:T(8,128)(2,1)S(1)}, u32[]{:S(2)}, u32[]{:S(2)}) collective-permute-start(bf16[352,1024]{1,0:T(8,128)(2,1)S(1)} %dynamic-slice_bitcast_fusion.5), channel_id=1, source_target_pairs={{0,8},{8,0},{16,24},{24,16},{1,9},{9,1},{17,25},{25,17},{2,10},{10... | collective-permute-start | bytes 2162696 | tf_op jit(solution)/shard_map/ppermute | solution.py:391
  241.3 31.6 %collective-permute-start.37 = (bf16[2,128,1024]{2,1,0:T(8,128)(2,1)}, bf16[2,128,1024]{2,1,0:T(8,128)(2,1)}, u32[]{:S(2)}, u32[]{:S(2)}) collective-permute-start(bf16[2,128,1024]{2,1,0:T(8,128)(2,1)} %dynamic-slice_bitcast_fusion.7), channel_id=1, source_target_pairs={{0,16},{8,24},{16,0},{24,8},{1,17},{9,25},{17,1},{25,9},{2,18},{10... | collective-permute-start | bytes 1572872 | tf_op jit(solution)/shard_map/ppermute | solution.py:391
  263.8 16.9 %collective-permute-start.49 = (bf16[3,4,128,256]{3,2,0,1:T(8,128)(2,1)}, bf16[3,4,128,256]{3,2,0,1:T(8,128)(2,1)}, u32[]{:S(2)}, u32[]{:S(2)}) collective-permute-start(bf16[3,4,128,256]{3,2,0,1:T(8,128)(2,1)} %bitcast.243), channel_id=1, source_target_pairs={{0,4},{4,0},{1,5},{5,1},{2,6},{6,2},{3,7},{7,3},{8,12},{12,8},{9,1... | collective-permute-start | bytes 2359304 | tf_op jit(solution)/shard_map/ppermute | solution.py:391
  267.6 109.2 %all-gather.11.cloned.1.call-start = ((), (), s32[]{:S(2)}) async-start(), calls=%async_computation.4 | async-start | bytes 7372800 | tf_op jit(solution)/shard_map/all_gather | solution.py:658
  290.9 13.8 %collective-permute-start.43 = (bf16[128,1024]{1,0:T(8,128)(2,1)S(1)}, bf16[128,1024]{1,0:T(8,128)(2,1)S(1)}, u32[]{:S(2)}, u32[]{:S(2)}) collective-permute-start(bf16[128,1024]{1,0:T(8,128)(2,1)S(1)} %get-tuple-element.171), channel_id=1, source_target_pairs={{0,1},{4,5},{8,9},{12,13},{16,17},{20,21},{24,25},{28,29}} | collective-permute-start | bytes 786440 | tf_op jit(solution)/shard_map/ppermute | solution.py:405
  296.7 13.5 %collective-permute-start.50 = (bf16[2,384,256]{2,1,0:T(8,128)(2,1)S(1)}, bf16[2,384,256]{2,1,0:T(8,128)(2,1)S(1)}, u32[]{:S(2)}, u32[]{:S(2)}) collective-permute-start(bf16[2,384,256]{2,1,0:T(8,128)(2,1)S(1)} %dynamic-slice_bitcast_fusion.8), channel_id=1, source_target_pairs={{0,8},{8,0},{16,24},{24,16},{1,9},{9,1},{17,25},{25,17},{2,10},{10... | collective-permute-start | bytes 1179656 | tf_op jit(solution)/shard_map/ppermute | solution.py:391
  310.3 13.3 %collective-permute-start.51 = (bf16[384,256]{1,0:T(8,128)(2,1)S(1)}, bf16[384,256]{1,0:T(8,128)(2,1)S(1)}, u32[]{:S(2)}, u32[]{:S(2)}) collective-permute-start(bf16[384,256]{1,0:T(8,128)(2,1)S(1)} %dynamic-slice_bitcast_fusion.12), channel_id=1, source_target_pairs={{0,16},{8,24},{16,0},{24,8},{1,17},{9,25},{17,1},{25,9},{2,18},{10... | collective-permute-start | bytes 589832 | tf_op jit(solution)/shard_map/ppermute | solution.py:391
  353.8 13.1 %collective-permute-start.31 = (bf16[256,1024]{1,0:T(8,128)(2,1)S(1)}, bf16[256,1024]{1,0:T(8,128)(2,1)S(1)}, u32[]{:S(2)}, u32[]{:S(2)}) collective-permute-start(bf16[256,1024]{1,0:T(8,128)(2,1)S(1)} %get-tuple-element.113), channel_id=1, source_target_pairs={{0,1},{1,2},{2,3},{4,5},{5,6},{6,7},{8,9},{9,10},{10,11},{12,13},{... | collective-permute-start | bytes 1572872 | tf_op jit(solution)/shard_map/ppermute | solution.py:405
  (84 other events, 646.8 us)
Sparse Core Ops, SparseCore 0:
  33.0 36.2 all-gather.6
  74.0 58.5 all-gather.8
  267.7 40.4 reduce-scatter.1
  332.8 43.8 all-gather.10

commit v6 on v5

--- a/solution.py
+++ b/solution.py
@@ -245,7 +245,7 @@
 
 def feed_kernel(
     sizes, n_ref, c_ref, own_ref, gate_ref, rest_ref,
-    dg_ref, du_ref, dd_ref, in_ref, in_other_ref, out_ref, out_other_ref, in_held, out_held,
+    dgu_ref, dd_ref, in_ref, in_other_ref, out_ref, out_other_ref, in_held, out_held,
 ):
     piece, out_piece, ranks, group, steps = sizes
     step = pl.program_id(0)
@@ -271,8 +271,12 @@
     hid = (act * up_proj).astype(BF)
     gate_grad = (hid_grad * up_proj * (cdf + gate_proj * pdf)).astype(BF)
     up_grad = (hid_grad * act).astype(BF)
-    for ref, left, right in ((dg_ref, gate_grad, normed), (du_ref, up_grad, normed), (dd_ref, hid, cot)):
-        ref[...] = tn(left, right).astype(BF).reshape(ref.shape)
+    hidden = ranks * piece
+    dgu_ref[0, :hidden] = tn(gate_grad, normed).astype(BF)
+    dgu_ref[0, hidden:] = tn(up_grad, normed).astype(BF)
+    down_grad = tn(hid, cot)
+    for k in range(ranks):
+        dd_ref[k, 0] = down_grad[k * piece : (k + 1) * piece].astype(BF)
     in_part = nn(gate_grad, gate) + nn(up_grad, up)
     out_part = nn(hid, down)
 
@@ -302,7 +306,10 @@
     half = rows // 2
     group = 1
     same = pl.BlockSpec((rows, width), lambda i: (0, 0))
-    grad = pl.BlockSpec((group, hidden, width), lambda i: (i, 0, 0))
+    grads = [
+        pl.BlockSpec((1, 2 * hidden, width), lambda i: (i, 0, 0)),
+        pl.BlockSpec((others + 1, 1, piece, width), lambda i: (0, i, 0, 0)),
+    ]
     kept = pl.BlockSpec((half, width), lambda i: (0, 0))
     sizes = (piece, out_piece, others + 1, group, chips // group)
     return pl.pallas_call(
@@ -315,8 +322,11 @@
             pl.BlockSpec((group, others, piece, width), lambda i: (i, 0, 0, 0)),
             pl.BlockSpec((group, others, rest_rows, width), lambda i: (i, 0, 0, 0)),
         ],
-        out_specs=[grad] * 3 + [kept] * 4,
-        out_shape=[jax.ShapeDtypeStruct((chips, hidden, width), BF)] * 3
+        out_specs=grads + [kept] * 4,
+        out_shape=[
+            jax.ShapeDtypeStruct((chips, 2 * hidden, width), BF),
+            jax.ShapeDtypeStruct((others + 1, chips, piece, width), BF),
+        ]
         + [
             jax.ShapeDtypeStruct((half, width), F32),
             jax.ShapeDtypeStruct((half, width), BF),
@@ -336,7 +346,7 @@
 def assemble_kernel(sizes, in_ref, gu_ref, d_ref, o_ref, qkv_ref, held):
     cores, chips, share, per, piece, out_piece, qkv_part = sizes
     hidden = cores * share
-    firsts = (0, piece, 2 * piece + out_piece)
+    firsts = (0, piece, 2 * piece + out_piece + 8)
     for m, first in enumerate(firsts):
         for device in range(cores * chips):
             at = device // chips * share + device % chips * per
@@ -399,15 +409,32 @@
     return ups[1:], downs[1:]
 
 
-def scatter_ranks(blocks, count):
-    up, down = blocks[count - 1], blocks[1]
-    for step in range(1, count):
-        up = lax.ppermute(up, "tensor", [(z, z + 1) for z in range(step)])
-        down = lax.ppermute(down, "tensor", [(z, z - 1) for z in range(count - step, count)])
-        if step < count - 1:
-            up = (up.astype(F32) + blocks[count - 1 - step].astype(F32)).astype(BF)
-            down = (down.astype(F32) + blocks[step + 1].astype(F32)).astype(BF)
-    return blocks[0].astype(F32) + up.astype(F32) + down.astype(F32)
+class LineSum:
+    def __init__(self, blocks, count):
+        self.blocks, self.count, self.step, self.came = blocks, count, 0, None
+        self.up, self.down = blocks[count - 1], blocks[1]
+
+    def send(self):
+        self.step += 1
+        up = [(z, z + 1) for z in range(self.step)]
+        down = [(z, z - 1) for z in range(self.count - self.step, self.count)]
+        self.came = (lax.ppermute(self.up, "tensor", up), lax.ppermute(self.down, "tensor", down))
+
+    def take(self):
+        self.up, self.down = self.came
+        self.came = None
+        if self.step < self.count - 1:
+            up, down = self.blocks[self.count - 1 - self.step], self.blocks[self.step + 1]
+            self.up = (self.up.astype(F32) + up.astype(F32)).astype(BF)
+            self.down = (self.down.astype(F32) + down.astype(F32)).astype(BF)
+
+    def finish(self):
+        if self.came is not None:
+            self.take()
+        while self.step < self.count - 1:
+            self.send()
+            self.take()
+        return self.blocks[0].astype(F32) + self.up.astype(F32) + self.down.astype(F32)
 
 
 class Halving:
@@ -559,13 +586,16 @@
         normal_mlp, inverse_mlp = normalize(hidden_state)
         normed_mlp = (normal_mlp * gain_mlp).astype(BF)
         normed_pair = jnp.concatenate([normed_mlp, flip(normed_mlp, "core", 1, cores)])
-        gate_w_grad, up_w_grad, down_grad, in_part, in_other, mlp_part, mlp_other = feed(
+        gate_up_grad, down_grad, in_part, in_other, mlp_part, mlp_other = feed(
             normed_pair, cot_pair, own, gate_all, rest_all, piece, out_piece
         )
-        gate_sum = Halving(gate_w_grad, chip, chips, False)
-        up_sum = Halving(up_w_grad, chip, chips, True)
-        gate_sum.send()
-        up_sum.send()
+        gate_up_here = hold(
+            lax.psum_scatter(
+                gate_up_grad.reshape(-1, width), "chip", scatter_dimension=0, tiled=True
+            )
+        )
+        down_sum = LineSum(down_grad.reshape(ranks, chips * piece, width), ranks)
+        down_sum.send()
         normed_mlp_grad = in_part + flip(in_other, "core", 1, cores).astype(F32)
         gain_mlp_part = jnp.sum(normed_mlp_grad * normal_mlp, axis=0)
         hidden_grad = cot.astype(F32) + norm_back(
@@ -574,6 +604,18 @@
         branch_grad = hidden_grad.astype(BF)
 
         attended_grad = nt(branch_grad, out_weight).astype(BF)
+        def sum_cores(value, axis):
+            kept = lax.dynamic_index_in_dim(value, core, axis, keepdims=False)
+            sent = lax.dynamic_index_in_dim(value, 1 - core, axis, keepdims=False)
+            return (kept.astype(F32) + flip(sent, "core", 1, cores).astype(F32)).astype(BF)
+
+        out_w_grad = tn(attention, branch_grad).astype(BF)
+        out_blocks = out_w_grad.reshape(ranks, cores, chips, out_piece, width)
+        out_blocks = jnp.stack([out_blocks[(ranks - k) % ranks] for k in range(ranks)])
+        out_blocks = jnp.swapaxes(sum_cores(out_blocks, 1), 0, 1)
+        attended_grad, out_blocks = hold((attended_grad, out_blocks))
+        out_sum = Halving(out_blocks, chip, chips, True)
+        out_sum.send()
         attended_came = [
             shift(attended_grad[:, k * heads_rows : (k + 1) * heads_rows], -k, ranks)
             for k in range(1, ranks)
@@ -581,22 +623,8 @@
         mlp_out = mlp_part + flip(mlp_other, "core", 1, cores).astype(F32)
         layer_out = (hidden_state + mlp_out).astype(BF)
 
-        def sum_cores(value, axis):
-            kept = lax.dynamic_index_in_dim(value, core, axis, keepdims=False)
-            sent = lax.dynamic_index_in_dim(value, 1 - core, axis, keepdims=False)
-            return (kept.astype(F32) + flip(sent, "core", 1, cores).astype(F32)).astype(BF)
-
-        out_w_grad = tn(attention, branch_grad).astype(BF)
-        out_blocks = out_w_grad.reshape(ranks, cores, chips, out_piece, width)
-        out_blocks = jnp.stack([out_blocks[(ranks - k) % ranks] for k in range(ranks)])
-        out_blocks = jnp.swapaxes(sum_cores(out_blocks, 1), 0, 1)
-        cut = ranks * piece // 2
-        down_sums = [
-            Halving(down_grad[:, :cut], chip, chips, False),
-            Halving(down_grad[:, cut:], chip, chips, True),
-        ]
         attended_rows = jnp.concatenate([attended_grad[:, :heads_rows]] + attended_came)
-        attended_rows, layer_out, out_blocks = hold((attended_rows, layer_out, out_blocks))
+        attended_rows, layer_out = hold((attended_rows, layer_out))
 
         def in_rank_order(here):
             rows = here.shape[1]
@@ -604,15 +632,21 @@
             twice = jnp.concatenate([flat, flat])
             return lax.dynamic_slice_in_dim(twice, (ranks - rank) % ranks * rows, ranks * rows)
 
-        sums = [Halving(out_blocks, chip, chips, True)] + down_sums
-        for s in sums:
-            s.send()
+        attended_rows = tie(attended_rows, [down_sum, out_sum])
+        down_sum.send()
+        out_sum.send()
         dq, dk, dv = attend_back(
             by, queries, keys, values, attended_rows, logs, cos_table, sin_table, doc
         )
-        dq = tie(dq, [gate_sum, up_sum])
-        gate_sum.send()
-        up_sum.send()
+        dq = tie(dq, [down_sum, out_sum])
+        down_sum.send()
+        out_here = out_sum.finish().reshape(ranks, out_piece, width)
+        gate_up_here = gate_up_here.reshape(2, ranks, piece, width)
+        z_rows = in_rank_order(
+            jnp.concatenate([gate_up_here[0], gate_up_here[1], out_here], axis=1)
+        )
+        z_total = lax.psum_scatter(z_rows, "tensor", scatter_dimension=0, tiled=True)
+        dq, _ = hold((dq, z_rows))
         normed_attn_part = (
             nt(dq, query_key_value_weight[0])
             + nt(dk, query_key_value_weight[1])
@@ -622,24 +656,10 @@
         part_rows = normed_attn_part.astype(BF).reshape(ranks, own_rows, width)
         qkv_grad = jnp.stack([tn(normed_rows, g) for g in (dq, dk, dv)]).astype(BF)
         part_rows, qkv_grad, gain_attn_part = hold((part_rows, qkv_grad, gain_attn_part))
-        gate_up_here = in_rank_order(
-            jnp.concatenate(
-                [
-                    gate_sum.finish().reshape(ranks, piece, width),
-                    up_sum.finish().reshape(ranks, piece, width),
-                ],
-                axis=1,
-            )
-        )
-        gate_up_total = lax.psum_scatter(gate_up_here, "tensor", scatter_dimension=0, tiled=True)
-        tie(gate_up_here, sums)
-        gain_rows = jnp.pad(jnp.stack([gain_attn_part, gain_mlp_part]), ((0, 6), (0, 0))).astype(BF)
-        out_here = sums[0].finish().reshape(ranks, out_piece, width)
-        down_here = jnp.concatenate([s.finish() for s in sums[1:]]).reshape(ranks, piece, width)
-        rest_total = scatter_ranks(
-            [jnp.concatenate([out_here[k], down_here[k], gain_rows]) for k in range(ranks)], ranks
-        ).astype(BF)
-        normed_attn_grad = scatter_ranks(part_rows, ranks)
+        part_rows = tie(part_rows, [down_sum])
+        down_here = down_sum.finish().astype(BF).reshape(chips, piece, width)
+        down_total = Halving(down_here, chip, chips, False).finish()
+        normed_attn_grad = LineSum(part_rows, ranks).finish()
         input_grad = (
             hidden_grad + norm_back(normed_attn_grad, normal_attn, inverse_attn, gain_attn)
         ).astype(BF)
@@ -647,17 +667,21 @@
         qkv_rows = width // (cores * chips)
         qkv_blocks = qkv_grad.reshape(3, cores, chips, qkv_rows, heads_rows)
         qkv_blocks = jnp.swapaxes(sum_cores(qkv_blocks, 1), 0, 1)
-        qkv_here = Halving(qkv_blocks, chip, chips, False).finish()
+        gains = jnp.stack([gain_attn_part, gain_mlp_part])
+        for bit in (1 << b for b in range(ranks.bit_length() - 1)):
+            gains = gains + flip(gains, "tensor", bit, ranks)
+        gain_rows = jnp.pad(gains, ((0, 6), (0, 0))).astype(BF)
+        qkv_here = Halving(qkv_blocks, chip, chips, True).finish()
         groups = width // heads_rows
         qkv_part = qkv_rows // groups
         qkv_here = qkv_here.reshape(3, groups, qkv_part, heads_rows)
         qkv_here = jnp.concatenate(
             [qkv_here[:, g].reshape(3 * qkv_part, heads_rows) for g in range(groups)], axis=1
         )
-        pieces = jnp.concatenate([gate_up_total, rest_total, qkv_here])
+        pieces = jnp.concatenate([z_total, gain_rows, down_total, qkv_here])
         every = lax.all_gather(pieces, ("core", "chip"))
         grads = assemble(every, (cores, chips, share, per, piece, out_piece, qkv_part))
-        at = 3 * piece + out_piece
+        at = 2 * piece + out_piece
         grad_gain_attn, grad_gain_mlp = jnp.sum(every[:, at : at + 2].astype(F32), axis=0)
         grad_gateup = jnp.swapaxes(grads[0], 1, 2)
         down_weight_gradient = grads[1]

time: 398 us -> 382 us (0.960)
  waiting for transfers between devices: 154 us -> 135 us
  matrix products: 8.65 us -> 14.4 us
  local copies, waits for them, and re-layouts: 25.3 us -> 19.8 us
    ppermute x19 -> x15, waiting for transfers between devices: 39 us -> 19.7 us  [flip(): return lax.ppermute(value, axis, [(i, i ^ bit) for i in range(count)])]
    ppermute x9, waiting for transfers between devices: 24 us -> 35.3 us  [shift(): lax.ppermute(value, 'tensor', [(i, (i + by) % count) for i in range(count)])]
    ppermute x12, waiting for transfers between devices: 38.1 us -> 29.5 us  [the longest x6 25.2 us: send(): lax.ppermute(self.up, 'tensor', up)]
    convert_element_type x5 -> x6, other arithmetic: 1.14 us -> 8.95 us  [the longest x2 4.32 us: take(): self.down = (self.down.astype(F32) + down.astype(F32)).astype(BF)]
    convert_element_type x12 -> x6, other arithmetic: 9.06 us -> 1.64 us  [take(): self.held = (self.kept.astype(F32) + self.came.astype(F32)).astype(BF)]
    squeeze x12 -> x6, local copies, waits for them, and re-layouts: 6.92 us -> 0.97 us  [send(): sent = lax.dynamic_index_in_dim(self.held, 1 - mine, at, keepdims=False)]
    ppermute x19 -> x15, starting transfers between devices: 14.7 us -> 19.6 us  [flip(): return lax.ppermute(value, axis, [(i, i ^ bit) for i in range(count)])]
    slice x4 -> x2, local copies, waits for them, and re-layouts: 0.34 us -> 4.96 us  [the longest x1 3.52 us: finish(): self.blocks[0].astype(F32) + self.up.astype(F32) + self.down.astype(F32)]
  transfers between devices with their start and end apart: 56 -> 53, of which waited for: 30 -> 29; matrix products, arithmetic and copies ran while one was open for 13% -> 15% of each run, Pallas kernels for 8% -> 8%
where the time goes in v6:
time: 382 us; the launch traced here: 376 us
  waiting for transfers between devices  135 us (35%)
  starting transfers between devices  83.2 us (22%)
  Pallas kernels  64 us (17%)
  other arithmetic  43.8 us (11%)
  local copies, waits for them, and re-layouts  19.8 us (5%)
  between operations  15.9 us (4%)
  matrix products  14.4 us (4%)
    ppermute x6, waiting for transfers between devices, relay_ranks(): lax.ppermute(downs[-1], 'tensor', [(z, z - 1) for z in range(1, count - s...  36 us
    ppermute x9, waiting for transfers between devices, shift(): lax.ppermute(value, 'tensor', [(i, (i + by) % count) for i in range(count)])  35.3 us
    ppermute x6, starting transfers between devices, send(): lax.ppermute(self.up, 'tensor', up)  28.4 us
    pallas_call x1, Pallas kernels, feed(): pl.pallas_call(lambda *refs: feed_kernel(sizes, *refs), grid=(chips // gr...  25.5 us
    ppermute x6, waiting for transfers between devices, send(): lax.ppermute(self.up, 'tensor', up)  25.2 us
    ppermute x15, waiting for transfers between devices, flip(): return lax.ppermute(value, axis, [(i, i ^ bit) for i in range(count)])  19.7 us
    ppermute x15, starting transfers between devices, flip(): return lax.ppermute(value, axis, [(i, i ^ bit) for i in range(count)])  19.6 us
    pallas_call x1, Pallas kernels, attend_back(): pl.pallas_call(lambda *refs: attend_back_kernel(doc, *refs), grid=(pairs,...  14.5 us
  transfers between devices with their start and end apart: 53, of which 29 were waited for; matrix products, arithmetic and copies ran while one was open for 15% of the time, Pallas kernels for 8%

profile of v6, /device:TPU:0, one launch (start us, length us, event | category | flops | bytes accessed | tf_op | source)
XLA Modules:
  0.0 376.2 jit_solution(820104635881033877)
XLA Ops:
  10.3 5.0 %collective-permute-start.1 = (bf16[88,1024]{1,0:T(8,128)(2,1)}, bf16[88,1024]{1,0:T(8,128)(2,1)}, u32[]{:S(2)}, u32[]{:S(2)}) collective-permute-start(bf16[88,1024]{1,0:T(8,128)(2,1)} %get-tuple-element.146), channel_id=1, source_target_pairs={{0,3},{1,0},{2,1},{3,2},{4,7},{5,4},{6,5},{7,6},{8,11},{9,8},{10,9... | collective-permute-start | bytes 540680 | tf_op jit(solution)/shard_map/ppermute | solution.py:397
  20.6 10.3 %collective-permute-done.2 = bf16[88,1024]{1,0:T(8,128)(2,1)} collective-permute-done((bf16[88,1024]{1,0:T(8,128)(2,1)}, bf16[88,1024]{1,0:T(8,128)(2,1)}, u32[]{:S(2)}, u32[]{:S(2)}) %collective-permute-start.2) | collective-permute-done | bytes 180256 | tf_op jit(solution)/shard_map/ppermute | solution.py:397
  37.0 7.5 %collective-permute-done.5 = bf16[208,1024]{1,0:T(8,128)(2,1)S(1)} collective-permute-done((bf16[208,1024]{1,0:T(8,128)(2,1)}, bf16[208,1024]{1,0:T(8,128)(2,1)S(1)}, u32[]{:S(2)}, u32[]{:S(2)}) %collective-permute-start.5) | collective-permute-done | bytes 426016 | tf_op jit(solution)/shard_map/ppermute | solution.py:407
  51.7 9.6 %collective-permute-done.8 = bf16[208,1024]{1,0:T(8,128)(2,1)S(1)} collective-permute-done((bf16[208,1024]{1,0:T(8,128)(2,1)S(1)}, bf16[208,1024]{1,0:T(8,128)(2,1)S(1)}, u32[]{:S(2)}, u32[]{:S(2)}) %collective-permute-start.8) | collective-permute-done | bytes 426016 | tf_op jit(solution)/shard_map/ppermute | solution.py:408
  63.2 9.3 %collective-permute-done.9 = bf16[208,1024]{1,0:T(8,128)(2,1)S(1)} collective-permute-done((bf16[208,1024]{1,0:T(8,128)(2,1)S(1)}, bf16[208,1024]{1,0:T(8,128)(2,1)S(1)}, u32[]{:S(2)}, u32[]{:S(2)}) %collective-permute-start.9) | collective-permute-done | bytes 426016 | tf_op jit(solution)/shard_map/ppermute | solution.py:408
  77.4 6.2 %collective-permute-done.10.refs_2_ = bf16[256,1024]{1,0:T(8,128)(2,1)S(1)} collective-permute-done((bf16[256,1024]{1,0:T(8,128)(2,1)S(1)}, bf16[256,1024]{1,0:T(8,128)(2,1)S(1)}, u32[]{:S(2)}, u32[]{:S(2)}) %collective-permute-start.10) | collective-permute-done | bytes 524320 | tf_op jit(solution)/shard_map/ppermute | solution.py:407
  93.7 5.9 %collective-permute-done.14.refs_6_ = bf16[256,1024]{1,0:T(8,128)(2,1)} collective-permute-done((bf16[256,1024]{1,0:T(8,128)(2,1)S(1)}, bf16[256,1024]{1,0:T(8,128)(2,1)}, u32[]{:S(2)}, u32[]{:S(2)}) %collective-permute-start.14) | collective-permute-done | bytes 524320 | tf_op jit(solution)/shard_map/ppermute | solution.py:408
  111.0 4.7 %shard_map.152 = (bf16[1024,1024]{1,0:T(8,128)(2,1)S(1)}, bf16[1024,256]{1,0:T(8,128)(2,1)S(1)}, bf16[1024,256]{1,0:T(8,128)(2,1)S(1)}, bf16[1024,256]{1,0:T(8,128)(2,1)S(1)}) custom-call(s32[1]{0:T(128)} %bitcast.4.refs_0_, bf16[256,1024]{1,0:T(8,128)(2,1)S(1)} %fusion.18.refs_1_, bf16[256,1024]{1,0:T(8,128)(2,1)S(1)} %collective-permute-done.10.refs_2_, ...), custom_call_target="tpu_custom_call" | custom-call | flops 1610612736 | bytes 9437184 | tf_op jit(solution)/shard_map/pallas_call | solution.py:94
  117.1 11.5 %shard_map.153 = (bf16[1024,256]{1,0:T(8,128)(2,1)S(1)}, f32[2,2,896]{2,1,0:T(2,128)S(1)}, bf16[1024,256]{1,0:T(8,128)(2,1)S(1)}, bf16[1024,256]{1,0:T(8,128)(2,1)S(1)}, bf16[1024,256]{1,0:T(8,128)(2,1)S(1)}) custom-call(s32[1]{0:T(128)} %bitcast.3.refs_0_, bf16[1024,256]{1,0:T(8,128)(2,1)S(1)} %get-tuple-element.66.refs_1_, ...), custom_call_target="tpu_custom_call" | custom-call | flops 1644167168 | bytes 2097152 | tf_op jit(solution)/shard_map/pallas_call | solution.py:161
  151.2 25.5 %shard_map.154 = (bf16[4,704,1024]{2,1,0:T(8,128)(2,1)}, bf16[4,4,88,1024]{3,2,1,0:T(8,128)(2,1)}, f32[256,1024]{1,0:T(8,128)}, bf16[256,1024]{1,0:T(8,128)(2,1)...) custom-call(bf16[512,1024]{1,0:T(8,128)(2,1)} %pad_maximum_fusion.7.refs_0_, ...), custom_call_target="tpu_custom_call" | custom-call | flops 13287555072 | bytes 26214400 | tf_op jit(solution)/shard_map/pallas_call | solution.py:315
  189.9 4.8 %collective-permute-start.27 = (bf16[352,1024]{1,0:T(8,128)(2,1)}, bf16[352,1024]{1,0:T(8,128)(2,1)}, u32[]{:S(2)}, u32[]{:S(2)}) collective-permute-start(bf16[352,1024]{1,0:T(8,128)(2,1)} %bitcast.43), channel_id=1, source_target_pairs={{0,1},{4,5},{8,9},{12,13},{16,17},{20,21},{24,25},{28,29}} | collective-permute-start | bytes 2162696 | tf_op jit(solution)/shard_map/ppermute | solution.py:421
  202.4 10.9 %collective-permute-done.23 = bf16[256,256]{1,0:T(8,128)(2,1)S(1)} collective-permute-done((bf16[256,256]{1,0:T(8,128)(2,1)S(1)}, bf16[256,256]{1,0:T(8,128)(2,1)S(1)}, u32[]{:S(2)}, u32[]{:S(2)}) %collective-permute-start.23) | collective-permute-done | bytes 131104 | tf_op jit(solution)/shard_map/ppermute | solution.py:397
  216.1 5.4 %collective-permute-done.25 = bf16[256,256]{1,0:T(8,128)(2,1)S(1)} collective-permute-done((bf16[256,256]{1,0:T(8,128)(2,1)S(1)}, bf16[256,256]{1,0:T(8,128)(2,1)S(1)}, u32[]{:S(2)}, u32[]{:S(2)}) %collective-permute-start.25) | collective-permute-done | bytes 131104 | tf_op jit(solution)/shard_map/ppermute | solution.py:397
  233.4 14.5 %shard_map.155 = (bf16[1024,256]{1,0:T(8,128)(2,1)S(1)}, bf16[1024,256]{1,0:T(8,128)(2,1)S(1)}, bf16[1024,256]{1,0:T(8,128)(2,1)S(1)}) custom-call(s32[1]{0:T(128)} %bitcast.3.refs_0_, bf16[1024,256]{1,0:T(8,128)(2,1)S(1)} %copy-done.11, bf16[1024,256]{1,0:T(8,128)(2,1)S(1)} %copy-done.13, bf16[1024,256]{1,0:T(8,128)(2,1)S(1)} %copy-done.15, ...), custom_call_target="tpu_custom_call" | custom-call | bytes 1048576 | tf_op jit(solution)/shard_map/pallas_call | solution.py:229
  259.5 5.6 %collective-permute-start.33 = (bf16[352,1024]{1,0:T(8,128)(2,1)}, bf16[352,1024]{1,0:T(8,128)(2,1)}, u32[]{:S(2)}, u32[]{:S(2)}) collective-permute-start(bf16[352,1024]{1,0:T(8,128)(2,1)} %add_convert_fusion.1), channel_id=1, source_target_pairs={{0,1},{1,2},{2,3},{4,5},{5,6},{6,7},{8,9},{9,10},{10,11},{12,13},{... | collective-permute-start | bytes 2162696 | tf_op jit(solution)/shard_map/ppermute | solution.py:421
  278.1 6.4 %collective-permute-done.33 = bf16[352,1024]{1,0:T(8,128)(2,1)} collective-permute-done((bf16[352,1024]{1,0:T(8,128)(2,1)}, bf16[352,1024]{1,0:T(8,128)(2,1)}, u32[]{:S(2)}, u32[]{:S(2)}) %collective-permute-start.33) | collective-permute-done | bytes 720928 | tf_op jit(solution)/shard_map/ppermute | solution.py:421
  290.0 8.0 %collective-permute-start.42 = (f32[2,1024]{1,0:T(2,128)S(1)}, f32[2,1024]{1,0:T(2,128)S(1)}, u32[]{:S(2)}, u32[]{:S(2)}) collective-permute-start(f32[2,1024]{1,0:T(2,128)S(1)} %fusion.68), channel_id=1, source_target_pairs={{0,2},{1,3},{2,0},{3,1},{4,6},{5,7},{6,4},{7,5},{8,10},{9,11},{10,... | collective-permute-start | bytes 24584 | tf_op jit(solution)/shard_map/ppermute | solution.py:401
  314.1 4.5 %collective-permute-start.35 = (bf16[256,1024]{1,0:T(8,128)(2,1)S(1)}, bf16[256,1024]{1,0:T(8,128)(2,1)S(1)}, u32[]{:S(2)}, u32[]{:S(2)}) collective-permute-start(bf16[256,1024]{1,0:T(8,128)(2,1)S(1)} %get-tuple-element.131), channel_id=1, source_target_pairs={{0,1},{4,5},{8,9},{12,13},{16,17},{20,21},{24,25},{28,29}} | collective-permute-start | bytes 1572872 | tf_op jit(solution)/shard_map/ppermute | solution.py:421
  319.4 7.5 %collective-permute-done.35 = bf16[256,1024]{1,0:T(8,128)(2,1)S(1)} collective-permute-done((bf16[256,1024]{1,0:T(8,128)(2,1)S(1)}, bf16[256,1024]{1,0:T(8,128)(2,1)S(1)}, u32[]{:S(2)}, u32[]{:S(2)}) %collective-permute-start.35) | collective-permute-done | bytes 524320 | tf_op jit(solution)/shard_map/ppermute | solution.py:421
  327.3 4.5 %collective-permute-start.36 = (bf16[256,1024]{1,0:T(8,128)(2,1)S(1)}, bf16[256,1024]{1,0:T(8,128)(2,1)S(1)}, u32[]{:S(2)}, u32[]{:S(2)}) collective-permute-start(bf16[256,1024]{1,0:T(8,128)(2,1)S(1)} %get-tuple-element.129), channel_id=1, source_target_pairs={{0,1},{1,2},{4,5},{5,6},{8,9},{9,10},{12,13},{13,14},{16,17},{17,1... | collective-permute-start | bytes 1572872 | tf_op jit(solution)/shard_map/ppermute | solution.py:421
  332.7 5.8 %collective-permute-done.36 = bf16[256,1024]{1,0:T(8,128)(2,1)S(1)} collective-permute-done((bf16[256,1024]{1,0:T(8,128)(2,1)S(1)}, bf16[256,1024]{1,0:T(8,128)(2,1)S(1)}, u32[]{:S(2)}, u32[]{:S(2)}) %collective-permute-start.36) | collective-permute-done | bytes 524320 | tf_op jit(solution)/shard_map/ppermute | solution.py:421
  338.9 7.5 %collective-permute-start.37 = (bf16[256,1024]{1,0:T(8,128)(2,1)S(1)}, bf16[256,1024]{1,0:T(8,128)(2,1)S(1)}, u32[]{:S(2)}, u32[]{:S(2)}) collective-permute-start(bf16[256,1024]{1,0:T(8,128)(2,1)S(1)} %get-tuple-element.127), channel_id=1, source_target_pairs={{0,1},{1,2},{2,3},{4,5},{5,6},{6,7},{8,9},{9,10},{10,11},{12,13},{... | collective-permute-start | bytes 1572872 | tf_op jit(solution)/shard_map/ppermute | solution.py:421
  347.7 5.4 %collective-permute-done.37 = bf16[256,1024]{1,0:T(8,128)(2,1)S(1)} collective-permute-done((bf16[256,1024]{1,0:T(8,128)(2,1)S(1)}, bf16[256,1024]{1,0:T(8,128)(2,1)S(1)}, u32[]{:S(2)}, u32[]{:S(2)}) %collective-permute-start.37) | collective-permute-done | bytes 524320 | tf_op jit(solution)/shard_map/ppermute | solution.py:421
  360.1 7.8 %shard_map.156 = (f32[2,656,1024]{2,1,0:T(8,128)}, f32[656,1024]{1,0:T(8,128)}, f32[8,32,1024]{2,1,0:T(8,128)}, f32[3,8,4,32,256]{4,3,2,1,0:T(8,128)}) custom-call(bf16[8,400,1024]{2,1,0:T(8,128)(2,1)} %bitcast.238), custom_call_target="tpu_custom_call" | custom-call | bytes 18874368 | tf_op jit(solution)/shard_map/pallas_call | solution.py:374
  (286 shorter events, 166.2 us)
Async XLA Ops:
  7.2 132.0 %all-gather.7.cloned.1.call-start = ((), (), s32[]{:S(2)}) async-start(), calls=%async_computation.4 | async-start | bytes 2703360 | tf_op jit(solution)/shard_map/all_gather | solution.py:526
  15.3 15.6 %collective-permute-start.2 = (bf16[88,1024]{1,0:T(8,128)(2,1)}, bf16[88,1024]{1,0:T(8,128)(2,1)}, u32[]{:S(2)}, u32[]{:S(2)}) collective-permute-start(bf16[88,1024]{1,0:T(8,128)(2,1)} %get-tuple-element.146), channel_id=1, source_target_pairs={{0,2},{1,3},{2,0},{3,1},{4,6},{5,7},{6,4},{7,5},{8,10},{9,11},{10,... | collective-permute-start | bytes 540680 | tf_op jit(solution)/shard_map/ppermute | solution.py:397
  15.3 15.6 %collective-permute-start.3 = (bf16[88,1024]{1,0:T(8,128)(2,1)}, bf16[88,1024]{1,0:T(8,128)(2,1)}, u32[]{:S(2)}, u32[]{:S(2)}) collective-permute-start(bf16[88,1024]{1,0:T(8,128)(2,1)} %get-tuple-element.146), channel_id=1, source_target_pairs={{0,1},{1,2},{2,3},{3,0},{4,5},{5,6},{6,7},{7,4},{8,9},{9,10},{10,1... | collective-permute-start | bytes 540680 | tf_op jit(solution)/shard_map/ppermute | solution.py:397
  32.9 106.4 %all-gather.9.cloned.1.call-start = ((), (), s32[]{:S(2)}) async-start(), calls=%async_computation.5 | async-start | bytes 6389760 | tf_op jit(solution)/shard_map/all_gather | solution.py:530
  35.7 13.5 %collective-permute-start.4 = (bf16[208,1024]{1,0:T(8,128)(2,1)}, bf16[208,1024]{1,0:T(8,128)(2,1)S(1)}, u32[]{:S(2)}, u32[]{:S(2)}) collective-permute-start(bf16[208,1024]{1,0:T(8,128)(2,1)} %pad_maximum_fusion.12), channel_id=1, source_target_pairs={{1,0},{2,1},{3,2},{5,4},{6,5},{7,6},{9,8},{10,9},{11,10},{13,12},{... | collective-permute-start | bytes 1277960 | tf_op jit(solution)/shard_map/ppermute | solution.py:408
  73.8 191.4 %reduce-scatter.3.cloned.1.call-start = ((), (), s32[]{:S(2)}) async-start(), calls=%async_computation.2 | async-start | bytes 7208960 | tf_op jit(solution)/shard_map/reduce_scatter | solution.py:593
  75.4 12.3 %collective-permute-start.13 = (bf16[256,1024]{1,0:T(8,128)(2,1)S(1)}, bf16[256,1024]{1,0:T(8,128)(2,1)S(1)}, u32[]{:S(2)}, u32[]{:S(2)}) collective-permute-start(bf16[256,1024]{1,0:T(8,128)(2,1)S(1)} %fusion.18.refs_1_), channel_id=1, source_target_pairs={{1,0},{2,1},{3,2},{5,4},{6,5},{7,6},{9,8},{10,9},{11,10},{13,12},{... | collective-permute-start | bytes 1572872 | tf_op jit(solution)/shard_map/ppermute | solution.py:408
  76.7 27.1 %collective-permute-start = (bf16[256,1024]{1,0:T(8,128)(2,1)}, bf16[256,1024]{1,0:T(8,128)(2,1)}, u32[]{:S(2)}, u32[]{:S(2)}) collective-permute-start(bf16[256,1024]{1,0:T(8,128)(2,1)} %bitcast), channel_id=1, source_target_pairs={{0,4},{4,0},{1,5},{5,1},{2,6},{6,2},{3,7},{7,3},{8,12},{12,8},{9,1... | collective-permute-start | bytes 1572872 | tf_op jit(solution)/shard_map/ppermute | solution.py:401
  92.0 14.4 %collective-permute-start.12 = (bf16[256,1024]{1,0:T(8,128)(2,1)}, bf16[256,1024]{1,0:T(8,128)(2,1)}, u32[]{:S(2)}, u32[]{:S(2)}) collective-permute-start(bf16[256,1024]{1,0:T(8,128)(2,1)} %collective-permute-done.11.refs_3_), channel_id=1, source_target_pairs={{2,3},{6,7},{10,11},{14,15},{18,19},{22,23},{26,27},{30,31}} | collective-permute-start | bytes 1572872 | tf_op jit(solution)/shard_map/ppermute | solution.py:407
  176.8 135.2 %reduce-scatter.5.cloned.1.call-start = ((), (), s32[]{:S(2)}) async-start(), calls=%async_computation.3 | async-start | bytes 2129920 | tf_op jit(solution)/shard_map/reduce_scatter | solution.py:648
  189.9 31.6 %collective-permute-start.27 = (bf16[352,1024]{1,0:T(8,128)(2,1)}, bf16[352,1024]{1,0:T(8,128)(2,1)}, u32[]{:S(2)}, u32[]{:S(2)}) collective-permute-start(bf16[352,1024]{1,0:T(8,128)(2,1)} %bitcast.43), channel_id=1, source_target_pairs={{0,1},{4,5},{8,9},{12,13},{16,17},{20,21},{24,25},{28,29}} | collective-permute-start | bytes 2162696 | tf_op jit(solution)/shard_map/ppermute | solution.py:421
  194.8 26.8 %collective-permute-start.28 = (bf16[352,1024]{1,0:T(8,128)(2,1)}, bf16[352,1024]{1,0:T(8,128)(2,1)}, u32[]{:S(2)}, u32[]{:S(2)}) collective-permute-start(bf16[352,1024]{1,0:T(8,128)(2,1)} %bitcast.44), channel_id=1, source_target_pairs={{3,2},{7,6},{11,10},{15,14},{19,18},{23,22},{27,26},{31,30}} | collective-permute-start | bytes 2162696 | tf_op jit(solution)/shard_map/ppermute | solution.py:421
  199.7 26.0 %collective-permute-start.29 = (bf16[2,128,1024]{2,1,0:T(8,128)(2,1)}, bf16[2,128,1024]{2,1,0:T(8,128)(2,1)}, u32[]{:S(2)}, u32[]{:S(2)}) collective-permute-start(bf16[2,128,1024]{2,1,0:T(8,128)(2,1)} %dynamic-slice_bitcast_fusion.1), channel_id=1, source_target_pairs={{0,16},{8,24},{16,0},{24,8},{1,17},{9,25},{17,1},{25,9},{2,18},{10... | collective-permute-start | bytes 1572872 | tf_op jit(solution)/shard_map/ppermute | solution.py:401
  201.2 12.1 %collective-permute-start.23 = (bf16[256,256]{1,0:T(8,128)(2,1)S(1)}, bf16[256,256]{1,0:T(8,128)(2,1)S(1)}, u32[]{:S(2)}, u32[]{:S(2)}) collective-permute-start(bf16[256,256]{1,0:T(8,128)(2,1)S(1)} %get-tuple-element.168), channel_id=1, source_target_pairs={{0,3},{1,0},{2,1},{3,2},{4,7},{5,4},{6,5},{7,6},{8,11},{9,8},{10,9... | collective-permute-start | bytes 393224 | tf_op jit(solution)/shard_map/ppermute | solution.py:397
  202.4 13.7 %collective-permute-start.24 = (bf16[256,256]{1,0:T(8,128)(2,1)S(1)}, bf16[256,256]{1,0:T(8,128)(2,1)S(1)}, u32[]{:S(2)}, u32[]{:S(2)}) collective-permute-start(bf16[256,256]{1,0:T(8,128)(2,1)S(1)} %get-tuple-element.167), channel_id=1, source_target_pairs={{0,2},{1,3},{2,0},{3,1},{4,6},{5,7},{6,4},{7,5},{8,10},{9,11},{10,... | collective-permute-start | bytes 393224 | tf_op jit(solution)/shard_map/ppermute | solution.py:397
  227.0 26.7 %collective-permute-start.32 = (bf16[128,1024]{1,0:T(8,128)(2,1)S(1)}, bf16[128,1024]{1,0:T(8,128)(2,1)S(1)}, u32[]{:S(2)}, u32[]{:S(2)}) collective-permute-start(bf16[128,1024]{1,0:T(8,128)(2,1)S(1)} %dynamic-slice_bitcast_fusion.4), channel_id=1, source_target_pairs={{0,8},{8,0},{16,24},{24,16},{1,9},{9,1},{17,25},{25,17},{2,10},{10... | collective-permute-start | bytes 786440 | tf_op jit(solution)/shard_map/ppermute | solution.py:401
  230.7 23.1 %collective-permute-start.30 = (bf16[352,1024]{1,0:T(8,128)(2,1)S(1)}, bf16[352,1024]{1,0:T(8,128)(2,1)S(1)}, u32[]{:S(2)}, u32[]{:S(2)}) collective-permute-start(bf16[352,1024]{1,0:T(8,128)(2,1)S(1)} %get-tuple-element.164), channel_id=1, source_target_pairs={{0,1},{1,2},{4,5},{5,6},{8,9},{9,10},{12,13},{13,14},{16,17},{17,1... | collective-permute-start | bytes 2162696 | tf_op jit(solution)/shard_map/ppermute | solution.py:421
  232.2 21.6 %collective-permute-start.31 = (bf16[352,1024]{1,0:T(8,128)(2,1)S(1)}, bf16[352,1024]{1,0:T(8,128)(2,1)S(1)}, u32[]{:S(2)}, u32[]{:S(2)}) collective-permute-start(bf16[352,1024]{1,0:T(8,128)(2,1)S(1)} %get-tuple-element.163), channel_id=1, source_target_pairs={{2,1},{3,2},{6,5},{7,6},{10,9},{11,10},{14,13},{15,14},{18,17},{19... | collective-permute-start | bytes 2162696 | tf_op jit(solution)/shard_map/ppermute | solution.py:421
  256.0 22.0 %collective-permute-start.34 = (bf16[352,1024]{1,0:T(8,128)(2,1)}, bf16[352,1024]{1,0:T(8,128)(2,1)}, u32[]{:S(2)}, u32[]{:S(2)}) collective-permute-start(bf16[352,1024]{1,0:T(8,128)(2,1)} %add_convert_fusion), channel_id=1, source_target_pairs={{1,0},{2,1},{3,2},{5,4},{6,5},{7,6},{9,8},{10,9},{11,10},{13,12},{... | collective-permute-start | bytes 2162696 | tf_op jit(solution)/shard_map/ppermute | solution.py:421
  259.5 24.9 %collective-permute-start.33 = (bf16[352,1024]{1,0:T(8,128)(2,1)}, bf16[352,1024]{1,0:T(8,128)(2,1)}, u32[]{:S(2)}, u32[]{:S(2)}) collective-permute-start(bf16[352,1024]{1,0:T(8,128)(2,1)} %add_convert_fusion.1), channel_id=1, source_target_pairs={{0,1},{1,2},{2,3},{4,5},{5,6},{6,7},{8,9},{9,10},{10,11},{12,13},{... | collective-permute-start | bytes 2162696 | tf_op jit(solution)/shard_map/ppermute | solution.py:421
  270.3 89.9 %all-gather.11.cloned.1.call-start = ((), (), s32[]{:S(2)}) async-start(), calls=%async_computation.6 | async-start | bytes 7372800 | tf_op jit(solution)/shard_map/all_gather | solution.py:682
  278.0 19.9 %collective-permute-start.45 = (bf16[3,4,128,256]{3,2,0,1:T(8,128)(2,1)S(1)}, bf16[3,4,128,256]{3,2,0,1:T(8,128)(2,1)S(1)}, u32[]{:S(2)}, u32[]{:S(2)}) collective-permute-start(bf16[3,4,128,256]{3,2,0,1:T(8,128)(2,1)S(1)} %bitcast.257), channel_id=1, source_target_pairs={{0,4},{4,0},{1,5},{5,1},{2,6},{6,2},{3,7},{7,3},{8,12},{12,8},{9,1... | collective-permute-start | bytes 2359304 | tf_op jit(solution)/shard_map/ppermute | solution.py:401
  314.1 12.8 %collective-permute-start.35 = (bf16[256,1024]{1,0:T(8,128)(2,1)S(1)}, bf16[256,1024]{1,0:T(8,128)(2,1)S(1)}, u32[]{:S(2)}, u32[]{:S(2)}) collective-permute-start(bf16[256,1024]{1,0:T(8,128)(2,1)S(1)} %get-tuple-element.131), channel_id=1, source_target_pairs={{0,1},{4,5},{8,9},{12,13},{16,17},{20,21},{24,25},{28,29}} | collective-permute-start | bytes 1572872 | tf_op jit(solution)/shard_map/ppermute | solution.py:421
  338.9 14.3 %collective-permute-start.37 = (bf16[256,1024]{1,0:T(8,128)(2,1)S(1)}, bf16[256,1024]{1,0:T(8,128)(2,1)S(1)}, u32[]{:S(2)}, u32[]{:S(2)}) collective-permute-start(bf16[256,1024]{1,0:T(8,128)(2,1)S(1)} %get-tuple-element.127), channel_id=1, source_target_pairs={{0,1},{1,2},{2,3},{4,5},{5,6},{6,7},{8,9},{9,10},{10,11},{12,13},{... | collective-permute-start | bytes 1572872 | tf_op jit(solution)/shard_map/ppermute | solution.py:421
  (76 other events, 609.6 us)
Sparse Core Ops, SparseCore 0:
  33.0 36.2 all-gather.6
  74.0 58.5 all-gather.8
  176.9 76.9 reduce-scatter.2
  270.4 37.3 reduce-scatter.4
  314.2 45.9 all-gather.10

commit v7 on v6

--- a/solution.py
+++ b/solution.py
@@ -125,33 +125,45 @@
         at += size
 
 
-def turn(value, by):
-    return pltpu.roll(value.astype(F32), by, 0)
-
-
-def attend_kernel(doc, by_ref, q_ref, k_ref, v_ref, o_ref, l_ref, qd_ref, kd_ref, vd_ref, od_ref):
+def put_twice(held, at, value):
+    length = held.shape[0] // 2
+    size = value.shape[0]
+    held[at : at + size, :] = value
+    held[length + at : length + at + size, :] = value
+
+
+def from_row(held, start):
+    return held[pl.ds(start, held.shape[0] // 2), :]
+
+
+def attend_kernel(doc, by_ref, q_ref, k_ref, v_ref, o_ref, l_ref, qd_ref, kd_ref, vd_ref, held):
     length = q_ref.shape[0]
-    into = lax.rem(length - by_ref[0], length)
-    qd_ref[...] = turn(q_ref[...], into).astype(BF)
-    kd_ref[...] = turn(k_ref[...], into).astype(BF)
-    values = turn(v_ref[...], into)
-    vd_ref[...] = values.astype(BF)
-    od_ref[doc:, :] = values[doc:, :]
+    turned = []
+    for i, (ref, out) in enumerate(((q_ref, qd_ref), (k_ref, kd_ref), (v_ref, vd_ref))):
+        put_twice(held.at[i], 0, ref[...].astype(F32))
+        turned.append(from_row(held.at[i], by_ref[0]))
+        out[...] = turned[i].astype(BF)
     keys = kd_ref[:doc, :]
-    values_t = values[:doc, :].T.astype(BF)
+    values = vd_ref[:doc, :]
+    lane = lax.broadcasted_iota(jnp.int32, values.shape, 1)
+    summed = [jnp.where(lane // HD == h, values, jnp.ones_like(values)) for h in range(2)]
     for at, size in row_blocks(doc):
         queries = qd_ref[at : at + size, :]
         mixed = []
         for half in range(2):
-            scores = nt(keys, half_mask(queries, half))
-            largest = jnp.max(scores, axis=0, keepdims=True)
-            weights = jnp.exp(scores - largest)
-            total = jnp.sum(weights, axis=0, keepdims=True)
-            mix = nn(values_t[half * HD : half * HD + HD], weights.astype(BF))
+            scores = nt(half_mask(queries, half), keys)
+            largest = jnp.max(scores, axis=1, keepdims=True)
+            weights = jnp.exp(scores - largest).astype(BF)
+            mix = nn(weights, summed[half])
+            other = (1 - half) * HD
+            total = mix[:, other : other + 1]
             mixed.append(mix * (1.0 / total))
-            l_ref[0, half : half + 1, at : at + size] = largest + jnp.log(total)
-        od_ref[at : at + size, :] = jnp.concatenate(mixed, axis=0).T
-    o_ref[...] = turn(od_ref[...], by_ref[0]).astype(BF)
+            log = jnp.broadcast_to(largest + jnp.log(total), (size, 128))
+            l_ref[0, half : half + 1, at : at + size] = log.T[0:1, :]
+        lane = lax.broadcasted_iota(jnp.int32, (size, 128), 1)
+        put_twice(held.at[3], at, jnp.where(lane < HD, mixed[0], mixed[1]))
+    put_twice(held.at[3], doc, turned[2][doc:, :])
+    o_ref[...] = from_row(held.at[3], length - by_ref[0]).astype(BF)
 
 
 def attend(by, queries, keys, values, doc):
@@ -168,7 +180,7 @@
             jax.ShapeDtypeStruct((pairs, 2, doc), F32),
         ]
         + [jax.ShapeDtypeStruct((length, cols), BF)] * 3,
-        scratch_shapes=[pltpu.VMEM((length, 128), F32)],
+        scratch_shapes=[pltpu.VMEM((4, 2 * length, 128), F32)],
         compiler_params=pltpu.CompilerParams(vmem_limit_bytes=48 * 2**20),
         cost_estimate=pl.CostEstimate(
             flops=8 * doc * doc * cols, bytes_accessed=2 * 2**20, transcendentals=doc * doc * 4
@@ -178,16 +190,12 @@
 
 def attend_back_kernel(
     doc, by_ref, q_ref, k_ref, v_ref, d_ref, l_ref, cos_ref, sin_ref,
-    dq_ref, dk_ref, dv_ref, qa_ref, ka_ref, va_ref, dd_ref,
+    dq_ref, dk_ref, dv_ref, ka_ref, va_ref, dd_ref, held,
 ):
     length = q_ref.shape[0]
-    into = lax.rem(length - by_ref[0], length)
-    turned = turn(d_ref[...], into)
+    put_twice(held.at[0], 0, d_ref[...].astype(F32))
+    turned = from_row(held.at[0], by_ref[0])
     dd_ref[...] = turned.astype(BF)
-    zero = jnp.zeros((length - doc, 128), F32)
-    qa_ref[doc:, :] = zero
-    ka_ref[doc:, :] = zero
-    va_ref[doc:, :] = turned[doc:, :]
     keys = k_ref[:doc, :]
     keys_t = keys.T
     values = v_ref[:doc, :]
@@ -206,19 +214,27 @@
             value_part = nn(probs.astype(BF), grad)
             key_part = nn(score_grad, query)
             if first:
-                va_ref[:doc, :] = value_part
-                ka_ref[:doc, :] = key_part
+                va_ref[...] = value_part
+                ka_ref[...] = key_part
                 first = False
             else:
-                va_ref[:doc, :] += value_part
-                ka_ref[:doc, :] += key_part
+                va_ref[...] += value_part
+                ka_ref[...] += key_part
             back.append(nn(keys_t[half * HD : half * HD + HD], score_grad))
-        qa_ref[at : at + size, :] = jnp.concatenate(back, axis=0).T * (1.0 / math.sqrt(HD))
+        query_grad = jnp.concatenate(back, axis=0).T * (1.0 / math.sqrt(HD))
+        put_twice(held.at[1], at, query_grad)
+    zero = jnp.zeros((length - doc, 128), F32)
+    put_twice(held.at[1], doc, zero)
+    put_twice(held.at[2], 0, ka_ref[...])
+    put_twice(held.at[2], doc, zero)
+    put_twice(held.at[3], 0, va_ref[...])
+    put_twice(held.at[3], doc, turned[doc:, :])
+    back_row = length - by_ref[0]
     cos, sin = cos_ref[...], sin_ref[...]
-    for held, out in ((qa_ref, dq_ref), (ka_ref, dk_ref)):
-        grad = turn(held[...], by_ref[0])
+    for i, out in ((1, dq_ref), (2, dk_ref)):
+        grad = from_row(held.at[i], back_row)
         out[...] = (grad * cos - swap_halves(grad) * sin).astype(BF)
-    dv_ref[...] = turn(va_ref[...], by_ref[0]).astype(BF)
+    dv_ref[...] = from_row(held.at[3], back_row).astype(BF)
 
 
 def attend_back(by, queries, keys, values, grads, logs, cos, sin, doc):
@@ -235,7 +251,8 @@
         + [table] * 2,
         out_specs=[spec] * 3,
         out_shape=[jax.ShapeDtypeStruct((length, cols), BF)] * 3,
-        scratch_shapes=[pltpu.VMEM((length, 128), F32)] * 3 + [pltpu.VMEM((length, 128), BF)],
+        scratch_shapes=[pltpu.VMEM((doc, 128), F32)] * 2
+        + [pltpu.VMEM((length, 128), BF), pltpu.VMEM((4, 2 * length, 128), F32)],
         compiler_params=pltpu.CompilerParams(vmem_limit_bytes=48 * 2**20),
         cost_estimate=pl.CostEstimate(
             flops=0, bytes_accessed=2**20, transcendentals=0
@@ -262,9 +279,9 @@
     up = join(1, rest_ref, 0)
     down = join(2, rest_ref, piece + out_piece)
     normed, cot = n_ref[...], c_ref[...]
-    gate_proj = nt(normed, gate)
-    up_proj = nt(normed, up)
-    hid_grad = nt(cot, down)
+    gate_proj = nt(gate, normed)
+    up_proj = nt(up, normed)
+    hid_grad = nt(down, cot)
     cdf = 0.5 * (1.0 + lax.erf(gate_proj * (1.0 / math.sqrt(2.0))))
     pdf = jnp.exp(-0.5 * gate_proj * gate_proj) * (1.0 / math.sqrt(2.0 * math.pi))
     act = gate_proj * cdf
@@ -272,13 +289,13 @@
     gate_grad = (hid_grad * up_proj * (cdf + gate_proj * pdf)).astype(BF)
     up_grad = (hid_grad * act).astype(BF)
     hidden = ranks * piece
-    dgu_ref[0, :hidden] = tn(gate_grad, normed).astype(BF)
-    dgu_ref[0, hidden:] = tn(up_grad, normed).astype(BF)
-    down_grad = tn(hid, cot)
+    dgu_ref[0, :hidden] = nn(gate_grad, normed).astype(BF)
+    dgu_ref[0, hidden:] = nn(up_grad, normed).astype(BF)
+    down_grad = nn(hid, cot)
     for k in range(ranks):
         dd_ref[k, 0] = down_grad[k * piece : (k + 1) * piece].astype(BF)
-    in_part = nn(gate_grad, gate) + nn(up_grad, up)
-    out_part = nn(hid, down)
+    in_part = tn(jnp.concatenate([gate_grad, up_grad]), jnp.concatenate([gate, up]))
+    out_part = tn(hid, down)
 
     @pl.when(step == 0)
     def _():

time: 382 us -> 375 us (0.982)
  Pallas kernels: 64 us -> 57.7 us
  transfers between devices with their start and end apart: 53 -> 53, of which waited for: 29 -> 29; matrix products, arithmetic and copies ran while one was open for 15% -> 15% of each run, Pallas kernels for 8% -> 7%
where the time goes in v7:
time: 375 us; the launch traced here: 370 us
  waiting for transfers between devices  135 us (36%)
  starting transfers between devices  83 us (22%)
  Pallas kernels  57.7 us (15%)
  other arithmetic  43.8 us (12%)
  local copies, waits for them, and re-layouts  19.8 us (5%)
  between operations  16.1 us (4%)
  matrix products  14.4 us (4%)
    ppermute x6, waiting for transfers between devices, relay_ranks(): lax.ppermute(downs[-1], 'tensor', [(z, z - 1) for z in range(1, count - s...  35.7 us
    ppermute x9, waiting for transfers between devices, shift(): lax.ppermute(value, 'tensor', [(i, (i + by) % count) for i in range(count)])  35.4 us
    ppermute x6, starting transfers between devices, send(): lax.ppermute(self.up, 'tensor', up)  27.7 us
    ppermute x6, waiting for transfers between devices, send(): lax.ppermute(self.up, 'tensor', up)  25.2 us
    pallas_call x1, Pallas kernels, feed(): pl.pallas_call(lambda *refs: feed_kernel(sizes, *refs), grid=(chips // gr...  22.6 us
    ppermute x15, starting transfers between devices, flip(): return lax.ppermute(value, axis, [(i, i ^ bit) for i in range(count)])  19.9 us
    ppermute x15, waiting for transfers between devices, flip(): return lax.ppermute(value, axis, [(i, i ^ bit) for i in range(count)])  19.4 us
    pallas_call x1, Pallas kernels, attend_back(): pl.pallas_call(lambda *refs: attend_back_kernel(doc, *refs), grid=(pairs,...  13.7 us
  transfers between devices with their start and end apart: 53, of which 29 were waited for; matrix products, arithmetic and copies ran while one was open for 15% of the time, Pallas kernels for 7%

profile of v7, /device:TPU:0, one launch (start us, length us, event | category | flops | bytes accessed | tf_op | source)
XLA Modules:
  0.0 369.5 jit_solution(2599611883709946351)
XLA Ops:
  10.3 5.0 %collective-permute-start.1 = (bf16[88,1024]{1,0:T(8,128)(2,1)}, bf16[88,1024]{1,0:T(8,128)(2,1)}, u32[]{:S(2)}, u32[]{:S(2)}) collective-permute-start(bf16[88,1024]{1,0:T(8,128)(2,1)} %get-tuple-element.146), channel_id=1, source_target_pairs={{0,3},{1,0},{2,1},{3,2},{4,7},{5,4},{6,5},{7,6},{8,11},{9,8},{10,9... | collective-permute-start | bytes 540680 | tf_op jit(solution)/shard_map/ppermute | solution.py:414
  20.6 10.3 %collective-permute-done.2 = bf16[88,1024]{1,0:T(8,128)(2,1)} collective-permute-done((bf16[88,1024]{1,0:T(8,128)(2,1)}, bf16[88,1024]{1,0:T(8,128)(2,1)}, u32[]{:S(2)}, u32[]{:S(2)}) %collective-permute-start.2) | collective-permute-done | bytes 180256 | tf_op jit(solution)/shard_map/ppermute | solution.py:414
  37.0 7.5 %collective-permute-done.5 = bf16[208,1024]{1,0:T(8,128)(2,1)S(1)} collective-permute-done((bf16[208,1024]{1,0:T(8,128)(2,1)}, bf16[208,1024]{1,0:T(8,128)(2,1)S(1)}, u32[]{:S(2)}, u32[]{:S(2)}) %collective-permute-start.5) | collective-permute-done | bytes 426016 | tf_op jit(solution)/shard_map/ppermute | solution.py:424
  51.7 9.6 %collective-permute-done.8 = bf16[208,1024]{1,0:T(8,128)(2,1)S(1)} collective-permute-done((bf16[208,1024]{1,0:T(8,128)(2,1)S(1)}, bf16[208,1024]{1,0:T(8,128)(2,1)S(1)}, u32[]{:S(2)}, u32[]{:S(2)}) %collective-permute-start.8) | collective-permute-done | bytes 426016 | tf_op jit(solution)/shard_map/ppermute | solution.py:425
  63.2 9.3 %collective-permute-done.9 = bf16[208,1024]{1,0:T(8,128)(2,1)S(1)} collective-permute-done((bf16[208,1024]{1,0:T(8,128)(2,1)S(1)}, bf16[208,1024]{1,0:T(8,128)(2,1)S(1)}, u32[]{:S(2)}, u32[]{:S(2)}) %collective-permute-start.9) | collective-permute-done | bytes 426016 | tf_op jit(solution)/shard_map/ppermute | solution.py:425
  77.4 6.2 %collective-permute-done.10.refs_2_ = bf16[256,1024]{1,0:T(8,128)(2,1)S(1)} collective-permute-done((bf16[256,1024]{1,0:T(8,128)(2,1)S(1)}, bf16[256,1024]{1,0:T(8,128)(2,1)S(1)}, u32[]{:S(2)}, u32[]{:S(2)}) %collective-permute-start.10) | collective-permute-done | bytes 524320 | tf_op jit(solution)/shard_map/ppermute | solution.py:424
  93.7 5.9 %collective-permute-done.14.refs_6_ = bf16[256,1024]{1,0:T(8,128)(2,1)} collective-permute-done((bf16[256,1024]{1,0:T(8,128)(2,1)S(1)}, bf16[256,1024]{1,0:T(8,128)(2,1)}, u32[]{:S(2)}, u32[]{:S(2)}) %collective-permute-start.14) | collective-permute-done | bytes 524320 | tf_op jit(solution)/shard_map/ppermute | solution.py:425
  111.0 4.8 %shard_map.152 = (bf16[1024,1024]{1,0:T(8,128)(2,1)S(1)}, bf16[1024,256]{1,0:T(8,128)(2,1)S(1)}, bf16[1024,256]{1,0:T(8,128)(2,1)S(1)}, bf16[1024,256]{1,0:T(8,128)(2,1)S(1)}) custom-call(s32[1]{0:T(128)} %bitcast.4.refs_0_, bf16[256,1024]{1,0:T(8,128)(2,1)S(1)} %fusion.18.refs_1_, bf16[256,1024]{1,0:T(8,128)(2,1)S(1)} %collective-permute-done.10.refs_2_, ...), custom_call_target="tpu_custom_call" | custom-call | flops 1610612736 | bytes 9437184 | tf_op jit(solution)/shard_map/pallas_call | solution.py:94
  117.1 8.9 %shard_map.153 = (bf16[1024,256]{1,0:T(8,128)(2,1)S(1)}, f32[2,2,896]{2,1,0:T(2,128)S(1)}, bf16[1024,256]{1,0:T(8,128)(2,1)S(1)}, bf16[1024,256]{1,0:T(8,128)(2,1)S(1)}, bf16[1024,256]{1,0:T(8,128)(2,1)S(1)}) custom-call(s32[1]{0:T(128)} %bitcast.3.refs_0_, bf16[1024,256]{1,0:T(8,128)(2,1)S(1)} %get-tuple-element.66.refs_1_, ...), custom_call_target="tpu_custom_call" | custom-call | flops 1644167168 | bytes 2097152 | tf_op jit(solution)/shard_map/pallas_call | solution.py:173
  148.6 22.6 %shard_map.154 = (bf16[4,704,1024]{2,1,0:T(8,128)(2,1)}, bf16[4,4,88,1024]{3,2,1,0:T(8,128)(2,1)}, f32[256,1024]{1,0:T(8,128)}, bf16[256,1024]{1,0:T(8,128)(2,1)...) custom-call(bf16[512,1024]{1,0:T(8,128)(2,1)} %pad_maximum_fusion.7.refs_0_, ...), custom_call_target="tpu_custom_call" | custom-call | flops 13287555072 | bytes 26214400 | tf_op jit(solution)/shard_map/pallas_call | solution.py:332
  184.4 4.8 %collective-permute-start.27 = (bf16[352,1024]{1,0:T(8,128)(2,1)}, bf16[352,1024]{1,0:T(8,128)(2,1)}, u32[]{:S(2)}, u32[]{:S(2)}) collective-permute-start(bf16[352,1024]{1,0:T(8,128)(2,1)} %bitcast.43), channel_id=1, source_target_pairs={{0,1},{4,5},{8,9},{12,13},{16,17},{20,21},{24,25},{28,29}} | collective-permute-start | bytes 2162696 | tf_op jit(solution)/shard_map/ppermute | solution.py:438
  196.9 10.9 %collective-permute-done.23 = bf16[256,256]{1,0:T(8,128)(2,1)S(1)} collective-permute-done((bf16[256,256]{1,0:T(8,128)(2,1)S(1)}, bf16[256,256]{1,0:T(8,128)(2,1)S(1)}, u32[]{:S(2)}, u32[]{:S(2)}) %collective-permute-start.23) | collective-permute-done | bytes 131104 | tf_op jit(solution)/shard_map/ppermute | solution.py:414
  210.6 5.4 %collective-permute-done.25 = bf16[256,256]{1,0:T(8,128)(2,1)S(1)} collective-permute-done((bf16[256,256]{1,0:T(8,128)(2,1)S(1)}, bf16[256,256]{1,0:T(8,128)(2,1)S(1)}, u32[]{:S(2)}, u32[]{:S(2)}) %collective-permute-start.25) | collective-permute-done | bytes 131104 | tf_op jit(solution)/shard_map/ppermute | solution.py:414
  227.6 13.7 %shard_map.155 = (bf16[1024,256]{1,0:T(8,128)(2,1)S(1)}, bf16[1024,256]{1,0:T(8,128)(2,1)S(1)}, bf16[1024,256]{1,0:T(8,128)(2,1)S(1)}) custom-call(s32[1]{0:T(128)} %bitcast.3.refs_0_, bf16[1024,256]{1,0:T(8,128)(2,1)S(1)} %copy-done.11, bf16[1024,256]{1,0:T(8,128)(2,1)S(1)} %copy-done.13, bf16[1024,256]{1,0:T(8,128)(2,1)S(1)} %copy-done.15, ...), custom_call_target="tpu_custom_call" | custom-call | bytes 1048576 | tf_op jit(solution)/shard_map/pallas_call | solution.py:245
  253.0 5.4 %collective-permute-start.33 = (bf16[352,1024]{1,0:T(8,128)(2,1)}, bf16[352,1024]{1,0:T(8,128)(2,1)}, u32[]{:S(2)}, u32[]{:S(2)}) collective-permute-start(bf16[352,1024]{1,0:T(8,128)(2,1)} %add_convert_fusion.1), channel_id=1, source_target_pairs={{0,1},{1,2},{2,3},{4,5},{5,6},{6,7},{8,9},{9,10},{10,11},{12,13},{... | collective-permute-start | bytes 2162696 | tf_op jit(solution)/shard_map/ppermute | solution.py:438
  265.5 4.5 %multiply_reduce_fusion = (f32[1024]{0:T(1024)S(1)}, bf16[1024,1024]{1,0:T(8,128)(2,1)}) fusion(bf16[1024,1024]{1,0:T(8,128)(2,1)S(1)} %copy-done.7, bf16[1024,256]{1,0:T(8,128)(2,1)S(1)} %get-tuple-element.100, bf16[3,1024,256]{2,1,0:T(8,128)(2,1)S(1)} %copy-done, f32[1024,1024]{1,0:T(8,128)S(1)} %fusion.47, f32[1024,1024]{1,0:T(8,128)} %fusion.45), kind=kOutput, calls=%fused_computation | convolution fusion | flops 543161344 | bytes 13635584 | tf_op jit(solution)/shard_map/dot_general | solution.py:34
  271.6 6.5 %collective-permute-done.33 = bf16[352,1024]{1,0:T(8,128)(2,1)} collective-permute-done((bf16[352,1024]{1,0:T(8,128)(2,1)}, bf16[352,1024]{1,0:T(8,128)(2,1)}, u32[]{:S(2)}, u32[]{:S(2)}) %collective-permute-start.33) | collective-permute-done | bytes 720928 | tf_op jit(solution)/shard_map/ppermute | solution.py:438
  283.2 8.4 %collective-permute-start.42 = (f32[2,1024]{1,0:T(2,128)S(1)}, f32[2,1024]{1,0:T(2,128)S(1)}, u32[]{:S(2)}, u32[]{:S(2)}) collective-permute-start(f32[2,1024]{1,0:T(2,128)S(1)} %fusion.68), channel_id=1, source_target_pairs={{0,2},{1,3},{2,0},{3,1},{4,6},{5,7},{6,4},{7,5},{8,10},{9,11},{10,... | collective-permute-start | bytes 24584 | tf_op jit(solution)/shard_map/ppermute | solution.py:418
  312.6 7.5 %collective-permute-done.35 = bf16[256,1024]{1,0:T(8,128)(2,1)S(1)} collective-permute-done((bf16[256,1024]{1,0:T(8,128)(2,1)S(1)}, bf16[256,1024]{1,0:T(8,128)(2,1)S(1)}, u32[]{:S(2)}, u32[]{:S(2)}) %collective-permute-start.35) | collective-permute-done | bytes 524320 | tf_op jit(solution)/shard_map/ppermute | solution.py:438
  320.5 4.5 %collective-permute-start.36 = (bf16[256,1024]{1,0:T(8,128)(2,1)S(1)}, bf16[256,1024]{1,0:T(8,128)(2,1)S(1)}, u32[]{:S(2)}, u32[]{:S(2)}) collective-permute-start(bf16[256,1024]{1,0:T(8,128)(2,1)S(1)} %get-tuple-element.129), channel_id=1, source_target_pairs={{0,1},{1,2},{4,5},{5,6},{8,9},{9,10},{12,13},{13,14},{16,17},{17,1... | collective-permute-start | bytes 1572872 | tf_op jit(solution)/shard_map/ppermute | solution.py:438
  325.9 5.8 %collective-permute-done.36 = bf16[256,1024]{1,0:T(8,128)(2,1)S(1)} collective-permute-done((bf16[256,1024]{1,0:T(8,128)(2,1)S(1)}, bf16[256,1024]{1,0:T(8,128)(2,1)S(1)}, u32[]{:S(2)}, u32[]{:S(2)}) %collective-permute-start.36) | collective-permute-done | bytes 524320 | tf_op jit(solution)/shard_map/ppermute | solution.py:438
  332.1 7.4 %collective-permute-start.37 = (bf16[256,1024]{1,0:T(8,128)(2,1)S(1)}, bf16[256,1024]{1,0:T(8,128)(2,1)S(1)}, u32[]{:S(2)}, u32[]{:S(2)}) collective-permute-start(bf16[256,1024]{1,0:T(8,128)(2,1)S(1)} %get-tuple-element.127), channel_id=1, source_target_pairs={{0,1},{1,2},{2,3},{4,5},{5,6},{6,7},{8,9},{9,10},{10,11},{12,13},{... | collective-permute-start | bytes 1572872 | tf_op jit(solution)/shard_map/ppermute | solution.py:438
  340.8 5.3 %collective-permute-done.37 = bf16[256,1024]{1,0:T(8,128)(2,1)S(1)} collective-permute-done((bf16[256,1024]{1,0:T(8,128)(2,1)S(1)}, bf16[256,1024]{1,0:T(8,128)(2,1)S(1)}, u32[]{:S(2)}, u32[]{:S(2)}) %collective-permute-start.37) | collective-permute-done | bytes 524320 | tf_op jit(solution)/shard_map/ppermute | solution.py:438
  353.2 7.8 %shard_map.156 = (f32[2,656,1024]{2,1,0:T(8,128)}, f32[656,1024]{1,0:T(8,128)}, f32[8,32,1024]{2,1,0:T(8,128)}, f32[3,8,4,32,256]{4,3,2,1,0:T(8,128)}) custom-call(bf16[8,400,1024]{2,1,0:T(8,128)(2,1)} %bitcast.238), custom_call_target="tpu_custom_call" | custom-call | bytes 18874368 | tf_op jit(solution)/shard_map/pallas_call | solution.py:391
  (286 shorter events, 165.5 us)
Async XLA Ops:
  7.2 129.4 %all-gather.7.cloned.1.call-start = ((), (), s32[]{:S(2)}) async-start(), calls=%async_computation.4 | async-start | bytes 2703360 | tf_op jit(solution)/shard_map/all_gather | solution.py:543
  15.3 15.6 %collective-permute-start.2 = (bf16[88,1024]{1,0:T(8,128)(2,1)}, bf16[88,1024]{1,0:T(8,128)(2,1)}, u32[]{:S(2)}, u32[]{:S(2)}) collective-permute-start(bf16[88,1024]{1,0:T(8,128)(2,1)} %get-tuple-element.146), channel_id=1, source_target_pairs={{0,2},{1,3},{2,0},{3,1},{4,6},{5,7},{6,4},{7,5},{8,10},{9,11},{10,... | collective-permute-start | bytes 540680 | tf_op jit(solution)/shard_map/ppermute | solution.py:414
  15.3 15.6 %collective-permute-start.3 = (bf16[88,1024]{1,0:T(8,128)(2,1)}, bf16[88,1024]{1,0:T(8,128)(2,1)}, u32[]{:S(2)}, u32[]{:S(2)}) collective-permute-start(bf16[88,1024]{1,0:T(8,128)(2,1)} %get-tuple-element.146), channel_id=1, source_target_pairs={{0,1},{1,2},{2,3},{3,0},{4,5},{5,6},{6,7},{7,4},{8,9},{9,10},{10,1... | collective-permute-start | bytes 540680 | tf_op jit(solution)/shard_map/ppermute | solution.py:414
  32.9 103.7 %all-gather.9.cloned.1.call-start = ((), (), s32[]{:S(2)}) async-start(), calls=%async_computation.5 | async-start | bytes 6389760 | tf_op jit(solution)/shard_map/all_gather | solution.py:547
  35.7 13.5 %collective-permute-start.4 = (bf16[208,1024]{1,0:T(8,128)(2,1)}, bf16[208,1024]{1,0:T(8,128)(2,1)S(1)}, u32[]{:S(2)}, u32[]{:S(2)}) collective-permute-start(bf16[208,1024]{1,0:T(8,128)(2,1)} %pad_maximum_fusion.12), channel_id=1, source_target_pairs={{1,0},{2,1},{3,2},{5,4},{6,5},{7,6},{9,8},{10,9},{11,10},{13,12},{... | collective-permute-start | bytes 1277960 | tf_op jit(solution)/shard_map/ppermute | solution.py:425
  51.0 12.1 %collective-permute-start.7 = (bf16[208,1024]{1,0:T(8,128)(2,1)S(1)}, bf16[208,1024]{1,0:T(8,128)(2,1)S(1)}, u32[]{:S(2)}, u32[]{:S(2)}) collective-permute-start(bf16[208,1024]{1,0:T(8,128)(2,1)S(1)} %collective-permute-done.6), channel_id=1, source_target_pairs={{2,3},{6,7},{10,11},{14,15},{18,19},{22,23},{26,27},{30,31}} | collective-permute-start | bytes 1277960 | tf_op jit(solution)/shard_map/ppermute | solution.py:424
  73.8 184.7 %reduce-scatter.3.cloned.1.call-start = ((), (), s32[]{:S(2)}) async-start(), calls=%async_computation.2 | async-start | bytes 7208960 | tf_op jit(solution)/shard_map/reduce_scatter | solution.py:610
  75.4 12.3 %collective-permute-start.13 = (bf16[256,1024]{1,0:T(8,128)(2,1)S(1)}, bf16[256,1024]{1,0:T(8,128)(2,1)S(1)}, u32[]{:S(2)}, u32[]{:S(2)}) collective-permute-start(bf16[256,1024]{1,0:T(8,128)(2,1)S(1)} %fusion.18.refs_1_), channel_id=1, source_target_pairs={{1,0},{2,1},{3,2},{5,4},{6,5},{7,6},{9,8},{10,9},{11,10},{13,12},{... | collective-permute-start | bytes 1572872 | tf_op jit(solution)/shard_map/ppermute | solution.py:425
  76.7 27.4 %collective-permute-start = (bf16[256,1024]{1,0:T(8,128)(2,1)}, bf16[256,1024]{1,0:T(8,128)(2,1)}, u32[]{:S(2)}, u32[]{:S(2)}) collective-permute-start(bf16[256,1024]{1,0:T(8,128)(2,1)} %bitcast), channel_id=1, source_target_pairs={{0,4},{4,0},{1,5},{5,1},{2,6},{6,2},{3,7},{7,3},{8,12},{12,8},{9,1... | collective-permute-start | bytes 1572872 | tf_op jit(solution)/shard_map/ppermute | solution.py:418
  92.0 14.7 %collective-permute-start.12 = (bf16[256,1024]{1,0:T(8,128)(2,1)}, bf16[256,1024]{1,0:T(8,128)(2,1)}, u32[]{:S(2)}, u32[]{:S(2)}) collective-permute-start(bf16[256,1024]{1,0:T(8,128)(2,1)} %collective-permute-done.11.refs_3_), channel_id=1, source_target_pairs={{2,3},{6,7},{10,11},{14,15},{18,19},{22,23},{26,27},{30,31}} | collective-permute-start | bytes 1572872 | tf_op jit(solution)/shard_map/ppermute | solution.py:424
  171.3 134.4 %reduce-scatter.5.cloned.1.call-start = ((), (), s32[]{:S(2)}) async-start(), calls=%async_computation.3 | async-start | bytes 2129920 | tf_op jit(solution)/shard_map/reduce_scatter | solution.py:665
  184.4 31.6 %collective-permute-start.27 = (bf16[352,1024]{1,0:T(8,128)(2,1)}, bf16[352,1024]{1,0:T(8,128)(2,1)}, u32[]{:S(2)}, u32[]{:S(2)}) collective-permute-start(bf16[352,1024]{1,0:T(8,128)(2,1)} %bitcast.43), channel_id=1, source_target_pairs={{0,1},{4,5},{8,9},{12,13},{16,17},{20,21},{24,25},{28,29}} | collective-permute-start | bytes 2162696 | tf_op jit(solution)/shard_map/ppermute | solution.py:438
  189.2 26.8 %collective-permute-start.28 = (bf16[352,1024]{1,0:T(8,128)(2,1)}, bf16[352,1024]{1,0:T(8,128)(2,1)}, u32[]{:S(2)}, u32[]{:S(2)}) collective-permute-start(bf16[352,1024]{1,0:T(8,128)(2,1)} %bitcast.44), channel_id=1, source_target_pairs={{3,2},{7,6},{11,10},{15,14},{19,18},{23,22},{27,26},{31,30}} | collective-permute-start | bytes 2162696 | tf_op jit(solution)/shard_map/ppermute | solution.py:438
  194.2 26.0 %collective-permute-start.29 = (bf16[2,128,1024]{2,1,0:T(8,128)(2,1)}, bf16[2,128,1024]{2,1,0:T(8,128)(2,1)}, u32[]{:S(2)}, u32[]{:S(2)}) collective-permute-start(bf16[2,128,1024]{2,1,0:T(8,128)(2,1)} %dynamic-slice_bitcast_fusion.1), channel_id=1, source_target_pairs={{0,16},{8,24},{16,0},{24,8},{1,17},{9,25},{17,1},{25,9},{2,18},{10... | collective-permute-start | bytes 1572872 | tf_op jit(solution)/shard_map/ppermute | solution.py:418
  196.9 13.7 %collective-permute-start.24 = (bf16[256,256]{1,0:T(8,128)(2,1)S(1)}, bf16[256,256]{1,0:T(8,128)(2,1)S(1)}, u32[]{:S(2)}, u32[]{:S(2)}) collective-permute-start(bf16[256,256]{1,0:T(8,128)(2,1)S(1)} %get-tuple-element.167), channel_id=1, source_target_pairs={{0,2},{1,3},{2,0},{3,1},{4,6},{5,7},{6,4},{7,5},{8,10},{9,11},{10,... | collective-permute-start | bytes 393224 | tf_op jit(solution)/shard_map/ppermute | solution.py:414
  221.5 25.7 %collective-permute-start.32 = (bf16[128,1024]{1,0:T(8,128)(2,1)S(1)}, bf16[128,1024]{1,0:T(8,128)(2,1)S(1)}, u32[]{:S(2)}, u32[]{:S(2)}) collective-permute-start(bf16[128,1024]{1,0:T(8,128)(2,1)S(1)} %dynamic-slice_bitcast_fusion.4), channel_id=1, source_target_pairs={{0,8},{8,0},{16,24},{24,16},{1,9},{9,1},{17,25},{25,17},{2,10},{10... | collective-permute-start | bytes 786440 | tf_op jit(solution)/shard_map/ppermute | solution.py:418
  225.1 22.1 %collective-permute-start.30 = (bf16[352,1024]{1,0:T(8,128)(2,1)S(1)}, bf16[352,1024]{1,0:T(8,128)(2,1)S(1)}, u32[]{:S(2)}, u32[]{:S(2)}) collective-permute-start(bf16[352,1024]{1,0:T(8,128)(2,1)S(1)} %get-tuple-element.164), channel_id=1, source_target_pairs={{0,1},{1,2},{4,5},{5,6},{8,9},{9,10},{12,13},{13,14},{16,17},{17,1... | collective-permute-start | bytes 2162696 | tf_op jit(solution)/shard_map/ppermute | solution.py:438
  226.6 20.6 %collective-permute-start.31 = (bf16[352,1024]{1,0:T(8,128)(2,1)S(1)}, bf16[352,1024]{1,0:T(8,128)(2,1)S(1)}, u32[]{:S(2)}, u32[]{:S(2)}) collective-permute-start(bf16[352,1024]{1,0:T(8,128)(2,1)S(1)} %get-tuple-element.163), channel_id=1, source_target_pairs={{2,1},{3,2},{6,5},{7,6},{10,9},{11,10},{14,13},{15,14},{18,17},{19... | collective-permute-start | bytes 2162696 | tf_op jit(solution)/shard_map/ppermute | solution.py:438
  249.5 22.1 %collective-permute-start.34 = (bf16[352,1024]{1,0:T(8,128)(2,1)}, bf16[352,1024]{1,0:T(8,128)(2,1)}, u32[]{:S(2)}, u32[]{:S(2)}) collective-permute-start(bf16[352,1024]{1,0:T(8,128)(2,1)} %add_convert_fusion), channel_id=1, source_target_pairs={{1,0},{2,1},{3,2},{5,4},{6,5},{7,6},{9,8},{10,9},{11,10},{13,12},{... | collective-permute-start | bytes 2162696 | tf_op jit(solution)/shard_map/ppermute | solution.py:438
  253.0 25.1 %collective-permute-start.33 = (bf16[352,1024]{1,0:T(8,128)(2,1)}, bf16[352,1024]{1,0:T(8,128)(2,1)}, u32[]{:S(2)}, u32[]{:S(2)}) collective-permute-start(bf16[352,1024]{1,0:T(8,128)(2,1)} %add_convert_fusion.1), channel_id=1, source_target_pairs={{0,1},{1,2},{2,3},{4,5},{5,6},{6,7},{8,9},{9,10},{10,11},{12,13},{... | collective-permute-start | bytes 2162696 | tf_op jit(solution)/shard_map/ppermute | solution.py:438
  263.6 89.7 %all-gather.11.cloned.1.call-start = ((), (), s32[]{:S(2)}) async-start(), calls=%async_computation.6 | async-start | bytes 7372800 | tf_op jit(solution)/shard_map/all_gather | solution.py:699
  271.5 20.0 %collective-permute-start.45 = (bf16[3,4,128,256]{3,2,0,1:T(8,128)(2,1)S(1)}, bf16[3,4,128,256]{3,2,0,1:T(8,128)(2,1)S(1)}, u32[]{:S(2)}, u32[]{:S(2)}) collective-permute-start(bf16[3,4,128,256]{3,2,0,1:T(8,128)(2,1)S(1)} %bitcast.257), channel_id=1, source_target_pairs={{0,4},{4,0},{1,5},{5,1},{2,6},{6,2},{3,7},{7,3},{8,12},{12,8},{9,1... | collective-permute-start | bytes 2359304 | tf_op jit(solution)/shard_map/ppermute | solution.py:418
  307.8 12.3 %collective-permute-start.35 = (bf16[256,1024]{1,0:T(8,128)(2,1)S(1)}, bf16[256,1024]{1,0:T(8,128)(2,1)S(1)}, u32[]{:S(2)}, u32[]{:S(2)}) collective-permute-start(bf16[256,1024]{1,0:T(8,128)(2,1)S(1)} %get-tuple-element.131), channel_id=1, source_target_pairs={{0,1},{4,5},{8,9},{12,13},{16,17},{20,21},{24,25},{28,29}} | collective-permute-start | bytes 1572872 | tf_op jit(solution)/shard_map/ppermute | solution.py:438
  332.1 14.1 %collective-permute-start.37 = (bf16[256,1024]{1,0:T(8,128)(2,1)S(1)}, bf16[256,1024]{1,0:T(8,128)(2,1)S(1)}, u32[]{:S(2)}, u32[]{:S(2)}) collective-permute-start(bf16[256,1024]{1,0:T(8,128)(2,1)S(1)} %get-tuple-element.127), channel_id=1, source_target_pairs={{0,1},{1,2},{2,3},{4,5},{5,6},{6,7},{8,9},{9,10},{10,11},{12,13},{... | collective-permute-start | bytes 1572872 | tf_op jit(solution)/shard_map/ppermute | solution.py:438
  (76 other events, 606.7 us)
Sparse Core Ops, SparseCore 0:
  33.0 36.2 all-gather.6
  74.0 58.5 all-gather.8
  171.4 76.8 reduce-scatter.2
  263.7 37.2 reduce-scatter.4
  307.8 45.3 all-gather.10

commit v8 on v7

--- a/solution.py
+++ b/solution.py
@@ -262,9 +262,11 @@
 
 def feed_kernel(
     sizes, n_ref, c_ref, own_ref, gate_ref, rest_ref,
-    dgu_ref, dd_ref, in_ref, in_other_ref, out_ref, out_other_ref, in_held, out_held,
+    dgu_ref, *refs,
 ):
     piece, out_piece, ranks, group, steps = sizes
+    dd_refs, refs = refs[:ranks], refs[ranks:]
+    in_ref, in_other_ref, out_ref, out_other_ref, in_held, out_held = refs
     step = pl.program_id(0)
 
     def join(m, ref, first):
@@ -293,7 +295,7 @@
     dgu_ref[0, hidden:] = nn(up_grad, normed).astype(BF)
     down_grad = nn(hid, cot)
     for k in range(ranks):
-        dd_ref[k, 0] = down_grad[k * piece : (k + 1) * piece].astype(BF)
+        dd_refs[k][0] = down_grad[k * piece : (k + 1) * piece].astype(BF)
     in_part = tn(jnp.concatenate([gate_grad, up_grad]), jnp.concatenate([gate, up]))
     out_part = tn(hid, down)
 
@@ -325,7 +327,7 @@
     same = pl.BlockSpec((rows, width), lambda i: (0, 0))
     grads = [
         pl.BlockSpec((1, 2 * hidden, width), lambda i: (i, 0, 0)),
-        pl.BlockSpec((others + 1, 1, piece, width), lambda i: (0, i, 0, 0)),
+        *[pl.BlockSpec((1, piece, width), lambda i: (i, 0, 0))] * (others + 1),
     ]
     kept = pl.BlockSpec((half, width), lambda i: (0, 0))
     sizes = (piece, out_piece, others + 1, group, chips // group)
@@ -342,7 +344,7 @@
         out_specs=grads + [kept] * 4,
         out_shape=[
             jax.ShapeDtypeStruct((chips, 2 * hidden, width), BF),
-            jax.ShapeDtypeStruct((others + 1, chips, piece, width), BF),
+            *[jax.ShapeDtypeStruct((chips, piece, width), BF)] * (others + 1),
         ]
         + [
             jax.ShapeDtypeStruct((half, width), F32),
@@ -603,7 +605,7 @@
         normal_mlp, inverse_mlp = normalize(hidden_state)
         normed_mlp = (normal_mlp * gain_mlp).astype(BF)
         normed_pair = jnp.concatenate([normed_mlp, flip(normed_mlp, "core", 1, cores)])
-        gate_up_grad, down_grad, in_part, in_other, mlp_part, mlp_other = feed(
+        gate_up_grad, *down_grad, in_part, in_other, mlp_part, mlp_other = feed(
             normed_pair, cot_pair, own, gate_all, rest_all, piece, out_piece
         )
         gate_up_here = hold(
@@ -611,7 +613,7 @@
                 gate_up_grad.reshape(-1, width), "chip", scatter_dimension=0, tiled=True
             )
         )
-        down_sum = LineSum(down_grad.reshape(ranks, chips * piece, width), ranks)
+        down_sum = LineSum([g.reshape(chips * piece, width) for g in down_grad], ranks)
         down_sum.send()
         normed_mlp_grad = in_part + flip(in_other, "core", 1, cores).astype(F32)
         gain_mlp_part = jnp.sum(normed_mlp_grad * normal_mlp, axis=0)

time: 375 us -> 372 us (level)
    unnamed x94 -> x90, local copies, waits for them, and re-layouts: 7.93 us -> 7.9 us
  transfers between devices with their start and end apart: 53 -> 53, of which waited for: 29 -> 29; matrix products, arithmetic and copies ran while one was open for 15% -> 14% of each run, Pallas kernels for 7% -> 7%
where the time goes in v8:
time: 372 us; the launch traced here: 367 us
  waiting for transfers between devices  135 us (36%)
  starting transfers between devices  83.1 us (22%)
  Pallas kernels  57.8 us (16%)
  other arithmetic  41.6 us (11%)
  local copies, waits for them, and re-layouts  17.2 us (5%)
  between operations  16.1 us (4%)
  matrix products  16 us (4%)
    ppermute x6, waiting for transfers between devices, relay_ranks(): lax.ppermute(downs[-1], 'tensor', [(z, z - 1) for z in range(1, count - s...  35.8 us
    ppermute x9, waiting for transfers between devices, shift(): lax.ppermute(value, 'tensor', [(i, (i + by) % count) for i in range(count)])  34 us
    ppermute x6, starting transfers between devices, send(): lax.ppermute(self.up, 'tensor', up)  27.8 us
    ppermute x6, waiting for transfers between devices, send(): lax.ppermute(self.up, 'tensor', up)  25.3 us
    pallas_call x1, Pallas kernels, feed(): pl.pallas_call(lambda *refs: feed_kernel(sizes, *refs), grid=(chips // gr...  22.8 us
    ppermute x15, waiting for transfers between devices, flip(): return lax.ppermute(value, axis, [(i, i ^ bit) for i in range(count)])  20.6 us
    ppermute x15, starting transfers between devices, flip(): return lax.ppermute(value, axis, [(i, i ^ bit) for i in range(count)])  20.4 us
    ppermute x6, waiting for transfers between devices, relay_ranks(): lax.ppermute(ups[-1], 'tensor', [(z, z + 1) for z in range(step - 1, coun...  13.7 us
  transfers between devices with their start and end apart: 53, of which 29 were waited for; matrix products, arithmetic and copies ran while one was open for 14% of the time, Pallas kernels for 7%

profile of v8, /device:TPU:0, one launch (start us, length us, event | category | flops | bytes accessed | tf_op | source)
XLA Modules:
  0.0 366.5 jit_solution(9727667707287246537)
XLA Ops:
  10.3 5.0 %collective-permute-start.1 = (bf16[88,1024]{1,0:T(8,128)(2,1)}, bf16[88,1024]{1,0:T(8,128)(2,1)}, u32[]{:S(2)}, u32[]{:S(2)}) collective-permute-start(bf16[88,1024]{1,0:T(8,128)(2,1)} %get-tuple-element.148), channel_id=1, source_target_pairs={{0,3},{1,0},{2,1},{3,2},{4,7},{5,4},{6,5},{7,6},{8,11},{9,8},{10,9... | collective-permute-start | bytes 540680 | tf_op jit(solution)/shard_map/ppermute | solution.py:416
  20.6 10.3 %collective-permute-done.2 = bf16[88,1024]{1,0:T(8,128)(2,1)} collective-permute-done((bf16[88,1024]{1,0:T(8,128)(2,1)}, bf16[88,1024]{1,0:T(8,128)(2,1)}, u32[]{:S(2)}, u32[]{:S(2)}) %collective-permute-start.2) | collective-permute-done | bytes 180256 | tf_op jit(solution)/shard_map/ppermute | solution.py:416
  37.0 7.5 %collective-permute-done.5 = bf16[208,1024]{1,0:T(8,128)(2,1)S(1)} collective-permute-done((bf16[208,1024]{1,0:T(8,128)(2,1)}, bf16[208,1024]{1,0:T(8,128)(2,1)S(1)}, u32[]{:S(2)}, u32[]{:S(2)}) %collective-permute-start.5) | collective-permute-done | bytes 426016 | tf_op jit(solution)/shard_map/ppermute | solution.py:426
  51.7 9.6 %collective-permute-done.8 = bf16[208,1024]{1,0:T(8,128)(2,1)S(1)} collective-permute-done((bf16[208,1024]{1,0:T(8,128)(2,1)S(1)}, bf16[208,1024]{1,0:T(8,128)(2,1)S(1)}, u32[]{:S(2)}, u32[]{:S(2)}) %collective-permute-start.8) | collective-permute-done | bytes 426016 | tf_op jit(solution)/shard_map/ppermute | solution.py:427
  63.2 9.3 %collective-permute-done.9 = bf16[208,1024]{1,0:T(8,128)(2,1)S(1)} collective-permute-done((bf16[208,1024]{1,0:T(8,128)(2,1)S(1)}, bf16[208,1024]{1,0:T(8,128)(2,1)S(1)}, u32[]{:S(2)}, u32[]{:S(2)}) %collective-permute-start.9) | collective-permute-done | bytes 426016 | tf_op jit(solution)/shard_map/ppermute | solution.py:427
  77.4 6.2 %collective-permute-done.10.refs_2_ = bf16[256,1024]{1,0:T(8,128)(2,1)S(1)} collective-permute-done((bf16[256,1024]{1,0:T(8,128)(2,1)S(1)}, bf16[256,1024]{1,0:T(8,128)(2,1)S(1)}, u32[]{:S(2)}, u32[]{:S(2)}) %collective-permute-start.10) | collective-permute-done | bytes 524320 | tf_op jit(solution)/shard_map/ppermute | solution.py:426
  93.7 5.9 %collective-permute-done.14.refs_6_ = bf16[256,1024]{1,0:T(8,128)(2,1)} collective-permute-done((bf16[256,1024]{1,0:T(8,128)(2,1)S(1)}, bf16[256,1024]{1,0:T(8,128)(2,1)}, u32[]{:S(2)}, u32[]{:S(2)}) %collective-permute-start.14) | collective-permute-done | bytes 524320 | tf_op jit(solution)/shard_map/ppermute | solution.py:427
  111.0 4.8 %shard_map.152 = (bf16[1024,1024]{1,0:T(8,128)(2,1)S(1)}, bf16[1024,256]{1,0:T(8,128)(2,1)S(1)}, bf16[1024,256]{1,0:T(8,128)(2,1)S(1)}, bf16[1024,256]{1,0:T(8,128)(2,1)S(1)}) custom-call(s32[1]{0:T(128)} %bitcast.4.refs_0_, bf16[256,1024]{1,0:T(8,128)(2,1)S(1)} %fusion.18.refs_1_, bf16[256,1024]{1,0:T(8,128)(2,1)S(1)} %collective-permute-done.10.refs_2_, ...), custom_call_target="tpu_custom_call" | custom-call | flops 1610612736 | bytes 9437184 | tf_op jit(solution)/shard_map/pallas_call | solution.py:94
  117.1 8.9 %shard_map.153 = (bf16[1024,256]{1,0:T(8,128)(2,1)S(1)}, f32[2,2,896]{2,1,0:T(2,128)S(1)}, bf16[1024,256]{1,0:T(8,128)(2,1)S(1)}, bf16[1024,256]{1,0:T(8,128)(2,1)S(1)}, bf16[1024,256]{1,0:T(8,128)(2,1)S(1)}) custom-call(s32[1]{0:T(128)} %bitcast.3.refs_0_, bf16[1024,256]{1,0:T(8,128)(2,1)S(1)} %get-tuple-element.69.refs_1_, ...), custom_call_target="tpu_custom_call" | custom-call | flops 1644167168 | bytes 2097152 | tf_op jit(solution)/shard_map/pallas_call | solution.py:173
  148.6 22.8 %shard_map.154 = (bf16[4,704,1024]{2,1,0:T(8,128)(2,1)}, bf16[4,88,1024]{2,1,0:T(8,128)(2,1)}, bf16[4,88,1024]{2,1,0:T(8,128)(2,1)}, bf16[4,88,1024]{2,1,0:T(8,1...) custom-call(bf16[512,1024]{1,0:T(8,128)(2,1)} %pad_maximum_fusion.7., ...), custom_call_target="tpu_custom_call" | custom-call | flops 13287555072 | bytes 26214400 | tf_op jit(solution)/shard_map/pallas_call | solution.py:334
  182.0 4.7 %collective-permute-start.27 = (bf16[352,1024]{1,0:T(8,128)(2,1)}, bf16[352,1024]{1,0:T(8,128)(2,1)}, u32[]{:S(2)}, u32[]{:S(2)}) collective-permute-start(bf16[352,1024]{1,0:T(8,128)(2,1)} %bitcast.260), channel_id=1, source_target_pairs={{0,1},{4,5},{8,9},{12,13},{16,17},{20,21},{24,25},{28,29}} | collective-permute-start | bytes 2162696 | tf_op jit(solution)/shard_map/ppermute | solution.py:440
  195.8 9.6 %collective-permute-done.23 = bf16[256,256]{1,0:T(8,128)(2,1)S(1)} collective-permute-done((bf16[256,256]{1,0:T(8,128)(2,1)S(1)}, bf16[256,256]{1,0:T(8,128)(2,1)S(1)}, u32[]{:S(2)}, u32[]{:S(2)}) %collective-permute-start.23) | collective-permute-done | bytes 131104 | tf_op jit(solution)/shard_map/ppermute | solution.py:416
  208.1 5.4 %collective-permute-done.25 = bf16[256,256]{1,0:T(8,128)(2,1)S(1)} collective-permute-done((bf16[256,256]{1,0:T(8,128)(2,1)S(1)}, bf16[256,256]{1,0:T(8,128)(2,1)S(1)}, u32[]{:S(2)}, u32[]{:S(2)}) %collective-permute-start.25) | collective-permute-done | bytes 131104 | tf_op jit(solution)/shard_map/ppermute | solution.py:416
  213.5 5.7 %collective-permute-done.29 = bf16[2,128,1024]{2,1,0:T(8,128)(2,1)} collective-permute-done((bf16[2,128,1024]{2,1,0:T(8,128)(2,1)}, bf16[2,128,1024]{2,1,0:T(8,128)(2,1)}, u32[]{:S(2)}, u32[]{:S(2)}) %collective-permute-start.29) | collective-permute-done | bytes 524320 | tf_op jit(solution)/shard_map/ppermute | solution.py:420
  226.8 13.7 %shard_map.155 = (bf16[1024,256]{1,0:T(8,128)(2,1)S(1)}, bf16[1024,256]{1,0:T(8,128)(2,1)S(1)}, bf16[1024,256]{1,0:T(8,128)(2,1)S(1)}) custom-call(s32[1]{0:T(128)} %bitcast.3.refs_0_, bf16[1024,256]{1,0:T(8,128)(2,1)S(1)} %copy-done.11, bf16[1024,256]{1,0:T(8,128)(2,1)S(1)} %copy-done.13, bf16[1024,256]{1,0:T(8,128)(2,1)S(1)} %copy-done.15, ...), custom_call_target="tpu_custom_call" | custom-call | bytes 1048576 | tf_op jit(solution)/shard_map/pallas_call | solution.py:245
  250.0 5.4 %collective-permute-start.33 = (bf16[352,1024]{1,0:T(8,128)(2,1)}, bf16[352,1024]{1,0:T(8,128)(2,1)}, u32[]{:S(2)}, u32[]{:S(2)}) collective-permute-start(bf16[352,1024]{1,0:T(8,128)(2,1)} %add_convert_fusion.1), channel_id=1, source_target_pairs={{0,1},{1,2},{2,3},{4,5},{5,6},{6,7},{8,9},{9,10},{10,11},{12,13},{... | collective-permute-start | bytes 2162696 | tf_op jit(solution)/shard_map/ppermute | solution.py:440
  268.7 6.6 %collective-permute-done.33 = bf16[352,1024]{1,0:T(8,128)(2,1)} collective-permute-done((bf16[352,1024]{1,0:T(8,128)(2,1)}, bf16[352,1024]{1,0:T(8,128)(2,1)}, u32[]{:S(2)}, u32[]{:S(2)}) %collective-permute-start.33) | collective-permute-done | bytes 720928 | tf_op jit(solution)/shard_map/ppermute | solution.py:440
  280.3 8.3 %collective-permute-start.42 = (f32[2,1024]{1,0:T(2,128)S(1)}, f32[2,1024]{1,0:T(2,128)S(1)}, u32[]{:S(2)}, u32[]{:S(2)}) collective-permute-start(f32[2,1024]{1,0:T(2,128)S(1)} %fusion.68), channel_id=1, source_target_pairs={{0,2},{1,3},{2,0},{3,1},{4,6},{5,7},{6,4},{7,5},{8,10},{9,11},{10,... | collective-permute-start | bytes 24584 | tf_op jit(solution)/shard_map/ppermute | solution.py:420
  309.8 7.5 %collective-permute-done.35 = bf16[256,1024]{1,0:T(8,128)(2,1)S(1)} collective-permute-done((bf16[256,1024]{1,0:T(8,128)(2,1)S(1)}, bf16[256,1024]{1,0:T(8,128)(2,1)S(1)}, u32[]{:S(2)}, u32[]{:S(2)}) %collective-permute-start.35) | collective-permute-done | bytes 524320 | tf_op jit(solution)/shard_map/ppermute | solution.py:440
  317.7 4.5 %collective-permute-start.36 = (bf16[256,1024]{1,0:T(8,128)(2,1)S(1)}, bf16[256,1024]{1,0:T(8,128)(2,1)S(1)}, u32[]{:S(2)}, u32[]{:S(2)}) collective-permute-start(bf16[256,1024]{1,0:T(8,128)(2,1)S(1)} %get-tuple-element.131), channel_id=1, source_target_pairs={{0,1},{1,2},{4,5},{5,6},{8,9},{9,10},{12,13},{13,14},{16,17},{17,1... | collective-permute-start | bytes 1572872 | tf_op jit(solution)/shard_map/ppermute | solution.py:440
  323.1 5.8 %collective-permute-done.36 = bf16[256,1024]{1,0:T(8,128)(2,1)S(1)} collective-permute-done((bf16[256,1024]{1,0:T(8,128)(2,1)S(1)}, bf16[256,1024]{1,0:T(8,128)(2,1)S(1)}, u32[]{:S(2)}, u32[]{:S(2)}) %collective-permute-start.36) | collective-permute-done | bytes 524320 | tf_op jit(solution)/shard_map/ppermute | solution.py:440
  329.3 7.3 %collective-permute-start.37 = (bf16[256,1024]{1,0:T(8,128)(2,1)S(1)}, bf16[256,1024]{1,0:T(8,128)(2,1)S(1)}, u32[]{:S(2)}, u32[]{:S(2)}) collective-permute-start(bf16[256,1024]{1,0:T(8,128)(2,1)S(1)} %get-tuple-element.129), channel_id=1, source_target_pairs={{0,1},{1,2},{2,3},{4,5},{5,6},{6,7},{8,9},{9,10},{10,11},{12,13},{... | collective-permute-start | bytes 1572872 | tf_op jit(solution)/shard_map/ppermute | solution.py:440
  337.9 5.3 %collective-permute-done.37 = bf16[256,1024]{1,0:T(8,128)(2,1)S(1)} collective-permute-done((bf16[256,1024]{1,0:T(8,128)(2,1)S(1)}, bf16[256,1024]{1,0:T(8,128)(2,1)S(1)}, u32[]{:S(2)}, u32[]{:S(2)}) %collective-permute-start.37) | collective-permute-done | bytes 524320 | tf_op jit(solution)/shard_map/ppermute | solution.py:440
  350.2 7.8 %shard_map.156 = (f32[2,656,1024]{2,1,0:T(8,128)}, f32[656,1024]{1,0:T(8,128)}, f32[8,32,1024]{2,1,0:T(8,128)}, f32[3,8,4,32,256]{4,3,2,1,0:T(8,128)}) custom-call(bf16[8,400,1024]{2,1,0:T(8,128)(2,1)} %bitcast.238), custom_call_target="tpu_custom_call" | custom-call | bytes 18874368 | tf_op jit(solution)/shard_map/pallas_call | solution.py:393
  (281 shorter events, 162.5 us)
Async XLA Ops:
  7.2 129.4 %all-gather.7.cloned.1.call-start = ((), (), s32[]{:S(2)}) async-start(), calls=%async_computation.4 | async-start | bytes 2703360 | tf_op jit(solution)/shard_map/all_gather | solution.py:545
  15.3 15.6 %collective-permute-start.2 = (bf16[88,1024]{1,0:T(8,128)(2,1)}, bf16[88,1024]{1,0:T(8,128)(2,1)}, u32[]{:S(2)}, u32[]{:S(2)}) collective-permute-start(bf16[88,1024]{1,0:T(8,128)(2,1)} %get-tuple-element.148), channel_id=1, source_target_pairs={{0,2},{1,3},{2,0},{3,1},{4,6},{5,7},{6,4},{7,5},{8,10},{9,11},{10,... | collective-permute-start | bytes 540680 | tf_op jit(solution)/shard_map/ppermute | solution.py:416
  15.3 15.6 %collective-permute-start.3 = (bf16[88,1024]{1,0:T(8,128)(2,1)}, bf16[88,1024]{1,0:T(8,128)(2,1)}, u32[]{:S(2)}, u32[]{:S(2)}) collective-permute-start(bf16[88,1024]{1,0:T(8,128)(2,1)} %get-tuple-element.148), channel_id=1, source_target_pairs={{0,1},{1,2},{2,3},{3,0},{4,5},{5,6},{6,7},{7,4},{8,9},{9,10},{10,1... | collective-permute-start | bytes 540680 | tf_op jit(solution)/shard_map/ppermute | solution.py:416
  32.9 103.7 %all-gather.9.cloned.1.call-start = ((), (), s32[]{:S(2)}) async-start(), calls=%async_computation.5 | async-start | bytes 6389760 | tf_op jit(solution)/shard_map/all_gather | solution.py:549
  35.7 13.5 %collective-permute-start.4 = (bf16[208,1024]{1,0:T(8,128)(2,1)}, bf16[208,1024]{1,0:T(8,128)(2,1)S(1)}, u32[]{:S(2)}, u32[]{:S(2)}) collective-permute-start(bf16[208,1024]{1,0:T(8,128)(2,1)} %pad_maximum_fusion.12), channel_id=1, source_target_pairs={{1,0},{2,1},{3,2},{5,4},{6,5},{7,6},{9,8},{10,9},{11,10},{13,12},{... | collective-permute-start | bytes 1277960 | tf_op jit(solution)/shard_map/ppermute | solution.py:427
  51.0 12.1 %collective-permute-start.7 = (bf16[208,1024]{1,0:T(8,128)(2,1)S(1)}, bf16[208,1024]{1,0:T(8,128)(2,1)S(1)}, u32[]{:S(2)}, u32[]{:S(2)}) collective-permute-start(bf16[208,1024]{1,0:T(8,128)(2,1)S(1)} %collective-permute-done.6), channel_id=1, source_target_pairs={{2,3},{6,7},{10,11},{14,15},{18,19},{22,23},{26,27},{30,31}} | collective-permute-start | bytes 1277960 | tf_op jit(solution)/shard_map/ppermute | solution.py:426
  73.8 181.7 %reduce-scatter.3.cloned.1.call-start = ((), (), s32[]{:S(2)}) async-start(), calls=%async_computation.2 | async-start | bytes 7208960 | tf_op jit(solution)/shard_map/reduce_scatter | solution.py:612
  75.4 12.3 %collective-permute-start.13 = (bf16[256,1024]{1,0:T(8,128)(2,1)S(1)}, bf16[256,1024]{1,0:T(8,128)(2,1)S(1)}, u32[]{:S(2)}, u32[]{:S(2)}) collective-permute-start(bf16[256,1024]{1,0:T(8,128)(2,1)S(1)} %fusion.18.refs_1_), channel_id=1, source_target_pairs={{1,0},{2,1},{3,2},{5,4},{6,5},{7,6},{9,8},{10,9},{11,10},{13,12},{... | collective-permute-start | bytes 1572872 | tf_op jit(solution)/shard_map/ppermute | solution.py:427
  76.7 27.4 %collective-permute-start = (bf16[256,1024]{1,0:T(8,128)(2,1)}, bf16[256,1024]{1,0:T(8,128)(2,1)}, u32[]{:S(2)}, u32[]{:S(2)}) collective-permute-start(bf16[256,1024]{1,0:T(8,128)(2,1)} %bitcast), channel_id=1, source_target_pairs={{0,4},{4,0},{1,5},{5,1},{2,6},{6,2},{3,7},{7,3},{8,12},{12,8},{9,1... | collective-permute-start | bytes 1572872 | tf_op jit(solution)/shard_map/ppermute | solution.py:420
  92.0 14.7 %collective-permute-start.12 = (bf16[256,1024]{1,0:T(8,128)(2,1)}, bf16[256,1024]{1,0:T(8,128)(2,1)}, u32[]{:S(2)}, u32[]{:S(2)}) collective-permute-start(bf16[256,1024]{1,0:T(8,128)(2,1)} %collective-permute-done.11.refs_3_), channel_id=1, source_target_pairs={{2,3},{6,7},{10,11},{14,15},{18,19},{22,23},{26,27},{30,31}} | collective-permute-start | bytes 1572872 | tf_op jit(solution)/shard_map/ppermute | solution.py:426
  171.4 131.2 %reduce-scatter.5.cloned.1.call-start = ((), (), s32[]{:S(2)}) async-start(), calls=%async_computation.3 | async-start | bytes 2129920 | tf_op jit(solution)/shard_map/reduce_scatter | solution.py:667
  182.0 31.6 %collective-permute-start.27 = (bf16[352,1024]{1,0:T(8,128)(2,1)}, bf16[352,1024]{1,0:T(8,128)(2,1)}, u32[]{:S(2)}, u32[]{:S(2)}) collective-permute-start(bf16[352,1024]{1,0:T(8,128)(2,1)} %bitcast.260), channel_id=1, source_target_pairs={{0,1},{4,5},{8,9},{12,13},{16,17},{20,21},{24,25},{28,29}} | collective-permute-start | bytes 2162696 | tf_op jit(solution)/shard_map/ppermute | solution.py:440
  186.7 26.8 %collective-permute-start.28 = (bf16[352,1024]{1,0:T(8,128)(2,1)}, bf16[352,1024]{1,0:T(8,128)(2,1)}, u32[]{:S(2)}, u32[]{:S(2)}) collective-permute-start(bf16[352,1024]{1,0:T(8,128)(2,1)} %bitcast.259), channel_id=1, source_target_pairs={{3,2},{7,6},{11,10},{15,14},{19,18},{23,22},{27,26},{31,30}} | collective-permute-start | bytes 2162696 | tf_op jit(solution)/shard_map/ppermute | solution.py:440
  193.2 26.1 %collective-permute-start.29 = (bf16[2,128,1024]{2,1,0:T(8,128)(2,1)}, bf16[2,128,1024]{2,1,0:T(8,128)(2,1)}, u32[]{:S(2)}, u32[]{:S(2)}) collective-permute-start(bf16[2,128,1024]{2,1,0:T(8,128)(2,1)} %dynamic-slice_bitcast_fusion.1), channel_id=1, source_target_pairs={{0,16},{8,24},{16,0},{24,8},{1,17},{9,25},{17,1},{25,9},{2,18},{10... | collective-permute-start | bytes 1572872 | tf_op jit(solution)/shard_map/ppermute | solution.py:420
  195.7 12.4 %collective-permute-start.24 = (bf16[256,256]{1,0:T(8,128)(2,1)S(1)}, bf16[256,256]{1,0:T(8,128)(2,1)S(1)}, u32[]{:S(2)}, u32[]{:S(2)}) collective-permute-start(bf16[256,256]{1,0:T(8,128)(2,1)S(1)} %get-tuple-element.169), channel_id=1, source_target_pairs={{0,2},{1,3},{2,0},{3,1},{4,6},{5,7},{6,4},{7,5},{8,10},{9,11},{10,... | collective-permute-start | bytes 393224 | tf_op jit(solution)/shard_map/ppermute | solution.py:416
  220.6 25.7 %collective-permute-start.32 = (bf16[128,1024]{1,0:T(8,128)(2,1)S(1)}, bf16[128,1024]{1,0:T(8,128)(2,1)S(1)}, u32[]{:S(2)}, u32[]{:S(2)}) collective-permute-start(bf16[128,1024]{1,0:T(8,128)(2,1)S(1)} %dynamic-slice_bitcast_fusion.4), channel_id=1, source_target_pairs={{0,8},{8,0},{16,24},{24,16},{1,9},{9,1},{17,25},{25,17},{2,10},{10... | collective-permute-start | bytes 786440 | tf_op jit(solution)/shard_map/ppermute | solution.py:420
  224.3 22.0 %collective-permute-start.30 = (bf16[352,1024]{1,0:T(8,128)(2,1)S(1)}, bf16[352,1024]{1,0:T(8,128)(2,1)S(1)}, u32[]{:S(2)}, u32[]{:S(2)}) collective-permute-start(bf16[352,1024]{1,0:T(8,128)(2,1)S(1)} %get-tuple-element.166), channel_id=1, source_target_pairs={{0,1},{1,2},{4,5},{5,6},{8,9},{9,10},{12,13},{13,14},{16,17},{17,1... | collective-permute-start | bytes 2162696 | tf_op jit(solution)/shard_map/ppermute | solution.py:440
  225.8 20.5 %collective-permute-start.31 = (bf16[352,1024]{1,0:T(8,128)(2,1)S(1)}, bf16[352,1024]{1,0:T(8,128)(2,1)S(1)}, u32[]{:S(2)}, u32[]{:S(2)}) collective-permute-start(bf16[352,1024]{1,0:T(8,128)(2,1)S(1)} %get-tuple-element.165), channel_id=1, source_target_pairs={{2,1},{3,2},{6,5},{7,6},{10,9},{11,10},{14,13},{15,14},{18,17},{19... | collective-permute-start | bytes 2162696 | tf_op jit(solution)/shard_map/ppermute | solution.py:440
  247.5 21.1 %collective-permute-start.34 = (bf16[352,1024]{1,0:T(8,128)(2,1)}, bf16[352,1024]{1,0:T(8,128)(2,1)}, u32[]{:S(2)}, u32[]{:S(2)}) collective-permute-start(bf16[352,1024]{1,0:T(8,128)(2,1)} %add_convert_fusion), channel_id=1, source_target_pairs={{1,0},{2,1},{3,2},{5,4},{6,5},{7,6},{9,8},{10,9},{11,10},{13,12},{... | collective-permute-start | bytes 2162696 | tf_op jit(solution)/shard_map/ppermute | solution.py:440
  250.0 25.3 %collective-permute-start.33 = (bf16[352,1024]{1,0:T(8,128)(2,1)}, bf16[352,1024]{1,0:T(8,128)(2,1)}, u32[]{:S(2)}, u32[]{:S(2)}) collective-permute-start(bf16[352,1024]{1,0:T(8,128)(2,1)} %add_convert_fusion.1), channel_id=1, source_target_pairs={{0,1},{1,2},{2,3},{4,5},{5,6},{6,7},{8,9},{9,10},{10,11},{12,13},{... | collective-permute-start | bytes 2162696 | tf_op jit(solution)/shard_map/ppermute | solution.py:440
  260.6 89.6 %all-gather.11.cloned.1.call-start = ((), (), s32[]{:S(2)}) async-start(), calls=%async_computation.6 | async-start | bytes 7372800 | tf_op jit(solution)/shard_map/all_gather | solution.py:701
  268.6 20.0 %collective-permute-start.45 = (bf16[3,4,128,256]{3,2,0,1:T(8,128)(2,1)S(1)}, bf16[3,4,128,256]{3,2,0,1:T(8,128)(2,1)S(1)}, u32[]{:S(2)}, u32[]{:S(2)}) collective-permute-start(bf16[3,4,128,256]{3,2,0,1:T(8,128)(2,1)S(1)} %bitcast.257), channel_id=1, source_target_pairs={{0,4},{4,0},{1,5},{5,1},{2,6},{6,2},{3,7},{7,3},{8,12},{12,8},{9,1... | collective-permute-start | bytes 2359304 | tf_op jit(solution)/shard_map/ppermute | solution.py:420
  304.8 12.6 %collective-permute-start.35 = (bf16[256,1024]{1,0:T(8,128)(2,1)S(1)}, bf16[256,1024]{1,0:T(8,128)(2,1)S(1)}, u32[]{:S(2)}, u32[]{:S(2)}) collective-permute-start(bf16[256,1024]{1,0:T(8,128)(2,1)S(1)} %get-tuple-element.133), channel_id=1, source_target_pairs={{0,1},{4,5},{8,9},{12,13},{16,17},{20,21},{24,25},{28,29}} | collective-permute-start | bytes 1572872 | tf_op jit(solution)/shard_map/ppermute | solution.py:440
  329.3 13.9 %collective-permute-start.37 = (bf16[256,1024]{1,0:T(8,128)(2,1)S(1)}, bf16[256,1024]{1,0:T(8,128)(2,1)S(1)}, u32[]{:S(2)}, u32[]{:S(2)}) collective-permute-start(bf16[256,1024]{1,0:T(8,128)(2,1)S(1)} %get-tuple-element.129), channel_id=1, source_target_pairs={{0,1},{1,2},{2,3},{4,5},{5,6},{6,7},{8,9},{9,10},{10,11},{12,13},{... | collective-permute-start | bytes 1572872 | tf_op jit(solution)/shard_map/ppermute | solution.py:440
  (74 other events, 566.1 us)
Sparse Core Ops, SparseCore 0:
  33.0 36.2 all-gather.6
  74.0 58.5 all-gather.8
  171.6 76.9 reduce-scatter.2
  260.7 37.4 reduce-scatter.4
  304.8 45.3 all-gather.10

commit v9 on v8

--- a/solution.py
+++ b/solution.py
@@ -281,8 +281,10 @@
     up = join(1, rest_ref, 0)
     down = join(2, rest_ref, piece + out_piece)
     normed, cot = n_ref[...], c_ref[...]
-    gate_proj = nt(gate, normed)
-    up_proj = nt(up, normed)
+    hidden = ranks * piece
+    gate_up = jnp.concatenate([gate, up])
+    both = nt(gate_up, normed)
+    gate_proj, up_proj = both[:hidden], both[hidden:]
     hid_grad = nt(down, cot)
     cdf = 0.5 * (1.0 + lax.erf(gate_proj * (1.0 / math.sqrt(2.0))))
     pdf = jnp.exp(-0.5 * gate_proj * gate_proj) * (1.0 / math.sqrt(2.0 * math.pi))
@@ -290,13 +292,12 @@
     hid = (act * up_proj).astype(BF)
     gate_grad = (hid_grad * up_proj * (cdf + gate_proj * pdf)).astype(BF)
     up_grad = (hid_grad * act).astype(BF)
-    hidden = ranks * piece
-    dgu_ref[0, :hidden] = nn(gate_grad, normed).astype(BF)
-    dgu_ref[0, hidden:] = nn(up_grad, normed).astype(BF)
+    both_grad = jnp.concatenate([gate_grad, up_grad])
+    dgu_ref[0] = nn(both_grad, normed).astype(BF)
     down_grad = nn(hid, cot)
     for k in range(ranks):
         dd_refs[k][0] = down_grad[k * piece : (k + 1) * piece].astype(BF)
-    in_part = tn(jnp.concatenate([gate_grad, up_grad]), jnp.concatenate([gate, up]))
+    in_part = tn(both_grad, gate_up)
     out_part = tn(hid, down)
 
     @pl.when(step == 0)

time: 372 us -> 372 us (level)
  no operation moved by 1% of the time
where the time goes in v9:
time: 372 us; the launch traced here: 367 us
  waiting for transfers between devices  135 us (36%)
  starting transfers between devices  82.9 us (22%)
  Pallas kernels  58.1 us (16%)
  other arithmetic  41.6 us (11%)
  local copies, waits for them, and re-layouts  17.2 us (5%)
  between operations  16.1 us (4%)
  matrix products  16 us (4%)
    ppermute x6, waiting for transfers between devices, relay_ranks(): lax.ppermute(downs[-1], 'tensor', [(z, z - 1) for z in range(1, count - s...  35.8 us
    ppermute x9, waiting for transfers between devices, shift(): lax.ppermute(value, 'tensor', [(i, (i + by) % count) for i in range(count)])  34.1 us
    ppermute x6, starting transfers between devices, send(): lax.ppermute(self.up, 'tensor', up)  27.8 us
    ppermute x6, waiting for transfers between devices, send(): lax.ppermute(self.up, 'tensor', up)  25.2 us
    pallas_call x1, Pallas kernels, feed(): pl.pallas_call(lambda *refs: feed_kernel(sizes, *refs), grid=(chips // gr...  23 us
    ppermute x15, waiting for transfers between devices, flip(): return lax.ppermute(value, axis, [(i, i ^ bit) for i in range(count)])  20.6 us
    ppermute x15, starting transfers between devices, flip(): return lax.ppermute(value, axis, [(i, i ^ bit) for i in range(count)])  20.2 us
    pallas_call x1, Pallas kernels, attend_back(): pl.pallas_call(lambda *refs: attend_back_kernel(doc, *refs), grid=(pairs,...  13.7 us
  transfers between devices with their start and end apart: 53, of which 29 were waited for; matrix products, arithmetic and copies ran while one was open for 14% of the time, Pallas kernels for 7%

profile of v9, /device:TPU:0, one launch (start us, length us, event | category | flops | bytes accessed | tf_op | source)
XLA Modules:
  0.0 366.7 jit_solution(7243721069507744568)
XLA Ops:
  10.3 5.0 %collective-permute-start.1 = (bf16[88,1024]{1,0:T(8,128)(2,1)}, bf16[88,1024]{1,0:T(8,128)(2,1)}, u32[]{:S(2)}, u32[]{:S(2)}) collective-permute-start(bf16[88,1024]{1,0:T(8,128)(2,1)} %get-tuple-element.148), channel_id=1, source_target_pairs={{0,3},{1,0},{2,1},{3,2},{4,7},{5,4},{6,5},{7,6},{8,11},{9,8},{10,9... | collective-permute-start | bytes 540680 | tf_op jit(solution)/shard_map/ppermute | solution.py:417
  20.6 10.3 %collective-permute-done.2 = bf16[88,1024]{1,0:T(8,128)(2,1)} collective-permute-done((bf16[88,1024]{1,0:T(8,128)(2,1)}, bf16[88,1024]{1,0:T(8,128)(2,1)}, u32[]{:S(2)}, u32[]{:S(2)}) %collective-permute-start.2) | collective-permute-done | bytes 180256 | tf_op jit(solution)/shard_map/ppermute | solution.py:417
  37.0 7.5 %collective-permute-done.5 = bf16[208,1024]{1,0:T(8,128)(2,1)S(1)} collective-permute-done((bf16[208,1024]{1,0:T(8,128)(2,1)}, bf16[208,1024]{1,0:T(8,128)(2,1)S(1)}, u32[]{:S(2)}, u32[]{:S(2)}) %collective-permute-start.5) | collective-permute-done | bytes 426016 | tf_op jit(solution)/shard_map/ppermute | solution.py:427
  51.7 9.6 %collective-permute-done.8 = bf16[208,1024]{1,0:T(8,128)(2,1)S(1)} collective-permute-done((bf16[208,1024]{1,0:T(8,128)(2,1)S(1)}, bf16[208,1024]{1,0:T(8,128)(2,1)S(1)}, u32[]{:S(2)}, u32[]{:S(2)}) %collective-permute-start.8) | collective-permute-done | bytes 426016 | tf_op jit(solution)/shard_map/ppermute | solution.py:428
  63.2 9.3 %collective-permute-done.9 = bf16[208,1024]{1,0:T(8,128)(2,1)S(1)} collective-permute-done((bf16[208,1024]{1,0:T(8,128)(2,1)S(1)}, bf16[208,1024]{1,0:T(8,128)(2,1)S(1)}, u32[]{:S(2)}, u32[]{:S(2)}) %collective-permute-start.9) | collective-permute-done | bytes 426016 | tf_op jit(solution)/shard_map/ppermute | solution.py:428
  77.4 6.2 %collective-permute-done.10.refs_2_ = bf16[256,1024]{1,0:T(8,128)(2,1)S(1)} collective-permute-done((bf16[256,1024]{1,0:T(8,128)(2,1)S(1)}, bf16[256,1024]{1,0:T(8,128)(2,1)S(1)}, u32[]{:S(2)}, u32[]{:S(2)}) %collective-permute-start.10) | collective-permute-done | bytes 524320 | tf_op jit(solution)/shard_map/ppermute | solution.py:427
  93.7 5.9 %collective-permute-done.14.refs_6_ = bf16[256,1024]{1,0:T(8,128)(2,1)} collective-permute-done((bf16[256,1024]{1,0:T(8,128)(2,1)S(1)}, bf16[256,1024]{1,0:T(8,128)(2,1)}, u32[]{:S(2)}, u32[]{:S(2)}) %collective-permute-start.14) | collective-permute-done | bytes 524320 | tf_op jit(solution)/shard_map/ppermute | solution.py:428
  111.0 4.8 %shard_map.152 = (bf16[1024,1024]{1,0:T(8,128)(2,1)S(1)}, bf16[1024,256]{1,0:T(8,128)(2,1)S(1)}, bf16[1024,256]{1,0:T(8,128)(2,1)S(1)}, bf16[1024,256]{1,0:T(8,128)(2,1)S(1)}) custom-call(s32[1]{0:T(128)} %bitcast.4.refs_0_, bf16[256,1024]{1,0:T(8,128)(2,1)S(1)} %fusion.18.refs_1_, bf16[256,1024]{1,0:T(8,128)(2,1)S(1)} %collective-permute-done.10.refs_2_, ...), custom_call_target="tpu_custom_call" | custom-call | flops 1610612736 | bytes 9437184 | tf_op jit(solution)/shard_map/pallas_call | solution.py:94
  117.1 8.9 %shard_map.153 = (bf16[1024,256]{1,0:T(8,128)(2,1)S(1)}, f32[2,2,896]{2,1,0:T(2,128)S(1)}, bf16[1024,256]{1,0:T(8,128)(2,1)S(1)}, bf16[1024,256]{1,0:T(8,128)(2,1)S(1)}, bf16[1024,256]{1,0:T(8,128)(2,1)S(1)}) custom-call(s32[1]{0:T(128)} %bitcast.3.refs_0_, bf16[1024,256]{1,0:T(8,128)(2,1)S(1)} %get-tuple-element.69.refs_1_, ...), custom_call_target="tpu_custom_call" | custom-call | flops 1644167168 | bytes 2097152 | tf_op jit(solution)/shard_map/pallas_call | solution.py:173
  148.6 23.0 %shard_map.154 = (bf16[4,704,1024]{2,1,0:T(8,128)(2,1)}, bf16[4,88,1024]{2,1,0:T(8,128)(2,1)}, bf16[4,88,1024]{2,1,0:T(8,128)(2,1)}, bf16[4,88,1024]{2,1,0:T(8,1...) custom-call(bf16[512,1024]{1,0:T(8,128)(2,1)} %pad_maximum_fusion.7., ...), custom_call_target="tpu_custom_call" | custom-call | flops 13287555072 | bytes 26214400 | tf_op jit(solution)/shard_map/pallas_call | solution.py:335
  182.2 4.7 %collective-permute-start.27 = (bf16[352,1024]{1,0:T(8,128)(2,1)}, bf16[352,1024]{1,0:T(8,128)(2,1)}, u32[]{:S(2)}, u32[]{:S(2)}) collective-permute-start(bf16[352,1024]{1,0:T(8,128)(2,1)} %bitcast.260), channel_id=1, source_target_pairs={{0,1},{4,5},{8,9},{12,13},{16,17},{20,21},{24,25},{28,29}} | collective-permute-start | bytes 2162696 | tf_op jit(solution)/shard_map/ppermute | solution.py:441
  195.9 9.6 %collective-permute-done.23 = bf16[256,256]{1,0:T(8,128)(2,1)S(1)} collective-permute-done((bf16[256,256]{1,0:T(8,128)(2,1)S(1)}, bf16[256,256]{1,0:T(8,128)(2,1)S(1)}, u32[]{:S(2)}, u32[]{:S(2)}) %collective-permute-start.23) | collective-permute-done | bytes 131104 | tf_op jit(solution)/shard_map/ppermute | solution.py:417
  208.3 5.4 %collective-permute-done.25 = bf16[256,256]{1,0:T(8,128)(2,1)S(1)} collective-permute-done((bf16[256,256]{1,0:T(8,128)(2,1)S(1)}, bf16[256,256]{1,0:T(8,128)(2,1)S(1)}, u32[]{:S(2)}, u32[]{:S(2)}) %collective-permute-start.25) | collective-permute-done | bytes 131104 | tf_op jit(solution)/shard_map/ppermute | solution.py:417
  213.7 5.7 %collective-permute-done.29 = bf16[2,128,1024]{2,1,0:T(8,128)(2,1)} collective-permute-done((bf16[2,128,1024]{2,1,0:T(8,128)(2,1)}, bf16[2,128,1024]{2,1,0:T(8,128)(2,1)}, u32[]{:S(2)}, u32[]{:S(2)}) %collective-permute-start.29) | collective-permute-done | bytes 524320 | tf_op jit(solution)/shard_map/ppermute | solution.py:421
  227.0 13.7 %shard_map.155 = (bf16[1024,256]{1,0:T(8,128)(2,1)S(1)}, bf16[1024,256]{1,0:T(8,128)(2,1)S(1)}, bf16[1024,256]{1,0:T(8,128)(2,1)S(1)}) custom-call(s32[1]{0:T(128)} %bitcast.3.refs_0_, bf16[1024,256]{1,0:T(8,128)(2,1)S(1)} %copy-done.11, bf16[1024,256]{1,0:T(8,128)(2,1)S(1)} %copy-done.13, bf16[1024,256]{1,0:T(8,128)(2,1)S(1)} %copy-done.15, ...), custom_call_target="tpu_custom_call" | custom-call | bytes 1048576 | tf_op jit(solution)/shard_map/pallas_call | solution.py:245
  250.2 5.4 %collective-permute-start.33 = (bf16[352,1024]{1,0:T(8,128)(2,1)}, bf16[352,1024]{1,0:T(8,128)(2,1)}, u32[]{:S(2)}, u32[]{:S(2)}) collective-permute-start(bf16[352,1024]{1,0:T(8,128)(2,1)} %add_convert_fusion.1), channel_id=1, source_target_pairs={{0,1},{1,2},{2,3},{4,5},{5,6},{6,7},{8,9},{9,10},{10,11},{12,13},{... | collective-permute-start | bytes 2162696 | tf_op jit(solution)/shard_map/ppermute | solution.py:441
  268.9 6.5 %collective-permute-done.33 = bf16[352,1024]{1,0:T(8,128)(2,1)} collective-permute-done((bf16[352,1024]{1,0:T(8,128)(2,1)}, bf16[352,1024]{1,0:T(8,128)(2,1)}, u32[]{:S(2)}, u32[]{:S(2)}) %collective-permute-start.33) | collective-permute-done | bytes 720928 | tf_op jit(solution)/shard_map/ppermute | solution.py:441
  280.5 8.1 %collective-permute-start.42 = (f32[2,1024]{1,0:T(2,128)S(1)}, f32[2,1024]{1,0:T(2,128)S(1)}, u32[]{:S(2)}, u32[]{:S(2)}) collective-permute-start(f32[2,1024]{1,0:T(2,128)S(1)} %fusion.68), channel_id=1, source_target_pairs={{0,2},{1,3},{2,0},{3,1},{4,6},{5,7},{6,4},{7,5},{8,10},{9,11},{10,... | collective-permute-start | bytes 24584 | tf_op jit(solution)/shard_map/ppermute | solution.py:421
  309.9 7.5 %collective-permute-done.35 = bf16[256,1024]{1,0:T(8,128)(2,1)S(1)} collective-permute-done((bf16[256,1024]{1,0:T(8,128)(2,1)S(1)}, bf16[256,1024]{1,0:T(8,128)(2,1)S(1)}, u32[]{:S(2)}, u32[]{:S(2)}) %collective-permute-start.35) | collective-permute-done | bytes 524320 | tf_op jit(solution)/shard_map/ppermute | solution.py:441
  317.8 4.5 %collective-permute-start.36 = (bf16[256,1024]{1,0:T(8,128)(2,1)S(1)}, bf16[256,1024]{1,0:T(8,128)(2,1)S(1)}, u32[]{:S(2)}, u32[]{:S(2)}) collective-permute-start(bf16[256,1024]{1,0:T(8,128)(2,1)S(1)} %get-tuple-element.131), channel_id=1, source_target_pairs={{0,1},{1,2},{4,5},{5,6},{8,9},{9,10},{12,13},{13,14},{16,17},{17,1... | collective-permute-start | bytes 1572872 | tf_op jit(solution)/shard_map/ppermute | solution.py:441
  323.2 5.8 %collective-permute-done.36 = bf16[256,1024]{1,0:T(8,128)(2,1)S(1)} collective-permute-done((bf16[256,1024]{1,0:T(8,128)(2,1)S(1)}, bf16[256,1024]{1,0:T(8,128)(2,1)S(1)}, u32[]{:S(2)}, u32[]{:S(2)}) %collective-permute-start.36) | collective-permute-done | bytes 524320 | tf_op jit(solution)/shard_map/ppermute | solution.py:441
  329.4 7.2 %collective-permute-start.37 = (bf16[256,1024]{1,0:T(8,128)(2,1)S(1)}, bf16[256,1024]{1,0:T(8,128)(2,1)S(1)}, u32[]{:S(2)}, u32[]{:S(2)}) collective-permute-start(bf16[256,1024]{1,0:T(8,128)(2,1)S(1)} %get-tuple-element.129), channel_id=1, source_target_pairs={{0,1},{1,2},{2,3},{4,5},{5,6},{6,7},{8,9},{9,10},{10,11},{12,13},{... | collective-permute-start | bytes 1572872 | tf_op jit(solution)/shard_map/ppermute | solution.py:441
  337.9 5.3 %collective-permute-done.37 = bf16[256,1024]{1,0:T(8,128)(2,1)S(1)} collective-permute-done((bf16[256,1024]{1,0:T(8,128)(2,1)S(1)}, bf16[256,1024]{1,0:T(8,128)(2,1)S(1)}, u32[]{:S(2)}, u32[]{:S(2)}) %collective-permute-start.37) | collective-permute-done | bytes 524320 | tf_op jit(solution)/shard_map/ppermute | solution.py:441
  350.4 7.8 %shard_map.156 = (f32[2,656,1024]{2,1,0:T(8,128)}, f32[656,1024]{1,0:T(8,128)}, f32[8,32,1024]{2,1,0:T(8,128)}, f32[3,8,4,32,256]{4,3,2,1,0:T(8,128)}) custom-call(bf16[8,400,1024]{2,1,0:T(8,128)(2,1)} %bitcast.238), custom_call_target="tpu_custom_call" | custom-call | bytes 18874368 | tf_op jit(solution)/shard_map/pallas_call | solution.py:394
  (281 shorter events, 162.7 us)
Async XLA Ops:
  7.2 129.4 %all-gather.7.cloned.1.call-start = ((), (), s32[]{:S(2)}) async-start(), calls=%async_computation.4 | async-start | bytes 2703360 | tf_op jit(solution)/shard_map/all_gather | solution.py:546
  15.3 15.6 %collective-permute-start.2 = (bf16[88,1024]{1,0:T(8,128)(2,1)}, bf16[88,1024]{1,0:T(8,128)(2,1)}, u32[]{:S(2)}, u32[]{:S(2)}) collective-permute-start(bf16[88,1024]{1,0:T(8,128)(2,1)} %get-tuple-element.148), channel_id=1, source_target_pairs={{0,2},{1,3},{2,0},{3,1},{4,6},{5,7},{6,4},{7,5},{8,10},{9,11},{10,... | collective-permute-start | bytes 540680 | tf_op jit(solution)/shard_map/ppermute | solution.py:417
  15.3 15.6 %collective-permute-start.3 = (bf16[88,1024]{1,0:T(8,128)(2,1)}, bf16[88,1024]{1,0:T(8,128)(2,1)}, u32[]{:S(2)}, u32[]{:S(2)}) collective-permute-start(bf16[88,1024]{1,0:T(8,128)(2,1)} %get-tuple-element.148), channel_id=1, source_target_pairs={{0,1},{1,2},{2,3},{3,0},{4,5},{5,6},{6,7},{7,4},{8,9},{9,10},{10,1... | collective-permute-start | bytes 540680 | tf_op jit(solution)/shard_map/ppermute | solution.py:417
  32.9 103.7 %all-gather.9.cloned.1.call-start = ((), (), s32[]{:S(2)}) async-start(), calls=%async_computation.5 | async-start | bytes 6389760 | tf_op jit(solution)/shard_map/all_gather | solution.py:550
  35.7 13.5 %collective-permute-start.4 = (bf16[208,1024]{1,0:T(8,128)(2,1)}, bf16[208,1024]{1,0:T(8,128)(2,1)S(1)}, u32[]{:S(2)}, u32[]{:S(2)}) collective-permute-start(bf16[208,1024]{1,0:T(8,128)(2,1)} %pad_maximum_fusion.12), channel_id=1, source_target_pairs={{1,0},{2,1},{3,2},{5,4},{6,5},{7,6},{9,8},{10,9},{11,10},{13,12},{... | collective-permute-start | bytes 1277960 | tf_op jit(solution)/shard_map/ppermute | solution.py:428
  51.0 12.1 %collective-permute-start.7 = (bf16[208,1024]{1,0:T(8,128)(2,1)S(1)}, bf16[208,1024]{1,0:T(8,128)(2,1)S(1)}, u32[]{:S(2)}, u32[]{:S(2)}) collective-permute-start(bf16[208,1024]{1,0:T(8,128)(2,1)S(1)} %collective-permute-done.6), channel_id=1, source_target_pairs={{2,3},{6,7},{10,11},{14,15},{18,19},{22,23},{26,27},{30,31}} | collective-permute-start | bytes 1277960 | tf_op jit(solution)/shard_map/ppermute | solution.py:427
  73.8 181.9 %reduce-scatter.3.cloned.1.call-start = ((), (), s32[]{:S(2)}) async-start(), calls=%async_computation.2 | async-start | bytes 7208960 | tf_op jit(solution)/shard_map/reduce_scatter | solution.py:613
  75.4 12.3 %collective-permute-start.13 = (bf16[256,1024]{1,0:T(8,128)(2,1)S(1)}, bf16[256,1024]{1,0:T(8,128)(2,1)S(1)}, u32[]{:S(2)}, u32[]{:S(2)}) collective-permute-start(bf16[256,1024]{1,0:T(8,128)(2,1)S(1)} %fusion.18.refs_1_), channel_id=1, source_target_pairs={{1,0},{2,1},{3,2},{5,4},{6,5},{7,6},{9,8},{10,9},{11,10},{13,12},{... | collective-permute-start | bytes 1572872 | tf_op jit(solution)/shard_map/ppermute | solution.py:428
  76.7 27.4 %collective-permute-start = (bf16[256,1024]{1,0:T(8,128)(2,1)}, bf16[256,1024]{1,0:T(8,128)(2,1)}, u32[]{:S(2)}, u32[]{:S(2)}) collective-permute-start(bf16[256,1024]{1,0:T(8,128)(2,1)} %bitcast), channel_id=1, source_target_pairs={{0,4},{4,0},{1,5},{5,1},{2,6},{6,2},{3,7},{7,3},{8,12},{12,8},{9,1... | collective-permute-start | bytes 1572872 | tf_op jit(solution)/shard_map/ppermute | solution.py:421
  92.0 14.7 %collective-permute-start.12 = (bf16[256,1024]{1,0:T(8,128)(2,1)}, bf16[256,1024]{1,0:T(8,128)(2,1)}, u32[]{:S(2)}, u32[]{:S(2)}) collective-permute-start(bf16[256,1024]{1,0:T(8,128)(2,1)} %collective-permute-done.11.refs_3_), channel_id=1, source_target_pairs={{2,3},{6,7},{10,11},{14,15},{18,19},{22,23},{26,27},{30,31}} | collective-permute-start | bytes 1572872 | tf_op jit(solution)/shard_map/ppermute | solution.py:427
  171.7 131.1 %reduce-scatter.5.cloned.1.call-start = ((), (), s32[]{:S(2)}) async-start(), calls=%async_computation.3 | async-start | bytes 2129920 | tf_op jit(solution)/shard_map/reduce_scatter | solution.py:668
  182.2 31.6 %collective-permute-start.27 = (bf16[352,1024]{1,0:T(8,128)(2,1)}, bf16[352,1024]{1,0:T(8,128)(2,1)}, u32[]{:S(2)}, u32[]{:S(2)}) collective-permute-start(bf16[352,1024]{1,0:T(8,128)(2,1)} %bitcast.260), channel_id=1, source_target_pairs={{0,1},{4,5},{8,9},{12,13},{16,17},{20,21},{24,25},{28,29}} | collective-permute-start | bytes 2162696 | tf_op jit(solution)/shard_map/ppermute | solution.py:441
  186.9 26.8 %collective-permute-start.28 = (bf16[352,1024]{1,0:T(8,128)(2,1)}, bf16[352,1024]{1,0:T(8,128)(2,1)}, u32[]{:S(2)}, u32[]{:S(2)}) collective-permute-start(bf16[352,1024]{1,0:T(8,128)(2,1)} %bitcast.259), channel_id=1, source_target_pairs={{3,2},{7,6},{11,10},{15,14},{19,18},{23,22},{27,26},{31,30}} | collective-permute-start | bytes 2162696 | tf_op jit(solution)/shard_map/ppermute | solution.py:441
  193.4 26.1 %collective-permute-start.29 = (bf16[2,128,1024]{2,1,0:T(8,128)(2,1)}, bf16[2,128,1024]{2,1,0:T(8,128)(2,1)}, u32[]{:S(2)}, u32[]{:S(2)}) collective-permute-start(bf16[2,128,1024]{2,1,0:T(8,128)(2,1)} %dynamic-slice_bitcast_fusion.1), channel_id=1, source_target_pairs={{0,16},{8,24},{16,0},{24,8},{1,17},{9,25},{17,1},{25,9},{2,18},{10... | collective-permute-start | bytes 1572872 | tf_op jit(solution)/shard_map/ppermute | solution.py:421
  195.9 12.5 %collective-permute-start.24 = (bf16[256,256]{1,0:T(8,128)(2,1)S(1)}, bf16[256,256]{1,0:T(8,128)(2,1)S(1)}, u32[]{:S(2)}, u32[]{:S(2)}) collective-permute-start(bf16[256,256]{1,0:T(8,128)(2,1)S(1)} %get-tuple-element.169), channel_id=1, source_target_pairs={{0,2},{1,3},{2,0},{3,1},{4,6},{5,7},{6,4},{7,5},{8,10},{9,11},{10,... | collective-permute-start | bytes 393224 | tf_op jit(solution)/shard_map/ppermute | solution.py:417
  220.8 25.7 %collective-permute-start.32 = (bf16[128,1024]{1,0:T(8,128)(2,1)S(1)}, bf16[128,1024]{1,0:T(8,128)(2,1)S(1)}, u32[]{:S(2)}, u32[]{:S(2)}) collective-permute-start(bf16[128,1024]{1,0:T(8,128)(2,1)S(1)} %dynamic-slice_bitcast_fusion.4), channel_id=1, source_target_pairs={{0,8},{8,0},{16,24},{24,16},{1,9},{9,1},{17,25},{25,17},{2,10},{10... | collective-permute-start | bytes 786440 | tf_op jit(solution)/shard_map/ppermute | solution.py:421
  224.5 22.1 %collective-permute-start.30 = (bf16[352,1024]{1,0:T(8,128)(2,1)S(1)}, bf16[352,1024]{1,0:T(8,128)(2,1)S(1)}, u32[]{:S(2)}, u32[]{:S(2)}) collective-permute-start(bf16[352,1024]{1,0:T(8,128)(2,1)S(1)} %get-tuple-element.166), channel_id=1, source_target_pairs={{0,1},{1,2},{4,5},{5,6},{8,9},{9,10},{12,13},{13,14},{16,17},{17,1... | collective-permute-start | bytes 2162696 | tf_op jit(solution)/shard_map/ppermute | solution.py:441
  226.0 20.6 %collective-permute-start.31 = (bf16[352,1024]{1,0:T(8,128)(2,1)S(1)}, bf16[352,1024]{1,0:T(8,128)(2,1)S(1)}, u32[]{:S(2)}, u32[]{:S(2)}) collective-permute-start(bf16[352,1024]{1,0:T(8,128)(2,1)S(1)} %get-tuple-element.165), channel_id=1, source_target_pairs={{2,1},{3,2},{6,5},{7,6},{10,9},{11,10},{14,13},{15,14},{18,17},{19... | collective-permute-start | bytes 2162696 | tf_op jit(solution)/shard_map/ppermute | solution.py:441
  247.8 21.1 %collective-permute-start.34 = (bf16[352,1024]{1,0:T(8,128)(2,1)}, bf16[352,1024]{1,0:T(8,128)(2,1)}, u32[]{:S(2)}, u32[]{:S(2)}) collective-permute-start(bf16[352,1024]{1,0:T(8,128)(2,1)} %add_convert_fusion), channel_id=1, source_target_pairs={{1,0},{2,1},{3,2},{5,4},{6,5},{7,6},{9,8},{10,9},{11,10},{13,12},{... | collective-permute-start | bytes 2162696 | tf_op jit(solution)/shard_map/ppermute | solution.py:441
  250.2 25.1 %collective-permute-start.33 = (bf16[352,1024]{1,0:T(8,128)(2,1)}, bf16[352,1024]{1,0:T(8,128)(2,1)}, u32[]{:S(2)}, u32[]{:S(2)}) collective-permute-start(bf16[352,1024]{1,0:T(8,128)(2,1)} %add_convert_fusion.1), channel_id=1, source_target_pairs={{0,1},{1,2},{2,3},{4,5},{5,6},{6,7},{8,9},{9,10},{10,11},{12,13},{... | collective-permute-start | bytes 2162696 | tf_op jit(solution)/shard_map/ppermute | solution.py:441
  260.8 89.5 %all-gather.11.cloned.1.call-start = ((), (), s32[]{:S(2)}) async-start(), calls=%async_computation.6 | async-start | bytes 7372800 | tf_op jit(solution)/shard_map/all_gather | solution.py:702
  268.8 19.8 %collective-permute-start.45 = (bf16[3,4,128,256]{3,2,0,1:T(8,128)(2,1)S(1)}, bf16[3,4,128,256]{3,2,0,1:T(8,128)(2,1)S(1)}, u32[]{:S(2)}, u32[]{:S(2)}) collective-permute-start(bf16[3,4,128,256]{3,2,0,1:T(8,128)(2,1)S(1)} %bitcast.257), channel_id=1, source_target_pairs={{0,4},{4,0},{1,5},{5,1},{2,6},{6,2},{3,7},{7,3},{8,12},{12,8},{9,1... | collective-permute-start | bytes 2359304 | tf_op jit(solution)/shard_map/ppermute | solution.py:421
  304.8 12.6 %collective-permute-start.35 = (bf16[256,1024]{1,0:T(8,128)(2,1)S(1)}, bf16[256,1024]{1,0:T(8,128)(2,1)S(1)}, u32[]{:S(2)}, u32[]{:S(2)}) collective-permute-start(bf16[256,1024]{1,0:T(8,128)(2,1)S(1)} %get-tuple-element.133), channel_id=1, source_target_pairs={{0,1},{4,5},{8,9},{12,13},{16,17},{20,21},{24,25},{28,29}} | collective-permute-start | bytes 1572872 | tf_op jit(solution)/shard_map/ppermute | solution.py:441
  329.4 13.9 %collective-permute-start.37 = (bf16[256,1024]{1,0:T(8,128)(2,1)S(1)}, bf16[256,1024]{1,0:T(8,128)(2,1)S(1)}, u32[]{:S(2)}, u32[]{:S(2)}) collective-permute-start(bf16[256,1024]{1,0:T(8,128)(2,1)S(1)} %get-tuple-element.129), channel_id=1, source_target_pairs={{0,1},{1,2},{2,3},{4,5},{5,6},{6,7},{8,9},{9,10},{10,11},{12,13},{... | collective-permute-start | bytes 1572872 | tf_op jit(solution)/shard_map/ppermute | solution.py:441
  (74 other events, 565.7 us)
Sparse Core Ops, SparseCore 0:
  33.0 36.2 all-gather.6
  74.0 58.5 all-gather.8
  171.8 76.8 reduce-scatter.2
  261.0 37.3 reduce-scatter.4
  304.9 45.4 all-gather.10
